TPU v7x, 32 devices: a whole 2x2x4 slice. The times are simulated.
32 devices in a mesh: rep: 8 (over z, core), shard: 4 (over y, x).
Axes of the slice: x: 2, y: 2, z: 4, core: 2. Of those that a mesh axis runs over, the one named last changes fastest.
Arguments:
- tokens: bfloat16 [16, 1536, 1280], P('rep', 'shard'), may hold values from -6 to 6
- lengths: int32 [16], P('rep'), may hold values from 1200 to 1500, as said below
- cotangent: bfloat16 [16, 1536, 1280], P('rep', 'shard'), may hold values from -6 to 6
- first_gain: bfloat16 [1280], P('shard'), may hold values from 0.5 to 1.5
- first_shift: bfloat16 [1280], P('shard'), may hold values from -1 to 1
- query_weight: bfloat16 [1280, 1280], P('shard'), may hold values from -0.3125 to 0.3125
- query_bias: bfloat16 [1280], P('shard'), may hold values from -1 to 1
- key_weight: bfloat16 [1280, 1280], P('shard'), may hold values from -0.15625 to 0.15625
- value_weight: bfloat16 [1280, 1280], P('shard'), may hold values from -0.15625 to 0.15625
- value_bias: bfloat16 [1280], P('shard'), may hold values from -1 to 1
- out_weight: bfloat16 [1280, 1280], P('shard'), may hold values from -1 to 1
- out_bias: bfloat16 [1280], P('shard'), may hold values from -1 to 1
- second_gain: bfloat16 [1280], P('shard'), may hold values from 0.5 to 1.5
- second_shift: bfloat16 [1280], P('shard'), may hold values from -1 to 1
- up_weight: bfloat16 [1280, 5120], P('shard'), may hold values from -0.15625 to 0.15625
- up_bias: bfloat16 [5120], P('shard'), may hold values from -1 to 1
- down_weight: bfloat16 [5120, 1280], P('shard'), may hold values from -0.078125 to 0.078125
- down_bias: bfloat16 [1280], P('shard'), may hold values from -1 to 1
Outputs:
- layer_out: bfloat16 [16, 1536, 1280], P('rep', 'shard')
- tokens_grad: bfloat16 [16, 1536, 1280], P('rep', 'shard')
- first_gain_grad: float32 [1280], P('shard')
- first_shift_grad: float32 [1280], P('shard')
- query_weight_grad: float32 [1280, 1280], P('shard')
- query_bias_grad: float32 [1280], P('shard')
- key_weight_grad: float32 [1280, 1280], P('shard')
- value_weight_grad: float32 [1280, 1280], P('shard')
- value_bias_grad: float32 [1280], P('shard')
- out_weight_grad: float32 [1280, 1280], P('shard')
- out_bias_grad: float32 [1280], P('shard')
- second_gain_grad: float32 [1280], P('shard')
- second_shift_grad: float32 [1280], P('shard')
- up_weight_grad: float32 [1280, 5120], P('shard')
- up_bias_grad: float32 [5120], P('shard')
- down_weight_grad: float32 [5120, 1280], P('shard')
- down_bias_grad: float32 [1280], P('shard')
Inputs may be any that keep to these rules, and one draw needn't show every extreme that they name: `lengths`: in each aligned block of 2 clips (those of one index of rep) at least one clip has more than 1152 live tokens; some clip of the whole array has exactly 1500.
All inputs are finite; a program needn't handle non-finite values.
Results may differ from a plain program's by a relative error of at most 0.02.
Values may be sent and summed in bfloat16 or wider, within the bound.
A program may use at most 320 MiB of HBM per device.

v0:
```python
import jax
import jax.numpy as jnp
from jax import lax
from jax.sharding import PartitionSpec as P

HEAD = 80


masked_score = -1e30


def for_sending(x):

    def short(part):
        return part.astype(jnp.bfloat16) if part.dtype == jnp.float32 else part

    return jax.tree.map(short, x)


def norm_rows(rows_in, gain, shift):
    centre = jnp.mean(rows_in, axis=-1, keepdims=True)
    centred = rows_in - centre
    spread = jnp.mean(centred * centred, axis=-1, keepdims=True)
    return centred * lax.rsqrt(spread + 1e-05) * gain + shift


def gelu_exact(values):
    return jax.nn.gelu(values, approximate=False)


def project(left, weight):
    return jnp.einsum("crd,df->crf", left, weight, preferred_element_type=jnp.float32)


def project_back(grad_rows, weight):
    return jnp.einsum("crf,df->crd", grad_rows, weight, preferred_element_type=jnp.float32)


def weight_grad(left, grad_rows):
    return jnp.einsum("crd,crf->df", left, grad_rows, preferred_element_type=jnp.float32)


def row_total(grad_rows):
    return jnp.sum(grad_rows.astype(jnp.float32), axis=(0, 1))


def split_heads(rows_in):
    count, length, _ = rows_in.shape
    return rows_in.reshape(count, length, -1, HEAD).transpose(2, 0, 1, 3)


def join_heads(heads_in):
    _, count, length, _ = heads_in.shape
    return heads_in.transpose(1, 2, 0, 3).reshape(count, length, -1)


def on_device(
    tokens,
    lengths,
    cotangent,
    first_gain,
    first_shift,
    query_weight,
    query_bias,
    key_weight,
    value_weight,
    value_bias,
    out_weight,
    out_bias,
    second_gain,
    second_shift,
    up_weight,
    up_bias,
    down_weight,
    down_bias,
):
    rows = tokens.shape[1]
    groups = lax.axis_size("shard")
    scale = HEAD ** (-0.5)
    positions = lax.axis_index("shard") * rows + jnp.arange(rows, dtype=jnp.int32)
    live_rows = positions[None, :] < lengths[:, None]
    key_live = jnp.arange(rows * groups, dtype=jnp.int32)[None, :] < lengths[:, None]

    def head_forward(parts):
        query_head, key_head, value_head = parts
        raw_scores = jnp.einsum(
            "crd,cpd->crp", query_head, key_head, preferred_element_type=jnp.float32
        )
        scores = jnp.where(key_live[:, None, :], raw_scores * scale, masked_score)
        peak = jnp.max(scores, axis=-1, keepdims=True)
        expo = jnp.exp(scores - peak)
        total = jnp.sum(expo, axis=-1, keepdims=True)
        attention = (expo / total).astype(jnp.bfloat16)
        mixed = jnp.einsum(
            "crp,cpd->crd", attention, value_head, preferred_element_type=jnp.float32
        )
        return (mixed.astype(jnp.bfloat16), (peak + jnp.log(total))[..., 0])

    def head_backward(parts):
        query_head, key_head, value_head, grad_head, log_total = parts
        raw_scores = jnp.einsum(
            "crd,cpd->crp", query_head, key_head, preferred_element_type=jnp.float32
        )
        scores = jnp.where(key_live[:, None, :], raw_scores * scale, masked_score)
        attention = jnp.exp(scores - log_total[..., None])
        attention_low = attention.astype(jnp.bfloat16)
        attn_grad = jnp.einsum(
            "crd,cpd->crp", grad_head, value_head, preferred_element_type=jnp.float32
        )
        weighted = jnp.sum(attn_grad * attention, axis=-1, keepdims=True)
        score_grad = (attention * (attn_grad - weighted) * scale).astype(jnp.bfloat16)
        query_part = jnp.einsum(
            "crp,cpd->crd", score_grad, key_head, preferred_element_type=jnp.float32
        )
        key_part = jnp.einsum(
            "crp,crd->cpd", score_grad, query_head, preferred_element_type=jnp.float32
        )
        value_part = jnp.einsum(
            "crp,crd->cpd", attention_low, grad_head, preferred_element_type=jnp.float32
        )
        return (query_part, key_part, value_part)

    (
        gain_one,
        shift_one,
        query_full,
        qbias_full,
        key_full,
        value_full,
        vbias_full,
        out_full,
        obias_full,
    ) = (
        lax.all_gather(first_gain, "shard", axis=0, tiled=True),
        lax.all_gather(first_shift, "shard", axis=0, tiled=True),
        lax.all_gather(query_weight, "shard", axis=0, tiled=True),
        lax.all_gather(query_bias, "shard", axis=0, tiled=True),
        lax.all_gather(key_weight, "shard", axis=0, tiled=True),
        lax.all_gather(value_weight, "shard", axis=0, tiled=True),
        lax.all_gather(value_bias, "shard", axis=0, tiled=True),
        lax.all_gather(out_weight, "shard", axis=0, tiled=True),
        lax.all_gather(out_bias, "shard", axis=0, tiled=True),
    )
    gain_two, shift_two, up_full, ubias_full, down_full, dbias_full = (
        lax.all_gather(second_gain, "shard", axis=0, tiled=True),
        lax.all_gather(second_shift, "shard", axis=0, tiled=True),
        lax.all_gather(up_weight, "shard", axis=0, tiled=True),
        lax.all_gather(up_bias, "shard", axis=0, tiled=True),
        lax.all_gather(down_weight, "shard", axis=0, tiled=True),
        lax.all_gather(down_bias, "shard", axis=0, tiled=True),
    )
    inputs = tokens.astype(jnp.float32)
    normed_one = norm_rows(
        inputs, gain_one.astype(jnp.float32), shift_one.astype(jnp.float32)
    ).astype(jnp.bfloat16)
    query_rows = (project(normed_one, query_full) + qbias_full.astype(jnp.float32)).astype(
        jnp.bfloat16
    )
    key_rows = project(normed_one, key_full).astype(jnp.bfloat16)
    value_rows = (project(normed_one, value_full) + vbias_full.astype(jnp.float32)).astype(
        jnp.bfloat16
    )
    keys_all, values_all = (
        lax.all_gather(key_rows, "shard", axis=1, tiled=True),
        lax.all_gather(value_rows, "shard", axis=1, tiled=True),
    )
    query_heads = split_heads(query_rows)
    mixed_heads, log_totals = lax.map(
        head_forward, (query_heads, split_heads(keys_all), split_heads(values_all))
    )
    attended = join_heads(mixed_heads)
    middle = inputs + (project(attended, out_full) + obias_full.astype(jnp.float32))
    normed_two = norm_rows(
        middle, gain_two.astype(jnp.float32), shift_two.astype(jnp.float32)
    ).astype(jnp.bfloat16)
    hidden_pre = project(normed_two, up_full) + ubias_full.astype(jnp.float32)
    hidden_act = gelu_exact(hidden_pre).astype(jnp.bfloat16)
    layer_out = (middle + (project(hidden_act, down_full) + dbias_full.astype(jnp.float32))).astype(
        jnp.bfloat16
    )
    grad_out = jnp.where(live_rows[:, :, None], cotangent, jnp.zeros_like(cotangent))
    back_mlp = (
        lax.all_gather(second_gain, "shard", axis=0, tiled=True),
        lax.all_gather(second_shift, "shard", axis=0, tiled=True),
        lax.all_gather(up_weight, "shard", axis=0, tiled=True),
        lax.all_gather(down_weight, "shard", axis=0, tiled=True),
    )
    gain_two_back, shift_two_back, up_back, down_back = back_mlp
    down_grad = weight_grad(hidden_act, grad_out)
    down_bias_total = row_total(grad_out)
    act_grad = project_back(grad_out, down_back)
    pre_grad = jax.vjp(gelu_exact, hidden_pre)[1](act_grad)[0].astype(jnp.bfloat16)
    up_grad = weight_grad(normed_two, pre_grad)
    up_bias_total = row_total(pre_grad)
    normed_two_grad = project_back(pre_grad, up_back)
    norm_two_pull = jax.vjp(
        norm_rows, middle, gain_two_back.astype(jnp.float32), shift_two_back.astype(jnp.float32)
    )[1]
    middle_part, gain_two_grad, shift_two_grad = norm_two_pull(normed_two_grad)
    middle_grad = grad_out.astype(jnp.float32) + middle_part
    mlp_terms = (gain_two_grad, shift_two_grad, up_grad, up_bias_total, down_grad, down_bias_total)
    back_attn = (
        lax.all_gather(first_gain, "shard", axis=0, tiled=True),
        lax.all_gather(first_shift, "shard", axis=0, tiled=True),
        lax.all_gather(query_weight, "shard", axis=0, tiled=True),
        lax.all_gather(key_weight, "shard", axis=0, tiled=True),
        lax.all_gather(value_weight, "shard", axis=0, tiled=True),
        lax.all_gather(out_weight, "shard", axis=0, tiled=True),
    )
    gain_one_back, shift_one_back, query_back, key_back, value_back, out_back = back_attn
    branch_grad = middle_grad.astype(jnp.bfloat16)
    out_grad = weight_grad(attended, branch_grad)
    out_bias_total = row_total(branch_grad)
    attended_grad = project_back(branch_grad, out_back).astype(jnp.bfloat16)
    keys_back, values_back = (
        lax.all_gather(key_rows, "shard", axis=1, tiled=True),
        lax.all_gather(value_rows, "shard", axis=1, tiled=True),
    )
    query_parts, key_parts, value_parts = lax.map(
        head_backward,
        (
            query_heads,
            split_heads(keys_back),
            split_heads(values_back),
            split_heads(attended_grad),
            log_totals,
        ),
    )
    query_grad_rows = join_heads(query_parts).astype(jnp.bfloat16)
    key_share, value_share = (
        lax.psum_scatter(
            join_heads(key_parts).astype(jnp.bfloat16), "shard", scatter_dimension=1, tiled=True
        ).astype(jnp.float32),
        lax.psum_scatter(
            join_heads(value_parts).astype(jnp.bfloat16), "shard", scatter_dimension=1, tiled=True
        ).astype(jnp.float32),
    )
    key_grad_rows = key_share.astype(jnp.bfloat16)
    value_grad_rows = value_share.astype(jnp.bfloat16)
    query_grad = weight_grad(normed_one, query_grad_rows)
    query_bias_total = row_total(query_grad_rows)
    key_grad = weight_grad(normed_one, key_grad_rows)
    value_grad = weight_grad(normed_one, value_grad_rows)
    value_bias_total = row_total(value_grad_rows)
    normed_one_grad = (
        project_back(query_grad_rows, query_back)
        + project_back(key_grad_rows, key_back)
        + project_back(value_grad_rows, value_back)
    )
    norm_one_pull = jax.vjp(
        norm_rows, inputs, gain_one_back.astype(jnp.float32), shift_one_back.astype(jnp.float32)
    )[1]
    input_part, gain_one_grad, shift_one_grad = norm_one_pull(normed_one_grad)
    tokens_grad = (middle_grad + input_part).astype(jnp.bfloat16)
    attn_terms = (
        gain_one_grad,
        shift_one_grad,
        query_grad,
        query_bias_total,
        key_grad,
        value_grad,
        value_bias_total,
        out_grad,
        out_bias_total,
    )
    grad_owned = jax.tree.map(
        lambda part: part.astype(jnp.float32),
        lax.psum_scatter(
            for_sending(attn_terms + mlp_terms), "shard", scatter_dimension=0, tiled=True
        ),
    )
    grad_slices = jax.tree.map(
        lambda part: part.astype(jnp.float32),
        lax.psum_scatter(for_sending(grad_owned), "rep", scatter_dimension=0, tiled=True),
    )
    grand_totals = tuple(
        jax.tree.map(
            lambda part, own: part.astype(own.dtype),
            lax.all_gather(for_sending(grad_slices), "rep", axis=0, tiled=True),
            grad_slices,
        )
    )
    return (layer_out, tokens_grad) + grand_totals


def solution(mesh):
    return jax.shard_map(
        on_device,
        mesh=mesh,
        in_specs=(
            P("rep", "shard", None),
            P("rep"),
            P("rep", "shard", None),
            P("shard"),
            P("shard"),
            P("shard", None),
            P("shard"),
            P("shard", None),
            P("shard", None),
            P("shard"),
            P("shard", None),
            P("shard"),
            P("shard"),
            P("shard"),
            P("shard", None),
            P("shard"),
            P("shard", None),
            P("shard"),
        ),
        out_specs=(
            P("rep", "shard", None),
            P("rep", "shard", None),
            P("shard"),
            P("shard"),
            P("shard", None),
            P("shard"),
            P("shard", None),
            P("shard", None),
            P("shard"),
            P("shard", None),
            P("shard"),
            P("shard"),
            P("shard"),
            P("shard", None),
            P("shard"),
            P("shard", None),
            P("shard"),
        ),
        check_vma=False,
    )
```

profile of v0, /device:TPU:0, one launch (start us, length us, event | category | flops | bytes accessed | tf_op | source)
XLA Modules:
  0.0 2127.7 jit_solution(9771065330673254968)
XLA Ops:
  17.6 18.2 all-reduce.38
  36.9 21.3 %all-gather.18.cloned.1.call-done = bf16[1280,1280]{1,0:T(8,128)(2,1)} async-done(((bf16[320,1280]{1,0:T(8,128)(2,1)}), bf16[1280,1280]{1,0:T(8,128)(2,1)}) %all-gather.18.cloned.1.call-update) | async-done | bytes 3276816 | tf_op jit(solution)/shard_map/all_gather | solution.py:139
  64.4 40.8 %all-gather.14.cloned.1.call-done = bf16[1280,1280]{1,0:T(8,128)(2,1)} async-done(((bf16[320,1280]{1,0:T(8,128)(2,1)}), bf16[1280,1280]{1,0:T(8,128)(2,1)}) %all-gather.14.cloned.1.call-update) | async-done | bytes 3276816 | tf_op jit(solution)/shard_map/all_gather | solution.py:138
  122.1 30.1 %all-gather.12.cloned.1.call-done = bf16[1280,1280]{1,0:T(8,128)(2,1)} async-done(((bf16[320,1280]{1,0:T(8,128)(2,1)}), bf16[1280,1280]{1,0:T(8,128)(2,1)}) %all-gather.12.cloned.1.call-update) | async-done | bytes 3276816 | tf_op jit(solution)/shard_map/all_gather | solution.py:136
  165.6 71.6 %all-gather.20.cloned.1.call-done = bf16[2,1536,1280]{2,1,0:T(8,128)(2,1)} async-done(((bf16[2,384,1280]{2,1,0:T(8,128)(2,1)}), bf16[2,1536,1280]{2,1,0:T(8,128)(2,1)}) %all-gather.20.cloned.1.call-update) | async-done | bytes 7864336 | tf_op jit(solution)/shard_map/all_gather | solution.py:165
  256.1 66.7 %all-gather.16.cloned.1.call-done = bf16[2,1536,1280]{2,1,0:T(8,128)(2,1)} async-done(((bf16[2,384,1280]{2,1,0:T(8,128)(2,1)}), bf16[2,1536,1280]{2,1,0:T(8,128)(2,1)}) %all-gather.16.cloned.1.call-update) | async-done | bytes 7864336 | tf_op jit(solution)/shard_map/all_gather | solution.py:164
  340.6 99.8 %while.28 = (s32[]{:T(128)}, bf16[16,2,384,80]{2,3,0,1:T(8,128)(2,1)}, f32[16,2,384]{2,1,0:T(2,128)S(1)}, bf16[16,2,384,80]{2,3,1,0:T(8,128)(2,1)}, bf16[16,2,15...) while((s32[]{:T(128)}, ...), condition=%wide.region_5.6_spmd.clone, body=%wide.region_2.5_spmd.clone.sunk | while | flops 391706880 | bytes 15423585 | solution.py:168
  448.6 49.7 %all-gather.24.cloned.1.call-done = bf16[1280,5120]{1,0:T(8,128)(2,1)} async-done(((bf16[320,5120]{1,0:T(8,128)(2,1)}), bf16[1280,5120]{1,0:T(8,128)(2,1)}) %all-gather.24.cloned.1.call-update) | async-done | bytes 13107216 | tf_op jit(solution)/shard_map/all_gather | solution.py:147
  498.3 24.5 %fusion.101 = (u8[384,5120]{1,0:T(8,128)(4,1)}, u8[384,5120]{1,0:T(8,128)(4,1)}, f32[2,384,5120]{2,1,0:T(8,128)}) fusion(f32[5120]{0:T(1024)S(1)} %bitcast.226, bf16[1280,5120]{1,0:T(8,128)(2,1)} %all-gather.24.cloned.1.call-done, f32[2,384,1280]{2,1,0:T(8,128)} %copy-done.2, f32[1280]{0:T(1024)S(1)} %convert_element_type.269, ...), kind=kOutput, calls=%fused_computation.132 | convolution fusion | flops 10122362880 | bytes 36737024 | tf_op jit(solution)/shard_map/crd,df->crf/dot_general | solution.py:32
  522.8 39.8 %multiply_convert_fusion.1 = (bf16[2,384,5120]{2,1,0:T(8,128)(2,1)}, f32[2,384,5120]{2,1,0:T(8,128)}) fusion(f32[2,384,5120]{2,1,0:T(8,128)} %get-tuple-element.281, f32[5120]{0:T(1024)S(1)} %bitcast.227, u8[384,5120]{1,0:T(8,128)(4,1)} %get-tuple-element.189, u8[384,5120]{1,0:T(8,128)(4,1)} %get-tuple-element.188), kind=kLoop, calls=%fused_computation.76 | loop fusion | flops 279183360 | bytes 43274240 | tf_op jit(solution)/shard_map/convert_element_type | solution.py:177
  562.6 64.5 %all-gather.26.cloned.1.call-done = bf16[5120,1280]{1,0:T(8,128)(2,1)} async-done(((bf16[1280,1280]{1,0:T(8,128)(2,1)}), bf16[5120,1280]{1,0:T(8,128)(2,1)}) %all-gather.26.cloned.1.call-update) | async-done | bytes 13107216 | tf_op jit(solution)/shard_map/all_gather | solution.py:149
  627.1 25.9 %fusion.139 = (bf16[5120]{0:T(1024)(128)(2,1)}, bf16[2,384,5120]{2,1,0:T(8,128)(2,1)}) fusion(f32[2,384,5120]{2,1,0:T(8,128)} %get-tuple-element.271, bf16[5120,1280]{1,0:T(8,128)(2,1)} %all-gather.26.cloned.1.call-done, bf16[2,384,1280]{2,1,0:T(8,128)(2,1)S(1)} %copy-done.6, pred[2,384]{1,0:T(4,128)(4,1)S(1)} %broadcast_compare_fusion, ...), kind=kOutput, calls=%fused_computation.172 | convolution fusion | flops 10130222080 | bytes 54426368 | tf_op jit(solution)/shard_map/crf,df->crd/dot_general | solution.py:36
  653.0 19.4 multiply_reduce_fusion.1
  686.3 474.9 %while.29 = (s32[]{:T(128)}, bf16[16,2,384,80]{2,3,0,1:T(8,128)(2,1)}, bf16[16,2,1536,80]{2,3,0,1:T(8,128)(2,1)}, bf16[16,2,1536,80]{2,3,0,1:T(8,128)(2,1)}, bf1...) while((s32[]{:T(128)}, ...), condition=%wide.region_12.13_spmd.clone, body=%wide.region_10.12_spmd.clone.sunk | while | flops 960241152 | bytes 56103032 | solution.py:219
  1161.1 20.0 copy.111
  1189.2 20.3 copy.113
  1218.6 18.0 bitcast_convert_fusion.1
  1291.1 67.8 %reduce-scatter.45.cloned.1.call-done = bf16[384,2560]{1,0:T(8,128)(2,1)} async-done(((bf16[1536,2560]{1,0:T(8,128)(2,1)}), bf16[384,2560]{1,0:T(8,128)(2,1)}) %reduce-scatter.45.cloned.1.call-update) | async-done | bytes 1966096
  1377.7 109.3 %reduce-scatter.35.cloned.1.call-done = bf16[320,5120]{1,0:T(8,128)(2,1)} async-done(((bf16[1280,5120]{1,0:T(8,128)(2,1)}), bf16[320,5120]{1,0:T(8,128)(2,1)}) %reduce-scatter.35.cloned.1.call-update) | async-done | bytes 3276816 | tf_op jit(solution)/shard_map/reduce_scatter | solution.py:268
  1487.1 47.9 %reduce-scatter.31.cloned.1.call-done = bf16[320,1280]{1,0:T(8,128)(2,1)} async-done(((bf16[1280,1280]{1,0:T(8,128)(2,1)}), bf16[320,1280]{1,0:T(8,128)(2,1)}) %reduce-scatter.31.cloned.1.call-update) | async-done | bytes 819216 | tf_op jit(solution)/shard_map/reduce_scatter | solution.py:268
  1535.1 48.6 %reduce-scatter.19.cloned.1.call-done = bf16[320,1280]{1,0:T(8,128)(2,1)} async-done(((bf16[1280,1280]{1,0:T(8,128)(2,1)}), bf16[320,1280]{1,0:T(8,128)(2,1)}) %reduce-scatter.19.cloned.1.call-update) | async-done | bytes 819216 | tf_op jit(solution)/shard_map/reduce_scatter | solution.py:268
  1583.7 128.0 %reduce-scatter.39.cloned.1.call-done = bf16[1280,1280]{1,0:T(8,128)(2,1)} async-done(((bf16[5120,1280]{1,0:T(8,128)(2,1)}), bf16[1280,1280]{1,0:T(8,128)(2,1)}) %reduce-scatter.39.cloned.1.call-update) | async-done | bytes 3276816 | tf_op jit(solution)/shard_map/reduce_scatter | solution.py:268
  1711.8 48.5 %reduce-scatter.23.cloned.1.call-done = bf16[320,1280]{1,0:T(8,128)(2,1)} async-done(((bf16[1280,1280]{1,0:T(8,128)(2,1)}), bf16[320,1280]{1,0:T(8,128)(2,1)}) %reduce-scatter.23.cloned.1.call-update) | async-done | bytes 819216 | tf_op jit(solution)/shard_map/reduce_scatter | solution.py:268
  1760.3 47.9 %reduce-scatter.27.cloned.1.call-done = bf16[320,1280]{1,0:T(8,128)(2,1)} async-done(((bf16[1280,1280]{1,0:T(8,128)(2,1)}), bf16[320,1280]{1,0:T(8,128)(2,1)}) %reduce-scatter.27.cloned.1.call-update) | async-done | bytes 819216 | tf_op jit(solution)/shard_map/reduce_scatter | solution.py:268
  1808.3 43.5 %reduce-scatter.37.cloned.1.call-done = bf16[40,5120]{1,0:T(8,128)(2,1)} async-done(((bf16[320,5120]{1,0:T(8,128)(2,1)}), bf16[40,5120]{1,0:T(8,128)(2,1)}) %reduce-scatter.37.cloned.1.call-update) | async-done | bytes 409616 | tf_op jit(solution)/shard_map/reduce_scatter | solution.py:274
  1865.2 19.4 reduce-scatter.33.cloned.1.call-done
  1917.6 18.9 all_gather.125
  1985.4 26.2 %all-reduce.36 = (bf16[320]{0:T(512)(128)(2,1)S(1)}, bf16[320]{0:T(512)(128)(2,1)S(1)}, bf16[320]{0:T(512)(128)(2,1)S(1)}, bf16[320]{0:T(512)(128)(2,1)S(1)}, bf...) all-reduce(bf16[320]{0:T(512)(128)(2,1)S(1)} %dynamic-slice.18, ...), channel_id=5, replica_groups=mesh['rep'=8,'shard'=4] {'rep'}, use_global_device_ids=true, to_apply=%region_19.20.clone | all-reduce | flops 3840 | bytes 15360
  2014.2 26.0 %all-reduce.35 = (bf16[320]{0:T(512)(128)(2,1)S(1)}, bf16[320]{0:T(512)(128)(2,1)S(1)}, bf16[320]{0:T(512)(128)(2,1)S(1)}, bf16[320]{0:T(512)(128)(2,1)S(1)}, bf...) all-reduce(bf16[320]{0:T(512)(128)(2,1)S(1)} %dynamic-update-slice., ...), channel_id=1, replica_groups=mesh['rep'=8,'shard'=4] {'rep'}, use_global_device_ids=true, to_apply=%add.8 | all-reduce | flops 3840 | bytes 15360
  2051.5 17.3 add_convert_fusion.2
  2068.7 18.5 all_gather.127
  2088.6 19.6 all_gather.128
  (450 shorter events, 889.4 us)
Async XLA Ops:
  7.2 51.0 %all-gather.18.cloned.1.call-start = ((), (), s32[]{:S(2)}) async-start(), calls=%async_computation.17 | async-start | bytes 4096000 | tf_op jit(solution)/shard_map/all_gather | solution.py:139
  7.9 97.2 %all-gather.14.cloned.1.call-start = ((), (), s32[]{:S(2)}) async-start(), calls=%async_computation.15 | async-start | bytes 4096000 | tf_op jit(solution)/shard_map/all_gather | solution.py:138
  8.7 143.5 %all-gather.12.cloned.1.call-start = ((), (), s32[]{:S(2)}) async-start(), calls=%async_computation.14 | async-start | bytes 4096000 | tf_op jit(solution)/shard_map/all_gather | solution.py:136
  9.4 227.8 %all-gather.20.cloned.1.call-start = ((), (), s32[]{:S(2)}) async-start(), calls=%async_computation.18 | async-start | bytes 9830400 | tf_op jit(solution)/shard_map/all_gather | solution.py:165
  35.8 116.4 %copy-start.11 = (f32[1280]{0:T(1024)}, f32[1280]{0:T(1024)S(1)}, u32[]{:S(2)}) copy-start(f32[1280]{0:T(1024)S(1)} %convert_element_type.133) | copy-start | bytes 15364
  35.8 116.4 %copy-start.25 = (f32[1280]{0:T(1024)}, f32[1280]{0:T(1024)S(1)}, u32[]{:S(2)}) copy-start(f32[1280]{0:T(1024)S(1)} %convert_element_type.260) | copy-start | bytes 15364
  36.2 116.0 %copy-start.14 = (f32[2,384]{1,0:T(2,128)}, f32[2,384]{1,0:T(2,128)S(1)}, u32[]{:S(2)}) copy-start(f32[2,384]{1,0:T(2,128)S(1)} %broadcast_multiply_fusion.1) | copy-start | bytes 9220
  36.9 115.3 %copy-start.16 = (f32[2,384]{1,0:T(2,128)}, f32[2,384]{1,0:T(2,128)S(1)}, u32[]{:S(2)}) copy-start(f32[2,384]{1,0:T(2,128)S(1)} %fusion.121) | copy-start | bytes 9220
  64.3 258.4 %all-gather.16.cloned.1.call-start = ((), (), s32[]{:S(2)}) async-start(), calls=%async_computation.16 | async-start | bytes 9830400 | tf_op jit(solution)/shard_map/all_gather | solution.py:164
  111.3 329.1 %all-gather.22.cloned.1.call-start = ((), (), s32[]{:S(2)}) async-start(), calls=%async_computation.19 | async-start | bytes 4096000 | tf_op jit(solution)/shard_map/all_gather | solution.py:141
  111.9 386.4 %all-gather.24.cloned.1.call-start = ((), (), s32[]{:S(2)}) async-start(), calls=%async_computation.20 | async-start | bytes 16384000 | tf_op jit(solution)/shard_map/all_gather | solution.py:147
  112.6 514.5 %all-gather.26.cloned.1.call-start = ((), (), s32[]{:S(2)}) async-start(), calls=%async_computation.21 | async-start | bytes 16384000 | tf_op jit(solution)/shard_map/all_gather | solution.py:149
  113.4 1159.3 %reduce-scatter.43.cloned.1.call-start = ((), (), s32[]{:S(2)}) async-start(), calls=%async_computation.36 | async-start | bytes 9830400
  113.5 384.8 %copy-start.27 = (f32[1280]{0:T(1024)}, f32[1280]{0:T(1024)S(1)}, u32[]{:S(2)}) copy-start(f32[1280]{0:T(1024)S(1)} %convert_element_type.269) | copy-start | bytes 15364
  522.8 104.3 %copy-start.6 = (bf16[2,384,1280]{2,1,0:T(8,128)(2,1)S(1)}, bf16[2,384,1280]{2,1,0:T(8,128)(2,1)}, u32[]{:S(2)}) copy-start(bf16[2,384,1280]{2,1,0:T(8,128)(2,1)} %param.24) | copy-start | bytes 5898244
  1189.1 169.7 %reduce-scatter.45.cloned.1.call-start = ((), (), s32[]{:S(2)}) async-start(), calls=%async_computation.37 | async-start | bytes 9830400
  1218.0 269.1 %reduce-scatter.35.cloned.1.call-start = ((), (), s32[]{:S(2)}) async-start(), calls=%async_computation.30 | async-start | bytes 16384000 | tf_op jit(solution)/shard_map/reduce_scatter | solution.py:268
  1236.7 298.3 %reduce-scatter.31.cloned.1.call-start = ((), (), s32[]{:S(2)}) async-start(), calls=%async_computation.28 | async-start | bytes 4096000 | tf_op jit(solution)/shard_map/reduce_scatter | solution.py:268
  1243.4 340.2 %reduce-scatter.19.cloned.1.call-start = ((), (), s32[]{:S(2)}) async-start(), calls=%async_computation.22 | async-start | bytes 4096000 | tf_op jit(solution)/shard_map/reduce_scatter | solution.py:268
  1250.0 461.7 %reduce-scatter.39.cloned.1.call-start = ((), (), s32[]{:S(2)}) async-start(), calls=%async_computation.33 | async-start | bytes 16384000 | tf_op jit(solution)/shard_map/reduce_scatter | solution.py:268
  1266.6 493.6 %reduce-scatter.23.cloned.1.call-start = ((), (), s32[]{:S(2)}) async-start(), calls=%async_computation.24 | async-start | bytes 4096000 | tf_op jit(solution)/shard_map/reduce_scatter | solution.py:268
  1291.0 517.2 %reduce-scatter.27.cloned.1.call-start = ((), (), s32[]{:S(2)}) async-start(), calls=%async_computation.26 | async-start | bytes 4096000 | tf_op jit(solution)/shard_map/reduce_scatter | solution.py:268
  1377.7 474.0 %reduce-scatter.37.cloned.1.call-start = ((), (), s32[]{:S(2)}) async-start(), calls=%async_computation.31 | async-start | bytes 3686400 | tf_op jit(solution)/shard_map/reduce_scatter | solution.py:274
  1487.1 368.6 %copy-start.32 = (bf16[320]{0:T(512)(128)(2,1)S(1)}, bf16[320]{0:T(512)(128)(2,1)}, u32[]{:S(2)}) copy-start(bf16[320]{0:T(512)(128)(2,1)} %param.39) | copy-start | bytes 1924
  1487.1 397.5 %reduce-scatter.33.cloned.1.call-start = ((), (), s32[]{:S(2)}) async-start(), calls=%async_computation.29 | async-start | bytes 921600 | tf_op jit(solution)/shard_map/reduce_scatter | solution.py:274
  1535.0 382.6 %reduce-scatter.21.cloned.1.call-start = ((), (), s32[]{:S(2)}) async-start(), calls=%async_computation.23 | async-start | bytes 921600 | tf_op jit(solution)/shard_map/reduce_scatter | solution.py:274
  1583.7 378.0 %reduce-scatter.41.cloned.1.call-start = ((), (), s32[]{:S(2)}) async-start(), calls=%async_computation.34 | async-start | bytes 3686400 | tf_op jit(solution)/shard_map/reduce_scatter | solution.py:274
  1711.7 357.0 %reduce-scatter.25.cloned.1.call-start = ((), (), s32[]{:S(2)}) async-start(), calls=%async_computation.25 | async-start | bytes 921600 | tf_op jit(solution)/shard_map/reduce_scatter | solution.py:274
  1760.3 328.3 %reduce-scatter.29.cloned.1.call-start = ((), (), s32[]{:S(2)}) async-start(), calls=%async_computation.27 | async-start | bytes 921600 | tf_op jit(solution)/shard_map/reduce_scatter | solution.py:274
  1808.2 301.2 %all-gather.28.cloned.1.call-start = ((), (), s32[]{:S(2)}) async-start(), calls=%async_computation.32 | async-start | bytes 3686400 | tf_op jit(solution)/shard_map/all_gather | solution.py:279
  1851.7 263.6 %all-gather.30.cloned.1.call-start = ((), (), s32[]{:S(2)}) async-start(), calls=%async_computation.35 | async-start | bytes 3686400 | tf_op jit(solution)/shard_map/all_gather | solution.py:279
  1961.8 83.7 %copy-start.19 = (f32[2,384]{1,0:T(2,128)S(1)}, f32[2,384]{1,0:T(2,128)}, u32[]{:S(2)}) copy-start(f32[2,384]{1,0:T(2,128)} %copy-done.18) | copy-start | bytes 9220
  (27 other events, 198.2 us)
Sparse Core Ops, SparseCore 0:
  9.9 48.3 all-gather.17
  60.1 45.0 all-gather.13
  107.0 45.1 all-gather.11
  153.9 83.2 all-gather.19
  239.5 83.2 all-gather.15
  324.4 45.0 all-gather.21
  371.4 126.8 all-gather.23
  500.1 126.8 all-gather.25
  1189.2 83.3 reduce-scatter.42
  1275.5 83.3 reduce-scatter.44
  1362.0 124.9 reduce-scatter.34
  1489.9 45.0 reduce-scatter.30
  1538.6 45.0 reduce-scatter.18
  1586.7 124.9 reduce-scatter.38
  1715.1 45.0 reduce-scatter.22
  1763.1 45.0 reduce-scatter.26
  1810.3 41.3 reduce-scatter.36
  1854.0 30.5 reduce-scatter.32
  1886.9 30.6 reduce-scatter.20
  1919.9 41.8 reduce-scatter.40
  1964.0 30.4 reduce-scatter.24
  1996.9 30.0 reduce-scatter.28
  2028.6 37.5 all-gather.27
  2067.7 47.6 all-gather.29
where the time goes:
time: 2140 us; the launch traced here: 2130 us
  waiting for transfers between devices  945 us (44%)
  matrix products  748 us (35%)
  blocking collectives  168 us (8%)
  local copies, waits for them, and re-layouts  144 us (7%)
  other arithmetic  101 us (5%)
    reduce_scatter x6, waiting for transfers between devices, on_device(): lax.psum_scatter(for_sending(attn_terms + mlp_terms), 'shard', scatter_di...  430 us
    dot_general x16, matrix products, head_backward(): jnp.einsum('crp,crd->cpd', score_grad, query_head, preferred_element_type...  139 us
    dot_general x16, matrix products, head_backward(): jnp.einsum('crp,cpd->crd', score_grad, key_head, preferred_element_type=j...  139 us
    unnamed x135, local copies, waits for them, and re-layouts  116 us
    reduce_scatter x6, waiting for transfers between devices, on_device(): lax.psum_scatter(for_sending(grad_owned), 'rep', scatter_dimension=0, til...  91.5 us
    unnamed x4, blocking collectives  86.9 us
    unnamed x26, waiting for transfers between devices  78 us
    all_gather x4, blocking collectives, on_device(): lax.all_gather(for_sending(grad_slices), 'rep', axis=0, tiled=True)  73 us
  transfers between devices with their start and end apart: 24, of which 20 were waited for; matrix products, arithmetic and copies ran while one was open for 20% of the time, Pallas kernels for 0%

commit v1 on v0

v1 whole, which is shorter than its diff:
```python
import functools
import math

import jax
import jax.numpy as jnp
from jax import lax
from jax.experimental import pallas as pl
from jax.experimental.pallas import tpu as pltpu
from jax.sharding import PartitionSpec as P

HEAD = 80
WIN = 256
AUG = 192
EPS = 1e-5
SCALE = HEAD**-0.5
SCALE2 = SCALE * math.log2(math.e)
DEAD = -1e30
ROWS = 256
f32 = jnp.float32
bf16 = jnp.bfloat16

ERF_P = 0.35
ERF_C = (0.19458996, 0.23381038, -0.00165479, 0.67243411, -0.66868964, 0.76616445, -0.19665448)


def params(limit=60):
    return pltpu.CompilerParams(vmem_limit_bytes=limit * 2**20)


def cost(flops, size):
    return pl.CostEstimate(flops=int(flops), bytes_accessed=int(size), transcendentals=0)


def dot(a, b):
    return jnp.dot(a, b, preferred_element_type=f32)


def dot_nt(a, b):
    return lax.dot_general(a, b, (((1,), (1,)), ((), ())), preferred_element_type=f32)


def dot_tn(a, b):
    return lax.dot_general(a, b, (((0,), (0,)), ((), ())), preferred_element_type=f32)


def gelu_pair(a):
    expo = jnp.exp2(a * a * (-0.5 * math.log2(math.e)))
    t = 1.0 / (1.0 + jnp.abs(a) * (ERF_P * math.sqrt(0.5)))
    total = ERF_C[-1]
    for c in ERF_C[-2::-1]:
        total = total * t + c
    tail = 0.5 * expo * (total * t)
    cdf = jnp.where(a >= 0, 1.0 - tail, tail)
    return a * cdf, cdf + a * (expo * (1.0 / math.sqrt(2.0 * math.pi)))


def whole(shape):
    return pl.BlockSpec(shape, lambda *_: (0,) * len(shape))


def row_block(rows, cols):
    return pl.BlockSpec((rows, cols), lambda i: (i, 0))


def standardize(x):
    centred = x - jnp.mean(x, axis=-1, keepdims=True)
    inv = lax.rsqrt(jnp.mean(centred * centred, axis=-1, keepdims=True) + EPS)
    return centred * inv, inv


def qkv_kernel(x_ref, g_ref, b_ref, w_ref, bias_ref, h_ref, q_ref, k_ref, v_ref):
    xhat, _ = standardize(x_ref[...].astype(f32))
    h = (xhat * g_ref[...] + b_ref[...]).astype(bf16)
    h_ref[...] = h
    z = dot(h, w_ref[...]) + bias_ref[...]
    width = z.shape[1] // 3
    for i, ref in enumerate((q_ref, k_ref, v_ref)):
        ref[:, :width] = z[:, i * width : (i + 1) * width].astype(bf16)
        ref[:, width:] = jnp.zeros((ref.shape[0], ref.shape[1] - width), bf16)


def qkv_call(x, gain, shift, w, bias, wide):
    n, d = x.shape
    out = jax.ShapeDtypeStruct((n, wide), bf16)
    return pl.pallas_call(
        qkv_kernel,
        grid=(n // ROWS,),
        in_specs=[
            row_block(ROWS, d),
            whole((1, d)),
            whole((1, d)),
            whole(w.shape),
            whole(bias.shape),
        ],
        out_specs=[row_block(ROWS, d)] + [row_block(ROWS, wide)] * 3,
        out_shape=[jax.ShapeDtypeStruct((n, d), bf16), out, out, out],
        compiler_params=params(),
        cost_estimate=cost(2 * n * d * w.shape[1], 4 * n * d + 2 * w.size + 6 * n * wide),
        name="project",
    )(x, gain, shift, w, bias)


def head_window(h):
    start = h * HEAD
    base = (start // 128) * 128
    off = start - base
    lane = lax.broadcasted_iota(jnp.int32, (1, WIN), 1)
    keep = jnp.where((lane >= off) & (lane < off + HEAD), 1.0, 0.0)
    return pl.ds(pl.multiple_of(base, 128), WIN), keep, lane


def put3(x, lane, first, value):
    hi = value.astype(bf16).astype(f32)
    rest = value - hi
    mid = rest.astype(bf16).astype(f32)
    low = rest - mid
    return jnp.where(
        lane == first,
        hi,
        jnp.where(lane == first + 1, mid, jnp.where(lane == first + 2, low, x)),
    )


def key_extra(rows, length):
    lane = lax.broadcasted_iota(jnp.int32, (rows, WIN), 1)
    row = lax.broadcasted_iota(jnp.int32, (rows, WIN), 0)
    dead = jnp.where(row >= length, DEAD, 0.0)
    minus = jnp.where((lane > AUG) & (lane <= AUG + 3), -1.0, 0.0)
    return jnp.where(lane == AUG, dead, minus).astype(bf16)


def attn_fwd_kernel(len_ref, q_ref, k_ref, v_ref, o_ref, lse_ref, acc, kx, *, bq):
    h = pl.program_id(0)
    n = q_ref.shape[0]
    width = o_ref.shape[1]

    @pl.when(h == 0)
    def _():
        acc[...] = jnp.zeros_like(acc)
        lse_ref[...] = jnp.zeros_like(lse_ref)
        kx[...] = key_extra(n, len_ref[0])

    win, keep, lane = head_window(h)
    low = keep.astype(bf16)
    q_one = jnp.where(lane == AUG, 1.0, 0.0).astype(bf16)
    v_one = jnp.where((lane >= AUG) & (lane < AUG + 3), 1.0, 0.0).astype(bf16)
    k = k_ref[:, win] * low + kx[...]
    v = v_ref[:, win] * low + v_one
    for i in range(n // bq):
        rows = slice(i * bq, (i + 1) * bq)
        s = dot_nt(q_ref[rows, win] * low + q_one, k)
        peak = jnp.max(s, axis=-1, keepdims=True)
        p = jnp.exp2((s - peak) * SCALE2).astype(bf16)
        o = dot(p, v)
        total = o[:, AUG : AUG + 1]
        acc[rows, win] += o * (keep * (1.0 / total))
        here = lax.broadcasted_iota(jnp.int32, (bq, 128), 1) == h
        lse = peak + jnp.log(total) * (1.0 / SCALE)
        lse_ref[rows, :] = jnp.where(here, lse, lse_ref[rows, :])

    @pl.when(h == pl.num_programs(0) - 1)
    def _():
        o_ref[...] = acc[:, :width].astype(bf16)


def attn_fwd_call(length, q, k, v, width, heads):
    n, wide = q.shape
    return pl.pallas_call(
        functools.partial(attn_fwd_kernel, bq=256),
        grid=(heads,),
        in_specs=[pl.BlockSpec(memory_space=pltpu.SMEM)] + [whole((n, wide))] * 3,
        out_specs=[whole((n, width)), whole((n, 128))],
        out_shape=[jax.ShapeDtypeStruct((n, width), bf16), jax.ShapeDtypeStruct((n, 128), f32)],
        scratch_shapes=[pltpu.VMEM((n, wide), f32), pltpu.VMEM((n, WIN), bf16)],
        compiler_params=params(),
        cost_estimate=cost(4 * n * n * WIN * heads, 8 * n * wide),
        name="attend",
    )(length, q, k, v)


def attn_bwd_kernel(
    len_ref, q_ref, k_ref, v_ref, o_ref, do_ref, lse_ref, g_ref, sum_ref, dq, dk, dv, part, qa, da, kx, *, bk
):
    h = pl.program_id(0)
    n = q_ref.shape[0]
    width = o_ref.shape[1]

    @pl.when(h == 0)
    def _():
        for ref in (dq, dk, dv):
            ref[...] = jnp.zeros_like(ref)
        kx[...] = key_extra(n, len_ref[0])

    win, keep, lane = head_window(h)
    low = keep.astype(bf16)
    v_one = jnp.where((lane >= AUG) & (lane < AUG + 3), 1.0, 0.0).astype(bf16)
    for i in range(n // ROWS):
        rows = slice(i * ROWS, (i + 1) * ROWS)
        here = lax.broadcasted_iota(jnp.int32, (ROWS, 128), 1) == h
        lse = jnp.sum(jnp.where(here, lse_ref[rows, :], 0.0), axis=-1, keepdims=True)
        q = q_ref[rows, win].astype(f32) * keep
        qa[rows, :] = jnp.where(lane == AUG, 1.0, put3(q, lane, AUG + 1, lse)).astype(bf16)
        d = do_ref[rows, win].astype(f32) * keep
        delta = jnp.sum(d * o_ref[rows, win].astype(f32), axis=-1, keepdims=True)
        da[rows, :] = put3(d, lane, AUG, -delta).astype(bf16)
    for i in range(n // bk):
        rows = slice(i * bk, (i + 1) * bk)
        k = k_ref[rows, win] * low + kx[rows, :]
        v = v_ref[rows, win] * low + v_one
        p = jnp.exp2(dot_nt(k, qa[...]) * SCALE2)
        ds = (p * dot_nt(v, da[...])).astype(bf16)
        dv[rows, win] += dot(p.astype(bf16), da[...]) * keep
        dk[rows, win] += dot(ds, qa[...]) * keep
        new = dot_tn(ds, k)
        part[...] = new if i == 0 else part[...] + new
    dq[:, win] += part[...] * keep

    @pl.when(h == pl.num_programs(0) - 1)
    def _():
        for i, (ref, factor) in enumerate(((dq, SCALE), (dk, SCALE), (dv, 1.0))):
            value = (ref[:, : g_ref.shape[1] // 3] * factor).astype(bf16)
            cols = slice(i * value.shape[1], (i + 1) * value.shape[1])
            g_ref[:, cols] = value
            sum_ref[:, cols] = jnp.sum(value.astype(f32), axis=0, keepdims=True)


def attn_bwd_call(length, q, k, v, o, do, lse, width, heads):
    n, wide = q.shape
    return pl.pallas_call(
        functools.partial(attn_bwd_kernel, bk=256),
        grid=(heads,),
        in_specs=[pl.BlockSpec(memory_space=pltpu.SMEM)]
        + [whole((n, wide))] * 5
        + [whole((n, 128))],
        out_specs=[whole((n, 3 * width)), whole((1, 3 * width))],
        out_shape=[
            jax.ShapeDtypeStruct((n, 3 * width), bf16),
            jax.ShapeDtypeStruct((1, 3 * width), f32),
        ],
        scratch_shapes=[pltpu.VMEM((n, wide), f32)] * 3
        + [pltpu.VMEM((n, WIN), f32)]
        + [pltpu.VMEM((n, WIN), bf16)] * 3,
        compiler_params=params(),
        cost_estimate=cost(10 * n * n * WIN * heads, 20 * n * wide),
        name="attend_back",
    )(length, q, k, v, o, do, lse)


def matmul_kernel(a_ref, w_ref, out_ref):
    out_ref[...] = dot(a_ref[...], w_ref[...]).astype(out_ref.dtype)


def matmul_nt_kernel(a_ref, w_ref, out_ref):
    out_ref[...] = dot_nt(a_ref[...], w_ref[...]).astype(out_ref.dtype)


def matmul_call(kernel, a, w, cols, name):
    n = a.shape[0]
    return pl.pallas_call(
        kernel,
        grid=(n // ROWS,),
        in_specs=[row_block(ROWS, a.shape[1]), whole(w.shape)],
        out_specs=row_block(ROWS, cols),
        out_shape=jax.ShapeDtypeStruct((n, cols), bf16),
        compiler_params=params(),
        cost_estimate=cost(2 * n * w.size, 2 * (a.size + w.size + n * cols)),
        name=name,
    )(a, w)


def middle_kernel(x_ref, y_ref, z_ref, bias_ref, g_ref, b_ref, mid_ref, h_ref):
    mid = x_ref[...].astype(f32) + (y_ref[...].astype(f32) + z_ref[...].astype(f32) + bias_ref[...])
    mid_ref[...] = mid
    xhat, _ = standardize(mid)
    h_ref[...] = (xhat * g_ref[...] + b_ref[...]).astype(bf16)


def middle_call(x, y, z, bias, gain, shift):
    n, d = x.shape
    block = row_block(ROWS, d)
    return pl.pallas_call(
        middle_kernel,
        grid=(n // ROWS,),
        in_specs=[block] * 3 + [whole((1, d))] * 3,
        out_specs=[block] * 2,
        out_shape=[jax.ShapeDtypeStruct((n, d), f32), jax.ShapeDtypeStruct((n, d), bf16)],
        compiler_params=params(),
        cost_estimate=cost(20 * n * d, 12 * n * d),
        name="middle",
    )(x, y, z, bias, gain, shift)


def ffn_kernel(*refs, chained, mc):
    h_ref, dz_ref, up_ref, ub_ref, dn_ref = refs[:5]
    refs = refs[5:]
    if chained:
        old_out, old_dh = refs[:2]
        refs = refs[2:]
    out_ref, dh_ref, dup_ref, ddn_ref, dub_ref, acc, dh, ht, act, grad = refs[:10]
    t = pl.program_id(0)
    n = h_ref.shape[0]

    @pl.when(t == 0)
    def _():
        ht[...] = h_ref[...].T
        if chained:
            sem = refs[10]
            copies = [
                pltpu.make_async_copy(src, dst, sem.at[i])
                for i, (src, dst) in enumerate(((old_out, acc), (old_dh, dh)))
            ]
            for c in copies:
                c.start()
            for c in copies:
                c.wait()
        else:
            acc[...] = jnp.zeros_like(acc)
            dh[...] = jnp.zeros_like(dh)

    def step(i, carry):
        rows = pl.ds(pl.multiple_of(i * mc, mc), mc)
        g, slope = gelu_pair(dot(h_ref[rows, :], up_ref[...]) + ub_ref[...])
        g = g.astype(bf16)
        da = (dot_nt(dz_ref[rows, :], dn_ref[...]) * slope).astype(bf16)
        act[rows, :] = g
        grad[rows, :] = da
        acc[rows, :] += dot(g, dn_ref[...])
        dh[rows, :] += dot_nt(da, up_ref[...])
        return carry

    lax.fori_loop(0, n // mc, step, 0)
    dub_ref[...] = jnp.sum(grad[...].astype(f32), axis=0, keepdims=True)
    dup_ref[...] = dot(ht[...], grad[...]).astype(bf16)
    ddn_ref[...] = dot_tn(act[...], dz_ref[...]).astype(bf16)

    @pl.when(t == pl.num_programs(0) - 1)
    def _():
        out_ref[...] = acc[...].astype(out_ref.dtype)
        dh_ref[...] = dh[...].astype(dh_ref.dtype)


def ffn_call(h, dz, up, bias, down, old, last, name):
    n, d = h.shape
    hidden = up.shape[1]
    bt = 256
    out = jax.ShapeDtypeStruct((n, d), bf16 if last else f32)
    chained = old is not None
    scratch = [pltpu.VMEM((n, d), f32)] * 2 + [pltpu.VMEM((d, n), bf16)] + [pltpu.VMEM((n, bt), bf16)] * 2
    once = pl.BlockSpec((n, d), lambda t: (0, 0), pipeline_mode=pl.Buffered(1))
    return pl.pallas_call(
        functools.partial(ffn_kernel, chained=chained, mc=384),
        grid=(hidden // bt,),
        in_specs=[
            once,
            once,
            pl.BlockSpec((d, bt), lambda t: (0, t)),
            pl.BlockSpec((1, bt), lambda t: (0, t)),
            pl.BlockSpec((bt, d), lambda t: (t, 0)),
        ]
        + ([pl.BlockSpec(memory_space=pl.ANY)] * 2 if chained else []),
        out_specs=[
            once,
            once,
            pl.BlockSpec((d, bt), lambda t: (0, t)),
            pl.BlockSpec((bt, d), lambda t: (t, 0)),
            pl.BlockSpec((1, bt), lambda t: (0, t)),
        ],
        out_shape=[
            out,
            out,
            jax.ShapeDtypeStruct((d, hidden), bf16),
            jax.ShapeDtypeStruct((hidden, d), bf16),
            jax.ShapeDtypeStruct((1, hidden), f32),
        ],
        scratch_shapes=scratch + ([pltpu.SemaphoreType.DMA((2,))] if chained else []),
        compiler_params=params(),
        cost_estimate=cost(12 * n * d * hidden, 8 * d * hidden + 12 * n * d),
        name=name,
    )(h, dz, up, bias, down, *(old if chained else ()))


def second_back_kernel(
    mid_ref, dh1_ref, dh2_ref, dz_ref, g_ref, w_ref, o_ref, dmid_ref, do_ref, dw_ref, sums_ref, acc
):
    i = pl.program_id(0)
    xhat, inv = standardize(mid_ref[...])
    dh = dh1_ref[...].astype(f32) + dh2_ref[...].astype(f32)
    dx = dh * g_ref[...]
    dz = dz_ref[...].astype(f32)
    dmid = dz + inv * (
        dx - jnp.mean(dx, axis=-1, keepdims=True) - xhat * jnp.mean(dx * xhat, axis=-1, keepdims=True)
    )
    dmid_ref[...] = dmid
    dy = dmid.astype(bf16)
    width = w_ref.shape[0]
    do_ref[:, :width] = dot_nt(dy, w_ref[...]).astype(bf16)
    do_ref[:, width:] = jnp.zeros((do_ref.shape[0], do_ref.shape[1] - width), bf16)

    @pl.when(i == 0)
    def _():
        acc[...] = jnp.zeros_like(acc)
        sums_ref[...] = jnp.zeros_like(sums_ref)

    acc[...] += dot_tn(o_ref[...], dy)
    for row, value in enumerate((dh * xhat, dh, dy.astype(f32), dz)):
        sums_ref[row : row + 1, :] += jnp.sum(value, axis=0, keepdims=True)

    @pl.when(i == pl.num_programs(0) - 1)
    def _():
        dw_ref[...] = acc[...].astype(bf16)


def second_back_call(mid, dh1, dh2, dz, gain, w, o, wide):
    n, d = mid.shape
    width = w.shape[0]
    block = row_block(ROWS, d)
    return pl.pallas_call(
        second_back_kernel,
        grid=(n // ROWS,),
        in_specs=[block] * 4 + [whole((1, d)), whole(w.shape), row_block(ROWS, width)],
        out_specs=[block, row_block(ROWS, wide), whole((width, d)), whole((8, d))],
        out_shape=[
            jax.ShapeDtypeStruct((n, d), f32),
            jax.ShapeDtypeStruct((n, wide), bf16),
            jax.ShapeDtypeStruct((width, d), bf16),
            jax.ShapeDtypeStruct((8, d), f32),
        ],
        scratch_shapes=[pltpu.VMEM((width, d), f32)],
        compiler_params=params(),
        cost_estimate=cost(4 * n * d * width, 14 * n * d),
        name="second_back",
    )(mid, dh1, dh2, dz, gain, w, o)


def dw_kernel(h_ref, g_ref, out_ref):
    out_ref[...] = dot_tn(h_ref[...], g_ref[...]).astype(bf16)


def dw_call(h, grads):
    n, d = h.shape
    cols = grads.shape[1]
    return pl.pallas_call(
        dw_kernel,
        grid=(d // 256,),
        in_specs=[pl.BlockSpec((n, 256), lambda i: (0, i)), whole((n, cols))],
        out_specs=row_block(256, cols),
        out_shape=jax.ShapeDtypeStruct((d, cols), bf16),
        compiler_params=params(),
        cost_estimate=cost(2 * n * d * cols, 2 * (n * d + n * cols + d * cols)),
        name="project_grad",
    )(h, grads)


def first_back_kernel(x_ref, dh1_ref, dh2_ref, dmid_ref, g_ref, dx_ref, sums_ref):
    xhat, inv = standardize(x_ref[...].astype(f32))
    dh = dh1_ref[...].astype(f32) + dh2_ref[...].astype(f32)
    dx = dh * g_ref[...]
    dx_ref[...] = (
        dmid_ref[...]
        + inv * (dx - jnp.mean(dx, axis=-1, keepdims=True) - xhat * jnp.mean(dx * xhat, axis=-1, keepdims=True))
    ).astype(bf16)

    @pl.when(pl.program_id(0) == 0)
    def _():
        sums_ref[...] = jnp.zeros_like(sums_ref)

    for row, value in enumerate((dh * xhat, dh)):
        sums_ref[row : row + 1, :] += jnp.sum(value, axis=0, keepdims=True)


def first_back_call(x, dh1, dh2, dmid, gain):
    n, d = x.shape
    block = row_block(ROWS, d)
    return pl.pallas_call(
        first_back_kernel,
        grid=(n // ROWS,),
        in_specs=[block] * 4 + [whole((1, d))],
        out_specs=[block, whole((8, d))],
        out_shape=[jax.ShapeDtypeStruct((n, d), bf16), jax.ShapeDtypeStruct((8, d), f32)],
        compiler_params=params(),
        cost_estimate=cost(20 * n * d, 12 * n * d),
        name="first_back",
    )(x, dh1, dh2, dmid, gain)


class Place:
    def __init__(self):
        self.groups = lax.axis_size("shard")
        self.reps = lax.axis_size("rep")
        self.shard = lax.axis_index("shard")
        self.rep = lax.axis_index("rep")
        self.core = lax.rem(self.rep, 2)

    def swap_core(self, x):
        return lax.ppermute(x, "rep", [(r, r ^ 1) for r in range(self.reps)])

    def swap(self, x, bit):
        return lax.ppermute(x, "shard", [(s, s ^ bit) for s in range(self.groups)])

    def gather(self, block):
        if self.groups != 4:
            return lax.all_gather(block, "shard", axis=0)
        half = block.shape[0] // 2
        one = self.swap(block, 1)
        two = self.swap(block, 2)
        three = jnp.concatenate([self.swap(one[:half], 2), self.swap(two[half:], 1)], axis=0)
        out = jnp.zeros((4,) + block.shape, block.dtype)
        for i, part in enumerate((block, one, two, three)):
            out = lax.dynamic_update_index_in_dim(out, part, self.shard ^ i, 0)
        return out

    def reduce(self, blocks):
        groups, rows, cols = blocks.shape
        if groups != 4:
            return lax.psum_scatter(blocks.reshape(groups * rows, cols), "shard", scatter_dimension=0, tiled=True)
        half = rows // 2
        low, high = slice(0, half), slice(half, rows)

        def part(i, rows_of):
            return lax.dynamic_index_in_dim(blocks, self.shard ^ i, 0, keepdims=False)[rows_of]

        a = self.swap(jnp.stack([part(1, low), part(3, low)]), 1)
        b = self.swap(jnp.stack([part(2, high), part(3, high)]), 2)
        c = self.swap(part(2, low) + a[1], 2)
        d = self.swap(part(1, high) + b[1], 1)
        return jnp.concatenate([part(0, low) + a[0] + c, part(0, high) + b[0] + d], axis=0)

    def over_reps(self, own):
        planes = self.reps // 2
        sums = lax.psum_scatter(
            own,
            "rep",
            scatter_dimension=0,
            tiled=True,
            axis_index_groups=[[2 * z + c for z in range(planes)] for c in range(2)],
        )
        both = lax.all_gather(sums, "rep", axis=0)
        rows, cols = sums.shape
        return both.reshape(planes, 2, rows, cols).transpose(1, 0, 2, 3).reshape(2, planes * rows, cols)

    def clip_perm(self, k):
        g, cl = self.groups, self.groups // 2
        pairs = []
        for r in range(self.reps):
            for s in range(g):
                to = ((r & ~1) | (s // cl)) * g + (r & 1) * cl + (s + k) % cl
                pairs.append((r * g + s, to))
        return pairs

    def to_clip(self, x):
        cl = self.groups // 2
        parts = []
        for k in range(cl):
            send = lax.dynamic_index_in_dim(x, lax.rem(self.shard + k, cl), 0, keepdims=False)
            parts.append(lax.ppermute(send, ("rep", "shard"), self.clip_perm(k)))
        out = jnp.zeros((cl,) + x.shape[1:], x.dtype)
        for k, part in enumerate(parts):
            out = lax.dynamic_update_index_in_dim(out, part, lax.rem(self.shard + cl - k, cl), 0)
        return out.reshape((-1,) + x.shape[2:])

    def from_clip(self, x):
        cl = self.groups // 2
        x = x.reshape((cl, -1) + x.shape[1:])
        out = jnp.zeros_like(x)
        for k in range(cl):
            send = lax.dynamic_index_in_dim(x, lax.rem(self.shard + cl - k, cl), 0, keepdims=False)
            part = lax.ppermute(send, ("rep", "shard"), [(b, a) for a, b in self.clip_perm(k)])
            out = lax.dynamic_update_index_in_dim(out, part, lax.rem(self.shard + k, cl), 0)
        return out

    def both_halves(self, mine):
        other = self.swap_core(mine)
        n = mine.shape[0]
        out = jnp.zeros((2,) + mine.shape, mine.dtype)
        out = lax.dynamic_update_index_in_dim(out, mine, self.core, 0)
        out = lax.dynamic_update_index_in_dim(out, other, 1 - self.core, 0)
        return out.reshape((2 * n,) + mine.shape[1:])

    def half(self, x, which):
        n = x.shape[0] // 2
        return lax.dynamic_slice_in_dim(x, which * n, n, 0)


def on_device(
    tokens,
    lengths,
    cotangent,
    first_gain,
    first_shift,
    query_weight,
    query_bias,
    key_weight,
    value_weight,
    value_bias,
    out_weight,
    out_bias,
    second_gain,
    second_shift,
    up_weight,
    up_bias,
    down_weight,
    down_bias,
):
    at = Place()
    g, core, shard = at.groups, at.core, at.shard
    cl = g // 2
    d = tokens.shape[2]
    ff = up_weight.shape[1]
    own_d = d // g
    own_f = ff // g
    attn_cols = own_d // 2
    ffn_cols = own_f // 2
    width = d // 2
    heads = width // HEAD
    wide = pl.cdiv(width, 128) * 128 + 128
    first_n = ffn_cols * 2 // 5
    pieces = ((0, first_n), (first_n, ffn_cols))

    def core_cols(w, size):
        return lax.dynamic_index_in_dim(w.reshape(w.shape[0], g, 2, size), core, 2, keepdims=False)

    vectors = (first_gain, first_shift, query_bias, value_bias, out_bias, second_gain, second_shift, down_bias)
    small = jnp.concatenate([jnp.stack(vectors), up_bias.reshape(-1, own_d)], axis=0)
    small = lax.all_gather(small, "shard", axis=0).astype(f32)
    full = [small[:, i].reshape(1, d) for i in range(len(vectors))]
    gain1, shift1, qbias, vbias, obias, gain2, shift2, dbias = full
    ubias = small[:, len(vectors) :].reshape(g, 2, ffn_cols)

    lens = lengths.astype(f32)
    other_lens = at.swap_core(lens)
    mine = shard // cl == core
    length = jnp.where(mine, lens, other_lens)[lax.rem(shard, cl)].astype(jnp.int32).reshape(1)

    x = at.both_halves(at.to_clip(tokens))
    n = x.shape[0]

    qkv_own = jnp.concatenate(
        [core_cols(w, attn_cols).reshape(own_d, width) for w in (query_weight, key_weight, value_weight)], axis=1
    )
    w_qkv = at.gather(qkv_own).reshape(d, 3 * width)
    w_out = at.gather(at.half(out_weight, core)).reshape(width, d)

    def bias_cols(b):
        return core_cols(b, attn_cols).reshape(1, width)

    bias = jnp.concatenate([bias_cols(qbias), jnp.zeros((1, width), f32), bias_cols(vbias)], axis=1)
    up_own = core_cols(up_weight, ffn_cols)
    down_own = at.half(down_weight, core)
    ub_own = lax.dynamic_index_in_dim(ubias, core, 1, keepdims=False)

    cot = at.both_halves(at.to_clip(cotangent))
    live = jnp.arange(n, dtype=jnp.int32)[:, None] < length
    dz = jnp.where(live, cot, jnp.zeros_like(cot))

    ups, downs, ubs = [], [], []
    for a, b in pieces:
        ups.append(at.gather(up_own[:, :, a:b].reshape(own_d, -1)).reshape(d, -1))
        downs.append(at.gather(down_own[a:b]).reshape(-1, d))
        ubs.append(ub_own[:, a:b].reshape(1, -1))

    h1, q, k, v = qkv_call(x, gain1, shift1, w_qkv, bias, wide)
    o, lse = attn_fwd_call(length, q, k, v, width, heads)
    y = matmul_call(matmul_kernel, o, w_out, d, "out_project")
    mid, h2 = middle_call(x, y, at.swap_core(y), obias, gain2, shift2)

    old = None
    up_own_grads, down_own_grads, ub_grads = [], [], []
    for i in range(len(pieces)):
        last = i == len(pieces) - 1
        out, dh2, dup, ddn, dub = ffn_call(h2, dz, ups[i], ubs[i], downs[i], old, last, "hidden" + str(i))
        old = (out, dh2)
        up_own_grads.append(at.reduce(dup.reshape(g, own_d, -1)))
        down_own_grads.append(at.reduce(ddn.reshape(g, -1, d)))
        ub_grads.append(dub.reshape(g, -1))
    other_out = at.swap_core(at.half(out, 1 - core))
    layer_own = at.half(mid, core) + (at.half(out, core).astype(f32) + other_out.astype(f32) + dbias)
    layer_out = at.from_clip(layer_own.astype(bf16))

    dmid, do, dwo, sums2 = second_back_call(mid, dh2, at.swap_core(dh2), dz, gain2, w_out, o, wide)
    out_own_grad = at.reduce(dwo.reshape(g, -1, d))

    o_wide = jnp.pad(o, ((0, 0), (0, wide - width)))
    grads, bias_sums = attn_bwd_call(length, q, k, v, o_wide, do, lse, width, heads)
    dwqkv = dw_call(h1, grads)
    qkv_own_grad = at.reduce(dwqkv.reshape(g, own_d, 3 * width))
    dh1 = matmul_call(matmul_nt_kernel, grads, w_qkv, d, "project_back")
    other_dh1 = at.swap_core(at.half(dh1, 1 - core))
    dx, sums1 = first_back_call(at.half(x, core), at.half(dh1, core), other_dh1, at.half(dmid, core), gain1)
    tokens_grad = at.from_clip(dx)

    up_all = at.over_reps(jnp.concatenate([u.reshape(own_d, g, -1) for u in up_own_grads], axis=2).reshape(own_d, -1))
    up_grad = up_all.reshape(2, own_d, g, ffn_cols).transpose(1, 2, 0, 3).reshape(own_d, ff).astype(f32)
    down_grad = at.over_reps(jnp.concatenate(down_own_grads, axis=0)).reshape(own_f, d).astype(f32)
    out_grad = at.over_reps(out_own_grad).reshape(own_d, d).astype(f32)
    qkv_all = at.over_reps(qkv_own_grad).reshape(2, own_d, 3, g, attn_cols)
    qkv_grads = [qkv_all[:, :, i].transpose(1, 2, 0, 3).reshape(own_d, d).astype(f32) for i in range(3)]

    def spread(v, size):
        out = jnp.zeros((g, 2, size), f32)
        return lax.dynamic_update_index_in_dim(out, v.reshape(g, size), core, 1).reshape(-1, own_d)

    pieces_small = [
        sums1[0].reshape(g, own_d),
        sums1[1].reshape(g, own_d),
        spread(bias_sums[0, :width], attn_cols),
        spread(bias_sums[0, 2 * width :], attn_cols),
        (sums2[2] * 0.5).reshape(g, own_d),
        (sums2[0] * 0.5).reshape(g, own_d),
        (sums2[1] * 0.5).reshape(g, own_d),
        (sums2[3] * 0.5).reshape(g, own_d),
    ]
    ub_sum = jnp.zeros((g, 2, ffn_cols), f32)
    ub_sum = lax.dynamic_update_index_in_dim(ub_sum, jnp.concatenate(ub_grads, axis=1), core, 1)
    packed = jnp.concatenate(
        [jnp.stack(pieces_small, axis=1), ub_sum.reshape(g, -1, own_d)], axis=1
    )
    packed = lax.psum(packed, ("rep", "shard"))
    mine_small = lax.dynamic_index_in_dim(packed, shard, 0, keepdims=False)
    s_gain1, s_shift1, s_qb, s_vb, s_ob, s_gain2, s_shift2, s_db = [mine_small[i] for i in range(8)]
    s_ub = mine_small[8:].reshape(-1)

    return (
        layer_out,
        tokens_grad,
        s_gain1,
        s_shift1,
        qkv_grads[0],
        s_qb,
        qkv_grads[1],
        qkv_grads[2],
        s_vb,
        out_grad,
        s_ob,
        s_gain2,
        s_shift2,
        up_grad,
        s_ub,
        down_grad,
        s_db,
    )


def solution(mesh):
    row, mat, vec = P("rep", "shard", None), P("shard", None), P("shard")
    return jax.shard_map(
        on_device,
        mesh=mesh,
        in_specs=(row, P("rep"), row, vec, vec, mat, vec, mat, mat, vec, mat, vec, vec, vec, mat, vec, mat, vec),
        out_specs=(row, row, vec, vec, mat, vec, mat, mat, vec, mat, vec, vec, vec, mat, vec, mat, vec),
        check_vma=False,
    )
```

time: 2140 us -> 1020 us (0.48)
  matrix products: 748 us -> 0 us
  waiting for transfers between devices: 945 us -> 269 us
  Pallas kernels: 0 us -> 304 us
  starting transfers between devices: 0.95 us -> 94.8 us
  blocking collectives: 168 us -> 88.6 us
  other arithmetic: 101 us -> 48.5 us
  local copies, waits for them, and re-layouts: 144 us -> 193 us
    dot_general x130 -> x0, matrix products: 748 us -> none  [the longest x16 139 us: head_backward(): jnp.einsum('crp,crd->cpd', score_grad, query_head, preferred_element_type...]
    reduce_scatter x12 -> x4, waiting for transfers between devices: 522 us -> 0.04 us  [over_reps(): lax.psum_scatter(own, 'rep', scatter_dimension=0, tiled=True, axis_index_...]
    all_gather x10 -> x3, waiting for transfers between devices: 345 us -> 0.01 us  [over_reps(): both = lax.all_gather(sums, 'rep', axis=0)]
    pallas_call x0 -> x11, Pallas kernels: none -> 304 us  [the longest x2 113 us: ffn_call(): pl.pallas_call(functools.partial(ffn_kernel, chained=chained, mc=384), gr...]
    ppermute x0 -> x63, waiting for transfers between devices: none -> 268 us  [the longest x48 227 us: swap(): return lax.ppermute(x, 'shard', [(s, s ^ bit) for s in range(self.groups)])]
    unnamed x135 -> x106, local copies, waits for them, and re-layouts: 116 us -> 20.4 us
    ppermute x0 -> x63, starting transfers between devices: none -> 94.5 us  [the longest x48 70.1 us: swap(): return lax.ppermute(x, 'shard', [(s, s ^ bit) for s in range(self.groups)])]
    unnamed x4 -> x0, blocking collectives: 86.9 us -> none
  transfers between devices with their start and end apart: 24 -> 70, of which waited for: 20 -> 26; matrix products, arithmetic and copies ran while one was open for 20% -> 20% of each run, Pallas kernels for 0% -> 24%
where the time goes in v1:
time: 1020 us; the launch traced here: 1010 us
  Pallas kernels  304 us (30%)
  waiting for transfers between devices  269 us (26%)
  local copies, waits for them, and re-layouts  193 us (19%)
  starting transfers between devices  94.8 us (9%)
  blocking collectives  88.6 us (9%)
  other arithmetic  48.5 us (5%)
  between operations  16.3 us (2%)
    ppermute x48, waiting for transfers between devices, swap(): return lax.ppermute(x, 'shard', [(s, s ^ bit) for s in range(self.groups)])  227 us
    pallas_call x2, Pallas kernels, ffn_call(): pl.pallas_call(functools.partial(ffn_kernel, chained=chained, mc=384), gr...  113 us
    ppermute x48, starting transfers between devices, swap(): return lax.ppermute(x, 'shard', [(s, s ^ bit) for s in range(self.groups)])  70.1 us
    pallas_call x1, Pallas kernels, attn_bwd_call(): pl.pallas_call(functools.partial(attn_bwd_kernel, bk=256), grid=(heads,),...  67.9 us
    psum x1, blocking collectives, on_device(): packed = lax.psum(packed, ('rep', 'shard'))  40.4 us
    pallas_call x1, Pallas kernels, attn_fwd_call(): pl.pallas_call(functools.partial(attn_fwd_kernel, bq=256), grid=(heads,),...  34.6 us
    convert_element_type x4, local copies, waits for them, and re-layouts, on_device(): up_all.reshape(2, own_d, g, ffn_cols).transpose(1, 2, 0, 3)  31.3 us
    ppermute x4, waiting for transfers between devices, to_clip(): parts.append(lax.ppermute(send, ('rep', 'shard'), self.clip_perm(k)))  30.7 us
  transfers between devices with their start and end apart: 70, of which 26 were waited for; matrix products, arithmetic and copies ran while one was open for 20% of the time, Pallas kernels for 24%

profile of v1, /device:TPU:0, one launch (start us, length us, event | category | flops | bytes accessed | tf_op | source)
XLA Modules:
  0.0 1014.6 jit_solution(8606772259574598705)
XLA Ops:
  14.9 7.3 reshape.390
  28.8 18.9 %all-gather.5 = bf16[4,12,320]{2,1,0:T(8,128)(2,1)S(1)} all-gather(bf16[1,12,320]{2,1,0:T(8,128)(2,1)S(1)} %bitcast.318), channel_id=2, replica_groups=mesh['rep'=8,'shard'=4] {'shard'}, dimensions={0}, use_global_device_ids=true | all-gather | bytes 38400 | tf_op jit(solution)/shard_map/all_gather | solution.py:624
  97.7 8.4 collective-permute-done.11
  121.7 30.6 %collective-permute-done.1 = bf16[384,1280]{1,0:T(8,128)(2,1)S(1)} collective-permute-done((bf16[384,1280]{1,0:T(8,128)(2,1)S(1)}, bf16[384,1280]{1,0:T(8,128)(2,1)S(1)}, u32[]{:S(2)}, u32[]{:S(2)}) %collective-permute-start.1) | collective-permute-done | bytes 983072 | tf_op jit(solution)/shard_map/ppermute | solution.py:555
  153.3 21.9 %collective-permute-start.21 = (bf16[384,1280]{1,0:T(8,128)(2,1)S(1)}, bf16[384,1280]{1,0:T(8,128)(2,1)S(1)}, u32[]{:S(2)}, u32[]{:S(2)}) collective-permute-start(bf16[384,1280]{1,0:T(8,128)(2,1)S(1)} %get-tuple-element.147), channel_id=1, source_target_pairs={{0,2},{1,3},{2,0},{3,1},{4,6},{5,7},{6,4},{7,5},{8,10},{9,11},{10,... | collective-permute-start | bytes 2949128 | tf_op jit(solution)/shard_map/ppermute | solution.py:498
  179.5 6.7 collective-permute-done.20
  186.1 16.9 %collective-permute-start.2 = (bf16[768,1280]{1,0:T(8,128)(2,1)S(1)}, bf16[768,1280]{1,0:T(8,128)(2,1)S(1)}, u32[]{:S(2)}, u32[]{:S(2)}) collective-permute-start(bf16[768,1280]{1,0:T(8,128)(2,1)S(1)} %bitcast.273), channel_id=1, source_target_pairs={{0,4},{4,0},{8,12},{12,8},{16,20},{20,16},{24,28},{28,24},{1,5},{5... | collective-permute-start | bytes 5898248 | tf_op jit(solution)/shard_map/ppermute | solution.py:495
  209.1 32.5 %collective-permute-done.6 = bf16[160,1920]{1,0:T(8,128)(2,1)S(1)} collective-permute-done((bf16[160,1920]{1,0:T(8,128)(2,1)S(1)}, bf16[160,1920]{1,0:T(8,128)(2,1)S(1)}, u32[]{:S(2)}, u32[]{:S(2)}) %collective-permute-start.6) | collective-permute-done | bytes 614432 | tf_op jit(solution)/shard_map/ppermute | solution.py:498
  246.5 15.2 %project.1 = (bf16[1536,1280]{1,0:T(8,128)(2,1)}, bf16[1536,768]{1,0:T(8,128)(2,1)}, bf16[1536,768]{1,0:T(8,128)(2,1)}, bf16[1536,768]{1,0:T(8,128)(2,1)}) custom-call(bf16[1536,1280]{1,0:T(8,128)(2,1)} %bitcast.266, f32[1,1280]{1,0:T(1,128)} %reshape_squeeze.18.g_ref, f32[1,1280]{1,0:T(1,128)} %reshape_squeeze.19.b_ref, bf16[1280,1920]{1,0:T(8,128)(2,1)} %bitcast.19.w_ref, ...), custom_call_target="tpu_custom_call" | custom-call | flops 7549747200 | bytes 19857408 | tf_op jit(solution)/shard_map/project/pallas_call | solution.py:85
  261.8 34.6 %attend.1 = (bf16[1536,640]{1,0:T(8,128)(2,1)}, f32[1536,128]{1,0:T(8,128)}) custom-call(s32[1]{0:T(128)} %convert_element_type.99.len_ref, bf16[1536,768]{1,0:T(8,128)(2,1)} %get-tuple-element.43.q_ref, bf16[1536,768]{1,0:T(8,128)(2,1)} %get-tuple-element.44.k_ref, bf16[1536,768]{1,0:T(8,128)(2,1)} %get-tuple-element.45.v_ref), custom_call_target="tpu_custom_call" | custom-call | flops 19327352832 | bytes 9437184 | tf_op jit(solution)/shard_map/attend/pallas_call | solution.py:168
  296.3 7.6 out_project.1.y_ref
  349.2 10.2 %middle.1 = (f32[1536,1280]{1,0:T(8,128)}, bf16[1536,1280]{1,0:T(8,128)(2,1)}) custom-call(bf16[1536,1280]{1,0:T(8,128)(2,1)} %bitcast.267, bf16[1536,1280]{1,0:T(8,128)(2,1)} %out_project.1.y_ref, bf16[1536,1280]{1,0:T(8,128)(2,1)} %collective-permute-done.12.z_ref, f32[1,1280]{1,0:T(1,128)} %reshape_squeeze.20.bias_ref, f32[1,1280]{1,0:T(1,128)} %reshape_squeeze.21.g_ref, ...), custom_call_target="tpu_custom_call" | custom-call | flops 39321600 | bytes 23592960 | tf_op jit(solution)/shard_map/middle/pallas_call | solution.py:281
  359.4 47.3 %hidden0.1 = (f32[1536,1280]{1,0:T(8,128)}, f32[1536,1280]{1,0:T(8,128)}, bf16[1280,1024]{1,0:T(8,128)(2,1)}, bf16[1024,1280]{1,0:T(8,128)(2,1)}, f32[1,1024]{1,0:T(1,128)}) custom-call(bf16[1536,1280]{1,0:T(8,128)(2,1)} %get-tuple-element.48.refs_0_, bf16[1536,1280]{1,0:T(8,128)(2,1)} %bitcast_select_fusion.refs_1_.dz_ref, bf16[1280,1024]{1,0:T(8,128)(2,1)} %bitcast.296, ...), custom_call_target="tpu_custom_call" | custom-call | flops 24159191040 | bytes 34078720 | tf_op jit(solution)/shard_map/hidden0/pallas_call | solution.py:350
  409.6 65.5 %hidden1.1 = (bf16[1536,1280]{1,0:T(8,128)(2,1)}, bf16[1536,1280]{1,0:T(8,128)(2,1)}, bf16[1280,1536]{1,0:T(8,128)(2,1)}, bf16[1536,1280]{1,0:T(8,128)(2,1)}, f32[1,1536]{1,0:T(1,128)}) custom-call(bf16[1536,1280]{1,0:T(8,128)(2,1)} %get-tuple-element.48.refs_0_, bf16[1536,1280]{1,0:T(8,128)(2,1)} %bitcast_select_fusion.refs_1_.dz_ref, ...), custom_call_target="tpu_custom_call" | custom-call | flops 36238786560 | bytes 39321600 | tf_op jit(solution)/shard_map/hidden1/pallas_call | solution.py:350
  482.7 32.7 %collective-permute-done.47 = bf16[2,160,1024]{2,1,0:T(8,128)(2,1)S(1)} collective-permute-done((bf16[2,160,1024]{2,1,0:T(8,128)(2,1)S(1)}, bf16[2,160,1024]{2,1,0:T(8,128)(2,1)S(1)}, u32[]{:S(2)}, u32[]{:S(2)}) %collective-permute-start.47) | collective-permute-done | bytes 655392 | tf_op jit(solution)/shard_map/ppermute | solution.py:498
  518.7 15.2 %collective-permute-done.51 = bf16[2,160,1536]{2,1,0:T(8,128)(2,1)S(1)} collective-permute-done((bf16[2,160,1536]{2,1,0:T(8,128)(2,1)S(1)}, bf16[2,160,1536]{2,1,0:T(8,128)(2,1)S(1)}, u32[]{:S(2)}, u32[]{:S(2)}) %collective-permute-start.51) | collective-permute-done | bytes 983072 | tf_op jit(solution)/shard_map/ppermute | solution.py:498
  539.4 19.2 %collective-permute-done.61 = bf16[2,192,1280]{2,1,0:T(8,128)(2,1)S(1)} collective-permute-done((bf16[2,192,1280]{2,1,0:T(8,128)(2,1)S(1)}, bf16[2,192,1280]{2,1,0:T(8,128)(2,1)S(1)}, u32[]{:S(2)}, u32[]{:S(2)}) %collective-permute-start.61) | collective-permute-done | bytes 983072 | tf_op jit(solution)/shard_map/ppermute | solution.py:498
  561.0 8.2 collective-permute-done.58
  571.3 15.3 %collective-permute-done.53 = bf16[2,160,1536]{2,1,0:T(8,128)(2,1)S(1)} collective-permute-done((bf16[2,160,1536]{2,1,0:T(8,128)(2,1)S(1)}, bf16[2,160,1536]{2,1,0:T(8,128)(2,1)S(1)}, u32[]{:S(2)}, u32[]{:S(2)}) %collective-permute-start.53) | collective-permute-done | bytes 983072 | tf_op jit(solution)/shard_map/ppermute | solution.py:498
  589.0 8.1 collective-permute-done.60
  601.0 22.5 %second_back.1 = (f32[1536,1280]{1,0:T(8,128)}, bf16[1536,768]{1,0:T(8,128)(2,1)}, bf16[640,1280]{1,0:T(8,128)(2,1)}, f32[8,1280]{1,0:T(8,128)}) custom-call(f32[1536,1280]{1,0:T(8,128)} %get-tuple-element.47.mid_ref, bf16[1536,1280]{1,0:T(8,128)(2,1)} %get-tuple-element.52.dh1_ref, bf16[1536,1280]{1,0:T(8,128)(2,1)} %collective-permute-done.35.dh2_ref, ...), custom_call_target="tpu_custom_call" | custom-call | flops 5033164800 | bytes 27525120 | tf_op jit(solution)/shard_map/second_back/pallas_call | solution.py:417
  623.5 67.9 %attend_back.1 = (bf16[1536,1920]{1,0:T(8,128)(2,1)}, f32[1,1920]{1,0:T(1,128)}) custom-call(s32[1]{0:T(128)} %convert_element_type.99.len_ref, bf16[1536,768]{1,0:T(8,128)(2,1)} %get-tuple-element.43.q_ref, bf16[1536,768]{1,0:T(8,128)(2,1)} %get-tuple-element.44.k_ref, bf16[1536,768]{1,0:T(8,128)(2,1)} %get-tuple-element.45.v_ref, ...), custom_call_target="tpu_custom_call" | custom-call | flops 48318382080 | bytes 23592960 | tf_op jit(solution)/shard_map/attend_back/pallas_call | solution.py:229
  691.4 13.3 %project_grad.1 = bf16[1280,1920]{1,0:T(8,128)(2,1)} custom-call(bf16[1536,1280]{1,0:T(8,128)(2,1)} %get-tuple-element.63.h_ref, bf16[1536,1920]{1,0:T(8,128)(2,1)} %get-tuple-element.55.a_ref.g_ref), custom_call_target="tpu_custom_call" | custom-call | flops 7549747200 | bytes 14745600 | tf_op jit(solution)/shard_map/project_grad/pallas_call | solution.py:442
  715.0 14.0 %collective-permute-done.39 = bf16[2,160,1920]{2,1,0:T(8,128)(2,1)} collective-permute-done((bf16[2,160,1920]{2,1,0:T(8,128)(2,1)}, bf16[2,160,1920]{2,1,0:T(8,128)(2,1)}, u32[]{:S(2)}, u32[]{:S(2)}) %collective-permute-start.39) | collective-permute-done | bytes 1228832 | tf_op jit(solution)/shard_map/ppermute | solution.py:498
  733.9 25.3 %collective-permute-done.41 = bf16[2,160,1920]{2,1,0:T(8,128)(2,1)S(1)} collective-permute-done((bf16[2,160,1920]{2,1,0:T(8,128)(2,1)S(1)}, bf16[2,160,1920]{2,1,0:T(8,128)(2,1)S(1)}, u32[]{:S(2)}, u32[]{:S(2)}) %collective-permute-start.41) | collective-permute-done | bytes 1228832 | tf_op jit(solution)/shard_map/ppermute | solution.py:498
  805.7 13.0 %project_back.1 = bf16[1536,1280]{1,0:T(8,128)(2,1)} custom-call(bf16[1536,1920]{1,0:T(8,128)(2,1)} %get-tuple-element.55.a_ref.g_ref, bf16[1280,1920]{1,0:T(8,128)(2,1)} %bitcast.19.w_ref), custom_call_target="tpu_custom_call" | custom-call | flops 7549747200 | bytes 14745600 | tf_op jit(solution)/shard_map/project_back/pallas_call | solution.py:259
  839.5 7.3 first_back.1
  858.4 29.3 %all-gather.2 = bf16[320,1280]{1,0:T(8,128)(2,1)S(1)} all-gather(bf16[40,1280]{1,0:T(8,128)(2,1)} %reduce-scatter.7.cloned.1.call-done), channel_id=4, replica_groups=mesh['rep'=8,'shard'=4] {'rep'}, dimensions={0}, use_global_device_ids=true | all-gather | bytes 921600 | tf_op jit(solution)/shard_map/all_gather | solution.py:537
  890.1 40.4 %psum.7 = f32[4,12,320]{2,1,0:T(8,128)S(1)} all-reduce(f32[4,12,320]{2,1,0:T(8,128)S(1)} %concatenate.61), channel_id=1, replica_groups=mesh['rep'=8,'shard'=4] {'rep','shard'}, use_global_device_ids=true, to_apply=%region_0.1 | all-reduce | flops 15360 | bytes 122880 | tf_op jit(solution)/shard_map/psum | solution.py:717
  948.0 8.3 reshape.427
  956.2 10.7 %copy.136 = f32[320,4,2,640]{3,2,1,0:T(2,128)} copy(f32[320,4,2,640]{3,1,0,2:T(4,128)} %bitcast.265) | data formatting | bytes 13107200 | tf_op jit(solution)/shard_map/convert_element_type | solution.py:692
  966.9 9.1 reshape.421
  (441 shorter events, 314.8 us)
Async XLA Ops:
  7.2 786.7 %reduce-scatter.11.cloned.1.call-start = ((), (), s32[]{:S(2)}) async-start(), calls=%async_computation.7 | async-start | bytes 2048000 | tf_op jit(solution)/shard_map/reduce_scatter | solution.py:530
  10.5 78.0 %collective-permute-start.8 = (bf16[160,1280]{1,0:T(8,128)(2,1)}, bf16[160,1280]{1,0:T(8,128)(2,1)}, u32[]{:S(2)}, u32[]{:S(2)}) collective-permute-start(bf16[160,1280]{1,0:T(8,128)(2,1)} %get-tuple-element.149), channel_id=1, source_target_pairs={{0,1},{1,0},{2,3},{3,2},{4,5},{5,4},{6,7},{7,6},{8,9},{9,8},{10,11... | collective-permute-start | bytes 1228808 | tf_op jit(solution)/shard_map/ppermute | solution.py:498
  13.4 77.6 %collective-permute-start.9 = (bf16[160,1280]{1,0:T(8,128)(2,1)}, bf16[160,1280]{1,0:T(8,128)(2,1)}, u32[]{:S(2)}, u32[]{:S(2)}) collective-permute-start(bf16[160,1280]{1,0:T(8,128)(2,1)} %get-tuple-element.149), channel_id=1, source_target_pairs={{0,2},{1,3},{2,0},{3,1},{4,6},{5,7},{6,4},{7,5},{8,10},{9,11},{10,... | collective-permute-start | bytes 1228808 | tf_op jit(solution)/shard_map/ppermute | solution.py:498
  27.9 79.4 %collective-permute-start.24 = (bf16[320,1024]{1,0:T(8,128)(2,1)}, bf16[320,1024]{1,0:T(8,128)(2,1)}, u32[]{:S(2)}, u32[]{:S(2)}) collective-permute-start(bf16[320,1024]{1,0:T(8,128)(2,1)} %bitcast.126), channel_id=1, source_target_pairs={{0,1},{1,0},{2,3},{3,2},{4,5},{5,4},{6,7},{7,6},{8,9},{9,8},{10,11... | collective-permute-start | bytes 1966088 | tf_op jit(solution)/shard_map/ppermute | solution.py:498
  28.4 82.1 %collective-permute-start.25 = (bf16[320,1024]{1,0:T(8,128)(2,1)}, bf16[320,1024]{1,0:T(8,128)(2,1)}, u32[]{:S(2)}, u32[]{:S(2)}) collective-permute-start(bf16[320,1024]{1,0:T(8,128)(2,1)} %bitcast.126), channel_id=1, source_target_pairs={{0,2},{1,3},{2,0},{3,1},{4,6},{5,7},{6,4},{7,5},{8,10},{9,11},{10,... | collective-permute-start | bytes 1966088 | tf_op jit(solution)/shard_map/ppermute | solution.py:498
  28.4 58.3 %collective-permute-start.3 = (f32[2]{0:T(128)S(1)}, f32[2]{0:T(128)S(1)}, u32[]{:S(2)}, u32[]{:S(2)}) collective-permute-start(f32[2]{0:T(128)S(1)} %convert_element_type.98), channel_id=1, source_target_pairs={{0,4},{4,0},{8,12},{12,8},{16,20},{20,16},{24,28},{28,24},{1,5},{5... | collective-permute-start | bytes 32 | tf_op jit(solution)/shard_map/ppermute | solution.py:495
  106.0 98.9 %collective-permute-start.4 = (bf16[320,1920]{1,0:T(8,128)(2,1)S(1)}, bf16[320,1920]{1,0:T(8,128)(2,1)S(1)}, u32[]{:S(2)}, u32[]{:S(2)}) collective-permute-start(bf16[320,1920]{1,0:T(8,128)(2,1)S(1)} %copy-done.19), channel_id=1, source_target_pairs={{0,1},{1,0},{2,3},{3,2},{4,5},{5,4},{6,7},{7,6},{8,9},{9,8},{10,11... | collective-permute-start | bytes 3686408 | tf_op jit(solution)/shard_map/ppermute | solution.py:498
  107.3 98.7 %collective-permute-start.5 = (bf16[320,1920]{1,0:T(8,128)(2,1)S(1)}, bf16[320,1920]{1,0:T(8,128)(2,1)S(1)}, u32[]{:S(2)}, u32[]{:S(2)}) collective-permute-start(bf16[320,1920]{1,0:T(8,128)(2,1)S(1)} %copy-done.19), channel_id=1, source_target_pairs={{0,2},{1,3},{2,0},{3,1},{4,6},{5,7},{6,4},{7,5},{8,10},{9,11},{10,... | collective-permute-start | bytes 3686408 | tf_op jit(solution)/shard_map/ppermute | solution.py:498
  120.0 57.7 %collective-permute-start.14 = (bf16[384,1280]{1,0:T(8,128)(2,1)S(1)}, bf16[384,1280]{1,0:T(8,128)(2,1)S(1)}, u32[]{:S(2)}, u32[]{:S(2)}) collective-permute-start(bf16[384,1280]{1,0:T(8,128)(2,1)S(1)} %copy-done.21), channel_id=1, source_target_pairs={{0,1},{1,0},{2,5},{3,4},{4,3},{5,2},{6,7},{7,6},{8,9},{9,8},{10,13... | collective-permute-start | bytes 2949128 | tf_op jit(solution)/shard_map/ppermute | solution.py:555
  153.3 50.3 %collective-permute-start.21 = (bf16[384,1280]{1,0:T(8,128)(2,1)S(1)}, bf16[384,1280]{1,0:T(8,128)(2,1)S(1)}, u32[]{:S(2)}, u32[]{:S(2)}) collective-permute-start(bf16[384,1280]{1,0:T(8,128)(2,1)S(1)} %get-tuple-element.147), channel_id=1, source_target_pairs={{0,2},{1,3},{2,0},{3,1},{4,6},{5,7},{6,4},{7,5},{8,10},{9,11},{10,... | collective-permute-start | bytes 2949128 | tf_op jit(solution)/shard_map/ppermute | solution.py:498
  177.7 126.3 %collective-permute-start.16 = (bf16[320,1536]{1,0:T(8,128)(2,1)}, bf16[320,1536]{1,0:T(8,128)(2,1)}, u32[]{:S(2)}, u32[]{:S(2)}) collective-permute-start(bf16[320,1536]{1,0:T(8,128)(2,1)} %bitcast.124), channel_id=1, source_target_pairs={{0,1},{1,0},{2,3},{3,2},{4,5},{5,4},{6,7},{7,6},{8,9},{9,8},{10,11... | collective-permute-start | bytes 2949128 | tf_op jit(solution)/shard_map/ppermute | solution.py:498
  186.1 58.2 %collective-permute-start.2 = (bf16[768,1280]{1,0:T(8,128)(2,1)S(1)}, bf16[768,1280]{1,0:T(8,128)(2,1)S(1)}, u32[]{:S(2)}, u32[]{:S(2)}) collective-permute-start(bf16[768,1280]{1,0:T(8,128)(2,1)S(1)} %bitcast.273), channel_id=1, source_target_pairs={{0,4},{4,0},{8,12},{12,8},{16,20},{20,16},{24,28},{28,24},{1,5},{5... | collective-permute-start | bytes 5898248 | tf_op jit(solution)/shard_map/ppermute | solution.py:495
  203.6 105.5 %collective-permute-start.17 = (bf16[320,1536]{1,0:T(8,128)(2,1)}, bf16[320,1536]{1,0:T(8,128)(2,1)}, u32[]{:S(2)}, u32[]{:S(2)}) collective-permute-start(bf16[320,1536]{1,0:T(8,128)(2,1)} %bitcast.124), channel_id=1, source_target_pairs={{0,2},{1,3},{2,0},{3,1},{4,6},{5,7},{6,4},{7,5},{8,10},{9,11},{10,... | collective-permute-start | bytes 2949128 | tf_op jit(solution)/shard_map/ppermute | solution.py:498
  241.6 66.3 %collective-permute-start.26 = (bf16[160,1024]{1,0:T(8,128)(2,1)}, bf16[160,1024]{1,0:T(8,128)(2,1)}, u32[]{:S(2)}, u32[]{:S(2)}) collective-permute-start(bf16[160,1024]{1,0:T(8,128)(2,1)} %slice.552), channel_id=1, source_target_pairs={{0,2},{1,3},{2,0},{3,1},{4,6},{5,7},{6,4},{7,5},{8,10},{9,11},{10,... | collective-permute-start | bytes 983048 | tf_op jit(solution)/shard_map/ppermute | solution.py:498
  241.9 70.4 %collective-permute-start.27 = (bf16[160,1024]{1,0:T(8,128)(2,1)}, bf16[160,1024]{1,0:T(8,128)(2,1)}, u32[]{:S(2)}, u32[]{:S(2)}) collective-permute-start(bf16[160,1024]{1,0:T(8,128)(2,1)} %slice.553), channel_id=1, source_target_pairs={{0,1},{1,0},{2,3},{3,2},{4,5},{5,4},{6,7},{7,6},{8,9},{9,8},{10,11... | collective-permute-start | bytes 983048 | tf_op jit(solution)/shard_map/ppermute | solution.py:498
  244.3 100.8 %collective-permute-start.15 = (bf16[768,1280]{1,0:T(8,128)(2,1)}, bf16[768,1280]{1,0:T(8,128)(2,1)}, u32[]{:S(2)}, u32[]{:S(2)}) collective-permute-start(bf16[768,1280]{1,0:T(8,128)(2,1)} %bitcast.31), channel_id=1, source_target_pairs={{0,4},{4,0},{8,12},{12,8},{16,20},{20,16},{24,28},{28,24},{1,5},{5... | collective-permute-start | bytes 5898248 | tf_op jit(solution)/shard_map/ppermute | solution.py:495
  408.8 71.6 %collective-permute-start.55 = (bf16[2,128,1280]{2,1,0:T(8,128)(2,1)}, bf16[2,128,1280]{2,1,0:T(8,128)(2,1)}, u32[]{:S(2)}, u32[]{:S(2)}) collective-permute-start(bf16[2,128,1280]{2,1,0:T(8,128)(2,1)} %pad_maximum_fusion.14), channel_id=1, source_target_pairs={{0,1},{1,0},{2,3},{3,2},{4,5},{5,4},{6,7},{7,6},{8,9},{9,8},{10,11... | collective-permute-start | bytes 1966088 | tf_op jit(solution)/shard_map/ppermute | solution.py:498
  479.0 54.8 %collective-permute-start.51 = (bf16[2,160,1536]{2,1,0:T(8,128)(2,1)S(1)}, bf16[2,160,1536]{2,1,0:T(8,128)(2,1)S(1)}, u32[]{:S(2)}, u32[]{:S(2)}) collective-permute-start(bf16[2,160,1536]{2,1,0:T(8,128)(2,1)S(1)} %pad_maximum_fusion.6), channel_id=1, source_target_pairs={{0,1},{1,0},{2,3},{3,2},{4,5},{5,4},{6,7},{7,6},{8,9},{9,8},{10,11... | collective-permute-start | bytes 2949128 | tf_op jit(solution)/shard_map/ppermute | solution.py:498
  480.4 120.6 %collective-permute-start.35 = (bf16[1536,1280]{1,0:T(8,128)(2,1)}, bf16[1536,1280]{1,0:T(8,128)(2,1)}, u32[]{:S(2)}, u32[]{:S(2)}) collective-permute-start(bf16[1536,1280]{1,0:T(8,128)(2,1)} %get-tuple-element.52.dh1_ref), channel_id=1, source_target_pairs={{0,4},{4,0},{8,12},{12,8},{16,20},{20,16},{24,28},{28,24},{1,5},{5... | collective-permute-start | bytes 11796488 | tf_op jit(solution)/shard_map/ppermute | solution.py:495
  481.6 56.3 %collective-permute-start.57 = (bf16[2,128,1280]{2,1,0:T(8,128)(2,1)S(1)}, bf16[2,128,1280]{2,1,0:T(8,128)(2,1)S(1)}, u32[]{:S(2)}, u32[]{:S(2)}) collective-permute-start(bf16[2,128,1280]{2,1,0:T(8,128)(2,1)S(1)} %pad_maximum_fusion.15), channel_id=1, source_target_pairs={{0,2},{1,3},{2,0},{3,1},{4,6},{5,7},{6,4},{7,5},{8,10},{9,11},{10,... | collective-permute-start | bytes 1966088 | tf_op jit(solution)/shard_map/ppermute | solution.py:498
  536.4 172.0 %collective-permute-start.48 = (bf16[160,1024]{1,0:T(8,128)(2,1)}, bf16[160,1024]{1,0:T(8,128)(2,1)}, u32[]{:S(2)}, u32[]{:S(2)}) collective-permute-start(bf16[160,1024]{1,0:T(8,128)(2,1)} %get-tuple-element.185), channel_id=1, source_target_pairs={{0,2},{1,3},{2,0},{3,1},{4,6},{5,7},{6,4},{7,5},{8,10},{9,11},{10,... | collective-permute-start | bytes 983048 | tf_op jit(solution)/shard_map/ppermute | solution.py:498
  586.7 123.7 %collective-permute-start.52 = (bf16[160,1536]{1,0:T(8,128)(2,1)}, bf16[160,1536]{1,0:T(8,128)(2,1)}, u32[]{:S(2)}, u32[]{:S(2)}) collective-permute-start(bf16[160,1536]{1,0:T(8,128)(2,1)} %get-tuple-element.166), channel_id=1, source_target_pairs={{0,2},{1,3},{2,0},{3,1},{4,6},{5,7},{6,4},{7,5},{8,10},{9,11},{10,... | collective-permute-start | bytes 1474568 | tf_op jit(solution)/shard_map/ppermute | solution.py:498
  597.2 111.2 %collective-permute-start.50 = (bf16[160,1024]{1,0:T(8,128)(2,1)}, bf16[160,1024]{1,0:T(8,128)(2,1)}, u32[]{:S(2)}, u32[]{:S(2)}) collective-permute-start(bf16[160,1024]{1,0:T(8,128)(2,1)} %fusion.30), channel_id=1, source_target_pairs={{0,1},{1,0},{2,3},{3,2},{4,5},{5,4},{6,7},{7,6},{8,9},{9,8},{10,11... | collective-permute-start | bytes 983048 | tf_op jit(solution)/shard_map/ppermute | solution.py:498
  598.3 112.1 %collective-permute-start.54 = (bf16[160,1536]{1,0:T(8,128)(2,1)}, bf16[160,1536]{1,0:T(8,128)(2,1)}, u32[]{:S(2)}, u32[]{:S(2)}) collective-permute-start(bf16[160,1536]{1,0:T(8,128)(2,1)} %fusion.17), channel_id=1, source_target_pairs={{0,1},{1,0},{2,3},{3,2},{4,5},{5,4},{6,7},{7,6},{8,9},{9,8},{10,11... | collective-permute-start | bytes 1474568 | tf_op jit(solution)/shard_map/ppermute | solution.py:498
  600.9 193.6 %reduce-scatter.9.cloned.1.call-start = ((), (), s32[]{:S(2)}) async-start(), calls=%async_computation.6 | async-start | bytes 2048000 | tf_op jit(solution)/shard_map/reduce_scatter | solution.py:530
  715.0 116.3 %reduce-scatter.5.cloned.1.call-start = ((), (), s32[]{:S(2)}) async-start(), calls=%async_computation.4 | async-start | bytes 1536000 | tf_op jit(solution)/shard_map/reduce_scatter | solution.py:530
  774.2 84.2 %reduce-scatter.7.cloned.1.call-start = ((), (), s32[]{:S(2)}) async-start(), calls=%async_computation.5 | async-start | bytes 512000 | tf_op jit(solution)/shard_map/reduce_scatter | solution.py:530
  793.9 142.6 %all-gather.14.cloned.1.call-start = ((), (), s32[]{:S(2)}) async-start(), calls=%async_computation.10 | async-start | bytes 3686400 | tf_op jit(solution)/shard_map/all_gather | solution.py:537
  794.5 147.4 %all-gather.12.cloned.1.call-start = ((), (), s32[]{:S(2)}) async-start(), calls=%async_computation.9 | async-start | bytes 3686400 | tf_op jit(solution)/shard_map/all_gather | solution.py:537
  795.0 181.0 %all-gather.10.cloned.1.call-start = ((), (), s32[]{:S(2)}) async-start(), calls=%async_computation.8 | async-start | bytes 2764800 | tf_op jit(solution)/shard_map/all_gather | solution.py:537
  848.5 83.4 %collective-permute-start.37 = (bf16[384,1280]{1,0:T(8,128)(2,1)S(1)}, bf16[384,1280]{1,0:T(8,128)(2,1)S(1)}, u32[]{:S(2)}, u32[]{:S(2)}) collective-permute-start(bf16[384,1280]{1,0:T(8,128)(2,1)S(1)} %get-tuple-element.191), channel_id=1, source_target_pairs={{0,0},{1,1},{4,2},{5,3},{2,4},{3,5},{6,6},{7,7},{8,8},{9,9},{12,10... | collective-permute-start | bytes 2949128 | tf_op jit(solution)/shard_map/ppermute | solution.py:567
  858.1 76.2 %collective-permute-start.38 = (bf16[384,1280]{1,0:T(8,128)(2,1)S(1)}, bf16[384,1280]{1,0:T(8,128)(2,1)}, u32[]{:S(2)}, u32[]{:S(2)}) collective-permute-start(bf16[384,1280]{1,0:T(8,128)(2,1)S(1)} %get-tuple-element.190), channel_id=1, source_target_pairs={{1,0},{0,1},{5,2},{4,3},{3,4},{2,5},{7,6},{6,7},{9,8},{8,9},{13,10... | collective-permute-start | bytes 2949128 | tf_op jit(solution)/shard_map/ppermute | solution.py:567
  (84 other events, 1263.6 us)
Sparse Core Ops, SparseCore 0:
  601.0 36.7 reduce-scatter.10
  715.1 36.8 reduce-scatter.8
  774.3 29.7 reduce-scatter.4
  806.9 19.5 reduce-scatter.6
  828.0 37.6 all-gather.13
  867.2 42.6 all-gather.11
  911.5 31.5 all-gather.9

commit v2 on v1

v2 whole, which is shorter than its diff:
```python
import functools
import math

import jax
import jax.numpy as jnp
from jax import lax
from jax.experimental import pallas as pl
from jax.experimental.pallas import tpu as pltpu
from jax.sharding import PartitionSpec as P

HEAD = 80
WIN = 256
AUG = 192
EPS = 1e-5
SCALE = HEAD**-0.5
SCALE2 = SCALE * math.log2(math.e)
DEAD = -1e30
ROWS = 256
GAIN1, SHIFT1, QBIAS, VBIAS, OBIAS, GAIN2, SHIFT2, DBIAS, LENGTHS = [slice(i, i + 1) for i in range(9)]
UBIAS = 9
FFN_TILE = 256
FFN_ROWS = 384
f32 = jnp.float32
bf16 = jnp.bfloat16
MESH = pl.DeviceIdType.MESH

ERF_P = 0.35
ERF_C = (0.19458996, 0.23381038, -0.00165479, 0.67243411, -0.66868964, 0.76616445, -0.19665448)


def params(limit=60):
    return pltpu.CompilerParams(vmem_limit_bytes=limit * 2**20)


def cost(flops, size):
    return pl.CostEstimate(flops=int(flops), bytes_accessed=int(size), transcendentals=0)


def dot(a, b):
    return jnp.dot(a, b, preferred_element_type=f32)


def dot_nt(a, b):
    return lax.dot_general(a, b, (((1,), (1,)), ((), ())), preferred_element_type=f32)


def dot_tn(a, b):
    return lax.dot_general(a, b, (((0,), (0,)), ((), ())), preferred_element_type=f32)


def gelu_pair(a):
    expo = jnp.exp2(a * a * (-0.5 * math.log2(math.e)))
    t = 1.0 / (1.0 + jnp.abs(a) * (ERF_P * math.sqrt(0.5)))
    total = ERF_C[-1]
    for c in ERF_C[-2::-1]:
        total = total * t + c
    tail = 0.5 * expo * (total * t)
    cdf = jnp.where(a >= 0, 1.0 - tail, tail)
    return a * cdf, cdf + a * (expo * (1.0 / math.sqrt(2.0 * math.pi)))


def whole(shape):
    return pl.BlockSpec(shape, lambda *_: (0,) * len(shape))


def row_block(rows, cols):
    return pl.BlockSpec((rows, cols), lambda i: (i, 0))


def standardize(x):
    centred = x - jnp.mean(x, axis=-1, keepdims=True)
    inv = lax.rsqrt(jnp.mean(centred * centred, axis=-1, keepdims=True) + EPS)
    return centred * inv, inv


class Link:
    def __init__(self, sems):
        self.send, self.recv, self.local = sems
        self.next = 0
        self.next_local = 0
        self.groups = lax.axis_size("shard")
        self.rep = lax.axis_index("rep")
        self.shard = lax.axis_index("shard")
        self.core = lax.rem(self.rep, 2)
        self.half = self.groups // 2

    def meet_plane(self):
        barrier = pltpu.get_barrier_semaphore()
        base = self.rep - self.core
        for c in range(2):
            for p in range(self.groups):
                if c or p:
                    to = (base + (self.core ^ c), self.shard ^ p)
                    pl.semaphore_signal(barrier, inc=1, device_id=to, device_id_type=MESH)
        pl.semaphore_wait(barrier, 2 * self.groups - 1)

    def meet_core(self):
        barrier = pltpu.get_barrier_semaphore()
        pl.semaphore_signal(barrier, inc=1, device_id=self.sibling(), device_id_type=MESH)
        pl.semaphore_wait(barrier, 1)

    def sibling(self):
        return (self.rep ^ 1, self.shard)

    def slots(self, count):
        first = self.next
        self.next += count
        return first

    def local_slots(self, count):
        first = self.next_local
        self.next_local += count
        return first

    def remote(self, src, dst, send, recv, to):
        return pltpu.make_async_remote_copy(
            src_ref=src,
            dst_ref=dst,
            send_sem=self.send.at[send],
            recv_sem=self.recv.at[recv],
            device_id=to,
            device_id_type=MESH,
        )

    def here(self, src, dst, slot):
        return pltpu.make_async_copy(src, dst, self.local.at[slot])


class Gather:
    def __init__(self, link, src, dst):
        self.link, self.src, self.dst = link, src, dst
        self.rows = src.shape[0]
        self.base = link.slots(max(4, link.groups - 1))
        self.keep = link.here(src, dst.at[link.shard], link.local_slots(1))

    def first(self):
        link = self.link
        peers = (1, 2) if link.groups == 4 else range(1, link.groups)
        return [
            link.remote(self.src, self.dst.at[link.shard], self.base + i, self.base + i, (link.rep, link.shard ^ p))
            for i, p in enumerate(peers)
        ]

    def second(self):
        link = self.link
        if link.groups != 4:
            return []
        cut = self.rows // 2
        parts = ((1, 2, pl.ds(0, cut)), (2, 1, pl.ds(cut, self.rows - cut)))
        out = []
        for i, (origin, to, rows) in enumerate(parts):
            ref = self.dst.at[link.shard ^ origin, rows]
            out.append(link.remote(ref, ref, self.base + 2 + i, self.base + 2 + i, (link.rep, link.shard ^ to)))
        return out

    def start(self):
        self.keep.start()
        for c in self.first():
            c.start()

    def forward(self):
        for c, d in zip(self.first(), self.second()):
            c.wait_recv()
            d.start()

    def finish(self):
        second = self.second()
        for c in self.first():
            if not second:
                c.wait_recv()
            c.wait_send()
        for c in second:
            c.wait()
        self.keep.wait()


class ToClip:
    def __init__(self, link, src, dst):
        self.link, self.src, self.dst = link, src, dst
        self.rows = src.shape[1]
        self.base = link.slots(link.half + 1)
        self.keep = link.local_slots(1)

    def copy(self, j):
        link = self.link
        core = lax.div(link.shard, link.half)
        to = (link.rep - link.core + core, link.core * link.half + j)
        mine = (core == link.core) & (link.core * link.half + j == link.shard)
        dst = self.dst.at[pl.ds(pl.multiple_of(link.shard * self.rows, self.rows), self.rows)]
        there = link.remote(self.src.at[j], dst, self.base + j, self.base + lax.rem(link.shard, link.half), to)
        return mine, there, link.here(self.src.at[j], dst, self.keep)

    def arrival(self, t):
        link = self.link
        source = link.core * link.half + t
        mine = (lax.div(link.shard, link.half) == link.core) & (source == link.shard)
        dst = self.dst.at[pl.ds(pl.multiple_of(source * self.rows, self.rows), self.rows)]
        there = link.remote(self.src.at[0], dst, self.base, self.base + t, link.sibling())
        return mine, there, link.here(self.src.at[0], dst, self.keep)

    def to_sibling(self):
        link = self.link
        size = link.half * self.rows
        rows = pl.ds(pl.multiple_of(link.core * size, size), size)
        slot = self.base + link.half
        return link.remote(self.dst.at[rows], self.dst.at[rows], slot, slot, link.sibling())

    def start(self):
        for j in range(self.link.half):
            mine, there, here = self.copy(j)
            pl.when(mine)(here.start)
            pl.when(jnp.logical_not(mine))(there.start)

    def forward(self):
        for t in range(self.link.half):
            mine, there, here = self.arrival(t)
            pl.when(mine)(here.wait)
            pl.when(jnp.logical_not(mine))(there.wait_recv)
        self.to_sibling().start()

    def finish(self):
        self.to_sibling().wait()
        for j in range(self.link.half):
            mine, there, _ = self.copy(j)
            pl.when(jnp.logical_not(mine))(there.wait_send)


class FromClip:
    def __init__(self, link, src, dst):
        self.link, self.src, self.dst = link, src, dst
        self.rows = dst.shape[1]
        self.base = link.slots(link.half)
        self.keep = link.local_slots(1)

    def copy(self, t):
        link = self.link
        core = lax.div(link.shard, link.half)
        shard = link.core * link.half + t
        mine = (core == link.core) & (shard == link.shard)
        clip = lax.rem(link.shard, link.half)
        src = self.src.at[pl.ds(t * self.rows, self.rows)]
        dst = self.dst.at[clip]
        there = link.remote(src, dst, self.base + t, self.base + clip, (link.rep - link.core + core, shard))
        return mine, there, link.here(src, dst, self.keep)

    def arrival(self, j):
        link = self.link
        mine = (lax.div(link.shard, link.half) == link.core) & (link.core * link.half + j == link.shard)
        src = self.src.at[pl.ds(0, self.rows)]
        there = link.remote(src, self.dst.at[j], self.base, self.base + j, link.sibling())
        return mine, there, link.here(src, self.dst.at[j], self.keep)

    def start(self):
        for t in range(self.link.half):
            mine, there, here = self.copy(t)
            pl.when(mine)(here.start)
            pl.when(jnp.logical_not(mine))(there.start)

    def forward(self):
        pass

    def finish(self):
        for t in range(self.link.half):
            mine, there, here = self.copy(t)
            pl.when(jnp.logical_not(mine))(there.wait_send)
        for j in range(self.link.half):
            mine, there, here = self.arrival(j)
            pl.when(mine)(here.wait)
            pl.when(jnp.logical_not(mine))(there.wait_recv)


class Owners:
    def __init__(self, link, src, dst):
        self.link, self.src, self.dst = link, src, dst
        self.base = link.slots(link.groups - 1)

    def copies(self):
        link = self.link
        return [
            link.remote(
                self.src.at[link.shard ^ p],
                self.dst.at[p - 1],
                self.base + p - 1,
                self.base + p - 1,
                (link.rep, link.shard ^ p),
            )
            for p in range(1, link.groups)
        ]

    def start(self):
        for c in self.copies():
            c.start()

    def forward(self):
        pass

    def finish(self):
        for c in self.copies():
            c.wait()


class Jobs:
    def __init__(self, *jobs):
        self.jobs = jobs

    def sources(self):
        return [a for _, a, _ in self.jobs]

    def in_specs(self):
        return [pl.BlockSpec(memory_space=pl.ANY)] * len(self.jobs)

    def out_shapes(self):
        return [jax.ShapeDtypeStruct(shape, a.dtype) for _, a, shape in self.jobs]

    def scratch(self, extra=0):
        groups = lax.axis_size("shard")
        remote = len(self.jobs) * max(4, groups) + extra
        return [
            pltpu.SemaphoreType.DMA((remote,)),
            pltpu.SemaphoreType.DMA((remote,)),
            pltpu.SemaphoreType.DMA((len(self.jobs) + extra + 1,)),
        ]

    def bind(self, sems, srcs, dsts):
        link = Link(sems)
        return link, [kind(link, a, b) for (kind, _, _), a, b in zip(self.jobs, srcs, dsts)]


def comm_params(number, limit=60):
    return pltpu.CompilerParams(
        vmem_limit_bytes=limit * 2**20, collective_id=number, has_side_effects=True
    )


def exchange_call(jobs, sibling, number, name):
    count = len(jobs.jobs)

    def kernel(*refs):
        srcs, mine = refs[:count], refs[count]
        dsts, other = refs[count + 1 : 2 * count + 1], refs[2 * count + 1]
        link, bound = jobs.bind(refs[2 * count + 2 :], srcs, dsts)
        slot = link.slots(1)
        swap = link.remote(mine, other, slot, slot, link.sibling())
        link.meet_plane()
        swap.start()
        for job in bound:
            job.start()
        for job in bound:
            job.forward()
        for job in bound:
            job.finish()
        swap.wait()

    return pl.pallas_call(
        kernel,
        in_specs=jobs.in_specs() + [pl.BlockSpec(memory_space=pl.ANY)],
        out_specs=[pl.BlockSpec(memory_space=pl.ANY)] * (count + 1),
        out_shape=jobs.out_shapes() + [jax.ShapeDtypeStruct(sibling.shape, sibling.dtype)],
        scratch_shapes=jobs.scratch(1),
        compiler_params=comm_params(number),
        name=name,
    )(*jobs.sources(), sibling)


def qkv_kernel(x_ref, vec_ref, w_ref, bias_ref, h_ref, q_ref, k_ref, v_ref):
    xhat, _ = standardize(x_ref[...].astype(f32))
    h = (xhat * vec_ref[GAIN1] + vec_ref[SHIFT1]).astype(bf16)
    h_ref[...] = h
    z = dot(h, w_ref[...]) + bias_ref[...]
    width = z.shape[1] // 3
    for i, ref in enumerate((q_ref, k_ref, v_ref)):
        ref[:, :width] = z[:, i * width : (i + 1) * width].astype(bf16)
        ref[:, width:] = jnp.zeros((ref.shape[0], ref.shape[1] - width), bf16)


def qkv_call(x, vec, w, bias, wide):
    n, d = x.shape
    out = jax.ShapeDtypeStruct((n, wide), bf16)
    return pl.pallas_call(
        qkv_kernel,
        grid=(n // ROWS,),
        in_specs=[row_block(ROWS, d), whole(vec.shape), whole(w.shape), whole(bias.shape)],
        out_specs=[row_block(ROWS, d)] + [row_block(ROWS, wide)] * 3,
        out_shape=[jax.ShapeDtypeStruct((n, d), bf16), out, out, out],
        compiler_params=params(),
        cost_estimate=cost(2 * n * d * w.shape[1], 4 * n * d + 2 * w.size + 6 * n * wide),
        name="project",
    )(x, vec, w, bias)


def head_window(h):
    start = h * HEAD
    base = (start // 128) * 128
    off = start - base
    lane = lax.broadcasted_iota(jnp.int32, (1, WIN), 1)
    keep = jnp.where((lane >= off) & (lane < off + HEAD), 1.0, 0.0)
    return pl.ds(pl.multiple_of(base, 128), WIN), keep, lane


def put3(x, lane, first, value):
    hi = value.astype(bf16).astype(f32)
    rest = value - hi
    mid = rest.astype(bf16).astype(f32)
    low = rest - mid
    return jnp.where(
        lane == first,
        hi,
        jnp.where(lane == first + 1, mid, jnp.where(lane == first + 2, low, x)),
    )


def key_extra(rows, length):
    lane = lax.broadcasted_iota(jnp.int32, (rows, WIN), 1)
    row = lax.broadcasted_iota(jnp.int32, (rows, WIN), 0)
    dead = jnp.where(row >= length, DEAD, 0.0)
    minus = jnp.where((lane > AUG) & (lane <= AUG + 3), -1.0, 0.0)
    return jnp.where(lane == AUG, dead, minus).astype(bf16)


def attn_fwd_kernel(*refs, bq, jobs):
    count = len(jobs.jobs)
    len_ref, q_ref, k_ref, v_ref = refs[:4]
    o_ref, lse_ref = refs[4 + count : 6 + count]
    acc, kx = refs[6 + 2 * count : 8 + 2 * count]
    link, bound = jobs.bind(refs[8 + 2 * count :], refs[4 : 4 + count], refs[6 + count : 6 + 2 * count])
    h = pl.program_id(0)
    heads = pl.num_programs(0)
    n = q_ref.shape[0]
    width = o_ref.shape[1]

    @pl.when(h == 0)
    def _():
        link.meet_plane()
        for job in bound:
            job.start()
        acc[...] = jnp.zeros_like(acc)
        lse_ref[...] = jnp.zeros_like(lse_ref)
        kx[...] = key_extra(n, len_ref[0])

    @pl.when(h == heads - 2)
    def _():
        for job in bound:
            job.forward()

    win, keep, lane = head_window(h)
    low = keep.astype(bf16)
    q_one = jnp.where(lane == AUG, 1.0, 0.0).astype(bf16)
    v_one = jnp.where((lane >= AUG) & (lane < AUG + 3), 1.0, 0.0).astype(bf16)
    k = k_ref[:, win] * low + kx[...]
    v = v_ref[:, win] * low + v_one
    for i in range(n // bq):
        rows = slice(i * bq, (i + 1) * bq)
        s = dot_nt(q_ref[rows, win] * low + q_one, k)
        peak = jnp.max(s, axis=-1, keepdims=True)
        p = jnp.exp2((s - peak) * SCALE2).astype(bf16)
        o = dot(p, v)
        total = o[:, AUG : AUG + 1]
        acc[rows, win] += o * (keep * (1.0 / total))
        here = lax.broadcasted_iota(jnp.int32, (bq, 128), 1) == h
        lse = peak + jnp.log(total) * (1.0 / SCALE)
        lse_ref[rows, :] = jnp.where(here, lse, lse_ref[rows, :])

    @pl.when(h == heads - 1)
    def _():
        o_ref[:, :width] = acc[:, :width].astype(bf16)
        for job in bound:
            job.finish()


def attn_fwd_call(length, q, k, v, width, heads, jobs, number):
    n, wide = q.shape
    return pl.pallas_call(
        functools.partial(attn_fwd_kernel, bq=256, jobs=jobs),
        grid=(heads,),
        in_specs=[pl.BlockSpec(memory_space=pltpu.SMEM)] + [whole((n, wide))] * 3 + jobs.in_specs(),
        out_specs=[whole((n, width)), whole((n, 128))] + jobs.in_specs(),
        out_shape=[jax.ShapeDtypeStruct((n, width), bf16), jax.ShapeDtypeStruct((n, 128), f32)] + jobs.out_shapes(),
        scratch_shapes=[pltpu.VMEM((n, wide), f32), pltpu.VMEM((n, WIN), bf16)] + jobs.scratch(),
        compiler_params=comm_params(number),
        cost_estimate=cost(4 * n * n * WIN * heads, 8 * n * wide),
        name="attend",
    )(length, q, k, v, *jobs.sources())


def attn_bwd_kernel(*refs, bk, jobs):
    count = len(jobs.jobs)
    len_ref, q_ref, k_ref, v_ref, o_ref, do_ref, lse_ref = refs[:7]
    g_ref, sum_ref = refs[7 + count : 9 + count]
    dq, dk, dv, part, qa, da, kx = refs[9 + 2 * count : 16 + 2 * count]
    link, bound = jobs.bind(refs[16 + 2 * count :], refs[7 : 7 + count], refs[9 + count : 9 + 2 * count])
    h = pl.program_id(0)
    n = q_ref.shape[0]

    @pl.when(h == 0)
    def _():
        link.meet_plane()
        for job in bound:
            job.start()
        for ref in (dq, dk, dv):
            ref[...] = jnp.zeros_like(ref)
        kx[...] = key_extra(n, len_ref[0])

    win, keep, lane = head_window(h)
    low = keep.astype(bf16)
    v_one = jnp.where((lane >= AUG) & (lane < AUG + 3), 1.0, 0.0).astype(bf16)
    for i in range(n // ROWS):
        rows = slice(i * ROWS, (i + 1) * ROWS)
        here = lax.broadcasted_iota(jnp.int32, (ROWS, 128), 1) == h
        lse = jnp.sum(jnp.where(here, lse_ref[rows, :], 0.0), axis=-1, keepdims=True)
        q = q_ref[rows, win].astype(f32) * keep
        qa[rows, :] = jnp.where(lane == AUG, 1.0, put3(q, lane, AUG + 1, lse)).astype(bf16)
        d = do_ref[rows, win].astype(f32) * keep
        delta = jnp.sum(d * o_ref[rows, win].astype(f32), axis=-1, keepdims=True)
        da[rows, :] = put3(d, lane, AUG, -delta).astype(bf16)
    for i in range(n // bk):
        rows = slice(i * bk, (i + 1) * bk)
        k = k_ref[rows, win] * low + kx[rows, :]
        v = v_ref[rows, win] * low + v_one
        p = jnp.exp2(dot_nt(k, qa[...]) * SCALE2)
        ds = (p * dot_nt(v, da[...])).astype(bf16)
        dv[rows, win] += dot(p.astype(bf16), da[...]) * keep
        dk[rows, win] += dot(ds, qa[...]) * keep
        new = dot_tn(ds, k)
        part[...] = new if i == 0 else part[...] + new
    dq[:, win] += part[...] * keep

    @pl.when(h == pl.num_programs(0) - 1)
    def _():
        for i, (ref, factor) in enumerate(((dq, SCALE), (dk, SCALE), (dv, 1.0))):
            value = (ref[:, : g_ref.shape[1] // 3] * factor).astype(bf16)
            cols = slice(i * value.shape[1], (i + 1) * value.shape[1])
            g_ref[:, cols] = value
            sum_ref[:, cols] = jnp.sum(value.astype(f32), axis=0, keepdims=True)
        for job in bound:
            job.finish()


def attn_bwd_call(length, q, k, v, o, do, lse, width, heads, jobs, number):
    n, wide = q.shape
    return pl.pallas_call(
        functools.partial(attn_bwd_kernel, bk=256, jobs=jobs),
        grid=(heads,),
        in_specs=[pl.BlockSpec(memory_space=pltpu.SMEM)]
        + [whole((n, wide))] * 5
        + [whole((n, 128))]
        + jobs.in_specs(),
        out_specs=[whole((n, 3 * width)), whole((1, 3 * width))] + jobs.in_specs(),
        out_shape=[
            jax.ShapeDtypeStruct((n, 3 * width), bf16),
            jax.ShapeDtypeStruct((1, 3 * width), f32),
        ]
        + jobs.out_shapes(),
        scratch_shapes=[pltpu.VMEM((n, wide), f32)] * 3
        + [pltpu.VMEM((n, WIN), f32)]
        + [pltpu.VMEM((n, WIN), bf16)] * 3
        + jobs.scratch(),
        compiler_params=comm_params(number),
        cost_estimate=cost(10 * n * n * WIN * heads, 20 * n * wide),
        name="attend_back",
    )(length, q, k, v, o, do, lse, *jobs.sources())


def middle_kernel(o_ref, w_ref, x_ref, vec_ref, mid_ref, h_ref, owide_ref, mine, other, *sems):
    link = Link(sems)
    n = x_ref.shape[0]
    width = o_ref.shape[1]
    link.meet_core()

    def swap(i):
        rows = pl.ds(pl.multiple_of(i * ROWS, ROWS), ROWS)
        return rows, link.remote(mine.at[rows], other.at[rows], i, i, link.sibling())

    def project(i, carry):
        rows, copy = swap(i)
        mine[rows, :] = dot(o_ref[rows, :], w_ref[...]).astype(bf16)
        copy.start()
        return carry

    def norm(i, carry):
        rows, copy = swap(i)
        copy.wait_recv()
        mid = x_ref[rows, :].astype(f32) + (
            mine[rows, :].astype(f32) + other[rows, :].astype(f32) + vec_ref[OBIAS]
        )
        mid_ref[rows, :] = mid
        xhat, _ = standardize(mid)
        h_ref[rows, :] = (xhat * vec_ref[GAIN2] + vec_ref[SHIFT2]).astype(bf16)
        return carry

    lax.fori_loop(0, n // ROWS, project, 0)
    owide_ref[:, :width] = o_ref[...]
    owide_ref[:, width:] = jnp.zeros((n, owide_ref.shape[1] - width), bf16)
    lax.fori_loop(0, n // ROWS, norm, 0)
    for i in range(n // ROWS):
        swap(i)[1].wait_send()


def middle_call(o, w, x, vec, wide, number):
    n, d = x.shape
    sems = [pltpu.SemaphoreType.DMA((n // ROWS,))] * 2 + [pltpu.SemaphoreType.DMA((1,))]
    vmem = pl.BlockSpec(memory_space=pltpu.VMEM)
    return pl.pallas_call(
        middle_kernel,
        in_specs=[vmem] * 4,
        out_specs=[vmem] * 3,
        out_shape=[
            jax.ShapeDtypeStruct((n, d), f32),
            jax.ShapeDtypeStruct((n, d), bf16),
            jax.ShapeDtypeStruct((n, wide), bf16),
        ],
        scratch_shapes=[pltpu.VMEM((n, d), bf16)] * 2 + sems,
        compiler_params=comm_params(number),
        cost_estimate=cost(2 * n * w.size, 14 * n * d),
        name="middle",
    )(o, w, x, vec)


def ffn_kernel(*refs, chained, last, mc, jobs):
    count = len(jobs.jobs)
    h_ref, dz_ref, up_ref, ub_ref, dn_ref = refs[:5]
    refs = refs[5:]
    if chained:
        old_out, old_dh = refs[:2]
        refs = refs[2:]
    srcs, refs = refs[:count], refs[count:]
    out_ref, dh_ref, dup_ref, ddn_ref, dub_ref = refs[:5]
    dsts, refs = refs[5 : 5 + count], refs[5 + count :]
    ht, act, grad = refs[:3]
    acc, dh = refs[3:5] if last else (out_ref, dh_ref)
    refs = refs[5:] if last else refs[3:]
    link, bound = jobs.bind(refs[:3], srcs, dsts)
    t = pl.program_id(0)
    tiles = pl.num_programs(0)
    n = h_ref.shape[0]

    @pl.when(t == 0)
    def _():
        link.meet_plane()
        for job in bound:
            job.start()
        if chained:
            sem = refs[3]
            copies = [
                pltpu.make_async_copy(src, dst, sem.at[i])
                for i, (src, dst) in enumerate(((old_out, acc), (old_dh, dh)))
            ]
            for c in copies:
                c.start()
            ht[...] = h_ref[...].T
            for c in copies:
                c.wait()
        else:
            ht[...] = h_ref[...].T
            acc[...] = jnp.zeros_like(acc)
            dh[...] = jnp.zeros_like(dh)

    @pl.when(t == tiles - 1)
    def _():
        for job in bound:
            job.forward()

    def step(i, carry):
        rows = pl.ds(pl.multiple_of(i * mc, mc), mc)
        g, slope = gelu_pair(dot(h_ref[rows, :], up_ref[...]) + ub_ref[...])
        g = g.astype(bf16)
        da = (dot_nt(dz_ref[rows, :], dn_ref[...]) * slope).astype(bf16)
        act[rows, :] = g
        grad[rows, :] = da
        acc[rows, :] += dot(g, dn_ref[...])
        dh[rows, :] += dot_nt(da, up_ref[...])
        return carry

    lax.fori_loop(0, n // mc, step, 0)
    dub_ref[...] = jnp.sum(grad[...].astype(f32), axis=0, keepdims=True)
    dup_ref[...] = dot(ht[...], grad[...]).astype(bf16)
    ddn_ref[...] = dot_tn(act[...], dz_ref[...]).astype(bf16)

    @pl.when(t == tiles - 1)
    def _():
        if last:
            out_ref[...] = acc[...].astype(out_ref.dtype)
            dh_ref[...] = dh[...].astype(dh_ref.dtype)
        for job in bound:
            job.finish()


def ffn_call(h, dz, up, bias, down, old, last, jobs, number, name):
    n, d = h.shape
    hidden = up.shape[1]
    bt = FFN_TILE
    out = jax.ShapeDtypeStruct((n, d), bf16 if last else f32)
    chained = old is not None
    once = pl.BlockSpec((n, d), lambda t: (0, 0), pipeline_mode=pl.Buffered(1))
    return pl.pallas_call(
        functools.partial(ffn_kernel, chained=chained, last=last, mc=FFN_ROWS, jobs=jobs),
        grid=(hidden // bt,),
        in_specs=[
            once,
            once,
            pl.BlockSpec((d, bt), lambda t: (0, t)),
            pl.BlockSpec((1, bt), lambda t: (0, t)),
            pl.BlockSpec((bt, d), lambda t: (t, 0)),
        ]
        + ([pl.BlockSpec(memory_space=pl.ANY)] * 2 if chained else [])
        + jobs.in_specs(),
        out_specs=[
            once,
            once,
            pl.BlockSpec((d, bt), lambda t: (0, t)),
            pl.BlockSpec((bt, d), lambda t: (t, 0)),
            pl.BlockSpec((1, bt), lambda t: (0, t)),
        ]
        + jobs.in_specs(),
        out_shape=[
            out,
            out,
            jax.ShapeDtypeStruct((d, hidden), bf16),
            jax.ShapeDtypeStruct((hidden, d), bf16),
            jax.ShapeDtypeStruct((1, hidden), f32),
        ]
        + jobs.out_shapes(),
        scratch_shapes=[pltpu.VMEM((d, n), bf16)]
        + [pltpu.VMEM((n, bt), bf16)] * 2
        + ([pltpu.VMEM((n, d), f32)] * 2 if last else [])
        + jobs.scratch()
        + ([pltpu.SemaphoreType.DMA((2,))] if chained else []),
        compiler_params=comm_params(number),
        cost_estimate=cost(12 * n * d * hidden, 8 * d * hidden + 12 * n * d),
        name=name,
    )(h, dz, up, bias, down, *(old if chained else ()), *jobs.sources())


def second_back_kernel(
    mid_ref, dh_ref, out_ref, dz_ref, vec_ref, w_ref, o_ref, dh_any, out_any,
    dmid_ref, do_ref, dw_ref, sums_ref, layer_ref,
    acc, dh_other, out_other, *sems
):
    i = pl.program_id(0)
    blocks = pl.num_programs(0)
    link = Link(sems)
    half = layer_ref.shape[0] // ROWS
    width = w_ref.shape[0]

    def swap_dh(j):
        rows = pl.ds(pl.multiple_of(j * ROWS, ROWS), ROWS)
        return link.remote(dh_any.at[rows], dh_other.at[rows], j, j, link.sibling())

    def swap_out(j):
        src = pl.ds(pl.multiple_of(((1 - link.core) * half + j) * ROWS, ROWS), ROWS)
        dst = pl.ds(pl.multiple_of(j * ROWS, ROWS), ROWS)
        slot = 2 * half + j
        return link.remote(out_any.at[src], out_other.at[dst], slot, slot, link.sibling())

    @pl.when(i == 0)
    def _():
        link.meet_core()
        for j in range(2 * half):
            swap_dh(j).start()
        for j in range(half):
            swap_out(j).start()
        acc[...] = jnp.zeros_like(acc)
        sums_ref[...] = jnp.zeros_like(sums_ref)

    mid = mid_ref[...]
    xhat, inv = standardize(mid)
    swap_dh(i).wait_recv()
    rows = pl.ds(pl.multiple_of(i * ROWS, ROWS), ROWS)
    dh = dh_ref[...].astype(f32) + dh_other[rows, :].astype(f32)
    dx = dh * vec_ref[GAIN2]
    dz = dz_ref[...].astype(f32)
    dmid = dz + inv * (
        dx - jnp.mean(dx, axis=-1, keepdims=True) - xhat * jnp.mean(dx * xhat, axis=-1, keepdims=True)
    )
    dmid_ref[...] = dmid
    dy = dmid.astype(bf16)
    do_ref[:, :width] = dot_nt(dy, w_ref[...]).astype(bf16)
    do_ref[:, width:] = jnp.zeros((do_ref.shape[0], do_ref.shape[1] - width), bf16)
    acc[...] += dot_tn(o_ref[...], dy)
    for row, value in enumerate((dh * xhat, dh, dy.astype(f32), dz)):
        sums_ref[row : row + 1, :] += jnp.sum(value, axis=0, keepdims=True)

    j = i - link.core * half

    @pl.when((j >= 0) & (j < half))
    def _():
        swap_out(j).wait_recv()
        here = pl.ds(pl.multiple_of(j * ROWS, ROWS), ROWS)
        layer_ref[here, :] = (
            mid + (out_ref[...].astype(f32) + out_other[here, :].astype(f32) + vec_ref[DBIAS])
        ).astype(bf16)

    @pl.when(i == blocks - 1)
    def _():
        dw_ref[...] = acc[...].astype(bf16)
        for j in range(2 * half):
            swap_dh(j).wait_send()
        for j in range(half):
            swap_out(j).wait_send()


def second_back_call(mid, dh, out, dz, vec, w, o, wide, number):
    n, d = mid.shape
    width = w.shape[0]
    block = row_block(ROWS, d)
    count = 3 * n // ROWS // 2
    return pl.pallas_call(
        second_back_kernel,
        grid=(n // ROWS,),
        in_specs=[block] * 4
        + [whole(vec.shape), whole(w.shape), row_block(ROWS, width)]
        + [pl.BlockSpec(memory_space=pl.ANY)] * 2,
        out_specs=[block, row_block(ROWS, wide), whole((width, d)), whole((8, d)), whole((n // 2, d))],
        out_shape=[
            jax.ShapeDtypeStruct((n, d), f32),
            jax.ShapeDtypeStruct((n, wide), bf16),
            jax.ShapeDtypeStruct((width, d), bf16),
            jax.ShapeDtypeStruct((8, d), f32),
            jax.ShapeDtypeStruct((n // 2, d), bf16),
        ],
        scratch_shapes=[
            pltpu.VMEM((width, d), f32),
            pltpu.VMEM((n, d), bf16),
            pltpu.VMEM((n // 2, d), bf16),
            pltpu.SemaphoreType.DMA((count,)),
            pltpu.SemaphoreType.DMA((count,)),
            pltpu.SemaphoreType.DMA((1,)),
        ],
        compiler_params=comm_params(number),
        cost_estimate=cost(4 * n * d * width, 14 * n * d),
        name="second_back",
    )(mid, dh, out, dz, vec, w, o, dh, out)


def dw_kernel(h_ref, g_ref, out_ref):
    out_ref[...] = dot_tn(h_ref[...], g_ref[...]).astype(bf16)


def dw_call(h, grads):
    n, d = h.shape
    cols = grads.shape[1]
    return pl.pallas_call(
        dw_kernel,
        grid=(d // 256,),
        in_specs=[pl.BlockSpec((n, 256), lambda i: (0, i)), whole((n, cols))],
        out_specs=row_block(256, cols),
        out_shape=jax.ShapeDtypeStruct((d, cols), bf16),
        compiler_params=params(),
        cost_estimate=cost(2 * n * d * cols, 2 * (n * d + n * cols + d * cols)),
        name="project_grad",
    )(h, grads)


def first_back_kernel(*refs, jobs):
    count = len(jobs.jobs)
    g_ref, w_ref, vec_ref, x_any, dmid_any = refs[:5]
    dx_ref, sums_ref = refs[5 + count : 7 + count]
    x, dmid, mine, other = refs[7 + 2 * count : 11 + 2 * count]
    link, bound = jobs.bind(refs[11 + 2 * count :], refs[5 : 5 + count], refs[7 + count : 7 + 2 * count])
    size = dx_ref.shape[0]
    half = size // ROWS
    base = link.slots(half)
    keep = link.local_slots(2)
    own = pl.ds(pl.multiple_of(link.core * size, size), size)
    loads = [link.here(x_any.at[own], x, keep), link.here(dmid_any.at[own], dmid, keep + 1)]
    for c in loads:
        c.start()
    link.meet_plane()
    for job in bound:
        job.start()

    def product(j):
        rows = pl.ds(pl.multiple_of(j * ROWS, ROWS), ROWS)
        return dot_nt(g_ref[rows, :], w_ref[...])

    def swap(j):
        rows = pl.ds(pl.multiple_of(j * ROWS, ROWS), ROWS)
        return rows, link.remote(mine.at[rows], other.at[rows], base + j, base + j, link.sibling())

    def send(j, carry):
        rows, copy = swap(j)
        mine[rows, :] = product((1 - link.core) * half + j).astype(bf16)
        copy.start()
        return carry

    def norm(j, carry):
        rows, copy = swap(j)
        part = product(link.core * half + j)
        copy.wait_recv()
        xhat, inv = standardize(x[rows, :].astype(f32))
        dh = part + other[rows, :].astype(f32)
        dx = dh * vec_ref[GAIN1]
        dx_ref[rows, :] = (
            dmid[rows, :]
            + inv
            * (dx - jnp.mean(dx, axis=-1, keepdims=True) - xhat * jnp.mean(dx * xhat, axis=-1, keepdims=True))
        ).astype(bf16)
        for row, value in enumerate((dh * xhat, dh)):
            sums_ref[row : row + 1, :] += jnp.sum(value, axis=0, keepdims=True)
        return carry

    sums_ref[...] = jnp.zeros_like(sums_ref)
    lax.fori_loop(0, half, send, 0)
    for c in loads:
        c.wait()
    lax.fori_loop(0, half, norm, 0)
    for j in range(half):
        swap(j)[1].wait_send()
    for job in bound:
        job.forward()
    for job in bound:
        job.finish()


def first_back_call(grads, w, vec, x, dmid, jobs, number):
    n, d = x.shape
    size = n // 2
    vmem = pl.BlockSpec(memory_space=pltpu.VMEM)
    hbm = pl.BlockSpec(memory_space=pl.ANY)
    return pl.pallas_call(
        functools.partial(first_back_kernel, jobs=jobs),
        in_specs=[vmem] * 3 + [hbm] * 2 + jobs.in_specs(),
        out_specs=[vmem] * 2 + jobs.in_specs(),
        out_shape=[jax.ShapeDtypeStruct((size, d), bf16), jax.ShapeDtypeStruct((8, d), f32)] + jobs.out_shapes(),
        scratch_shapes=[
            pltpu.VMEM((size, d), bf16),
            pltpu.VMEM((size, d), f32),
            pltpu.VMEM((size, d), bf16),
            pltpu.VMEM((size, d), bf16),
        ]
        + jobs.scratch(size // ROWS),
        compiler_params=comm_params(number),
        cost_estimate=cost(2 * n * w.size, 12 * n * d),
        name="first_back",
    )(grads, w, vec, x, dmid, *jobs.sources())


def own_sum(blocks, others):
    shard = lax.axis_index("shard")
    total = lax.dynamic_index_in_dim(blocks, shard, 0, keepdims=False).astype(f32)
    for i in range(others.shape[0]):
        total = total + others[i].astype(f32)
    return total.astype(bf16)


def over_reps(own):
    planes = lax.axis_size("rep") // 2
    sums = lax.psum_scatter(
        own,
        "rep",
        scatter_dimension=0,
        tiled=True,
        axis_index_groups=[[2 * z + c for z in range(planes)] for c in range(2)],
    )
    both = lax.all_gather(sums, "rep", axis=0)
    rows, cols = sums.shape
    return both.reshape(planes, 2, rows, cols).transpose(1, 0, 2, 3).reshape(2, planes * rows, cols)


def on_device(
    tokens,
    lengths,
    cotangent,
    first_gain,
    first_shift,
    query_weight,
    query_bias,
    key_weight,
    value_weight,
    value_bias,
    out_weight,
    out_bias,
    second_gain,
    second_shift,
    up_weight,
    up_bias,
    down_weight,
    down_bias,
):
    g = lax.axis_size("shard")
    shard = lax.axis_index("shard")
    core = lax.rem(lax.axis_index("rep"), 2)
    cl, rows, d = tokens.shape
    n = 2 * cl * rows
    ff = up_weight.shape[1]
    own_d = d // g
    own_f = ff // g
    attn_cols = own_d // 2
    ffn_cols = own_f // 2
    width = d // 2
    heads = width // HEAD
    wide = pl.cdiv(width, 128) * 128 + 128
    first_n = ffn_cols * 2 // 5
    pieces = ((0, first_n), (first_n, ffn_cols))

    def core_cols(w, size, a, b):
        def of(c):
            return jnp.concatenate([w[:, (2 * s + c) * size + a : (2 * s + c) * size + b] for s in range(g)], axis=1)

        return jnp.where(core == 0, of(0), of(1))

    def core_rows(w):
        half = w.shape[0] // 2
        return lax.dynamic_slice_in_dim(w, core * half, half, 0)

    vectors = (first_gain, first_shift, query_bias, value_bias, out_bias, second_gain, second_shift, down_bias)
    lens = jnp.pad(lengths.astype(f32), (0, own_d - cl)).reshape(1, own_d)
    small = jnp.concatenate(
        [jnp.stack(vectors).astype(f32), lens, up_bias.astype(f32).reshape(-1, own_d)], axis=0
    )
    small = jnp.pad(small, ((0, 16 - small.shape[0]), (0, -own_d % 128)))
    qkv_own = jnp.concatenate(
        [core_cols(w, attn_cols, 0, attn_cols) for w in (query_weight, key_weight, value_weight)], axis=1
    )
    jobs = Jobs(
        (ToClip, tokens, (n, d)),
        (Gather, qkv_own, (g,) + qkv_own.shape),
        (Gather, small, (g,) + small.shape),
    )
    x, w_qkv, smalls, other_small = exchange_call(jobs, small, 0, "first_exchange")
    w_qkv = w_qkv.reshape(d, 3 * width)
    vec = smalls[:, :, :own_d].transpose(1, 0, 2).reshape(16, d)
    near = lax.div(shard, cl) == core
    lens = jnp.where(near, small[LENGTHS], other_small[LENGTHS])[0]
    length = lens[lax.rem(shard, cl)].astype(jnp.int32).reshape(1)

    def bias_cols(b):
        return lax.dynamic_index_in_dim(vec[b].reshape(1, g, 2, attn_cols), core, 2).reshape(1, width)

    bias = jnp.concatenate([bias_cols(QBIAS), jnp.zeros((1, width), f32), bias_cols(VBIAS)], axis=1)
    ubias = lax.dynamic_index_in_dim(
        vec[UBIAS : UBIAS + own_f // own_d].reshape(-1, g, own_d).transpose(1, 0, 2).reshape(g, 2, ffn_cols),
        core,
        1,
        keepdims=False,
    )
    ups = [core_cols(up_weight, ffn_cols, a, b) for a, b in pieces]
    down_own = core_rows(down_weight)
    downs = [down_own[a:b] for a, b in pieces]
    out_own = core_rows(out_weight)

    def gathered(a):
        return (Gather, a, (g,) + a.shape)

    h1, q, k, v = qkv_call(x, vec, w_qkv, bias, wide)
    jobs = Jobs(gathered(out_own), (ToClip, cotangent, (n, d)), gathered(ups[0]), gathered(downs[0]))
    o, lse, w_out, cot, up, down = attn_fwd_call(length, q, k, v, width, heads, jobs, 1)
    w_out = w_out.reshape(width, d)
    mid, h2, o_wide = middle_call(o, w_out, x, vec, wide, 2)
    live = jnp.arange(n, dtype=jnp.int32)[:, None] < length
    dz = jnp.where(live, cot, jnp.zeros_like(cot))

    def hidden_bias(piece):
        return ubias[:, piece[0] : piece[1]].reshape(1, -1)

    def to_owners(a):
        return (Owners, a, (g - 1,) + a.shape[1:])

    jobs = Jobs(gathered(ups[1]), gathered(downs[1]))
    out, dh2, dup0, ddn0, dub0, up1, down1 = ffn_call(
        h2, dz, up.reshape(d, -1), hidden_bias(pieces[0]), down.reshape(-1, d), None, False, jobs, 3, "hidden0"
    )
    dup0, ddn0 = dup0.reshape(g, own_d, -1), ddn0.reshape(g, -1, d)
    jobs = Jobs(to_owners(dup0), to_owners(ddn0))
    out, dh2, dup1, ddn1, dub1, dup0_in, ddn0_in = ffn_call(
        h2, dz, up1.reshape(d, -1), hidden_bias(pieces[1]), down1.reshape(-1, d), (out, dh2), True, jobs, 4, "hidden1"
    )
    dup1, ddn1 = dup1.reshape(g, own_d, -1), ddn1.reshape(g, -1, d)
    up0_all = over_reps(own_sum(dup0, dup0_in))
    down0_all = over_reps(own_sum(ddn0, ddn0_in))

    dmid, do, dwo, sums2, layer_own = second_back_call(mid, dh2, out, dz, vec, w_out, o, wide, 5)
    dwo = dwo.reshape(g, -1, d)

    jobs = Jobs(to_owners(dup1), to_owners(ddn1), to_owners(dwo), (FromClip, layer_own, (cl, rows, d)))
    grads, bias_sums, dup1_in, ddn1_in, dwo_in, layer_out = attn_bwd_call(
        length, q, k, v, o_wide, do, lse, width, heads, jobs, 6
    )
    up1_all = over_reps(own_sum(dup1, dup1_in))
    down1_all = over_reps(own_sum(ddn1, ddn1_in))
    out_grad = over_reps(own_sum(dwo, dwo_in)).reshape(own_d, d).astype(f32)
    dwqkv = dw_call(h1, grads).reshape(g, own_d, 3 * width)
    jobs = Jobs(to_owners(dwqkv))
    dx, sums1, dwqkv_in = first_back_call(grads, w_qkv, vec, x, dmid, jobs, 7)
    qkv_all = over_reps(own_sum(dwqkv, dwqkv_in)).reshape(2, own_d, 3, g, attn_cols)
    jobs = Jobs((FromClip, dx, (cl, rows, d)))
    tokens_grad, _ = exchange_call(jobs, sums1, 8, "last_exchange")

    up_all = jnp.concatenate([up0_all.reshape(2, own_d, g, -1), up1_all.reshape(2, own_d, g, -1)], axis=3)
    up_grad = up_all.transpose(1, 2, 0, 3).reshape(own_d, ff).astype(f32)
    down_grad = jnp.concatenate([down0_all, down1_all], axis=1).reshape(own_f, d).astype(f32)
    qkv_grads = [qkv_all[:, :, i].transpose(1, 2, 0, 3).reshape(own_d, d).astype(f32) for i in range(3)]

    def spread(v, size):
        out = jnp.zeros((g, 2, size), f32)
        return lax.dynamic_update_index_in_dim(out, v.reshape(g, size), core, 1).reshape(-1, own_d)

    pieces_small = [
        sums1[0].reshape(g, own_d),
        sums1[1].reshape(g, own_d),
        spread(bias_sums[0, :width], attn_cols),
        spread(bias_sums[0, 2 * width :], attn_cols),
        (sums2[2] * 0.5).reshape(g, own_d),
        (sums2[0] * 0.5).reshape(g, own_d),
        (sums2[1] * 0.5).reshape(g, own_d),
        (sums2[3] * 0.5).reshape(g, own_d),
    ]
    ub_sum = jnp.zeros((g, 2, ffn_cols), f32)
    ub_sum = lax.dynamic_update_index_in_dim(ub_sum, jnp.concatenate([dub0.reshape(g, -1), dub1.reshape(g, -1)], axis=1), core, 1)
    packed = jnp.concatenate(
        [jnp.stack(pieces_small, axis=1), ub_sum.reshape(g, -1, own_d)], axis=1
    )
    packed = lax.psum(packed, ("rep", "shard"))
    mine_small = lax.dynamic_index_in_dim(packed, shard, 0, keepdims=False)
    s_gain1, s_shift1, s_qb, s_vb, s_ob, s_gain2, s_shift2, s_db = [mine_small[i] for i in range(8)]
    s_ub = mine_small[8:].reshape(-1)

    return (
        layer_out,
        tokens_grad,
        s_gain1,
        s_shift1,
        qkv_grads[0],
        s_qb,
        qkv_grads[1],
        qkv_grads[2],
        s_vb,
        out_grad,
        s_ob,
        s_gain2,
        s_shift2,
        up_grad,
        s_ub,
        down_grad,
        s_db,
    )


def solution(mesh):
    row, mat, vec = P("rep", "shard", None), P("shard", None), P("shard")
    return jax.shard_map(
        on_device,
        mesh=mesh,
        in_specs=(row, P("rep"), row, vec, vec, mat, vec, mat, mat, vec, mat, vec, vec, vec, mat, vec, mat, vec),
        out_specs=(row, row, vec, vec, mat, vec, mat, mat, vec, mat, vec, vec, vec, mat, vec, mat, vec),
        check_vma=False,
    )
```

time: 1020 us -> 889 us (0.87)
  Pallas kernels: 304 us -> 610 us
  waiting for transfers between devices: 269 us -> 55.1 us
  local copies, waits for them, and re-layouts: 193 us -> 96.5 us
  starting transfers between devices: 94.8 us -> 0.44 us
  blocking collectives: 88.6 us -> 59.5 us
    pallas_call x8, Pallas kernels: 253 us -> 555 us  [the longest x2 146 us: ffn_call(): pl.pallas_call(functools.partial(ffn_kernel, chained=chained, last=last,...]
    ppermute x63 -> x0, waiting for transfers between devices: 268 us -> none  [the longest x48 227 us: swap(): return lax.ppermute(x, 'shard', [(s, s ^ bit) for s in range(self.groups)])]
    ppermute x63 -> x0, starting transfers between devices: 94.5 us -> none  [the longest x48 70.1 us: swap(): return lax.ppermute(x, 'shard', [(s, s ^ bit) for s in range(self.groups)])]
    dynamic_update_slice x31 -> x1, local copies, waits for them, and re-layouts: 34.8 us -> 0.07 us  [on_device(): lax.dynamic_update_index_in_dim(ub_sum, jnp.concatenate([dub0.reshape(g,...]
    all_gather x3 -> x5, waiting for transfers between devices: 0.01 us -> 28.2 us  [over_reps(): both = lax.all_gather(sums, 'rep', axis=0)]
    reduce_scatter x4 -> x6, waiting for transfers between devices: 0.04 us -> 24.3 us  [over_reps(): lax.psum_scatter(own, 'rep', scatter_dimension=0, tiled=True, axis_index_...]
    all_gather x1 -> x0, blocking collectives: 18.9 us -> none  [on_device(): small = lax.all_gather(small, 'shard', axis=0).astype(f32)]
    convert_element_type x6 -> x3, local copies, waits for them, and re-layouts: 38 us -> 21 us  [the longest x2 19.7 us: on_device(): up_grad = up_all.transpose(1, 2, 0, 3).reshape(own_d, ff).astype(f32)]
  transfers between devices with their start and end apart: 70 -> 11, of which waited for: 26 -> 3; matrix products, arithmetic and copies ran while one was open for 20% -> 7% of each run, Pallas kernels for 24% -> 31%
where the time goes in v2:
time: 889 us; the launch traced here: 883 us
  Pallas kernels  610 us (69%)
  local copies, waits for them, and re-layouts  96.5 us (11%)
  blocking collectives  59.5 us (7%)
  waiting for transfers between devices  55.1 us (6%)
  other arithmetic  45.9 us (5%)
  between operations  15.5 us (2%)
    pallas_call x2, Pallas kernels, ffn_call(): pl.pallas_call(functools.partial(ffn_kernel, chained=chained, last=last,...  146 us
    pallas_call x1, Pallas kernels, attn_bwd_call(): pl.pallas_call(functools.partial(attn_bwd_kernel, bk=256, jobs=jobs), gri...  135 us
    pallas_call x2, Pallas kernels, exchange_call(): pl.pallas_call(kernel, in_specs=jobs.in_specs() + [pl.BlockSpec(memory_sp...  106 us
    pallas_call x1, Pallas kernels, attn_fwd_call(): pl.pallas_call(functools.partial(attn_fwd_kernel, bq=256, jobs=jobs), gri...  88.6 us
    pallas_call x1, Pallas kernels, first_back_call(): pl.pallas_call(functools.partial(first_back_kernel, jobs=jobs), in_specs=...  62.6 us
    psum x1, blocking collectives, on_device(): packed = lax.psum(packed, ('rep', 'shard'))  39.4 us
    all_gather x5, waiting for transfers between devices, over_reps(): both = lax.all_gather(sums, 'rep', axis=0)  28.2 us
    pallas_call x1, Pallas kernels, second_back_call(): pl.pallas_call(second_back_kernel, grid=(n // ROWS,), in_specs=[block] *...  26 us
  transfers between devices with their start and end apart: 11, of which 3 were waited for; matrix products, arithmetic and copies ran while one was open for 7% of the time, Pallas kernels for 31%

profile of v2, /device:TPU:0, one launch (start us, length us, event | category | flops | bytes accessed | tf_op | source)
XLA Modules:
  0.0 882.9 jit_solution(10826273806214535438)
XLA Ops:
  7.3 3.0 fusion.21
  10.3 3.0 fusion.19
  21.2 73.0 %first_exchange.1 = (bf16[1536,1280]{1,0:T(8,128)(2,1)}, bf16[4,320,1920]{2,1,0:T(8,128)(2,1)}, f32[4,16,384]{2,1,0:T(8,128)}, f32[16,384]{1,0:T(8,128)}) custom-call(bf16[2,384,1280]{2,1,0:T(8,128)(2,1)} %refs_0_.1, bf16[320,1920]{1,0:T(8,128)(2,1)} %pad_maximum_fusion.1.refs_1_, f32[16,384]{1,0:T(8,128)} %copy-done.23, f32[16,384]{1,0:T(8,128)} %copy-done.23), custom_call_target="tpu_custom_call" | custom-call | tf_op jit(solution)/shard_map/first_exchange/pallas_call | solution.py:354
  115.4 15.4 %project.1 = (bf16[1536,1280]{1,0:T(8,128)(2,1)}, bf16[1536,768]{1,0:T(8,128)(2,1)}, bf16[1536,768]{1,0:T(8,128)(2,1)}, bf16[1536,768]{1,0:T(8,128)(2,1)}) custom-call(bf16[1536,1280]{1,0:T(8,128)(2,1)} %get-tuple-element.64.x_ref.refs_3_, f32[16,1280]{1,0:T(8,128)} %reshape.304.vec_ref.refs_2_, bf16[1280,1920]{1,0:T(8,128)(2,1)} %bitcast.135, ...), custom_call_target="tpu_custom_call" | custom-call | flops 7549747200 | bytes 19857408 | tf_op jit(solution)/shard_map/project/pallas_call | solution.py:379
  132.0 88.6 %attend.1 = (bf16[1536,640]{1,0:T(8,128)(2,1)}, f32[1536,128]{1,0:T(8,128)}, bf16[4,160,1280]{2,1,0:T(8,128)(2,1)}, bf16[1536,1280]{1,0:T(8,128)(2,1)}, bf16[4,3...) custom-call(s32[1]{0:T(128)} %bitcast.refs_0_, bf16[1536,768]{1,0:T(8,128)(2,1)} %get-tuple-element.67.refs_1_, ...), custom_call_target="tpu_custom_call" | custom-call | flops 19327352832 | bytes 9437184 | tf_op jit(solution)/shard_map/attend/pallas_call | solution.py:472
  220.6 16.4 %middle.1 = (f32[1536,1280]{1,0:T(8,128)}, bf16[1536,1280]{1,0:T(8,128)(2,1)}, bf16[1536,768]{1,0:T(8,128)(2,1)}) custom-call(bf16[1536,640]{1,0:T(8,128)(2,1)} %get-tuple-element.70.o_ref, bf16[640,1280]{1,0:T(8,128)(2,1)} %bitcast.115, bf16[1536,1280]{1,0:T(8,128)(2,1)} %get-tuple-element.64.x_ref.refs_3_, f32[16,1280]{1,0:T(8,128)} %reshape.304.vec_ref.refs_2_), custom_call_target="tpu_custom_call" | custom-call | flops 2516582400 | bytes 27525120 | tf_op jit(solution)/shard_map/middle/pallas_call | solution.py:602
  237.1 4.0 broadcast_select_fusion.refs_1_.dz_ref
  242.3 78.1 %hidden0.1 = (f32[1536,1280]{1,0:T(8,128)}, f32[1536,1280]{1,0:T(8,128)}, bf16[1280,1024]{1,0:T(8,128)(2,1)}, bf16[1024,1280]{1,0:T(8,128)(2,1)}, f32[1,1024]{1,...) custom-call(bf16[1536,1280]{1,0:T(8,128)(2,1)} %get-tuple-element.74.refs_0_, ...), custom_call_target="tpu_custom_call" | custom-call | flops 24159191040 | bytes 34078720 | tf_op jit(solution)/shard_map/hidden0/pallas_call | solution.py:694
  320.4 68.2 %hidden1.1 = (bf16[1536,1280]{1,0:T(8,128)(2,1)}, bf16[1536,1280]{1,0:T(8,128)(2,1)}, bf16[1280,1536]{1,0:T(8,128)(2,1)}, bf16[1536,1280]{1,0:T(8,128)(2,1)}, f3...) custom-call(bf16[1536,1280]{1,0:T(8,128)(2,1)} %get-tuple-element.74.refs_0_, ...), custom_call_target="tpu_custom_call" | custom-call | flops 36238786560 | bytes 39321600 | tf_op jit(solution)/shard_map/hidden1/pallas_call | solution.py:694
  388.6 3.1 fusion.3
  394.2 26.0 %second_back.1 = (f32[1536,1280]{1,0:T(8,128)}, bf16[1536,768]{1,0:T(8,128)(2,1)}, bf16[640,1280]{1,0:T(8,128)(2,1)}, f32[8,1280]{1,0:T(8,128)}, bf16[768,1280]{1,0:T(8,128)(2,1)}) custom-call(f32[1536,1280]{1,0:T(8,128)} %get-tuple-element.73.mid_ref, bf16[1536,1280]{1,0:T(8,128)(2,1)} %get-tuple-element.84.dh_ref.dh_any, ...), custom_call_target="tpu_custom_call" | custom-call | flops 5033164800 | bytes 27525120 | tf_op jit(solution)/shard_map/second_back/pallas_call | solution.py:806
  420.2 134.9 %attend_back.1 = (bf16[1536,1920]{1,0:T(8,128)(2,1)}, f32[1,1920]{1,0:T(1,128)}, bf16[3,320,1536]{2,1,0:T(8,128)(2,1)}, bf16[3,384,1280]{2,1,0:T(8,128)(2,1)}, b...) custom-call(s32[1]{0:T(128)} %bitcast.refs_0_, bf16[1536,768]{1,0:T(8,128)(2,1)} %get-tuple-element.67.refs_1_, ...), custom_call_target="tpu_custom_call" | custom-call | flops 48318382080 | bytes 23592960 | tf_op jit(solution)/shard_map/attend_back/pallas_call | solution.py:540
  555.1 3.7 fusion.1
  561.6 13.4 %project_grad.1 = bf16[1280,1920]{1,0:T(8,128)(2,1)} custom-call(bf16[1536,1280]{1,0:T(8,128)(2,1)} %get-tuple-element.95.h_ref, bf16[1536,1920]{1,0:T(8,128)(2,1)} %get-tuple-element.93.g_ref.refs_0_), custom_call_target="tpu_custom_call" | custom-call | flops 7549747200 | bytes 14745600 | tf_op jit(solution)/shard_map/project_grad/pallas_call | solution.py:841
  574.9 62.6 %first_back.1 = (bf16[768,1280]{1,0:T(8,128)(2,1)}, f32[8,1280]{1,0:T(8,128)}, bf16[3,320,1920]{2,1,0:T(8,128)(2,1)}) custom-call(bf16[1536,1920]{1,0:T(8,128)(2,1)} %get-tuple-element.93.g_ref.refs_0_, bf16[1280,1920]{1,0:T(8,128)(2,1)} %bitcast.136, f32[16,1280]{1,0:T(8,128)} %reshape.304.vec_ref.refs_2_, ...), custom_call_target="tpu_custom_call" | custom-call | flops 7549747200 | bytes 23592960 | tf_op jit(solution)/shard_map/first_back/pallas_call | solution.py:919
  637.5 4.0 fusion
  647.7 24.3 %reduce-scatter.7.cloned.1.call-done = bf16[80,1920]{1,0:T(8,128)(2,1)} async-done(((bf16[320,1920]{1,0:T(8,128)(2,1)}), bf16[80,1920]{1,0:T(8,128)(2,1)}) %reduce-scatter.7.cloned.1.call-update) | async-done | bytes 307216 | tf_op jit(solution)/shard_map/reduce_scatter | solution.py:947
  672.0 33.4 %last_exchange.1 = (bf16[2,384,1280]{2,1,0:T(8,128)(2,1)}, f32[8,1280]{1,0:T(8,128)}) custom-call(bf16[768,1280]{1,0:T(8,128)(2,1)} %get-tuple-element.96.refs_0_, f32[8,1280]{1,0:T(8,128)} %get-tuple-element.97.refs_1_), custom_call_target="tpu_custom_call" | custom-call | tf_op jit(solution)/shard_map/last_exchange/pallas_call | solution.py:354
  708.9 39.4 %psum.7 = f32[4,12,320]{2,1,0:T(8,128)S(1)} all-reduce(f32[4,12,320]{2,1,0:T(8,128)S(1)} %concatenate.65), channel_id=1, replica_groups=mesh['rep'=8,'shard'=4] {'rep','shard'}, use_global_device_ids=true, to_apply=%region_0.1 | all-reduce | flops 15360 | bytes 122880 | tf_op jit(solution)/shard_map/psum | solution.py:1112
  749.6 20.1 %all-gather.1 = bf16[320,1280]{1,0:T(8,128)(2,1)S(1)} all-gather(bf16[40,1280]{1,0:T(8,128)(2,1)} %reduce-scatter.9.cloned.1.call-done), channel_id=3, replica_groups=mesh['rep'=8,'shard'=4] {'rep'}, dimensions={0}, use_global_device_ids=true | all-gather | bytes 921600 | tf_op jit(solution)/shard_map/all_gather | solution.py:954
  777.5 3.0 copy.106
  780.5 3.3 reshape_reshape.12
  783.9 4.2 convert_bitcast_fusion
  788.1 10.7 %copy.90 = f32[320,4,2,640]{3,2,1,0:T(2,128)} copy(f32[320,4,2,640]{3,1,0,2:T(4,128)} %convert_bitcast_fusion) | data formatting | bytes 13107200 | tf_op jit(solution)/shard_map/convert_element_type | solution.py:1089
  798.7 9.1 %reshape.341 = f32[320,5120]{1,0:T(8,128)} reshape(f32[320,4,2,640]{3,2,1,0:T(2,128)} %copy.90) | data formatting | bytes 13107200 | tf_op jit(solution)/shard_map/convert_element_type | solution.py:1089
  809.9 3.5 bitcast_convert_fusion
  813.4 27.1 %all-gather.12.cloned.1.call-done = bf16[640,1920]{1,0:T(8,128)(2,1)} async-done(((bf16[80,1920]{1,0:T(8,128)(2,1)}), bf16[640,1920]{1,0:T(8,128)(2,1)}) %all-gather.12.cloned.1.call-update) | async-done | bytes 2457616 | tf_op jit(solution)/shard_map/all_gather | solution.py:954
  842.4 5.0 reshape_reshape.10
  847.5 5.4 convert_bitcast_fusion.1
  852.9 4.1 copy.84
  859.8 4.1 copy.85
  871.9 3.1 copy.115
  (207 shorter events, 70.1 us)
Async XLA Ops:
  7.2 103.3 %copy-start = (bf16[1280,1280]{1,0:T(8,128)(2,1)S(1)}, bf16[1280,1280]{1,0:T(8,128)(2,1)}, u32[]{:S(2)}) copy-start(bf16[1280,1280]{1,0:T(8,128)(2,1)} %param.34) | copy-start | bytes 9830404
  7.2 637.7 %reduce-scatter.11.cloned.1.call-start = ((), (), s32[]{:S(2)}) async-start(), calls=%async_computation.8 | async-start | bytes 819200 | tf_op jit(solution)/shard_map/reduce_scatter | solution.py:947
  10.3 4.6 copy-start.26
  15.3 4.8 copy-start.23
  98.9 5.6 slice-start
  115.4 15.5 %copy-start.15 = (bf16[320,256]{1,0:T(8,128)(2,1)S(1)}, bf16[320,256]{1,0:T(8,128)(2,1)}, u32[]{:S(2)}) copy-start(bf16[320,256]{1,0:T(8,128)(2,1)} %get-tuple-element.172) | copy-start | bytes 491524
  115.4 15.5 %copy-start.16 = (bf16[320,256]{1,0:T(8,128)(2,1)S(1)}, bf16[320,256]{1,0:T(8,128)(2,1)}, u32[]{:S(2)}) copy-start(bf16[320,256]{1,0:T(8,128)(2,1)} %get-tuple-element.173) | copy-start | bytes 491524
  115.4 15.5 %copy-start.17 = (bf16[320,256]{1,0:T(8,128)(2,1)S(1)}, bf16[320,256]{1,0:T(8,128)(2,1)}, u32[]{:S(2)}) copy-start(bf16[320,256]{1,0:T(8,128)(2,1)} %get-tuple-element.174) | copy-start | bytes 491524
  115.4 15.5 %copy-start.18 = (bf16[320,256]{1,0:T(8,128)(2,1)S(1)}, bf16[320,256]{1,0:T(8,128)(2,1)}, u32[]{:S(2)}) copy-start(bf16[320,256]{1,0:T(8,128)(2,1)} %get-tuple-element.175) | copy-start | bytes 491524
  115.4 15.5 %copy-start.19 = (bf16[320,256]{1,0:T(8,128)(2,1)S(1)}, bf16[320,256]{1,0:T(8,128)(2,1)}, u32[]{:S(2)}) copy-start(bf16[320,256]{1,0:T(8,128)(2,1)} %get-tuple-element.176) | copy-start | bytes 491524
  115.4 15.5 %copy-start.20 = (bf16[320,256]{1,0:T(8,128)(2,1)S(1)}, bf16[320,256]{1,0:T(8,128)(2,1)}, u32[]{:S(2)}) copy-start(bf16[320,256]{1,0:T(8,128)(2,1)} %get-tuple-element.177) | copy-start | bytes 491524
  115.4 15.5 %copy-start.21 = (bf16[320,256]{1,0:T(8,128)(2,1)S(1)}, bf16[320,256]{1,0:T(8,128)(2,1)}, u32[]{:S(2)}) copy-start(bf16[320,256]{1,0:T(8,128)(2,1)} %get-tuple-element.178) | copy-start | bytes 491524
  115.4 15.5 %copy-start.22 = (bf16[320,256]{1,0:T(8,128)(2,1)S(1)}, bf16[320,256]{1,0:T(8,128)(2,1)}, u32[]{:S(2)}) copy-start(bf16[320,256]{1,0:T(8,128)(2,1)} %get-tuple-element.179) | copy-start | bytes 491524
  237.0 4.1 copy-start.8
  237.0 4.1 copy-start.9
  237.0 4.1 copy-start.10
  237.0 4.1 copy-start.11
  391.8 253.8 %reduce-scatter.15.cloned.1.call-start = ((), (), s32[]{:S(2)}) async-start(), calls=%async_computation.10 | async-start | bytes 819200 | tf_op jit(solution)/shard_map/reduce_scatter | solution.py:947
  394.1 252.3 %reduce-scatter.13.cloned.1.call-start = ((), (), s32[]{:S(2)}) async-start(), calls=%async_computation.9 | async-start | bytes 1228800 | tf_op jit(solution)/shard_map/reduce_scatter | solution.py:947
  558.8 88.3 %reduce-scatter.17.cloned.1.call-start = ((), (), s32[]{:S(2)}) async-start(), calls=%async_computation.11 | async-start | bytes 1228800 | tf_op jit(solution)/shard_map/reduce_scatter | solution.py:947
  561.5 110.5 %reduce-scatter.7.cloned.1.call-start = ((), (), s32[]{:S(2)}) async-start(), calls=%async_computation.6 | async-start | bytes 1536000 | tf_op jit(solution)/shard_map/reduce_scatter | solution.py:947
  641.6 108.1 %reduce-scatter.9.cloned.1.call-start = ((), (), s32[]{:S(2)}) async-start(), calls=%async_computation.7 | async-start | bytes 512000 | tf_op jit(solution)/shard_map/reduce_scatter | solution.py:947
  644.8 61.7 %copy-start.28 = (f32[1,1920]{1,0:T(1,128)S(1)}, f32[1,1920]{1,0:T(1,128)}, u32[]{:S(2)}) copy-start(f32[1,1920]{1,0:T(1,128)} %get-tuple-element.99) | copy-start | bytes 23044
  644.8 62.2 %copy-start.24 = (f32[8,1280]{1,0:T(8,128)S(1)}, f32[8,1280]{1,0:T(8,128)}, u32[]{:S(2)}) copy-start(f32[8,1280]{1,0:T(8,128)} %get-tuple-element.100) | copy-start | bytes 122884
  644.8 62.6 %copy-start.25 = (f32[1,1536]{1,0:T(1,128)S(1)}, f32[1,1536]{1,0:T(1,128)}, u32[]{:S(2)}) copy-start(f32[1,1536]{1,0:T(1,128)} %get-tuple-element.102) | copy-start | bytes 18436
  644.8 63.1 %copy-start.27 = (f32[1,1024]{1,0:T(1,128)S(1)}, f32[1,1024]{1,0:T(1,128)}, u32[]{:S(2)}) copy-start(f32[1,1024]{1,0:T(1,128)} %get-tuple-element.101) | copy-start | bytes 12292
  644.8 126.3 %all-gather.14.cloned.1.call-start = ((), (), s32[]{:S(2)}) async-start(), calls=%async_computation.13 | async-start | bytes 1474560 | tf_op jit(solution)/shard_map/all_gather | solution.py:954
  645.6 128.5 %all-gather.18.cloned.1.call-start = ((), (), s32[]{:S(2)}) async-start(), calls=%async_computation.15 | async-start | bytes 1474560 | tf_op jit(solution)/shard_map/all_gather | solution.py:954
  646.3 131.2 %all-gather.16.cloned.1.call-start = ((), (), s32[]{:S(2)}) async-start(), calls=%async_computation.14 | async-start | bytes 2211840 | tf_op jit(solution)/shard_map/all_gather | solution.py:954
  647.1 160.7 %all-gather.20.cloned.1.call-start = ((), (), s32[]{:S(2)}) async-start(), calls=%async_computation.16 | async-start | bytes 2211840 | tf_op jit(solution)/shard_map/all_gather | solution.py:954
  647.7 192.9 %all-gather.12.cloned.1.call-start = ((), (), s32[]{:S(2)}) async-start(), calls=%async_computation.12 | async-start | bytes 2764800 | tf_op jit(solution)/shard_map/all_gather | solution.py:954
  871.9 4.4 copy-start.1
  (18 other events, 43.9 us)
Sparse Core Ops, SparseCore 0:
  391.9 22.4 reduce-scatter.10
  417.3 21.0 reduce-scatter.14
  558.9 26.2 reduce-scatter.12
  588.1 24.7 reduce-scatter.16
  641.7 30.2 reduce-scatter.6
  674.8 19.5 reduce-scatter.8
  696.1 21.7 all-gather.13
  719.5 23.4 all-gather.17
  744.6 32.8 all-gather.15
  779.0 27.8 all-gather.19
  808.6 31.9 all-gather.11

commit v3 on v2

--- a/solution.py
+++ b/solution.py
@@ -63,6 +63,10 @@
     return pl.BlockSpec(shape, lambda *_: (0,) * len(shape))
 
 
+def once(shape):
+    return pl.BlockSpec(shape, lambda *_: (0,) * len(shape), pipeline_mode=pl.Buffered(1))
+
+
 def row_block(rows, cols):
     return pl.BlockSpec((rows, cols), lambda i: (i, 0))
 
@@ -94,6 +98,35 @@
                     pl.semaphore_signal(barrier, inc=1, device_id=to, device_id_type=MESH)
         pl.semaphore_wait(barrier, 2 * self.groups - 1)
 
+    def meet_all(self):
+        barrier = pltpu.get_barrier_semaphore()
+        base = self.rep - self.core
+        for c in range(2):
+            for p in range(self.groups):
+                if c or p:
+                    to = (base + (self.core ^ c), self.shard ^ p)
+                    pl.semaphore_signal(barrier, inc=1, device_id=to, device_id_type=MESH)
+        pl.semaphore_signal(barrier, inc=1, device_id=self.inward(), device_id_type=MESH)
+
+        @pl.when(self.inner())
+        def _():
+            pl.semaphore_signal(barrier, inc=1, device_id=self.outward(), device_id_type=MESH)
+            pl.semaphore_wait(barrier, 2 * self.groups + 1)
+
+        @pl.when(jnp.logical_not(self.inner()))
+        def _():
+            pl.semaphore_wait(barrier, 2 * self.groups)
+
+    def inner(self):
+        plane = lax.div(self.rep, 2)
+        return (plane == 1) | (plane == 2)
+
+    def inward(self):
+        return (self.rep + jnp.where(self.rep < 4, 2, -2), self.shard)
+
+    def outward(self):
+        return (self.rep - jnp.where(self.rep < 4, 2, -2), self.shard)
+
     def meet_core(self):
         barrier = pltpu.get_barrier_semaphore()
         pl.semaphore_signal(barrier, inc=1, device_id=self.sibling(), device_id_type=MESH)
@@ -126,8 +159,26 @@
         return pltpu.make_async_copy(src, dst, self.local.at[slot])
 
 
-class Gather:
-    def __init__(self, link, src, dst):
+class Job:
+    @staticmethod
+    def buffers(source):
+        return []
+
+    def forward(self):
+        pass
+
+    def inward(self):
+        pass
+
+    def across(self):
+        pass
+
+    def outward(self):
+        pass
+
+
+class Gather(Job):
+    def __init__(self, link, src, dst, bufs):
         self.link, self.src, self.dst = link, src, dst
         self.rows = src.shape[0]
         self.base = link.slots(max(4, link.groups - 1))
@@ -174,8 +225,8 @@
         self.keep.wait()
 
 
-class ToClip:
-    def __init__(self, link, src, dst):
+class ToClip(Job):
+    def __init__(self, link, src, dst, bufs):
         self.link, self.src, self.dst = link, src, dst
         self.rows = src.shape[1]
         self.base = link.slots(link.half + 1)
@@ -225,8 +276,8 @@
             pl.when(jnp.logical_not(mine))(there.wait_send)
 
 
-class FromClip:
-    def __init__(self, link, src, dst):
+class FromClip(Job):
+    def __init__(self, link, src, dst, bufs):
         self.link, self.src, self.dst = link, src, dst
         self.rows = dst.shape[1]
         self.base = link.slots(link.half)
@@ -256,9 +307,6 @@
             pl.when(mine)(here.start)
             pl.when(jnp.logical_not(mine))(there.start)
 
-    def forward(self):
-        pass
-
     def finish(self):
         for t in range(self.link.half):
             mine, there, here = self.copy(t)
@@ -269,8 +317,8 @@
             pl.when(jnp.logical_not(mine))(there.wait_recv)
 
 
-class Owners:
-    def __init__(self, link, src, dst):
+class Owners(Job):
+    def __init__(self, link, src, dst, bufs):
         self.link, self.src, self.dst = link, src, dst
         self.base = link.slots(link.groups - 1)
 
@@ -291,17 +339,169 @@
         for c in self.copies():
             c.start()
 
-    def forward(self):
-        pass
-
     def finish(self):
         for c in self.copies():
             c.wait()
 
 
+def add_low(a, b):
+    return (a.astype(f32) + b.astype(f32)).astype(bf16)
+
+
+class Reduce(Job):
+    def __init__(self, link, src, dst, bufs):
+        self.link, self.src, self.dst = link, src, dst
+        self.a, self.b, self.low, self.high = bufs
+        self.base = link.slots(6)
+        self.keep = link.local_slots(2)
+        self.half = dst.shape[1]
+
+    @staticmethod
+    def buffers(source):
+        half = pltpu.VMEM((source.shape[1] // 2, source.shape[2]), source.dtype)
+        return [half] * 4
+
+    def block(self, i, part):
+        rows = pl.ds(part * self.half, self.half)
+        return self.src.at[self.link.shard ^ i, rows]
+
+    def hops(self):
+        link = self.link
+        x, y = (link.rep, link.shard ^ 1), (link.rep, link.shard ^ 2)
+        plan = (
+            (self.block(3, 0), self.a, x),
+            (self.block(3, 1), self.b, y),
+            (self.block(1, 0), self.dst.at[0], x),
+            (self.block(2, 1), self.dst.at[2], y),
+        )
+        return [link.remote(s, d, self.base + i, self.base + i, to) for i, (s, d, to) in enumerate(plan)]
+
+    def later(self):
+        link = self.link
+        x, y = (link.rep, link.shard ^ 1), (link.rep, link.shard ^ 2)
+        plan = ((self.low, self.dst.at[1], y), (self.high, self.dst.at[3], x))
+        return [link.remote(s, d, self.base + 4 + i, self.base + 4 + i, to) for i, (s, d, to) in enumerate(plan)]
+
+    def loads(self):
+        link = self.link
+        return (
+            link.here(self.block(2, 0), self.low, self.keep),
+            link.here(self.block(1, 1), self.high, self.keep + 1),
+        )
+
+    def start(self):
+        for c in self.hops():
+            c.start()
+        for c in self.loads():
+            c.start()
+
+    def forward(self):
+        hops, loads, later = self.hops(), self.loads(), self.later()
+        for i, (total, part) in enumerate(((self.low, self.a), (self.high, self.b))):
+            loads[i].wait()
+            hops[i].wait_recv()
+            total[...] = add_low(total[...], part[...])
+            later[i].start()
+
+    def finish(self):
+        hops, later = self.hops(), self.later()
+        for i in range(4):
+            hops[i].wait_send()
+        for i in (2, 3):
+            hops[i].wait_recv()
+        for c in later:
+            c.wait()
+
+
+class Chain(Job):
+    def __init__(self, link, src, dst, bufs):
+        self.link, self.src, self.dst = link, src, dst
+        self.own, self.one, self.two = bufs
+        self.base = link.slots(4)
+        self.keep = link.local_slots(2)
+
+    @staticmethod
+    def buffers(source):
+        return [pltpu.VMEM(source.shape, source.dtype)] * 3
+
+    def step(self, src, dst, slot, to):
+        return self.link.remote(src, dst, self.base + slot, self.base + slot, to)
+
+    def steps(self):
+        link = self.link
+        return (
+            self.step(self.src, self.one, 0, link.inward()),
+            self.step(self.own, self.two, 1, link.inward()),
+            self.step(self.one, self.two, 2, link.outward()),
+        )
+
+    def share(self, ref):
+        link = self.link
+        place = self.dst.at[link.core]
+        return self.step(ref, place, 3, link.sibling()), link.here(ref, place, self.keep + 1)
+
+    def start(self):
+        inner = self.link.inner()
+        pl.when(inner)(self.link.here(self.src, self.own, self.keep).start)
+        pl.when(jnp.logical_not(inner))(self.steps()[0].start)
+
+    def add(self, a, b):
+        return (a[...].astype(f32) + b[...].astype(f32)).astype(a.dtype)
+
+    def inward(self):
+        @pl.when(self.link.inner())
+        def _():
+            steps = self.steps()
+            self.link.here(self.src, self.own, self.keep).wait()
+            steps[0].wait_recv()
+            self.own[...] = self.add(self.own, self.one)
+            steps[1].start()
+
+    def across(self):
+        @pl.when(self.link.inner())
+        def _():
+            steps = self.steps()
+            steps[1].wait_recv()
+            self.one[...] = self.add(self.own, self.two)
+            steps[2].start()
+            for c in self.share(self.one):
+                c.start()
+
+    def outward(self):
+        @pl.when(jnp.logical_not(self.link.inner()))
+        def _():
+            self.steps()[2].wait_recv()
+            for c in self.share(self.two):
+                c.start()
+
+    def finish(self):
+        swap, here = self.share(self.one)
+        swap.wait()
+        here.wait()
+        inner = self.link.inner()
+
+        @pl.when(inner)
+        def _():
+            self.steps()[1].wait_send()
+            self.steps()[2].wait_send()
+
+        pl.when(jnp.logical_not(inner))(self.steps()[0].wait_send)
+
+
+def run_chains(chains):
+    for i in range(len(chains) + 1):
+        if i < len(chains):
+            chains[i].inward()
+        if i:
+            chains[i - 1].across()
+    for c in chains:
+        c.outward()
+
+
 class Jobs:
     def __init__(self, *jobs):
         self.jobs = jobs
+        self.bufs = [kind.buffers(a) for kind, a, _ in jobs]
 
     def sources(self):
         return [a for _, a, _ in self.jobs]
@@ -314,16 +514,21 @@
 
     def scratch(self, extra=0):
         groups = lax.axis_size("shard")
-        remote = len(self.jobs) * max(4, groups) + extra
-        return [
+        remote = len(self.jobs) * max(6, groups) + extra
+        return [b for bufs in self.bufs for b in bufs] + [
             pltpu.SemaphoreType.DMA((remote,)),
             pltpu.SemaphoreType.DMA((remote,)),
-            pltpu.SemaphoreType.DMA((len(self.jobs) + extra + 1,)),
+            pltpu.SemaphoreType.DMA((2 * len(self.jobs) + extra + 1,)),
         ]
 
-    def bind(self, sems, srcs, dsts):
-        link = Link(sems)
-        return link, [kind(link, a, b) for (kind, _, _), a, b in zip(self.jobs, srcs, dsts)]
+    def bind(self, rest, srcs, dsts):
+        rest = list(rest)
+        bufs = []
+        for shapes in self.bufs:
+            bufs.append([rest.pop(0) for _ in shapes])
+        link = Link(rest[:3])
+        bound = [kind(link, a, b, c) for (kind, _, _), a, b, c in zip(self.jobs, srcs, dsts, bufs)]
+        return link, bound, rest[3:]
 
 
 def comm_params(number, limit=60):
@@ -338,7 +543,7 @@
     def kernel(*refs):
         srcs, mine = refs[:count], refs[count]
         dsts, other = refs[count + 1 : 2 * count + 1], refs[2 * count + 1]
-        link, bound = jobs.bind(refs[2 * count + 2 :], srcs, dsts)
+        link, bound, _ = jobs.bind(refs[2 * count + 2 :], srcs, dsts)
         slot = link.slots(1)
         swap = link.remote(mine, other, slot, slot, link.sibling())
         link.meet_plane()
@@ -422,7 +627,7 @@
     len_ref, q_ref, k_ref, v_ref = refs[:4]
     o_ref, lse_ref = refs[4 + count : 6 + count]
     acc, kx = refs[6 + 2 * count : 8 + 2 * count]
-    link, bound = jobs.bind(refs[8 + 2 * count :], refs[4 : 4 + count], refs[6 + count : 6 + 2 * count])
+    link, bound, _ = jobs.bind(refs[8 + 2 * count :], refs[4 : 4 + count], refs[6 + count : 6 + 2 * count])
     h = pl.program_id(0)
     heads = pl.num_programs(0)
     n = q_ref.shape[0]
@@ -487,18 +692,35 @@
     len_ref, q_ref, k_ref, v_ref, o_ref, do_ref, lse_ref = refs[:7]
     g_ref, sum_ref = refs[7 + count : 9 + count]
     dq, dk, dv, part, qa, da, kx = refs[9 + 2 * count : 16 + 2 * count]
-    link, bound = jobs.bind(refs[16 + 2 * count :], refs[7 : 7 + count], refs[9 + count : 9 + 2 * count])
+    link, bound, _ = jobs.bind(refs[16 + 2 * count :], refs[7 : 7 + count], refs[9 + count : 9 + 2 * count])
+    chains = [job for job in bound if isinstance(job, Chain)]
     h = pl.program_id(0)
     n = q_ref.shape[0]
 
     @pl.when(h == 0)
     def _():
-        link.meet_plane()
+        if chains:
+            link.meet_all()
+        else:
+            link.meet_plane()
         for job in bound:
             job.start()
         for ref in (dq, dk, dv):
             ref[...] = jnp.zeros_like(ref)
         kx[...] = key_extra(n, len_ref[0])
+
+    heads = pl.num_programs(0)
+
+    def at_head(number, steps):
+        @pl.when(h == number)
+        def _():
+            for step in steps:
+                step()
+
+    if chains:
+        at_head(2, [c.inward for c in chains[:1]])
+        at_head(4, [c.inward for c in chains[1:]] + [c.across for c in chains[:1]])
+    at_head(heads - 2, [job.forward for job in bound] + [c.across for c in chains[1:]])
 
     win, keep, lane = head_window(h)
     low = keep.astype(bf16)
@@ -524,7 +746,7 @@
         part[...] = new if i == 0 else part[...] + new
     dq[:, win] += part[...] * keep
 
-    @pl.when(h == pl.num_programs(0) - 1)
+    @pl.when(h == heads - 1)
     def _():
         for i, (ref, factor) in enumerate(((dq, SCALE), (dk, SCALE), (dv, 1.0))):
             value = (ref[:, : g_ref.shape[1] // 3] * factor).astype(bf16)
@@ -532,6 +754,8 @@
             g_ref[:, cols] = value
             sum_ref[:, cols] = jnp.sum(value.astype(f32), axis=0, keepdims=True)
         for job in bound:
+            job.outward()
+        for job in bound:
             job.finish()
 
 
@@ -541,8 +765,8 @@
         functools.partial(attn_bwd_kernel, bk=256, jobs=jobs),
         grid=(heads,),
         in_specs=[pl.BlockSpec(memory_space=pltpu.SMEM)]
-        + [whole((n, wide))] * 5
-        + [whole((n, 128))]
+        + [once((n, wide))] * 5
+        + [once((n, 128))]
         + jobs.in_specs(),
         out_specs=[whole((n, 3 * width)), whole((1, 3 * width))] + jobs.in_specs(),
         out_shape=[
@@ -628,7 +852,7 @@
     ht, act, grad = refs[:3]
     acc, dh = refs[3:5] if last else (out_ref, dh_ref)
     refs = refs[5:] if last else refs[3:]
-    link, bound = jobs.bind(refs[:3], srcs, dsts)
+    link, bound, refs = jobs.bind(refs, srcs, dsts)
     t = pl.program_id(0)
     tiles = pl.num_programs(0)
     n = h_ref.shape[0]
@@ -639,7 +863,7 @@
         for job in bound:
             job.start()
         if chained:
-            sem = refs[3]
+            sem = refs[0]
             copies = [
                 pltpu.make_async_copy(src, dst, sem.at[i])
                 for i, (src, dst) in enumerate(((old_out, acc), (old_dh, dh)))
@@ -690,13 +914,13 @@
     bt = FFN_TILE
     out = jax.ShapeDtypeStruct((n, d), bf16 if last else f32)
     chained = old is not None
-    once = pl.BlockSpec((n, d), lambda t: (0, 0), pipeline_mode=pl.Buffered(1))
+    kept = once((n, d))
     return pl.pallas_call(
         functools.partial(ffn_kernel, chained=chained, last=last, mc=FFN_ROWS, jobs=jobs),
         grid=(hidden // bt,),
         in_specs=[
-            once,
-            once,
+            kept,
+            kept,
             pl.BlockSpec((d, bt), lambda t: (0, t)),
             pl.BlockSpec((1, bt), lambda t: (0, t)),
             pl.BlockSpec((bt, d), lambda t: (t, 0)),
@@ -704,8 +928,8 @@
         + ([pl.BlockSpec(memory_space=pl.ANY)] * 2 if chained else [])
         + jobs.in_specs(),
         out_specs=[
-            once,
-            once,
+            kept,
+            kept,
             pl.BlockSpec((d, bt), lambda t: (0, t)),
             pl.BlockSpec((bt, d), lambda t: (t, 0)),
             pl.BlockSpec((1, bt), lambda t: (0, t)),
@@ -855,7 +1079,7 @@
     g_ref, w_ref, vec_ref, x_any, dmid_any = refs[:5]
     dx_ref, sums_ref = refs[5 + count : 7 + count]
     x, dmid, mine, other = refs[7 + 2 * count : 11 + 2 * count]
-    link, bound = jobs.bind(refs[11 + 2 * count :], refs[5 : 5 + count], refs[7 + count : 7 + 2 * count])
+    link, bound, _ = jobs.bind(refs[11 + 2 * count :], refs[5 : 5 + count], refs[7 + count : 7 + 2 * count])
     size = dx_ref.shape[0]
     half = size // ROWS
     base = link.slots(half)
@@ -934,12 +1158,313 @@
     )(grads, w, vec, x, dmid, *jobs.sources())
 
 
+class Blocks:
+    def __init__(self, ref, rows):
+        self.ref, self.rows = ref, rows
+
+    @property
+    def at(self):
+        return self
+
+    def __getitem__(self, index):
+        block, part = index
+        first = pl.multiple_of(block * self.rows + part.start, 16)
+        return self.ref.at[pl.ds(first, part.size)]
+
+
+def back_kernel(*refs, jobs):
+    count = len(jobs.jobs)
+    g_ref, w_ref, vec_ref, h_ref, x_any, dmid_any = refs[:6]
+    dx_ref, sums_ref, own_ref = refs[6 + count : 9 + count]
+    x, dmid, mine, other, dw, left = refs[9 + 2 * count : 15 + 2 * count]
+    bufs = refs[15 + 2 * count : 19 + 2 * count]
+    link, chains, _ = jobs.bind(refs[19 + 2 * count :], refs[6 : 6 + count], refs[9 + count : 9 + 2 * count])
+    size, d = dx_ref.shape
+    half = size // ROWS
+    owned = own_ref.shape[0]
+    reduce = Reduce(link, Blocks(dw, owned), left, bufs)
+    base = link.slots(half)
+    keep = link.local_slots(2)
+    own = pl.ds(pl.multiple_of(link.core * size, size), size)
+    loads = [link.here(x_any.at[own], x, keep), link.here(dmid_any.at[own], dmid, keep + 1)]
+    for c in loads:
+        c.start()
+    link.meet_all()
+    for job in chains:
+        job.start()
+
+    def weight(i, carry):
+        part = pl.ds(pl.multiple_of(i * 256, 256), 256)
+        dw[part, :] = dot_tn(h_ref[:, part], g_ref[...]).astype(bf16)
+        return carry
+
+    lax.fori_loop(0, d // 256, weight, 0)
+    reduce.start()
+
+    def product(j):
+        rows = pl.ds(pl.multiple_of(j * ROWS, ROWS), ROWS)
+        return dot_nt(g_ref[rows, :], w_ref[...])
+
+    def swap(j):
+        rows = pl.ds(pl.multiple_of(j * ROWS, ROWS), ROWS)
+        return rows, link.remote(mine.at[rows], other.at[rows], base + j, base + j, link.sibling())
+
+    def send(j, carry):
+        rows, copy = swap(j)
+        mine[rows, :] = product((1 - link.core) * half + j).astype(bf16)
+        copy.start()
+        return carry
+
+    def norm(j, carry):
+        rows, copy = swap(j)
+        part = product(link.core * half + j)
+        copy.wait_recv()
+        xhat, inv = standardize(x[rows, :].astype(f32))
+        dh = part + other[rows, :].astype(f32)
+        dx = dh * vec_ref[GAIN1]
+        dx_ref[rows, :] = (
+            dmid[rows, :]
+            + inv
+            * (dx - jnp.mean(dx, axis=-1, keepdims=True) - xhat * jnp.mean(dx * xhat, axis=-1, keepdims=True))
+        ).astype(bf16)
+        for row, value in enumerate((dh * xhat, dh)):
+            sums_ref[row : row + 1, :] += jnp.sum(value, axis=0, keepdims=True)
+        return carry
+
+    sums_ref[...] = jnp.zeros_like(sums_ref)
+    lax.fori_loop(0, half, send, 0)
+    for c in loads:
+        c.wait()
+    chains[0].inward()
+    lax.fori_loop(0, half, norm, 0)
+    for j in range(half):
+        swap(j)[1].wait_send()
+    reduce.forward()
+    for i in range(1, len(chains) + 1):
+        if i < len(chains):
+            chains[i].inward()
+        chains[i - 1].across()
+    reduce.finish()
+    cut = owned // 2
+    for part in range(2):
+        first = pl.multiple_of(link.shard * owned + part * cut, 16)
+        block = dw[pl.ds(first, cut), :].astype(f32)
+        own_ref[part * cut : (part + 1) * cut, :] = (
+            block + left[2 * part].astype(f32) + left[2 * part + 1].astype(f32)
+        ).astype(bf16)
+    for job in chains:
+        job.outward()
+    for job in chains:
+        job.finish()
+
+
+def back_call(grads, w, vec, h, x, dmid, jobs, number):
+    n, d = x.shape
+    size = n // 2
+    cols = grads.shape[1]
+    owned = d // lax.axis_size("shard")
+    part = pltpu.VMEM((owned // 2, cols), bf16)
+    vmem = pl.BlockSpec(memory_space=pltpu.VMEM)
+    hbm = pl.BlockSpec(memory_space=pl.ANY)
+    return pl.pallas_call(
+        functools.partial(back_kernel, jobs=jobs),
+        in_specs=[vmem] * 4 + [hbm] * 2 + jobs.in_specs(),
+        out_specs=[vmem] * 3 + jobs.in_specs(),
+        out_shape=[
+            jax.ShapeDtypeStruct((size, d), bf16),
+            jax.ShapeDtypeStruct((8, d), f32),
+            jax.ShapeDtypeStruct((owned, cols), bf16),
+        ]
+        + jobs.out_shapes(),
+        scratch_shapes=[
+            pltpu.VMEM((size, d), bf16),
+            pltpu.VMEM((size, d), f32),
+            pltpu.VMEM((size, d), bf16),
+            pltpu.VMEM((size, d), bf16),
+            pltpu.VMEM((d, cols), bf16),
+            pltpu.VMEM((4, owned // 2, cols), bf16),
+        ]
+        + [part] * 4
+        + jobs.scratch(size // ROWS + 8),
+        compiler_params=comm_params(number, 62),
+        cost_estimate=cost(4 * n * w.size, 20 * n * d),
+        name="back",
+    )(grads, w, vec, h, x, dmid, *jobs.sources())
+
+
+def finish_kernel(*refs, jobs, parts):
+    count = len(jobs.jobs)
+    early_ref, late_ref, own_any = refs[:3]
+    small_ref, both_any = refs[3 + count : 5 + count]
+    rest = refs[5 + 2 * count :]
+    total, came, chain_bufs, rest = rest[0], rest[1], rest[2:5], rest[5:]
+    own_bufs, rest = rest[: 3 * parts], rest[3 * parts :]
+    link, bound, _ = jobs.bind(rest, refs[3 : 3 + count], refs[5 + count : 5 + 2 * count])
+    size = own_any.shape[0] // parts
+    chains = []
+    for i in range(parts):
+        rows = pl.ds(i * size, size)
+        chains.append(Chain(link, own_any.at[rows], both_any.at[:, rows], own_bufs[3 * i : 3 * i + 3]))
+    base = link.slots(3)
+    peers = [link.sibling()] + [(link.rep, link.shard ^ bit) for bit in (1, 2)]
+    swaps = [link.remote(total, came.at[i], base + i, base + i, to) for i, to in enumerate(peers)]
+    small = Chain(link, total, small_ref, chain_bufs)
+    first = early_ref.shape[0]
+    total[:first, :] = early_ref[...]
+    total[first:, :] = late_ref[...]
+    link.meet_all()
+    swaps[0].start()
+    for c in chains:
+        c.start()
+    for job in bound:
+        job.start()
+    for i in range(parts + 1):
+        if i < 3:
+            swaps[i].wait()
+            total[...] += came[i]
+            if i < 2:
+                swaps[i + 1].start()
+            else:
+                small.start()
+        if i < parts:
+            chains[i].inward()
+        if i:
+            chains[i - 1].across()
+        if i == 3:
+            small.inward()
+    small.across()
+    for c in chains:
+        c.outward()
+    small.outward()
+    for c in chains:
+        c.finish()
+    small.finish()
+    for job in bound:
+        job.finish()
+
+
+def finish_call(early, late, own, jobs, number):
+    rows = early.shape[0] + late.shape[0]
+    d = early.shape[1]
+    parts = 4
+    small = pltpu.VMEM((rows, d), f32)
+    vmem = pl.BlockSpec(memory_space=pltpu.VMEM)
+    hbm = pl.BlockSpec(memory_space=pl.ANY)
+    return pl.pallas_call(
+        functools.partial(finish_kernel, jobs=jobs, parts=parts),
+        in_specs=[vmem] * 2 + [hbm] + jobs.in_specs(),
+        out_specs=[vmem, hbm] + jobs.in_specs(),
+        out_shape=[
+            jax.ShapeDtypeStruct((2, rows, d), f32),
+            jax.ShapeDtypeStruct((2,) + own.shape, bf16),
+        ]
+        + jobs.out_shapes(),
+        scratch_shapes=[small, pltpu.VMEM((3, rows, d), f32)]
+        + [small] * 3
+        + [pltpu.VMEM((own.shape[0] // parts, own.shape[1]), bf16)] * (3 * parts)
+        + jobs.scratch(6 * parts + 8),
+        compiler_params=comm_params(number),
+        name="finish",
+    )(early, late, own, *jobs.sources())
+
+
+def place_up_kernel(a_ref, b_ref, out_ref):
+    first, second = a_ref.shape[2], b_ref.shape[2]
+    for c in range(2):
+        base = c * (first + second)
+        out_ref[:, base : base + first] = a_ref[c].astype(f32)
+        out_ref[:, base + first : base + first + second] = b_ref[c].astype(f32)
+
+
+def place_up_call(a, b, groups):
+    rows = a.shape[1]
+    first, second = a.shape[2] // groups, b.shape[2] // groups
+    return pl.pallas_call(
+        place_up_kernel,
+        grid=(groups,),
+        in_specs=[
+            pl.BlockSpec((2, rows, first), lambda i: (0, 0, i)),
+            pl.BlockSpec((2, rows, second), lambda i: (0, 0, i)),
+        ],
+        out_specs=pl.BlockSpec((rows, 2 * (first + second)), lambda i: (0, i)),
+        out_shape=jax.ShapeDtypeStruct((rows, 2 * (first + second) * groups), f32),
+        compiler_params=params(),
+        name="place_up",
+    )(a, b)
+
+
+def place_down_kernel(a_ref, b_ref, out_ref):
+    first, second = a_ref.shape[1], b_ref.shape[1]
+    for c in range(2):
+        base = c * (first + second)
+        out_ref[base : base + first, :] = a_ref[c].astype(f32)
+        out_ref[base + first : base + first + second, :] = b_ref[c].astype(f32)
+
+
+def place_down_call(a, b):
+    d = a.shape[2]
+    first, second = a.shape[1], b.shape[1]
+    return pl.pallas_call(
+        place_down_kernel,
+        grid=(d // 256,),
+        in_specs=[
+            pl.BlockSpec((2, first, 256), lambda i: (0, 0, i)),
+            pl.BlockSpec((2, second, 256), lambda i: (0, 0, i)),
+        ],
+        out_specs=pl.BlockSpec((2 * (first + second), 256), lambda i: (0, i)),
+        out_shape=jax.ShapeDtypeStruct((2 * (first + second), d), f32),
+        compiler_params=params(),
+        name="place_down",
+    )(a, b)
+
+
+def place_qkv_kernel(in_ref, *outs, groups):
+    rows = in_ref.shape[1]
+    width = in_ref.shape[2] // 3
+    part = width // groups
+    row = lax.broadcasted_iota(jnp.int32, (width, 2 * width), 0)
+    ahead = lax.broadcasted_iota(jnp.int32, (width, 2 * width), 1) - row
+    places = []
+    for c in range(2):
+        place = jnp.zeros((width, 2 * width), f32)
+        for s in range(groups):
+            here = (row >= s * part) & (row < (s + 1) * part) & (ahead == (s + c) * part)
+            place = jnp.where(here, 1.0, place)
+        places.append(place.astype(bf16))
+    for i, out in enumerate(outs):
+        cols = slice(i * width, (i + 1) * width)
+        out[...] = dot(in_ref[0, :, cols], places[0]) + dot(in_ref[1, :, cols], places[1])
+
+
+def place_qkv_call(both, groups):
+    _, rows, cols = both.shape
+    vmem = pl.BlockSpec(memory_space=pltpu.VMEM)
+    return pl.pallas_call(
+        functools.partial(place_qkv_kernel, groups=groups),
+        in_specs=[vmem],
+        out_specs=[vmem] * 3,
+        out_shape=[jax.ShapeDtypeStruct((rows, 2 * cols // 3), f32)] * 3,
+        compiler_params=params(),
+        name="place_qkv",
+    )(both)
+
+
 def own_sum(blocks, others):
     shard = lax.axis_index("shard")
     total = lax.dynamic_index_in_dim(blocks, shard, 0, keepdims=False).astype(f32)
     for i in range(others.shape[0]):
         total = total + others[i].astype(f32)
     return total.astype(bf16)
+
+
+def own_sum2(blocks, left):
+    shard = lax.axis_index("shard")
+    block = lax.dynamic_index_in_dim(blocks, shard, 0, keepdims=False).astype(f32)
+    cut = block.shape[0] // 2
+    left = left.astype(f32)
+    return jnp.concatenate(
+        [block[:cut] + left[0] + left[1], block[cut:] + left[2] + left[3]], axis=0
+    ).astype(bf16)
 
 
 def over_reps(own):
@@ -1052,8 +1577,18 @@
     def hidden_bias(piece):
         return ubias[:, piece[0] : piece[1]].reshape(1, -1)
 
+    fast = g == 4 and lax.axis_size("rep") == 8
+
     def to_owners(a):
+        if fast:
+            return (Reduce, a, (4, a.shape[1] // 2, a.shape[2]))
         return (Owners, a, (g - 1,) + a.shape[1:])
+
+    def owned(a, came):
+        return own_sum2(a, came) if fast else own_sum(a, came)
+
+    def chained(a):
+        return (Chain, a, (2,) + a.shape)
 
     jobs = Jobs(gathered(ups[1]), gathered(downs[1]))
     out, dh2, dup0, ddn0, dub0, up1, down1 = ffn_call(
@@ -1065,54 +1600,68 @@
         h2, dz, up1.reshape(d, -1), hidden_bias(pieces[1]), down1.reshape(-1, d), (out, dh2), True, jobs, 4, "hidden1"
     )
     dup1, ddn1 = dup1.reshape(g, own_d, -1), ddn1.reshape(g, -1, d)
-    up0_all = over_reps(own_sum(dup0, dup0_in))
-    down0_all = over_reps(own_sum(ddn0, ddn0_in))
+    up0_own, down0_own = owned(dup0, dup0_in), owned(ddn0, ddn0_in)
 
     dmid, do, dwo, sums2, layer_own = second_back_call(mid, dh2, out, dz, vec, w_out, o, wide, 5)
     dwo = dwo.reshape(g, -1, d)
 
-    jobs = Jobs(to_owners(dup1), to_owners(ddn1), to_owners(dwo), (FromClip, layer_own, (cl, rows, d)))
-    grads, bias_sums, dup1_in, ddn1_in, dwo_in, layer_out = attn_bwd_call(
-        length, q, k, v, o_wide, do, lse, width, heads, jobs, 6
+    jobs = [to_owners(dup1), to_owners(ddn1), to_owners(dwo), (FromClip, layer_own, (cl, rows, d))]
+    if fast:
+        jobs += [chained(up0_own), chained(down0_own)]
+    grads, bias_sums, dup1_in, ddn1_in, dwo_in, layer_out, *sums0 = attn_bwd_call(
+        length, q, k, v, o_wide, do, lse, width, heads, Jobs(*jobs), 6
     )
-    up1_all = over_reps(own_sum(dup1, dup1_in))
-    down1_all = over_reps(own_sum(ddn1, ddn1_in))
-    out_grad = over_reps(own_sum(dwo, dwo_in)).reshape(own_d, d).astype(f32)
-    dwqkv = dw_call(h1, grads).reshape(g, own_d, 3 * width)
-    jobs = Jobs(to_owners(dwqkv))
-    dx, sums1, dwqkv_in = first_back_call(grads, w_qkv, vec, x, dmid, jobs, 7)
-    qkv_all = over_reps(own_sum(dwqkv, dwqkv_in)).reshape(2, own_d, 3, g, attn_cols)
-    jobs = Jobs((FromClip, dx, (cl, rows, d)))
-    tokens_grad, _ = exchange_call(jobs, sums1, 8, "last_exchange")
-
-    up_all = jnp.concatenate([up0_all.reshape(2, own_d, g, -1), up1_all.reshape(2, own_d, g, -1)], axis=3)
-    up_grad = up_all.transpose(1, 2, 0, 3).reshape(own_d, ff).astype(f32)
-    down_grad = jnp.concatenate([down0_all, down1_all], axis=1).reshape(own_f, d).astype(f32)
-    qkv_grads = [qkv_all[:, :, i].transpose(1, 2, 0, 3).reshape(own_d, d).astype(f32) for i in range(3)]
+    up1_own, down1_own, out_own_grad = owned(dup1, dup1_in), owned(ddn1, ddn1_in), owned(dwo, dwo_in)
 
     def spread(v, size):
         out = jnp.zeros((g, 2, size), f32)
-        return lax.dynamic_update_index_in_dim(out, v.reshape(g, size), core, 1).reshape(-1, own_d)
-
-    pieces_small = [
-        sums1[0].reshape(g, own_d),
-        sums1[1].reshape(g, own_d),
-        spread(bias_sums[0, :width], attn_cols),
-        spread(bias_sums[0, 2 * width :], attn_cols),
-        (sums2[2] * 0.5).reshape(g, own_d),
-        (sums2[0] * 0.5).reshape(g, own_d),
-        (sums2[1] * 0.5).reshape(g, own_d),
-        (sums2[3] * 0.5).reshape(g, own_d),
-    ]
-    ub_sum = jnp.zeros((g, 2, ffn_cols), f32)
-    ub_sum = lax.dynamic_update_index_in_dim(ub_sum, jnp.concatenate([dub0.reshape(g, -1), dub1.reshape(g, -1)], axis=1), core, 1)
-    packed = jnp.concatenate(
-        [jnp.stack(pieces_small, axis=1), ub_sum.reshape(g, -1, own_d)], axis=1
+        return lax.dynamic_update_index_in_dim(out, v.reshape(g, size), core, 1)
+
+    ub_sums = jnp.concatenate([dub0.reshape(g, -1), dub1.reshape(g, -1)], axis=1)
+    early = jnp.concatenate(
+        [
+            spread(bias_sums[0, :width], attn_cols).reshape(1, d),
+            spread(bias_sums[0, 2 * width :], attn_cols).reshape(1, d),
+            sums2[:4] * 0.5,
+            spread(ub_sums, ffn_cols).reshape(-1, d),
+        ],
+        axis=0,
     )
-    packed = lax.psum(packed, ("rep", "shard"))
-    mine_small = lax.dynamic_index_in_dim(packed, shard, 0, keepdims=False)
-    s_gain1, s_shift1, s_qb, s_vb, s_ob, s_gain2, s_shift2, s_db = [mine_small[i] for i in range(8)]
-    s_ub = mine_small[8:].reshape(-1)
+    early = jnp.pad(early, ((0, -early.shape[0] % 8), (0, 0)))
+
+    def to_halves(a):
+        return [a[i * a.shape[0] // 2 : (i + 1) * a.shape[0] // 2] for i in range(2)]
+
+    if fast:
+        pieces_own = to_halves(up1_own) + to_halves(down1_own) + [out_own_grad]
+        jobs = Jobs(*[chained(a) for a in pieces_own])
+        dx, sums1, qkv_own_grad, *sums = back_call(grads, w_qkv, vec, h1, x, dmid, jobs, 7)
+        jobs = Jobs((FromClip, dx, (cl, rows, d)))
+        smalls, qkv_all, tokens_grad = finish_call(early, sums1, qkv_own_grad, jobs, 8)
+        up_grad = place_up_call(sums0[0], jnp.concatenate(sums[:2], axis=1), g)
+        down_grad = place_down_call(sums0[1], jnp.concatenate(sums[2:4], axis=1))
+        out_grad = sums[4].reshape(own_d, d).astype(f32)
+        qkv_grads = place_qkv_call(qkv_all, g)
+        smalls = lax.dynamic_index_in_dim(smalls, core, 0, keepdims=False)
+    else:
+        dwqkv = dw_call(h1, grads).reshape(g, own_d, 3 * width)
+        jobs = Jobs(to_owners(dwqkv))
+        dx, sums1, dwqkv_in = first_back_call(grads, w_qkv, vec, x, dmid, jobs, 7)
+        jobs = Jobs((FromClip, dx, (cl, rows, d)))
+        tokens_grad, _ = exchange_call(jobs, sums1, 8, "last_exchange")
+        ups_all = [over_reps(a).reshape(2, own_d, g, -1) for a in (up0_own, up1_own)]
+        up_grad = jnp.concatenate(ups_all, axis=3).transpose(1, 2, 0, 3).reshape(own_d, ff).astype(f32)
+        downs_all = [over_reps(a) for a in (down0_own, down1_own)]
+        down_grad = jnp.concatenate(downs_all, axis=1).reshape(own_f, d).astype(f32)
+        out_grad = over_reps(out_own_grad).reshape(own_d, d).astype(f32)
+        qkv_all = over_reps(owned(dwqkv, dwqkv_in)).reshape(2, own_d, 3, g, attn_cols)
+        qkv_grads = [qkv_all[:, :, i].transpose(1, 2, 0, 3).reshape(own_d, d).astype(f32) for i in range(3)]
+        smalls = lax.psum(jnp.concatenate([early, sums1], axis=0), ("rep", "shard"))
+
+    mine = lax.dynamic_slice_in_dim(smalls, shard * own_d, own_d, 1)
+    s_qb, s_vb, s_gain2, s_shift2, s_ob, s_db = [mine[i] for i in range(6)]
+    s_gain1, s_shift1 = [mine[early.shape[0] + i] for i in range(2)]
+    s_ub = lax.dynamic_slice_in_dim(smalls[6 : 6 + ff // d].reshape(-1), shard * own_f, own_f, 0)
 
     return (
         layer_out,

time: 889 us -> 717 us (0.81)
  local copies, waits for them, and re-layouts: 96.5 us -> 25.6 us
  blocking collectives: 59.5 us -> 0 us
  waiting for transfers between devices: 55.1 us -> 0 us
  Pallas kernels: 610 us -> 653 us
  other arithmetic: 45.9 us -> 31.9 us
  between operations: 15.5 us -> 2.26 us
    pallas_call x2 -> x5, Pallas kernels: 75.9 us -> 171 us  [the longest x1 91.4 us: back_call(): pl.pallas_call(functools.partial(back_kernel, jobs=jobs), in_specs=[vmem]...]
    psum x1 -> x0, blocking collectives: 39.4 us -> none  [on_device(): packed = lax.psum(packed, ('rep', 'shard'))]
    pallas_call x2 -> x1, Pallas kernels: 106 us -> 73.2 us  [exchange_call(): pl.pallas_call(kernel, in_specs=jobs.in_specs() + [pl.BlockSpec(memory_sp...]
    convert_element_type x6 -> x0, local copies, waits for them, and re-layouts: 31.8 us -> none  [the longest x2 19.7 us: on_device(): up_grad = up_all.transpose(1, 2, 0, 3).reshape(own_d, ff).astype(f32)]
    all_gather x5 -> x0, waiting for transfers between devices: 28.2 us -> none  [over_reps(): both = lax.all_gather(sums, 'rep', axis=0)]
    pallas_call x1, Pallas kernels: 135 us -> 109 us  [attn_bwd_call(): pl.pallas_call(functools.partial(attn_bwd_kernel, bk=256, jobs=jobs), gri...]
    reduce_scatter x6 -> x0, waiting for transfers between devices: 24.3 us -> none  [over_reps(): lax.psum_scatter(own, 'rep', scatter_dimension=0, tiled=True, axis_index_...]
    all_gather x1 -> x0, blocking collectives: 20.1 us -> none  [over_reps(): both = lax.all_gather(sums, 'rep', axis=0)]
  transfers between devices with their start and end apart: 11 -> 0, of which waited for: 3 -> 0; matrix products, arithmetic and copies ran while one was open for 7% -> 0% of each run, Pallas kernels for 31% -> 0%
where the time goes in v3:
time: 717 us; the launch traced here: 713 us
  Pallas kernels  653 us (91%)
  other arithmetic  31.9 us (4%)
  local copies, waits for them, and re-layouts  25.6 us (4%)
    pallas_call x2, Pallas kernels, ffn_call(): pl.pallas_call(functools.partial(ffn_kernel, chained=chained, last=last,...  154 us
    pallas_call x1, Pallas kernels, attn_bwd_call(): pl.pallas_call(functools.partial(attn_bwd_kernel, bk=256, jobs=jobs), gri...  109 us
    pallas_call x1, Pallas kernels, back_call(): pl.pallas_call(functools.partial(back_kernel, jobs=jobs), in_specs=[vmem]...  91.4 us
    pallas_call x1, Pallas kernels, attn_fwd_call(): pl.pallas_call(functools.partial(attn_fwd_kernel, bq=256, jobs=jobs), gri...  88.7 us
    pallas_call x1, Pallas kernels, exchange_call(): pl.pallas_call(kernel, in_specs=jobs.in_specs() + [pl.BlockSpec(memory_sp...  73.2 us
    pallas_call x1, Pallas kernels, finish_call(): pl.pallas_call(functools.partial(finish_kernel, jobs=jobs, parts=parts),...  61.7 us
    pallas_call x1, Pallas kernels, second_back_call(): pl.pallas_call(second_back_kernel, grid=(n // ROWS,), in_specs=[block] *...  25.8 us
    pallas_call x1, Pallas kernels, middle_call(): pl.pallas_call(middle_kernel, in_specs=[vmem] * 4, out_specs=[vmem] * 3,...  16.6 us

profile of v3, /device:TPU:0, one launch (start us, length us, event | category | flops | bytes accessed | tf_op | source)
XLA Modules:
  0.0 712.7 jit_solution(12030163917295608431)
XLA Ops:
  0.7 2.0 fusion.26
  7.7 73.2 %first_exchange.1 = (bf16[1536,1280]{1,0:T(8,128)(2,1)}, bf16[4,320,1920]{2,1,0:T(8,128)(2,1)}, f32[4,16,384]{2,1,0:T(8,128)}, f32[16,384]{1,0:T(8,128)}) custom-call(bf16[2,384,1280]{2,1,0:T(8,128)(2,1)} %refs_0_.1, bf16[320,1920]{1,0:T(8,128)(2,1)} %pad_maximum_fusion.2.refs_1_, f32[16,384]{1,0:T(8,128)} %select_maximum_fusion.3.refs_2_.refs_3_, ...), custom_call_target="tpu_custom_call" | custom-call | tf_op jit(solution)/shard_map/first_exchange/pallas_call | solution.py:559
  82.1 1.2 fusion.27
  86.8 15.2 %project.1 = (bf16[1536,1280]{1,0:T(8,128)(2,1)}, bf16[1536,768]{1,0:T(8,128)(2,1)}, bf16[1536,768]{1,0:T(8,128)(2,1)}, bf16[1536,768]{1,0:T(8,128)(2,1)}) custom-call(bf16[1536,1280]{1,0:T(8,128)(2,1)} %get-tuple-element.76.x_ref.refs_4_, f32[16,1280]{1,0:T(8,128)} %reshape.213.vec_ref.refs_2_, bf16[1280,1920]{1,0:T(8,128)(2,1)} %bitcast.72, ...), custom_call_target="tpu_custom_call" | custom-call | flops 7549747200 | bytes 19857408 | tf_op jit(solution)/shard_map/project/pallas_call | solution.py:584
  102.8 1.5 fusion.23
  105.3 2.0 constant_dynamic-slice_fusion.1.refs_7_
  107.2 88.7 %attend.1 = (bf16[1536,640]{1,0:T(8,128)(2,1)}, f32[1536,128]{1,0:T(8,128)}, bf16[4,160,1280]{2,1,0:T(8,128)(2,1)}, bf16[1536,1280]{1,0:T(8,128)(2,1)}, bf16[4,3...) custom-call(s32[1]{0:T(128)} %bitcast.refs_0_, bf16[1536,768]{1,0:T(8,128)(2,1)} %get-tuple-element.79.refs_1_, ...), custom_call_target="tpu_custom_call" | custom-call | flops 19327352832 | bytes 9437184 | tf_op jit(solution)/shard_map/attend/pallas_call | solution.py:677
  196.0 16.6 %middle.1 = (f32[1536,1280]{1,0:T(8,128)}, bf16[1536,1280]{1,0:T(8,128)(2,1)}, bf16[1536,768]{1,0:T(8,128)(2,1)}) custom-call(bf16[1536,640]{1,0:T(8,128)(2,1)} %get-tuple-element.82.o_ref, bf16[640,1280]{1,0:T(8,128)(2,1)} %bitcast.54, bf16[1536,1280]{1,0:T(8,128)(2,1)} %get-tuple-element.76.x_ref.refs_4_, f32[16,1280]{1,0:T(8,128)} %reshape.213.vec_ref.refs_2_), custom_call_target="tpu_custom_call" | custom-call | flops 2516582400 | bytes 27525120 | tf_op jit(solution)/shard_map/middle/pallas_call | solution.py:826
  212.6 2.4 broadcast_select_fusion.refs_1_.dz_ref
  215.8 1.8 fusion.22
  218.8 2.2 constant_dynamic-slice_fusion.5.refs_6_
  221.0 78.1 %hidden0.1 = (f32[1536,1280]{1,0:T(8,128)}, f32[1536,1280]{1,0:T(8,128)}, bf16[1280,1024]{1,0:T(8,128)(2,1)}, bf16[1024,1280]{1,0:T(8,128)(2,1)}, f32[1,1024]{1,...) custom-call(bf16[1536,1280]{1,0:T(8,128)(2,1)} %get-tuple-element.86.refs_0_, ...), custom_call_target="tpu_custom_call" | custom-call | flops 24159191040 | bytes 34078720 | tf_op jit(solution)/shard_map/hidden0/pallas_call | solution.py:918
  299.7 75.7 %hidden1.1 = (bf16[1536,1280]{1,0:T(8,128)(2,1)}, bf16[1536,1280]{1,0:T(8,128)(2,1)}, bf16[1280,1536]{1,0:T(8,128)(2,1)}, bf16[1536,1280]{1,0:T(8,128)(2,1)}, f3...) custom-call(bf16[1536,1280]{1,0:T(8,128)(2,1)} %get-tuple-element.86.refs_0_, ...), custom_call_target="tpu_custom_call" | custom-call | flops 36238786560 | bytes 39321600 | tf_op jit(solution)/shard_map/hidden1/pallas_call | solution.py:918
  375.4 25.8 %second_back.1 = (f32[1536,1280]{1,0:T(8,128)}, bf16[1536,768]{1,0:T(8,128)(2,1)}, bf16[640,1280]{1,0:T(8,128)(2,1)}, f32[8,1280]{1,0:T(8,128)}, bf16[768,1280]{1,0:T(8,128)(2,1)}) custom-call(f32[1536,1280]{1,0:T(8,128)} %get-tuple-element.85.mid_ref, bf16[1536,1280]{1,0:T(8,128)(2,1)} %get-tuple-element.96.dh_ref.dh_any, ...), custom_call_target="tpu_custom_call" | custom-call | flops 5033164800 | bytes 27525120 | tf_op jit(solution)/shard_map/second_back/pallas_call | solution.py:1030
  401.2 1.6 convert_element_type.70
  402.8 1.2 dynamic-slice_convert_fusion.3
  407.9 109.0 %attend_back.1 = (bf16[1536,1920]{1,0:T(8,128)(2,1)}, f32[1,1920]{1,0:T(1,128)}, bf16[4,160,1536]{2,1,0:T(8,128)(2,1)}, bf16[4,192,1280]{2,1,0:T(8,128)(2,1)}, b...) custom-call(s32[1]{0:T(128)} %bitcast.refs_0_, ...), custom_call_target="tpu_custom_call" | custom-call | flops 48318382080 | bytes 23592960 | tf_op jit(solution)/shard_map/attend_back/pallas_call | solution.py:764
  520.4 2.1 convert_element_type.74
  522.5 1.4 dynamic-slice_convert_fusion.1
  523.9 1.4 fusion.9
  526.2 1.3 dynamic-slice_convert_fusion
  530.8 91.4 %back.1 = (bf16[768,1280]{1,0:T(8,128)(2,1)}, f32[8,1280]{1,0:T(8,128)}, bf16[320,1920]{1,0:T(8,128)(2,1)}, bf16[2,160,1536]{2,1,0:T(8,128)(2,1)}, bf16[2,160,15...) custom-call(bf16[1536,1920]{1,0:T(8,128)(2,1)} %get-tuple-element.11, ...), custom_call_target="tpu_custom_call" | custom-call | flops 15099494400 | bytes 39321600 | tf_op jit(solution)/shard_map/back/pallas_call | solution.py:1269
  622.2 61.7 %finish.1 = (f32[2,24,1280]{2,1,0:T(8,128)}, bf16[2,320,1920]{2,1,0:T(8,128)(2,1)}, bf16[2,384,1280]{2,1,0:T(8,128)(2,1)}) custom-call(f32[16,1280]{1,0:T(8,128)} %select_maximum_fusion.refs_0_, f32[8,1280]{1,0:T(8,128)} %get-tuple-element.117.refs_1_, bf16[320,1920]{1,0:T(8,128)(2,1)} %get-tuple-element.118.refs_2_, ...), custom_call_target="tpu_custom_call" | custom-call | tf_op jit(solution)/shard_map/finish/pallas_call | solution.py:1353
  683.9 1.7 dynamic-slice_reduce_fusion.2
  685.6 6.5 place_qkv.1
  692.1 1.3 bitcast_convert_fusion
  693.4 1.4 pad_maximum_fusion.b_ref
  694.8 5.3 place_up.1
  701.7 1.4 pad_maximum_fusion.1.b_ref
  703.1 5.8 place_down.1
  708.9 1.3 copy.54
  711.2 1.3 copy.55
  (141 shorter events, 27.0 us)
Async XLA Ops:
  0.7 101.3 %copy-start = (bf16[320,1280]{1,0:T(8,128)(2,1)S(1)}, bf16[320,1280]{1,0:T(8,128)(2,1)}, u32[]{:S(2)}) copy-start(bf16[320,1280]{1,0:T(8,128)(2,1)} %param.28) | copy-start | bytes 2457604
  0.7 2.6 copy-start.3
  2.7 1.1 copy-start.4
  5.5 1.2 copy-start.17
  5.5 1.3 copy-start.27
  5.5 1.3 copy-start.19
  5.5 1.3 copy-start.20
  5.5 1.4 copy-start.21
  5.5 1.4 copy-start.22
  5.5 1.4 copy-start.23
  5.6 1.4 copy-start.24
  5.6 1.4 copy-start.25
  5.6 1.4 copy-start.26
  7.7 74.5 %slice-start = ((f32[16,384]{1,0:T(8,128)}), f32[1,384]{1,0:T(1,128)S(1)}, s32[]{:S(2)}) async-start(f32[16,384]{1,0:T(8,128)} %select_maximum_fusion.3.refs_2_.refs_3_), calls=%async_computation | async-start | bytes 3072 | tf_op jit(solution)/shard_map/slice | solution.py:1548
  196.0 16.7 %copy-start.2 = (bf16[1536,1280]{1,0:T(8,128)(2,1)S(1)}, bf16[1536,1280]{1,0:T(8,128)(2,1)}, u32[]{:S(2)}) copy-start(bf16[1536,1280]{1,0:T(8,128)(2,1)} %get-tuple-element.87) | copy-start | bytes 11796484
  404.1 1.3 copy-start.8
  407.9 109.1 %copy-start.16 = (f32[1,1536]{1,0:T(1,128)S(1)}, f32[1,1536]{1,0:T(1,128)}, u32[]{:S(2)}) copy-start(f32[1,1536]{1,0:T(1,128)} %get-tuple-element.110) | copy-start | bytes 18436
  407.9 109.6 %copy-start.18 = (f32[1,1024]{1,0:T(1,128)S(1)}, f32[1,1024]{1,0:T(1,128)}, u32[]{:S(2)}) copy-start(f32[1,1024]{1,0:T(1,128)} %get-tuple-element.109) | copy-start | bytes 12292
  407.9 110.4 %copy-start.15 = (f32[8,1280]{1,0:T(8,128)S(1)}, f32[8,1280]{1,0:T(8,128)}, u32[]{:S(2)}) copy-start(f32[8,1280]{1,0:T(8,128)} %get-tuple-element.108) | copy-start | bytes 122884
  523.9 1.9 copy-start.7
  527.5 1.2 copy-start.13
  683.9 8.2 %copy-start.14 = (bf16[2,160,1280]{2,1,0:T(8,128)(2,1)S(1)}, bf16[2,160,1280]{2,1,0:T(8,128)(2,1)}, u32[]{:S(2)}) copy-start(bf16[2,160,1280]{2,1,0:T(8,128)(2,1)} %get-tuple-element.126) | copy-start | bytes 2457604
  685.6 7.8 %copy-start.11 = (bf16[2,160,1536]{2,1,0:T(8,128)(2,1)S(1)}, bf16[2,160,1536]{2,1,0:T(8,128)(2,1)}, u32[]{:S(2)}) copy-start(bf16[2,160,1536]{2,1,0:T(8,128)(2,1)} %get-tuple-element.128) | copy-start | bytes 2949124
  685.6 7.8 %copy-start.12 = (bf16[2,160,1536]{2,1,0:T(8,128)(2,1)S(1)}, bf16[2,160,1536]{2,1,0:T(8,128)(2,1)}, u32[]{:S(2)}) copy-start(bf16[2,160,1536]{2,1,0:T(8,128)(2,1)} %get-tuple-element.129) | copy-start | bytes 2949124
  694.8 6.9 copy-start.9
  694.8 6.9 copy-start.10
  703.1 5.8 copy-start.5
  708.9 2.3 copy-start.6
  708.9 3.5 copy-start.1

commit v4 on v3

--- a/solution.py
+++ b/solution.py
@@ -18,8 +18,8 @@
 ROWS = 256
 GAIN1, SHIFT1, QBIAS, VBIAS, OBIAS, GAIN2, SHIFT2, DBIAS, LENGTHS = [slice(i, i + 1) for i in range(9)]
 UBIAS = 9
-FFN_TILE = 256
-FFN_ROWS = 384
+FFN_TILE = 512
+FFN_ROWS = 768
 f32 = jnp.float32
 bf16 = jnp.bfloat16
 MESH = pl.DeviceIdType.MESH
@@ -351,15 +351,15 @@
 class Reduce(Job):
     def __init__(self, link, src, dst, bufs):
         self.link, self.src, self.dst = link, src, dst
-        self.a, self.b, self.low, self.high = bufs
         self.base = link.slots(6)
-        self.keep = link.local_slots(2)
-        self.half = dst.shape[1]
+        self.keep = link.local_slots(4)
+        self.half = dst.shape[0] // 2
+        self.pass_in, self.pass_sum, self.near, self.far, self.own = (bufs[2 * i : 2 * i + 2] for i in range(5))
 
     @staticmethod
     def buffers(source):
         half = pltpu.VMEM((source.shape[1] // 2, source.shape[2]), source.dtype)
-        return [half] * 4
+        return [half] * 10
 
     def block(self, i, part):
         rows = pl.ds(part * self.half, self.half)
@@ -369,25 +369,31 @@
         link = self.link
         x, y = (link.rep, link.shard ^ 1), (link.rep, link.shard ^ 2)
         plan = (
-            (self.block(3, 0), self.a, x),
-            (self.block(3, 1), self.b, y),
-            (self.block(1, 0), self.dst.at[0], x),
-            (self.block(2, 1), self.dst.at[2], y),
+            (self.block(3, 0), self.pass_in[0], x),
+            (self.block(3, 1), self.pass_in[1], y),
+            (self.block(1, 0), self.near[0], x),
+            (self.block(2, 1), self.near[1], y),
         )
         return [link.remote(s, d, self.base + i, self.base + i, to) for i, (s, d, to) in enumerate(plan)]
 
     def later(self):
         link = self.link
         x, y = (link.rep, link.shard ^ 1), (link.rep, link.shard ^ 2)
-        plan = ((self.low, self.dst.at[1], y), (self.high, self.dst.at[3], x))
+        plan = zip(self.pass_sum, self.far, (y, x))
         return [link.remote(s, d, self.base + 4 + i, self.base + 4 + i, to) for i, (s, d, to) in enumerate(plan)]
 
     def loads(self):
-        link = self.link
-        return (
-            link.here(self.block(2, 0), self.low, self.keep),
-            link.here(self.block(1, 1), self.high, self.keep + 1),
+        plan = (
+            (self.block(2, 0), self.pass_sum[0]),
+            (self.block(1, 1), self.pass_sum[1]),
+            (self.block(0, 0), self.own[0]),
+            (self.block(0, 1), self.own[1]),
         )
+        return [self.link.here(s, d, self.keep + i) for i, (s, d) in enumerate(plan)]
+
+    def store(self, part):
+        rows = pl.ds(part * self.half, self.half)
+        return self.link.here(self.own[part], self.dst.at[rows], self.keep + part)
 
     def start(self):
         for c in self.hops():
@@ -397,20 +403,31 @@
 
     def forward(self):
         hops, loads, later = self.hops(), self.loads(), self.later()
-        for i, (total, part) in enumerate(((self.low, self.a), (self.high, self.b))):
+        for i in range(2):
             loads[i].wait()
             hops[i].wait_recv()
-            total[...] = add_low(total[...], part[...])
+            self.pass_sum[i][...] = add_low(self.pass_sum[i][...], self.pass_in[i][...])
             later[i].start()
 
+    def collect(self):
+        hops, loads, later = self.hops(), self.loads(), self.later()
+        for i in range(2):
+            loads[2 + i].wait()
+            hops[2 + i].wait_recv()
+            later[i].wait_recv()
+            total = self.own[i][...].astype(f32) + self.near[i][...].astype(f32) + self.far[i][...].astype(f32)
+            self.own[i][...] = total.astype(bf16)
+            self.store(i).start()
+        for i in range(2):
+            self.store(i).wait()
+
     def finish(self):
-        hops, later = self.hops(), self.later()
-        for i in range(4):
-            hops[i].wait_send()
-        for i in (2, 3):
-            hops[i].wait_recv()
-        for c in later:
-            c.wait()
+        self.collect()
+        self.close()
+
+    def close(self):
+        for c in self.hops() + self.later():
+            c.wait_send()
 
 
 class Chain(Job):
@@ -488,29 +505,26 @@
         pl.when(jnp.logical_not(inner))(self.steps()[0].wait_send)
 
 
-def run_chains(chains):
+def chain_steps(chains):
+    lists = []
     for i in range(len(chains) + 1):
-        if i < len(chains):
-            chains[i].inward()
-        if i:
-            chains[i - 1].across()
-    for c in chains:
-        c.outward()
+        lists.append([c.inward for c in chains[i : i + 1]] + [c.across for c in chains[max(i - 1, 0) : i]])
+    return lists
 
 
 class Jobs:
     def __init__(self, *jobs):
-        self.jobs = jobs
-        self.bufs = [kind.buffers(a) for kind, a, _ in jobs]
+        self.jobs = [(job + (None,))[:4] for job in jobs]
+        self.bufs = [kind.buffers(a) for kind, a, _, _ in self.jobs]
 
     def sources(self):
-        return [a for _, a, _ in self.jobs]
+        return [a for _, a, _, _ in self.jobs]
 
     def in_specs(self):
         return [pl.BlockSpec(memory_space=pl.ANY)] * len(self.jobs)
 
     def out_shapes(self):
-        return [jax.ShapeDtypeStruct(shape, a.dtype) for _, a, shape in self.jobs]
+        return [jax.ShapeDtypeStruct(shape, a.dtype) for _, a, shape, _ in self.jobs]
 
     def scratch(self, extra=0):
         groups = lax.axis_size("shard")
@@ -518,7 +532,7 @@
         return [b for bufs in self.bufs for b in bufs] + [
             pltpu.SemaphoreType.DMA((remote,)),
             pltpu.SemaphoreType.DMA((remote,)),
-            pltpu.SemaphoreType.DMA((2 * len(self.jobs) + extra + 1,)),
+            pltpu.SemaphoreType.DMA((4 * len(self.jobs) + extra + 1,)),
         ]
 
     def bind(self, rest, srcs, dsts):
@@ -527,7 +541,9 @@
         for shapes in self.bufs:
             bufs.append([rest.pop(0) for _ in shapes])
         link = Link(rest[:3])
-        bound = [kind(link, a, b, c) for (kind, _, _), a, b, c in zip(self.jobs, srcs, dsts, bufs)]
+        bound = [
+            kind(link, view(a) if view else a, b, c) for (kind, _, _, view), a, b, c in zip(self.jobs, srcs, dsts, bufs)
+        ]
         return link, bound, rest[3:]
 
 
@@ -567,7 +583,18 @@
     )(*jobs.sources(), sibling)
 
 
-def qkv_kernel(x_ref, vec_ref, w_ref, bias_ref, h_ref, q_ref, k_ref, v_ref):
+def qkv_kernel(*refs, jobs):
+    count = len(jobs.jobs)
+    x_ref, vec_ref, w_ref, bias_ref = refs[:4]
+    h_ref, q_ref, k_ref, v_ref = refs[4 + count : 8 + count]
+    link, bound, _ = jobs.bind(refs[8 + 2 * count :], refs[4 : 4 + count], refs[8 + count : 8 + 2 * count])
+
+    @pl.when(pl.program_id(0) == 0)
+    def _():
+        link.meet_plane()
+        for job in bound:
+            job.start()
+
     xhat, _ = standardize(x_ref[...].astype(f32))
     h = (xhat * vec_ref[GAIN1] + vec_ref[SHIFT1]).astype(bf16)
     h_ref[...] = h
@@ -577,20 +604,28 @@
         ref[:, :width] = z[:, i * width : (i + 1) * width].astype(bf16)
         ref[:, width:] = jnp.zeros((ref.shape[0], ref.shape[1] - width), bf16)
 
-
-def qkv_call(x, vec, w, bias, wide):
+    @pl.when(pl.program_id(0) == pl.num_programs(0) - 1)
+    def _():
+        for job in bound:
+            job.forward()
+        for job in bound:
+            job.finish()
+
+
+def qkv_call(x, vec, w, bias, wide, jobs, number):
     n, d = x.shape
     out = jax.ShapeDtypeStruct((n, wide), bf16)
     return pl.pallas_call(
-        qkv_kernel,
+        functools.partial(qkv_kernel, jobs=jobs),
         grid=(n // ROWS,),
-        in_specs=[row_block(ROWS, d), whole(vec.shape), whole(w.shape), whole(bias.shape)],
-        out_specs=[row_block(ROWS, d)] + [row_block(ROWS, wide)] * 3,
-        out_shape=[jax.ShapeDtypeStruct((n, d), bf16), out, out, out],
-        compiler_params=params(),
+        in_specs=[row_block(ROWS, d), whole(vec.shape), once(w.shape), whole(bias.shape)] + jobs.in_specs(),
+        out_specs=[row_block(ROWS, d)] + [row_block(ROWS, wide)] * 3 + jobs.in_specs(),
+        out_shape=[jax.ShapeDtypeStruct((n, d), bf16), out, out, out] + jobs.out_shapes(),
+        scratch_shapes=jobs.scratch(),
+        compiler_params=comm_params(number),
         cost_estimate=cost(2 * n * d * w.shape[1], 4 * n * d + 2 * w.size + 6 * n * wide),
         name="project",
-    )(x, vec, w, bias)
+    )(x, vec, w, bias, *jobs.sources())
 
 
 def head_window(h):
@@ -717,10 +752,10 @@
             for step in steps:
                 step()
 
-    if chains:
-        at_head(2, [c.inward for c in chains[:1]])
-        at_head(4, [c.inward for c in chains[1:]] + [c.across for c in chains[:1]])
-    at_head(heads - 2, [job.forward for job in bound] + [c.across for c in chains[1:]])
+    steps = chain_steps(chains) if chains else []
+    for number, some in zip((2, 4, 5, 6), steps):
+        at_head(number, some)
+    at_head(heads - 2, [job.forward for job in bound])
 
     win, keep, lane = head_window(h)
     low = keep.astype(bf16)
@@ -753,6 +788,9 @@
             cols = slice(i * value.shape[1], (i + 1) * value.shape[1])
             g_ref[:, cols] = value
             sum_ref[:, cols] = jnp.sum(value.astype(f32), axis=0, keepdims=True)
+        for some in steps[4:]:
+            for step in some:
+                step()
         for job in bound:
             job.outward()
         for job in bound:
@@ -768,7 +806,7 @@
         + [once((n, wide))] * 5
         + [once((n, 128))]
         + jobs.in_specs(),
-        out_specs=[whole((n, 3 * width)), whole((1, 3 * width))] + jobs.in_specs(),
+        out_specs=[once((n, 3 * width)), whole((1, 3 * width))] + jobs.in_specs(),
         out_shape=[
             jax.ShapeDtypeStruct((n, 3 * width), bf16),
             jax.ShapeDtypeStruct((1, 3 * width), f32),
@@ -784,15 +822,22 @@
     )(length, q, k, v, o, do, lse, *jobs.sources())
 
 
-def middle_kernel(o_ref, w_ref, x_ref, vec_ref, mid_ref, h_ref, owide_ref, mine, other, *sems):
-    link = Link(sems)
+def middle_kernel(*refs, jobs):
+    count = len(jobs.jobs)
+    o_ref, w_ref, x_ref, vec_ref = refs[:4]
+    mid_ref, h_ref, owide_ref = refs[4 + count : 7 + count]
+    mine, other = refs[7 + 2 * count : 9 + 2 * count]
+    link, bound, _ = jobs.bind(refs[9 + 2 * count :], refs[4 : 4 + count], refs[7 + count : 7 + 2 * count])
     n = x_ref.shape[0]
     width = o_ref.shape[1]
-    link.meet_core()
+    base = link.slots(n // ROWS)
+    link.meet_plane()
+    for job in bound:
+        job.start()
 
     def swap(i):
         rows = pl.ds(pl.multiple_of(i * ROWS, ROWS), ROWS)
-        return rows, link.remote(mine.at[rows], other.at[rows], i, i, link.sibling())
+        return rows, link.remote(mine.at[rows], other.at[rows], base + i, base + i, link.sibling())
 
     def project(i, carry):
         rows, copy = swap(i)
@@ -817,26 +862,30 @@
     lax.fori_loop(0, n // ROWS, norm, 0)
     for i in range(n // ROWS):
         swap(i)[1].wait_send()
-
-
-def middle_call(o, w, x, vec, wide, number):
+    for job in bound:
+        job.forward()
+    for job in bound:
+        job.finish()
+
+
+def middle_call(o, w, x, vec, wide, jobs, number):
     n, d = x.shape
-    sems = [pltpu.SemaphoreType.DMA((n // ROWS,))] * 2 + [pltpu.SemaphoreType.DMA((1,))]
     vmem = pl.BlockSpec(memory_space=pltpu.VMEM)
     return pl.pallas_call(
-        middle_kernel,
-        in_specs=[vmem] * 4,
-        out_specs=[vmem] * 3,
+        functools.partial(middle_kernel, jobs=jobs),
+        in_specs=[vmem] * 4 + jobs.in_specs(),
+        out_specs=[vmem] * 3 + jobs.in_specs(),
         out_shape=[
             jax.ShapeDtypeStruct((n, d), f32),
             jax.ShapeDtypeStruct((n, d), bf16),
             jax.ShapeDtypeStruct((n, wide), bf16),
-        ],
-        scratch_shapes=[pltpu.VMEM((n, d), bf16)] * 2 + sems,
+        ]
+        + jobs.out_shapes(),
+        scratch_shapes=[pltpu.VMEM((n, d), bf16)] * 2 + jobs.scratch(n // ROWS),
         compiler_params=comm_params(number),
         cost_estimate=cost(2 * n * w.size, 14 * n * d),
         name="middle",
-    )(o, w, x, vec)
+    )(o, w, x, vec, *jobs.sources())
 
 
 def ffn_kernel(*refs, chained, last, mc, jobs):
@@ -954,36 +1003,44 @@
     )(h, dz, up, bias, down, *(old if chained else ()), *jobs.sources())
 
 
-def second_back_kernel(
-    mid_ref, dh_ref, out_ref, dz_ref, vec_ref, w_ref, o_ref, dh_any, out_any,
-    dmid_ref, do_ref, dw_ref, sums_ref, layer_ref,
-    acc, dh_other, out_other, *sems
-):
+def second_back_kernel(*refs, jobs):
+    count = len(jobs.jobs)
+    mid_ref, dh_ref, out_ref, dz_ref, vec_ref, w_ref, o_ref, dh_any, out_any = refs[:9]
+    dmid_ref, do_ref, dw_ref, sums_ref, layer_ref = refs[9 + count : 14 + count]
+    acc, dh_other, out_other = refs[14 + 2 * count : 17 + 2 * count]
+    link, bound, _ = jobs.bind(refs[17 + 2 * count :], refs[9 : 9 + count], refs[14 + count : 14 + 2 * count])
     i = pl.program_id(0)
     blocks = pl.num_programs(0)
-    link = Link(sems)
     half = layer_ref.shape[0] // ROWS
     width = w_ref.shape[0]
+    base = link.slots(3 * half)
 
     def swap_dh(j):
         rows = pl.ds(pl.multiple_of(j * ROWS, ROWS), ROWS)
-        return link.remote(dh_any.at[rows], dh_other.at[rows], j, j, link.sibling())
+        return link.remote(dh_any.at[rows], dh_other.at[rows], base + j, base + j, link.sibling())
 
     def swap_out(j):
         src = pl.ds(pl.multiple_of(((1 - link.core) * half + j) * ROWS, ROWS), ROWS)
         dst = pl.ds(pl.multiple_of(j * ROWS, ROWS), ROWS)
-        slot = 2 * half + j
+        slot = base + 2 * half + j
         return link.remote(out_any.at[src], out_other.at[dst], slot, slot, link.sibling())
 
     @pl.when(i == 0)
     def _():
-        link.meet_core()
+        link.meet_plane()
         for j in range(2 * half):
             swap_dh(j).start()
         for j in range(half):
             swap_out(j).start()
+        for job in bound:
+            job.start()
         acc[...] = jnp.zeros_like(acc)
         sums_ref[...] = jnp.zeros_like(sums_ref)
+
+    @pl.when(i == blocks - 1)
+    def _():
+        for job in bound:
+            job.forward()
 
     mid = mid_ref[...]
     xhat, inv = standardize(mid)
@@ -1020,39 +1077,42 @@
             swap_dh(j).wait_send()
         for j in range(half):
             swap_out(j).wait_send()
-
-
-def second_back_call(mid, dh, out, dz, vec, w, o, wide, number):
+        for job in bound:
+            job.finish()
+
+
+def second_back_call(mid, dh, out, dz, vec, w, o, wide, jobs, number):
     n, d = mid.shape
     width = w.shape[0]
     block = row_block(ROWS, d)
     count = 3 * n // ROWS // 2
     return pl.pallas_call(
-        second_back_kernel,
+        functools.partial(second_back_kernel, jobs=jobs),
         grid=(n // ROWS,),
         in_specs=[block] * 4
         + [whole(vec.shape), whole(w.shape), row_block(ROWS, width)]
-        + [pl.BlockSpec(memory_space=pl.ANY)] * 2,
-        out_specs=[block, row_block(ROWS, wide), whole((width, d)), whole((8, d)), whole((n // 2, d))],
+        + [pl.BlockSpec(memory_space=pl.ANY)] * 2
+        + jobs.in_specs(),
+        out_specs=[block, row_block(ROWS, wide), whole((width, d)), whole((8, d)), whole((n // 2, d))]
+        + jobs.in_specs(),
         out_shape=[
             jax.ShapeDtypeStruct((n, d), f32),
             jax.ShapeDtypeStruct((n, wide), bf16),
             jax.ShapeDtypeStruct((width, d), bf16),
             jax.ShapeDtypeStruct((8, d), f32),
             jax.ShapeDtypeStruct((n // 2, d), bf16),
-        ],
+        ]
+        + jobs.out_shapes(),
         scratch_shapes=[
             pltpu.VMEM((width, d), f32),
             pltpu.VMEM((n, d), bf16),
             pltpu.VMEM((n // 2, d), bf16),
-            pltpu.SemaphoreType.DMA((count,)),
-            pltpu.SemaphoreType.DMA((count,)),
-            pltpu.SemaphoreType.DMA((1,)),
-        ],
+        ]
+        + jobs.scratch(count),
         compiler_params=comm_params(number),
         cost_estimate=cost(4 * n * d * width, 14 * n * d),
         name="second_back",
-    )(mid, dh, out, dz, vec, w, o, dh, out)
+    )(mid, dh, out, dz, vec, w, o, dh, out, *jobs.sources())
 
 
 def dw_kernel(h_ref, g_ref, out_ref):
@@ -1159,8 +1219,8 @@
 
 
 class Blocks:
-    def __init__(self, ref, rows):
-        self.ref, self.rows = ref, rows
+    def __init__(self, ref, stride, first):
+        self.ref, self.stride, self.first = ref, stride, first
 
     @property
     def at(self):
@@ -1168,29 +1228,45 @@
 
     def __getitem__(self, index):
         block, part = index
-        first = pl.multiple_of(block * self.rows + part.start, 16)
-        return self.ref.at[pl.ds(first, part.size)]
-
-
-def back_kernel(*refs, jobs):
+        start = pl.multiple_of(block * self.stride + (self.first + part.start), 16)
+        return self.ref.at[pl.ds(start, part.size)]
+
+
+def back_kernel(*refs, jobs, parts):
     count = len(jobs.jobs)
-    g_ref, w_ref, vec_ref, h_ref, x_any, dmid_any = refs[:6]
-    dx_ref, sums_ref, own_ref = refs[6 + count : 9 + count]
-    x, dmid, mine, other, dw, left = refs[9 + 2 * count : 15 + 2 * count]
-    bufs = refs[15 + 2 * count : 19 + 2 * count]
-    link, chains, _ = jobs.bind(refs[19 + 2 * count :], refs[6 : 6 + count], refs[9 + count : 9 + 2 * count])
-    size, d = dx_ref.shape
+    g_ref, w_ref, vec_ref, h_ref, early_ref, x_any, dmid_any = refs[:7]
+    tokens_any, small_ref, both_any = refs[7 + count : 10 + count]
+    rest = list(refs[10 + 2 * count :])
+    x, dmid, mine, other, dx, dw, own, total, came = rest[:9]
+    rest = rest[9:]
+    small_bufs, rest = rest[:3], rest[3:]
+    reduce_bufs, rest = [rest[10 * i : 10 * i + 10] for i in range(parts)], rest[10 * parts :]
+    chain_bufs, rest = [rest[3 * i : 3 * i + 3] for i in range(2 * parts)], rest[6 * parts :]
+    link, chains, _ = jobs.bind(rest, refs[7 : 7 + count], refs[10 + count : 10 + 2 * count])
+    size, d = dx.shape
     half = size // ROWS
-    owned = own_ref.shape[0]
-    reduce = Reduce(link, Blocks(dw, owned), left, bufs)
+    owned = own.shape[0]
+    piece = owned // parts
+    reduces = [
+        Reduce(link, Blocks(dw, owned, i * piece), own.at[pl.ds(i * piece, piece)], reduce_bufs[i]) for i in range(parts)
+    ]
+    for i in range(2 * parts):
+        rows = pl.ds(i * (piece // 2), piece // 2)
+        chains.append(Chain(link, own.at[rows], both_any.at[:, rows], chain_bufs[i]))
+    ready, last = chains[:count], chains[count:]
+    to_owners = FromClip(link, dx, tokens_any, None)
     base = link.slots(half)
     keep = link.local_slots(2)
-    own = pl.ds(pl.multiple_of(link.core * size, size), size)
-    loads = [link.here(x_any.at[own], x, keep), link.here(dmid_any.at[own], dmid, keep + 1)]
+    swap_base = link.slots(3)
+    peers = [link.sibling()] + [(link.rep, link.shard ^ bit) for bit in (1, 2)]
+    swaps = [link.remote(total, came.at[i], swap_base + i, swap_base + i, to) for i, to in enumerate(peers)]
+    small = Chain(link, total, small_ref, small_bufs)
+    mine_rows = pl.ds(pl.multiple_of(link.core * size, size), size)
+    loads = [link.here(x_any.at[mine_rows], x, keep), link.here(dmid_any.at[mine_rows], dmid, keep + 1)]
     for c in loads:
         c.start()
     link.meet_all()
-    for job in chains:
+    for job in ready:
         job.start()
 
     def weight(i, carry):
@@ -1199,7 +1275,8 @@
         return carry
 
     lax.fori_loop(0, d // 256, weight, 0)
-    reduce.start()
+    for job in reduces:
+        job.start()
 
     def product(j):
         rows = pl.ds(pl.multiple_of(j * ROWS, ROWS), ROWS)
@@ -1214,6 +1291,8 @@
         mine[rows, :] = product((1 - link.core) * half + j).astype(bf16)
         copy.start()
         return carry
+
+    first = early_ref.shape[0]
 
     def norm(j, carry):
         rows, copy = swap(j)
@@ -1221,59 +1300,90 @@
         copy.wait_recv()
         xhat, inv = standardize(x[rows, :].astype(f32))
         dh = part + other[rows, :].astype(f32)
-        dx = dh * vec_ref[GAIN1]
-        dx_ref[rows, :] = (
+        slope = dh * vec_ref[GAIN1]
+        dx[rows, :] = (
             dmid[rows, :]
             + inv
-            * (dx - jnp.mean(dx, axis=-1, keepdims=True) - xhat * jnp.mean(dx * xhat, axis=-1, keepdims=True))
+            * (
+                slope
+                - jnp.mean(slope, axis=-1, keepdims=True)
+                - xhat * jnp.mean(slope * xhat, axis=-1, keepdims=True)
+            )
         ).astype(bf16)
         for row, value in enumerate((dh * xhat, dh)):
-            sums_ref[row : row + 1, :] += jnp.sum(value, axis=0, keepdims=True)
+            total[first + row : first + row + 1, :] += jnp.sum(value, axis=0, keepdims=True)
         return carry
 
-    sums_ref[...] = jnp.zeros_like(sums_ref)
+    total[:first, :] = early_ref[...]
+    total[first:, :] = jnp.zeros((total.shape[0] - first, d), f32)
     lax.fori_loop(0, half, send, 0)
     for c in loads:
         c.wait()
-    chains[0].inward()
+    steps = chain_steps(ready)
+    for step in steps[0]:
+        step()
+    reduces[0].forward()
     lax.fori_loop(0, half, norm, 0)
+    swaps[0].start()
+    for some in steps[1:]:
+        for step in some:
+            step()
+    for job in reduces[1:]:
+        job.forward()
+    to_owners.start()
+    swaps[0].wait()
+    total[...] += came[0]
+    swaps[1].start()
+    reduces[0].collect()
+    for c in last[:2]:
+        c.start()
+    swaps[1].wait()
+    total[...] += came[1]
+    swaps[2].start()
+    for i in range(1, parts):
+        reduces[i].collect()
+        for c in last[2 * i : 2 * i + 2]:
+            c.start()
+    swaps[2].wait()
+    total[...] += came[2]
+    small.start()
+    for some in chain_steps(last):
+        for step in some:
+            step()
+    small.inward()
+    for c in ready + last:
+        c.outward()
+    small.across()
+    small.outward()
+    for job in ready + last + [small]:
+        job.finish()
+    for job in reduces:
+        job.close()
     for j in range(half):
         swap(j)[1].wait_send()
-    reduce.forward()
-    for i in range(1, len(chains) + 1):
-        if i < len(chains):
-            chains[i].inward()
-        chains[i - 1].across()
-    reduce.finish()
-    cut = owned // 2
-    for part in range(2):
-        first = pl.multiple_of(link.shard * owned + part * cut, 16)
-        block = dw[pl.ds(first, cut), :].astype(f32)
-        own_ref[part * cut : (part + 1) * cut, :] = (
-            block + left[2 * part].astype(f32) + left[2 * part + 1].astype(f32)
-        ).astype(bf16)
-    for job in chains:
-        job.outward()
-    for job in chains:
-        job.finish()
-
-
-def back_call(grads, w, vec, h, x, dmid, jobs, number):
+    to_owners.finish()
+
+
+def back_call(grads, w, vec, h, early, x, dmid, jobs, clips, number):
     n, d = x.shape
     size = n // 2
     cols = grads.shape[1]
-    owned = d // lax.axis_size("shard")
-    part = pltpu.VMEM((owned // 2, cols), bf16)
+    groups = lax.axis_size("shard")
+    owned = d // groups
+    parts = 2
+    rows = early.shape[0] + 8
+    small = pltpu.VMEM((rows, d), f32)
+    piece = owned // parts // 2
     vmem = pl.BlockSpec(memory_space=pltpu.VMEM)
     hbm = pl.BlockSpec(memory_space=pl.ANY)
     return pl.pallas_call(
-        functools.partial(back_kernel, jobs=jobs),
-        in_specs=[vmem] * 4 + [hbm] * 2 + jobs.in_specs(),
-        out_specs=[vmem] * 3 + jobs.in_specs(),
+        functools.partial(back_kernel, jobs=jobs, parts=parts),
+        in_specs=[vmem] * 5 + [hbm] * 2 + jobs.in_specs(),
+        out_specs=[hbm, vmem, hbm] + jobs.in_specs(),
         out_shape=[
-            jax.ShapeDtypeStruct((size, d), bf16),
-            jax.ShapeDtypeStruct((8, d), f32),
-            jax.ShapeDtypeStruct((owned, cols), bf16),
+            jax.ShapeDtypeStruct((clips, size // clips, d), bf16),
+            jax.ShapeDtypeStruct((2, rows, d), f32),
+            jax.ShapeDtypeStruct((2, owned, cols), bf16),
         ]
         + jobs.out_shapes(),
         scratch_shapes=[
@@ -1281,172 +1391,98 @@
             pltpu.VMEM((size, d), f32),
             pltpu.VMEM((size, d), bf16),
             pltpu.VMEM((size, d), bf16),
+            pltpu.VMEM((size, d), bf16),
             pltpu.VMEM((d, cols), bf16),
-            pltpu.VMEM((4, owned // 2, cols), bf16),
+            pltpu.VMEM((owned, cols), bf16),
+            small,
+            pltpu.VMEM((3, rows, d), f32),
         ]
-        + [part] * 4
-        + jobs.scratch(size // ROWS + 8),
+        + [small] * 3
+        + [pltpu.VMEM((piece, cols), bf16)] * (16 * parts)
+        + jobs.scratch(64),
         compiler_params=comm_params(number, 62),
         cost_estimate=cost(4 * n * w.size, 20 * n * d),
         name="back",
-    )(grads, w, vec, h, x, dmid, *jobs.sources())
-
-
-def finish_kernel(*refs, jobs, parts):
-    count = len(jobs.jobs)
-    early_ref, late_ref, own_any = refs[:3]
-    small_ref, both_any = refs[3 + count : 5 + count]
-    rest = refs[5 + 2 * count :]
-    total, came, chain_bufs, rest = rest[0], rest[1], rest[2:5], rest[5:]
-    own_bufs, rest = rest[: 3 * parts], rest[3 * parts :]
-    link, bound, _ = jobs.bind(rest, refs[3 : 3 + count], refs[5 + count : 5 + 2 * count])
-    size = own_any.shape[0] // parts
-    chains = []
-    for i in range(parts):
-        rows = pl.ds(i * size, size)
-        chains.append(Chain(link, own_any.at[rows], both_any.at[:, rows], own_bufs[3 * i : 3 * i + 3]))
-    base = link.slots(3)
-    peers = [link.sibling()] + [(link.rep, link.shard ^ bit) for bit in (1, 2)]
-    swaps = [link.remote(total, came.at[i], base + i, base + i, to) for i, to in enumerate(peers)]
-    small = Chain(link, total, small_ref, chain_bufs)
-    first = early_ref.shape[0]
-    total[:first, :] = early_ref[...]
-    total[first:, :] = late_ref[...]
-    link.meet_all()
-    swaps[0].start()
-    for c in chains:
-        c.start()
-    for job in bound:
-        job.start()
-    for i in range(parts + 1):
-        if i < 3:
-            swaps[i].wait()
-            total[...] += came[i]
-            if i < 2:
-                swaps[i + 1].start()
+    )(grads, w, vec, h, early, x, dmid, *jobs.sources())
+
+
+def place_kernel(*refs, groups):
+    up_refs, down_refs = refs[:3], refs[3:6]
+    out_ref, in_ref = refs[6:8]
+    up, down, wo = refs[8:11]
+    qkv = refs[11:14]
+    places = refs[14]
+    t = pl.program_id(0)
+
+    def put(target, axis, pieces):
+        first = 0
+        for value in pieces:
+            size = value.shape[axis]
+            span = slice(first, first + size)
+            if axis:
+                target[:, span] = value.astype(f32)
             else:
-                small.start()
-        if i < parts:
-            chains[i].inward()
-        if i:
-            chains[i - 1].across()
-        if i == 3:
-            small.inward()
-    small.across()
-    for c in chains:
-        c.outward()
-    small.outward()
-    for c in chains:
-        c.finish()
-    small.finish()
-    for job in bound:
-        job.finish()
-
-
-def finish_call(early, late, own, jobs, number):
-    rows = early.shape[0] + late.shape[0]
-    d = early.shape[1]
-    parts = 4
-    small = pltpu.VMEM((rows, d), f32)
-    vmem = pl.BlockSpec(memory_space=pltpu.VMEM)
-    hbm = pl.BlockSpec(memory_space=pl.ANY)
-    return pl.pallas_call(
-        functools.partial(finish_kernel, jobs=jobs, parts=parts),
-        in_specs=[vmem] * 2 + [hbm] + jobs.in_specs(),
-        out_specs=[vmem, hbm] + jobs.in_specs(),
-        out_shape=[
-            jax.ShapeDtypeStruct((2, rows, d), f32),
-            jax.ShapeDtypeStruct((2,) + own.shape, bf16),
-        ]
-        + jobs.out_shapes(),
-        scratch_shapes=[small, pltpu.VMEM((3, rows, d), f32)]
-        + [small] * 3
-        + [pltpu.VMEM((own.shape[0] // parts, own.shape[1]), bf16)] * (3 * parts)
-        + jobs.scratch(6 * parts + 8),
-        compiler_params=comm_params(number),
-        name="finish",
-    )(early, late, own, *jobs.sources())
-
-
-def place_up_kernel(a_ref, b_ref, out_ref):
-    first, second = a_ref.shape[2], b_ref.shape[2]
-    for c in range(2):
-        base = c * (first + second)
-        out_ref[:, base : base + first] = a_ref[c].astype(f32)
-        out_ref[:, base + first : base + first + second] = b_ref[c].astype(f32)
-
-
-def place_up_call(a, b, groups):
-    rows = a.shape[1]
-    first, second = a.shape[2] // groups, b.shape[2] // groups
-    return pl.pallas_call(
-        place_up_kernel,
-        grid=(groups,),
-        in_specs=[
-            pl.BlockSpec((2, rows, first), lambda i: (0, 0, i)),
-            pl.BlockSpec((2, rows, second), lambda i: (0, 0, i)),
-        ],
-        out_specs=pl.BlockSpec((rows, 2 * (first + second)), lambda i: (0, i)),
-        out_shape=jax.ShapeDtypeStruct((rows, 2 * (first + second) * groups), f32),
-        compiler_params=params(),
-        name="place_up",
-    )(a, b)
-
-
-def place_down_kernel(a_ref, b_ref, out_ref):
-    first, second = a_ref.shape[1], b_ref.shape[1]
-    for c in range(2):
-        base = c * (first + second)
-        out_ref[base : base + first, :] = a_ref[c].astype(f32)
-        out_ref[base + first : base + first + second, :] = b_ref[c].astype(f32)
-
-
-def place_down_call(a, b):
-    d = a.shape[2]
-    first, second = a.shape[1], b.shape[1]
-    return pl.pallas_call(
-        place_down_kernel,
-        grid=(d // 256,),
-        in_specs=[
-            pl.BlockSpec((2, first, 256), lambda i: (0, 0, i)),
-            pl.BlockSpec((2, second, 256), lambda i: (0, 0, i)),
-        ],
-        out_specs=pl.BlockSpec((2 * (first + second), 256), lambda i: (0, i)),
-        out_shape=jax.ShapeDtypeStruct((2 * (first + second), d), f32),
-        compiler_params=params(),
-        name="place_down",
-    )(a, b)
-
-
-def place_qkv_kernel(in_ref, *outs, groups):
+                target[span, :] = value.astype(f32)
+            first += size
+
+    halves = [jnp.concatenate([up_refs[1][c], up_refs[2][c]], axis=0) for c in range(2)]
+    put(up, 1, [up_refs[0][0], halves[0], up_refs[0][1], halves[1]])
+    put(down, 0, [r[c] for c in range(2) for r in down_refs])
+    put(wo, 0, [out_ref[c] for c in range(2)])
     rows = in_ref.shape[1]
     width = in_ref.shape[2] // 3
     part = width // groups
-    row = lax.broadcasted_iota(jnp.int32, (width, 2 * width), 0)
-    ahead = lax.broadcasted_iota(jnp.int32, (width, 2 * width), 1) - row
-    places = []
-    for c in range(2):
-        place = jnp.zeros((width, 2 * width), f32)
-        for s in range(groups):
-            here = (row >= s * part) & (row < (s + 1) * part) & (ahead == (s + c) * part)
-            place = jnp.where(here, 1.0, place)
-        places.append(place.astype(bf16))
-    for i, out in enumerate(outs):
+
+    @pl.when(t == 0)
+    def _():
+        row = lax.broadcasted_iota(jnp.int32, (width, 2 * width), 0)
+        ahead = lax.broadcasted_iota(jnp.int32, (width, 2 * width), 1) - row
+        for c in range(2):
+            place = jnp.zeros((width, 2 * width), f32)
+            for s in range(groups):
+                here = (row >= s * part) & (row < (s + 1) * part) & (ahead == (s + c) * part)
+                place = jnp.where(here, 1.0, place)
+            places[c] = place.astype(bf16)
+
+    for i, out in enumerate(qkv):
         cols = slice(i * width, (i + 1) * width)
         out[...] = dot(in_ref[0, :, cols], places[0]) + dot(in_ref[1, :, cols], places[1])
 
 
-def place_qkv_call(both, groups):
-    _, rows, cols = both.shape
-    vmem = pl.BlockSpec(memory_space=pltpu.VMEM)
+def place_call(ups, downs, wo, qkv, groups):
+    steps = 5
+    own_d, cols = qkv.shape[1:]
+    d = downs[0].shape[2]
+    own_f = 2 * sum(a.shape[1] for a in downs)
+    take = [pl.BlockSpec((2, a.shape[1], a.shape[2] // groups), lambda i: (0, 0, jnp.minimum(i, groups - 1))) for a in ups]
+    wide = d // steps
+    per = own_d // steps
+    ff = 2 * ups[0].shape[2] + 2 * ups[1].shape[2]
     return pl.pallas_call(
-        functools.partial(place_qkv_kernel, groups=groups),
-        in_specs=[vmem],
-        out_specs=[vmem] * 3,
-        out_shape=[jax.ShapeDtypeStruct((rows, 2 * cols // 3), f32)] * 3,
+        functools.partial(place_kernel, groups=groups),
+        grid=(steps,),
+        in_specs=take
+        + [pl.BlockSpec((2, a.shape[1], wide), lambda i: (0, 0, i)) for a in downs]
+        + [
+            pl.BlockSpec((2, wo.shape[1], wide), lambda i: (0, 0, i)),
+            pl.BlockSpec((2, per, cols), lambda i: (0, i, 0)),
+        ],
+        out_specs=[
+            pl.BlockSpec((own_d, ff // groups), lambda i: (0, jnp.minimum(i, groups - 1))),
+            pl.BlockSpec((own_f, wide), lambda i: (0, i)),
+            pl.BlockSpec((own_d, wide), lambda i: (0, i)),
+        ]
+        + [pl.BlockSpec((per, d), lambda i: (i, 0))] * 3,
+        out_shape=[
+            jax.ShapeDtypeStruct((own_d, ff), f32),
+            jax.ShapeDtypeStruct((own_f, d), f32),
+            jax.ShapeDtypeStruct((own_d, d), f32),
+        ]
+        + [jax.ShapeDtypeStruct((own_d, d), f32)] * 3,
+        scratch_shapes=[pltpu.VMEM((2, cols // 3, d), bf16)],
         compiler_params=params(),
-        name="place_qkv",
-    )(both)
+        name="place",
+    )(*ups, *downs, wo, qkv)
 
 
 def own_sum(blocks, others):
@@ -1455,16 +1491,6 @@
     for i in range(others.shape[0]):
         total = total + others[i].astype(f32)
     return total.astype(bf16)
-
-
-def own_sum2(blocks, left):
-    shard = lax.axis_index("shard")
-    block = lax.dynamic_index_in_dim(blocks, shard, 0, keepdims=False).astype(f32)
-    cut = block.shape[0] // 2
-    left = left.astype(f32)
-    return jnp.concatenate(
-        [block[:cut] + left[0] + left[1], block[cut:] + left[2] + left[3]], axis=0
-    ).astype(bf16)
 
 
 def over_reps(own):
@@ -1517,15 +1543,18 @@
     first_n = ffn_cols * 2 // 5
     pieces = ((0, first_n), (first_n, ffn_cols))
 
+    positions = shard * rows + jnp.arange(rows, dtype=jnp.int32)
+    live = positions[None, :] < lengths[:, None]
+    masked = jnp.where(live[:, :, None], cotangent, jnp.zeros_like(cotangent))
+
+    def core_of():
+        return lax.rem(lax.axis_index("rep"), 2)
+
     def core_cols(w, size, a, b):
         def of(c):
             return jnp.concatenate([w[:, (2 * s + c) * size + a : (2 * s + c) * size + b] for s in range(g)], axis=1)
 
         return jnp.where(core == 0, of(0), of(1))
-
-    def core_rows(w):
-        half = w.shape[0] // 2
-        return lax.dynamic_slice_in_dim(w, core * half, half, 0)
 
     vectors = (first_gain, first_shift, query_bias, value_bias, out_bias, second_gain, second_shift, down_bias)
     lens = jnp.pad(lengths.astype(f32), (0, own_d - cl)).reshape(1, own_d)
@@ -1559,20 +1588,32 @@
         keepdims=False,
     )
     ups = [core_cols(up_weight, ffn_cols, a, b) for a, b in pieces]
-    down_own = core_rows(down_weight)
-    downs = [down_own[a:b] for a, b in pieces]
-    out_own = core_rows(out_weight)
-
-    def gathered(a):
-        return (Gather, a, (g,) + a.shape)
-
-    h1, q, k, v = qkv_call(x, vec, w_qkv, bias, wide)
-    jobs = Jobs(gathered(out_own), (ToClip, cotangent, (n, d)), gathered(ups[0]), gathered(downs[0]))
-    o, lse, w_out, cot, up, down = attn_fwd_call(length, q, k, v, width, heads, jobs, 1)
+
+    def half_rows(w, first=0, last=None):
+        half = w.shape[0] // 2
+        size = (half if last is None else last) - first
+
+        def view(ref):
+            return ref.at[pl.ds(pl.multiple_of(core_of() * half + first, 16), size)]
+
+        return size, view
+
+    def gathered(a, part=None):
+        if part is None:
+            return (Gather, a, (g,) + a.shape)
+        return (Gather, a, (g, part[0]) + a.shape[1:], part[1])
+
+    jobs = Jobs((ToClip, masked, (n, d)))
+    h1, q, k, v, dz = qkv_call(x, vec, w_qkv, bias, wide, jobs, 9)
+    jobs = Jobs(
+        gathered(out_weight, half_rows(out_weight)),
+        gathered(ups[0]),
+        gathered(down_weight, half_rows(down_weight, *pieces[0])),
+    )
+    o, lse, w_out, up, down = attn_fwd_call(length, q, k, v, width, heads, jobs, 1)
     w_out = w_out.reshape(width, d)
-    mid, h2, o_wide = middle_call(o, w_out, x, vec, wide, 2)
-    live = jnp.arange(n, dtype=jnp.int32)[:, None] < length
-    dz = jnp.where(live, cot, jnp.zeros_like(cot))
+    jobs = Jobs(gathered(ups[1]))
+    mid, h2, o_wide, up1 = middle_call(o, w_out, x, vec, wide, jobs, 2)
 
     def hidden_bias(piece):
         return ubias[:, piece[0] : piece[1]].reshape(1, -1)
@@ -1581,17 +1622,21 @@
 
     def to_owners(a):
         if fast:
-            return (Reduce, a, (4, a.shape[1] // 2, a.shape[2]))
+            return (Reduce, a, a.shape[1:])
         return (Owners, a, (g - 1,) + a.shape[1:])
 
     def owned(a, came):
-        return own_sum2(a, came) if fast else own_sum(a, came)
+        return came if fast else own_sum(a, came)
 
     def chained(a):
         return (Chain, a, (2,) + a.shape)
 
-    jobs = Jobs(gathered(ups[1]), gathered(downs[1]))
-    out, dh2, dup0, ddn0, dub0, up1, down1 = ffn_call(
+    def upper(a):
+        half = a.shape[0] // 2
+        return [a[:half], a[half:]]
+
+    jobs = Jobs(gathered(down_weight, half_rows(down_weight, *pieces[1])))
+    out, dh2, dup0, ddn0, dub0, down1 = ffn_call(
         h2, dz, up.reshape(d, -1), hidden_bias(pieces[0]), down.reshape(-1, d), None, False, jobs, 3, "hidden0"
     )
     dup0, ddn0 = dup0.reshape(g, own_d, -1), ddn0.reshape(g, -1, d)
@@ -1602,16 +1647,18 @@
     dup1, ddn1 = dup1.reshape(g, own_d, -1), ddn1.reshape(g, -1, d)
     up0_own, down0_own = owned(dup0, dup0_in), owned(ddn0, ddn0_in)
 
-    dmid, do, dwo, sums2, layer_own = second_back_call(mid, dh2, out, dz, vec, w_out, o, wide, 5)
+    jobs = Jobs(to_owners(dup1))
+    dmid, do, dwo, sums2, layer_own, dup1_in = second_back_call(mid, dh2, out, dz, vec, w_out, o, wide, jobs, 5)
     dwo = dwo.reshape(g, -1, d)
-
-    jobs = [to_owners(dup1), to_owners(ddn1), to_owners(dwo), (FromClip, layer_own, (cl, rows, d))]
+    up1_own = owned(dup1, dup1_in)
+
+    jobs = [to_owners(ddn1), to_owners(dwo), (FromClip, layer_own, (cl, rows, d))]
     if fast:
-        jobs += [chained(up0_own), chained(down0_own)]
-    grads, bias_sums, dup1_in, ddn1_in, dwo_in, layer_out, *sums0 = attn_bwd_call(
+        jobs += [chained(a) for a in [up0_own, down0_own] + upper(up1_own)]
+    grads, bias_sums, ddn1_in, dwo_in, layer_out, *sums0 = attn_bwd_call(
         length, q, k, v, o_wide, do, lse, width, heads, Jobs(*jobs), 6
     )
-    up1_own, down1_own, out_own_grad = owned(dup1, dup1_in), owned(ddn1, ddn1_in), owned(dwo, dwo_in)
+    down1_own, out_own_grad = owned(ddn1, ddn1_in), owned(dwo, dwo_in)
 
     def spread(v, size):
         out = jnp.zeros((g, 2, size), f32)
@@ -1629,19 +1676,12 @@
     )
     early = jnp.pad(early, ((0, -early.shape[0] % 8), (0, 0)))
 
-    def to_halves(a):
-        return [a[i * a.shape[0] // 2 : (i + 1) * a.shape[0] // 2] for i in range(2)]
-
     if fast:
-        pieces_own = to_halves(up1_own) + to_halves(down1_own) + [out_own_grad]
-        jobs = Jobs(*[chained(a) for a in pieces_own])
-        dx, sums1, qkv_own_grad, *sums = back_call(grads, w_qkv, vec, h1, x, dmid, jobs, 7)
-        jobs = Jobs((FromClip, dx, (cl, rows, d)))
-        smalls, qkv_all, tokens_grad = finish_call(early, sums1, qkv_own_grad, jobs, 8)
-        up_grad = place_up_call(sums0[0], jnp.concatenate(sums[:2], axis=1), g)
-        down_grad = place_down_call(sums0[1], jnp.concatenate(sums[2:4], axis=1))
-        out_grad = sums[4].reshape(own_d, d).astype(f32)
-        qkv_grads = place_qkv_call(qkv_all, g)
+        jobs = Jobs(*[chained(a) for a in upper(down1_own) + [out_own_grad]])
+        tokens_grad, smalls, qkv_all, *sums = back_call(grads, w_qkv, vec, h1, early, x, dmid, jobs, cl, 7)
+        up_grad, down_grad, out_grad, *qkv_grads = place_call(
+            (sums0[0], sums0[2], sums0[3]), (sums0[1], sums[0], sums[1]), sums[2], qkv_all, g
+        )
         smalls = lax.dynamic_index_in_dim(smalls, core, 0, keepdims=False)
     else:
         dwqkv = dw_call(h1, grads).reshape(g, own_d, 3 * width)

time: 717 us -> 657 us (0.916)
  Pallas kernels: 653 us -> 619 us
  other arithmetic: 31.9 us -> 10.4 us
    pallas_call x2, Pallas kernels: 154 us -> 112 us  [ffn_call(): pl.pallas_call(functools.partial(ffn_kernel, chained=chained, last=last,...]
    pallas_call x8 -> x5, Pallas kernels: 228 us -> 270 us  [the longest x1 126 us: back_call(): pl.pallas_call(functools.partial(back_kernel, jobs=jobs, parts=parts), in...]
    pallas_call x1, Pallas kernels: 88.7 us -> 64.6 us  [attn_fwd_call(): pl.pallas_call(functools.partial(attn_fwd_kernel, bq=256, jobs=jobs), gri...]
    convert_element_type x11 -> x0, other arithmetic: 11.9 us -> none  [the longest x5 6.23 us: own_sum2(): lax.dynamic_index_in_dim(blocks, shard, 0, keepdims=False).astype(f32)]
    pallas_call x1, Pallas kernels: 109 us -> 99 us  [attn_bwd_call(): pl.pallas_call(functools.partial(attn_bwd_kernel, bk=256, jobs=jobs), gri...]
where the time goes in v4:
time: 657 us; the launch traced here: 652 us
  Pallas kernels  619 us (94%)
  local copies, waits for them, and re-layouts  21.3 us (3%)
  other arithmetic  10.4 us (2%)
    pallas_call x1, Pallas kernels, back_call(): pl.pallas_call(functools.partial(back_kernel, jobs=jobs, parts=parts), in...  126 us
    pallas_call x2, Pallas kernels, ffn_call(): pl.pallas_call(functools.partial(ffn_kernel, chained=chained, last=last,...  112 us
    pallas_call x1, Pallas kernels, attn_bwd_call(): pl.pallas_call(functools.partial(attn_bwd_kernel, bk=256, jobs=jobs), gri...  99 us
    pallas_call x1, Pallas kernels, exchange_call(): pl.pallas_call(kernel, in_specs=jobs.in_specs() + [pl.BlockSpec(memory_sp...  73.2 us
    pallas_call x1, Pallas kernels, attn_fwd_call(): pl.pallas_call(functools.partial(attn_fwd_kernel, bq=256, jobs=jobs), gri...  64.6 us
    pallas_call x1, Pallas kernels, middle_call(): pl.pallas_call(functools.partial(middle_kernel, jobs=jobs), in_specs=[vme...  45.8 us
    pallas_call x1, Pallas kernels, second_back_call(): pl.pallas_call(functools.partial(second_back_kernel, jobs=jobs), grid=(n...  42.6 us
    pallas_call x1, Pallas kernels, qkv_call(): pl.pallas_call(functools.partial(qkv_kernel, jobs=jobs), grid=(n // ROWS,...  39.9 us

profile of v4, /device:TPU:0, one launch (start us, length us, event | category | flops | bytes accessed | tf_op | source)
XLA Modules:
  0.0 652.2 jit_solution(12185071467283362064)
XLA Ops:
  0.7 2.0 fusion.8
  4.2 1.2 maximum_select_fusion.2
  5.5 1.1 pad_maximum_fusion.refs_1_
  7.0 0.6 select_maximum_fusion.3.refs_2_.refs_3_
  7.6 73.2 %first_exchange.1 = (bf16[1536,1280]{1,0:T(8,128)(2,1)}, bf16[4,320,1920]{2,1,0:T(8,128)(2,1)}, f32[4,16,384]{2,1,0:T(8,128)}, f32[16,384]{1,0:T(8,128)}) custom-call(bf16[2,384,1280]{2,1,0:T(8,128)(2,1)} %refs_0_.1, bf16[320,1920]{1,0:T(8,128)(2,1)} %pad_maximum_fusion.refs_1_, f32[16,384]{1,0:T(8,128)} %select_maximum_fusion.3.refs_2_.refs_3_, ...), custom_call_target="tpu_custom_call" | custom-call | tf_op jit(solution)/shard_map/first_exchange/pallas_call | solution.py:575
  80.8 0.7 slice.229
  82.1 1.2 fusion.9
  84.0 0.9 slice_bitcast_fusion
  85.0 0.8 reshape.189.refs_1_.refs_3_.refs_4_.refs_2_
  86.9 1.5 broadcast_select_fusion.refs_4_
  88.3 39.9 %project.1 = (bf16[1536,1280]{1,0:T(8,128)(2,1)}, bf16[1536,768]{1,0:T(8,128)(2,1)}, bf16[1536,768]{1,0:T(8,128)(2,1)}, bf16[1536,768]{1,0:T(8,128)(2,1)}, bf16[1536,1280]{1,0:T(8,128)(2,1)}) custom-call(bf16[1536,1280]{1,0:T(8,128)(2,1)} %get-tuple-element.76.refs_0_.refs_2_.refs_5_, f32[16,1280]{1,0:T(8,128)} %reshape.189.refs_1_.refs_3_.refs_4_.refs_2_, ...), custom_call_target="tpu_custom_call" | custom-call | flops 7549747200 | bytes 19857408 | tf_op jit(solution)/shard_map/project/pallas_call | solution.py:618
  128.3 1.0 maximum_select_fusion.1.refs_5_
  129.4 64.6 %attend.1 = (bf16[1536,640]{1,0:T(8,128)(2,1)}, f32[1536,128]{1,0:T(8,128)}, bf16[4,160,1280]{2,1,0:T(8,128)(2,1)}, bf16[4,320,1024]{2,1,0:T(8,128)(2,1)}, bf16[4,256,1280]{2,1,0:T(8,128)(2,1)}) custom-call(s32[1]{0:T(128)} %bitcast.refs_0_, bf16[1536,768]{1,0:T(8,128)(2,1)} %get-tuple-element.79.refs_1_, bf16[1536,768]{1,0:T(8,128)(2,1)} %get-tuple-element.80.refs_2_, ...), custom_call_target="tpu_custom_call" | custom-call | flops 19327352832 | bytes 9437184 | tf_op jit(solution)/shard_map/attend/pallas_call | solution.py:712
  194.2 1.2 maximum_select_fusion.refs_4_
  195.4 45.8 %middle.1 = (f32[1536,1280]{1,0:T(8,128)}, bf16[1536,1280]{1,0:T(8,128)(2,1)}, bf16[1536,768]{1,0:T(8,128)(2,1)}, bf16[4,320,1536]{2,1,0:T(8,128)(2,1)}) custom-call(bf16[1536,640]{1,0:T(8,128)(2,1)} %get-tuple-element.82.refs_0_.refs_6_, bf16[640,1280]{1,0:T(8,128)(2,1)} %bitcast.31, bf16[1536,1280]{1,0:T(8,128)(2,1)} %get-tuple-element.76.refs_0_.refs_2_.refs_5_, ...), custom_call_target="tpu_custom_call" | custom-call | flops 2516582400 | bytes 27525120 | tf_op jit(solution)/shard_map/middle/pallas_call | solution.py:874
  242.5 50.7 %hidden0.1 = (f32[1536,1280]{1,0:T(8,128)}, f32[1536,1280]{1,0:T(8,128)}, bf16[1280,1024]{1,0:T(8,128)(2,1)}, bf16[1024,1280]{1,0:T(8,128)(2,1)}, f32[1,1024]{1,0:T(1,128)}, /*index=5*/bf16[4,384,1280]{2,1,0:T(8,128)(2,1)}) custom-call(bf16[1536,1280]{1,0:T(8,128)(2,1)} %get-tuple-element.86.refs_0_, bf16[1536,1280]{1,0:T(8,128)(2,1)} %get-tuple-element.87.refs_1_.refs_3_, ...), custom_call_target="tpu_custom_call" | custom-call | flops 24159191040 | bytes 34078720 | tf_op jit(solution)/shard_map/hidden0/pallas_call | solution.py:967
  293.2 61.0 %hidden1.1 = (bf16[1536,1280]{1,0:T(8,128)(2,1)}, bf16[1536,1280]{1,0:T(8,128)(2,1)}, bf16[1280,1536]{1,0:T(8,128)(2,1)}, bf16[1536,1280]{1,0:T(8,128)(2,1)}, f3...) custom-call(bf16[1536,1280]{1,0:T(8,128)(2,1)} %get-tuple-element.86.refs_0_, ...), custom_call_target="tpu_custom_call" | custom-call | flops 36238786560 | bytes 39321600 | tf_op jit(solution)/shard_map/hidden1/pallas_call | solution.py:967
  354.2 42.6 %second_back.1 = (f32[1536,1280]{1,0:T(8,128)}, bf16[1536,768]{1,0:T(8,128)(2,1)}, bf16[640,1280]{1,0:T(8,128)(2,1)}, f32[8,1280]{1,0:T(8,128)}, bf16[768,1280]{1,0:T(8,128)(2,1)}, /*index=5*/bf16[320,1536]{1,0:T(8,128)(2,1)}) custom-call(f32[1536,1280]{1,0:T(8,128)} %get-tuple-element.85.refs_0_, bf16[1536,1280]{1,0:T(8,128)(2,1)} %get-tuple-element.96.refs_1_.refs_7_, ...), custom_call_target="tpu_custom_call" | custom-call | flops 5033164800 | bytes 27525120 | tf_op jit(solution)/shard_map/second_back/pallas_call | solution.py:1089
  396.8 2.2 fusion.5
  399.0 99.0 %attend_back.1 = (bf16[1536,1920]{1,0:T(8,128)(2,1)}, f32[1,1920]{1,0:T(1,128)}, bf16[384,1280]{1,0:T(8,128)(2,1)}, bf16[160,1280]{1,0:T(8,128)(2,1)}, bf16[2,38...) custom-call(s32[1]{0:T(128)} %bitcast.refs_0_, ...), custom_call_target="tpu_custom_call" | custom-call | flops 48318382080 | bytes 23592960 | tf_op jit(solution)/shard_map/attend_back/pallas_call | solution.py:802
  498.5 0.7 reduce.32
  499.4 0.7 slice_reduce_fusion.3
  500.5 0.7 select_maximum_fusion.refs_4_
  501.2 2.2 fusion.4
  503.4 125.8 %back.1 = (bf16[2,384,1280]{2,1,0:T(8,128)(2,1)}, f32[2,24,1280]{2,1,0:T(8,128)}, bf16[2,320,1920]{2,1,0:T(8,128)(2,1)}, bf16[2,192,1280]{2,1,0:T(8,128)(2,1)}, ...) custom-call(bf16[1536,1920]{1,0:T(8,128)(2,1)} %get-tuple-element.108.refs_0_, bf16[1280,1920]{1,0:T(8,128)(2,1)} %bitcast.40, ...), custom_call_target="tpu_custom_call" | custom-call | flops 15099494400 | bytes 39321600 | tf_op jit(solution)/shard_map/back/pallas_call | solution.py:1379
  629.2 1.7 dynamic-slice_reduce_fusion.2
  630.9 16.0 %place.1 = (f32[320,5120]{1,0:T(8,128)}, f32[1280,1280]{1,0:T(8,128)}, f32[320,1280]{1,0:T(8,128)}, f32[320,1280]{1,0:T(8,128)}, f32[320,1280]{1,0:T(8,128)}, /*index=5*/f32[320,1280]{1,0:T(8,128)}) custom-call(bf16[2,320,1024]{2,1,0:T(8,128)(2,1)} %get-tuple-element.119.refs_0_, bf16[2,160,1536]{2,1,0:T(8,128)(2,1)} %get-tuple-element.120.refs_1_, ...), custom_call_target="tpu_custom_call" | custom-call | tf_op jit(solution)/shard_map/place/pallas_call | solution.py:1461
  646.9 0.9 constant_dynamic-slice_fusion.2
  647.8 0.7 dynamic_slice.30
  648.5 1.3 copy.54
  649.8 1.0 copy-done.5
  650.8 1.3 copy.55
  (99 shorter events, 6.3 us)
Async XLA Ops:
  0.7 2.6 copy-start.1
  2.7 1.1 copy-start.2
  5.4 1.2 copy-start.8
  5.4 1.3 copy-start.18
  5.4 1.3 copy-start.10
  5.4 1.3 copy-start.11
  5.5 1.4 copy-start.12
  5.5 1.4 copy-start.13
  5.5 1.4 copy-start.14
  5.5 1.4 copy-start.15
  5.5 1.4 copy-start.16
  5.5 1.4 copy-start.17
  7.6 74.5 %slice-start = ((f32[16,384]{1,0:T(8,128)}), f32[1,384]{1,0:T(1,128)S(1)}, s32[]{:S(2)}) async-start(f32[16,384]{1,0:T(8,128)} %select_maximum_fusion.3.refs_2_.refs_3_), calls=%async_computation | async-start | bytes 3072 | tf_op jit(solution)/shard_map/slice | solution.py:1577
  7.6 79.3 %copy-start.3 = (bf16[2,384,1280]{2,1,0:T(8,128)(2,1)S(1)}, bf16[2,384,1280]{2,1,0:T(8,128)(2,1)}, u32[]{:S(2)}) copy-start(bf16[2,384,1280]{2,1,0:T(8,128)(2,1)} %param.20) | copy-start | bytes 5898244
  88.3 39.9 %copy-start = (bf16[320,5120]{1,0:T(8,128)(2,1)S(1)}, bf16[320,5120]{1,0:T(8,128)(2,1)}, u32[]{:S(2)}) copy-start(bf16[320,5120]{1,0:T(8,128)(2,1)} %param.32) | copy-start | bytes 9830404
  399.0 99.0 %copy-start.7 = (f32[1,1536]{1,0:T(1,128)S(1)}, f32[1,1536]{1,0:T(1,128)}, u32[]{:S(2)}) copy-start(f32[1,1536]{1,0:T(1,128)} %get-tuple-element.113) | copy-start | bytes 18436
  399.0 99.6 %copy-start.9 = (f32[1,1024]{1,0:T(1,128)S(1)}, f32[1,1024]{1,0:T(1,128)}, u32[]{:S(2)}) copy-start(f32[1,1024]{1,0:T(1,128)} %get-tuple-element.112) | copy-start | bytes 12292
  399.0 100.4 %copy-start.6 = (f32[8,1280]{1,0:T(8,128)S(1)}, f32[8,1280]{1,0:T(8,128)}, u32[]{:S(2)}) copy-start(f32[8,1280]{1,0:T(8,128)} %get-tuple-element.111) | copy-start | bytes 122884
  630.9 17.6 %copy-start.4 = (bf16[2,384,1280]{2,1,0:T(8,128)(2,1)S(1)}, bf16[2,384,1280]{2,1,0:T(8,128)(2,1)}, u32[]{:S(2)}) copy-start(bf16[2,384,1280]{2,1,0:T(8,128)(2,1)} %get-tuple-element.208) | copy-start | bytes 5898244
  648.5 2.3 copy-start.5

commit v5 on v4

--- a/solution.py
+++ b/solution.py
@@ -20,6 +20,7 @@
 UBIAS = 9
 FFN_TILE = 512
 FFN_ROWS = 768
+PAIR_SHARE = 3
 f32 = jnp.float32
 bf16 = jnp.bfloat16
 MESH = pl.DeviceIdType.MESH
@@ -88,7 +89,7 @@
         self.core = lax.rem(self.rep, 2)
         self.half = self.groups // 2
 
-    def meet_plane(self):
+    def meet_plane(self, pair=False):
         barrier = pltpu.get_barrier_semaphore()
         base = self.rep - self.core
         for c in range(2):
@@ -96,7 +97,12 @@
                 if c or p:
                     to = (base + (self.core ^ c), self.shard ^ p)
                     pl.semaphore_signal(barrier, inc=1, device_id=to, device_id_type=MESH)
-        pl.semaphore_wait(barrier, 2 * self.groups - 1)
+        if pair:
+            pl.semaphore_signal(barrier, inc=1, device_id=self.pair(), device_id_type=MESH)
+        pl.semaphore_wait(barrier, 2 * self.groups - 1 + int(pair))
+
+    def pair(self):
+        return (self.rep ^ 2, self.shard)
 
     def meet_all(self):
         barrier = pltpu.get_barrier_semaphore()
@@ -161,7 +167,7 @@
 
 class Job:
     @staticmethod
-    def buffers(source):
+    def buffers(source, shape):
         return []
 
     def forward(self):
@@ -175,6 +181,23 @@
 
     def outward(self):
         pass
+
+
+class Staged:
+    def __init__(self, link, src, dst, buf):
+        slot = link.local_slots(1)
+        self.load = link.here(src, buf, slot)
+        self.store = link.here(buf, dst, slot)
+
+    def start(self):
+        self.load.start()
+
+    def turn(self):
+        self.load.wait()
+        self.store.start()
+
+    def wait(self):
+        self.store.wait()
 
 
 class Gather(Job):
@@ -182,7 +205,11 @@
         self.link, self.src, self.dst = link, src, dst
         self.rows = src.shape[0]
         self.base = link.slots(max(4, link.groups - 1))
-        self.keep = link.here(src, dst.at[link.shard], link.local_slots(1))
+        self.keep = Staged(link, src, dst.at[link.shard], bufs[0])
+
+    @staticmethod
+    def buffers(source, shape):
+        return [pltpu.VMEM(shape[1:], source.dtype)]
 
     def first(self):
         link = self.link
@@ -210,6 +237,7 @@
             c.start()
 
     def forward(self):
+        self.keep.turn()
         for c, d in zip(self.first(), self.second()):
             c.wait_recv()
             d.start()
@@ -225,12 +253,82 @@
         self.keep.wait()
 
 
+class PairGather(Job):
+    def __init__(self, link, src, dst, bufs):
+        self.link, self.src, self.dst = link, src, dst
+        rows = src.shape[0]
+        outer = max(rows // PAIR_SHARE // 16, 1) * 16
+        second = lax.rem(lax.div(link.rep, 2), 2)
+        self.part = pl.ds(pl.multiple_of(second * outer, 16), rows - outer)
+        self.alone = pl.ds(pl.multiple_of(second * (rows - outer), 16), outer)
+        self.both = pl.ds(outer, rows - 2 * outer)
+        self.base = link.slots(7)
+        self.keep = Staged(link, src, dst.at[link.shard], bufs[0])
+
+    @staticmethod
+    def buffers(source, shape):
+        return [pltpu.VMEM(shape[1:], source.dtype)]
+
+    def step(self, src, dst, slot, to):
+        return self.link.remote(src, dst, self.base + slot, self.base + slot, to)
+
+    def near(self, bit):
+        return (self.link.rep, self.link.shard ^ bit)
+
+    def first(self):
+        mine = self.dst.at[self.link.shard, self.part]
+        return [self.step(self.src.at[self.part], mine, i, self.near(i + 1)) for i in range(2)]
+
+    def second(self):
+        one = self.dst.at[self.link.shard ^ 1, self.alone]
+        two = self.dst.at[self.link.shard ^ 2, self.both]
+        return [self.step(one, one, 2, self.near(2)), self.step(two, two, 3, self.near(1))]
+
+    def third(self):
+        out = []
+        for i in range(3):
+            ref = self.dst.at[self.link.shard ^ (i + 1), self.alone]
+            out.append(self.step(ref, ref, 4 + i, self.link.pair()))
+        return out
+
+    def start(self):
+        self.keep.start()
+        for c in self.first():
+            c.start()
+
+    def forward(self):
+        self.keep.turn()
+        for c, d, e in zip(self.first(), self.second(), self.third()):
+            c.wait_recv()
+            d.start()
+            e.start()
+
+    def inward(self):
+        self.second()[0].wait_recv()
+        self.third()[2].start()
+
+    def finish(self):
+        for c in self.first():
+            c.wait_send()
+        one, two = self.second()
+        one.wait_send()
+        two.wait()
+        for c in self.third():
+            c.wait()
+        self.keep.wait()
+
+
 class ToClip(Job):
     def __init__(self, link, src, dst, bufs):
         self.link, self.src, self.dst = link, src, dst
         self.rows = src.shape[1]
         self.base = link.slots(link.half + 1)
         self.keep = link.local_slots(1)
+        self.buf = bufs[0]
+
+    @staticmethod
+    def buffers(source, shape):
+        return [pltpu.VMEM(source.shape[1:], source.dtype)]
 
     def copy(self, j):
         link = self.link
@@ -239,7 +337,7 @@
         mine = (core == link.core) & (link.core * link.half + j == link.shard)
         dst = self.dst.at[pl.ds(pl.multiple_of(link.shard * self.rows, self.rows), self.rows)]
         there = link.remote(self.src.at[j], dst, self.base + j, self.base + lax.rem(link.shard, link.half), to)
-        return mine, there, link.here(self.src.at[j], dst, self.keep)
+        return mine, there, link.here(self.src.at[j], self.buf, self.keep)
 
     def arrival(self, t):
         link = self.link
@@ -247,7 +345,7 @@
         mine = (lax.div(link.shard, link.half) == link.core) & (source == link.shard)
         dst = self.dst.at[pl.ds(pl.multiple_of(source * self.rows, self.rows), self.rows)]
         there = link.remote(self.src.at[0], dst, self.base, self.base + t, link.sibling())
-        return mine, there, link.here(self.src.at[0], dst, self.keep)
+        return mine, there, link.here(self.buf, dst, self.keep)
 
     def to_sibling(self):
         link = self.link
@@ -265,7 +363,13 @@
     def forward(self):
         for t in range(self.link.half):
             mine, there, here = self.arrival(t)
-            pl.when(mine)(here.wait)
+
+            @pl.when(mine)
+            def _():
+                self.copy(0)[2].wait()
+                here.start()
+                here.wait()
+
             pl.when(jnp.logical_not(mine))(there.wait_recv)
         self.to_sibling().start()
 
@@ -282,6 +386,11 @@
         self.rows = dst.shape[1]
         self.base = link.slots(link.half)
         self.keep = link.local_slots(1)
+        self.buf = bufs[0]
+
+    @staticmethod
+    def buffers(source, shape):
+        return [pltpu.VMEM(shape[1:], source.dtype)]
 
     def copy(self, t):
         link = self.link
@@ -292,14 +401,14 @@
         src = self.src.at[pl.ds(t * self.rows, self.rows)]
         dst = self.dst.at[clip]
         there = link.remote(src, dst, self.base + t, self.base + clip, (link.rep - link.core + core, shard))
-        return mine, there, link.here(src, dst, self.keep)
+        return mine, there, link.here(src, self.buf, self.keep)
 
     def arrival(self, j):
         link = self.link
         mine = (lax.div(link.shard, link.half) == link.core) & (link.core * link.half + j == link.shard)
         src = self.src.at[pl.ds(0, self.rows)]
         there = link.remote(src, self.dst.at[j], self.base, self.base + j, link.sibling())
-        return mine, there, link.here(src, self.dst.at[j], self.keep)
+        return mine, there, link.here(self.buf, self.dst.at[j], self.keep)
 
     def start(self):
         for t in range(self.link.half):
@@ -313,7 +422,13 @@
             pl.when(jnp.logical_not(mine))(there.wait_send)
         for j in range(self.link.half):
             mine, there, here = self.arrival(j)
-            pl.when(mine)(here.wait)
+
+            @pl.when(mine)
+            def _():
+                self.copy(0)[2].wait()
+                here.start()
+                here.wait()
+
             pl.when(jnp.logical_not(mine))(there.wait_recv)
 
 
@@ -357,7 +472,7 @@
         self.pass_in, self.pass_sum, self.near, self.far, self.own = (bufs[2 * i : 2 * i + 2] for i in range(5))
 
     @staticmethod
-    def buffers(source):
+    def buffers(source, shape):
         half = pltpu.VMEM((source.shape[1] // 2, source.shape[2]), source.dtype)
         return [half] * 10
 
@@ -438,8 +553,8 @@
         self.keep = link.local_slots(2)
 
     @staticmethod
-    def buffers(source):
-        return [pltpu.VMEM(source.shape, source.dtype)] * 3
+    def buffers(source, shape):
+        return [pltpu.VMEM(shape[1:], source.dtype)] * 3
 
     def step(self, src, dst, slot, to):
         return self.link.remote(src, dst, self.base + slot, self.base + slot, to)
@@ -464,6 +579,9 @@
 
     def add(self, a, b):
         return (a[...].astype(f32) + b[...].astype(f32)).astype(a.dtype)
+
+    def sent(self):
+        pl.when(jnp.logical_not(self.link.inner()))(self.steps()[0].wait_send)
 
     def inward(self):
         @pl.when(self.link.inner())
@@ -502,20 +620,44 @@
             self.steps()[1].wait_send()
             self.steps()[2].wait_send()
 
-        pl.when(jnp.logical_not(inner))(self.steps()[0].wait_send)
-
 
 def chain_steps(chains):
     lists = []
     for i in range(len(chains) + 1):
-        lists.append([c.inward for c in chains[i : i + 1]] + [c.across for c in chains[max(i - 1, 0) : i]])
+        lists.append(
+            [step for c in chains[i : i + 1] for step in (c.inward, c.sent)]
+            + [c.start for c in chains[i + 1 : i + 2]]
+            + [c.across for c in chains[max(i - 1, 0) : i]]
+        )
     return lists
+
+
+def gather_steps(gathers):
+    lists = []
+    for i in range(len(gathers) + 2):
+        lists.append(
+            [c.start for c in gathers[i : i + 1]]
+            + [c.forward for c in gathers[max(i - 1, 0) : i]]
+            + [c.inward for c in gathers[max(i - 2, 0) : max(i - 1, 0)]]
+        )
+    return lists
+
+
+def run(steps):
+    for step in steps:
+        step()
+
+
+def split_gathers(bound):
+    gathers = [job for job in bound if isinstance(job, (Gather, PairGather))]
+    return gathers, [job for job in bound if job not in gathers]
 
 
 class Jobs:
     def __init__(self, *jobs):
         self.jobs = [(job + (None,))[:4] for job in jobs]
-        self.bufs = [kind.buffers(a) for kind, a, _, _ in self.jobs]
+        self.pairs = any(job[0] is PairGather for job in jobs)
+        self.bufs = [kind.buffers(a, shape) for kind, a, shape, _ in self.jobs]
 
     def sources(self):
         return [a for _, a, _, _ in self.jobs]
@@ -528,7 +670,7 @@
 
     def scratch(self, extra=0):
         groups = lax.axis_size("shard")
-        remote = len(self.jobs) * max(6, groups) + extra
+        remote = len(self.jobs) * max(7, groups) + extra
         return [b for bufs in self.bufs for b in bufs] + [
             pltpu.SemaphoreType.DMA((remote,)),
             pltpu.SemaphoreType.DMA((remote,)),
@@ -562,14 +704,16 @@
         link, bound, _ = jobs.bind(refs[2 * count + 2 :], srcs, dsts)
         slot = link.slots(1)
         swap = link.remote(mine, other, slot, slot, link.sibling())
-        link.meet_plane()
+        link.meet_plane(jobs.pairs)
         swap.start()
-        for job in bound:
-            job.start()
-        for job in bound:
-            job.forward()
-        for job in bound:
-            job.finish()
+        gathers, others = split_gathers(bound)
+        steps = gather_steps(gathers)
+        run([job.start for job in others] + steps[0])
+        for i, some in enumerate(steps[1:]):
+            if i == 1:
+                run([job.forward for job in others])
+            run(some)
+        run([job.finish for job in bound])
         swap.wait()
 
     return pl.pallas_call(
@@ -583,49 +727,30 @@
     )(*jobs.sources(), sibling)
 
 
-def qkv_kernel(*refs, jobs):
-    count = len(jobs.jobs)
-    x_ref, vec_ref, w_ref, bias_ref = refs[:4]
-    h_ref, q_ref, k_ref, v_ref = refs[4 + count : 8 + count]
-    link, bound, _ = jobs.bind(refs[8 + 2 * count :], refs[4 : 4 + count], refs[8 + count : 8 + 2 * count])
-
-    @pl.when(pl.program_id(0) == 0)
-    def _():
-        link.meet_plane()
-        for job in bound:
-            job.start()
-
+def qkv_kernel(x_ref, vec_ref, bias_ref, wq_ref, wk_ref, wv_ref, h_ref, q_ref, k_ref, v_ref):
     xhat, _ = standardize(x_ref[...].astype(f32))
     h = (xhat * vec_ref[GAIN1] + vec_ref[SHIFT1]).astype(bf16)
     h_ref[...] = h
-    z = dot(h, w_ref[...]) + bias_ref[...]
-    width = z.shape[1] // 3
-    for i, ref in enumerate((q_ref, k_ref, v_ref)):
-        ref[:, :width] = z[:, i * width : (i + 1) * width].astype(bf16)
+    for i, (w_ref, ref) in enumerate(((wq_ref, q_ref), (wk_ref, k_ref), (wv_ref, v_ref))):
+        width = w_ref.shape[1]
+        z = dot(h, w_ref[...]) + bias_ref[:, i * width : (i + 1) * width]
+        ref[:, :width] = z.astype(bf16)
         ref[:, width:] = jnp.zeros((ref.shape[0], ref.shape[1] - width), bf16)
 
-    @pl.when(pl.program_id(0) == pl.num_programs(0) - 1)
-    def _():
-        for job in bound:
-            job.forward()
-        for job in bound:
-            job.finish()
-
-
-def qkv_call(x, vec, w, bias, wide, jobs, number):
+
+def qkv_call(x, vec, bias, weights, wide):
     n, d = x.shape
     out = jax.ShapeDtypeStruct((n, wide), bf16)
     return pl.pallas_call(
-        functools.partial(qkv_kernel, jobs=jobs),
+        qkv_kernel,
         grid=(n // ROWS,),
-        in_specs=[row_block(ROWS, d), whole(vec.shape), once(w.shape), whole(bias.shape)] + jobs.in_specs(),
-        out_specs=[row_block(ROWS, d)] + [row_block(ROWS, wide)] * 3 + jobs.in_specs(),
-        out_shape=[jax.ShapeDtypeStruct((n, d), bf16), out, out, out] + jobs.out_shapes(),
-        scratch_shapes=jobs.scratch(),
-        compiler_params=comm_params(number),
-        cost_estimate=cost(2 * n * d * w.shape[1], 4 * n * d + 2 * w.size + 6 * n * wide),
+        in_specs=[row_block(ROWS, d), whole(vec.shape), whole(bias.shape)] + [once(w.shape) for w in weights],
+        out_specs=[row_block(ROWS, d)] + [row_block(ROWS, wide)] * 3,
+        out_shape=[jax.ShapeDtypeStruct((n, d), bf16), out, out, out],
+        compiler_params=params(),
+        cost_estimate=cost(6 * n * weights[0].size, 4 * n * d + 6 * weights[0].size + 6 * n * wide),
         name="project",
-    )(x, vec, w, bias, *jobs.sources())
+    )(x, vec, bias, *weights)
 
 
 def head_window(h):
@@ -668,19 +793,22 @@
     n = q_ref.shape[0]
     width = o_ref.shape[1]
 
+    gathers, others = split_gathers(bound)
+    steps = gather_steps(gathers)
+
     @pl.when(h == 0)
     def _():
-        link.meet_plane()
-        for job in bound:
-            job.start()
+        link.meet_plane(jobs.pairs)
+        run([job.start for job in others] + steps[0])
         acc[...] = jnp.zeros_like(acc)
         lse_ref[...] = jnp.zeros_like(lse_ref)
         kx[...] = key_extra(n, len_ref[0])
 
-    @pl.when(h == heads - 2)
-    def _():
-        for job in bound:
-            job.forward()
+    for number, some in zip((2, 4, 6, 7), steps[1:]):
+
+        @pl.when(h == number * heads // 8)
+        def _():
+            run(some)
 
     win, keep, lane = head_window(h)
     low = keep.astype(bf16)
@@ -703,8 +831,9 @@
     @pl.when(h == heads - 1)
     def _():
         o_ref[:, :width] = acc[:, :width].astype(bf16)
-        for job in bound:
-            job.finish()
+        for some in steps[5:]:
+            run(some)
+        run([job.finish for job in bound])
 
 
 def attn_fwd_call(length, q, k, v, width, heads, jobs, number):
@@ -737,9 +866,10 @@
         if chains:
             link.meet_all()
         else:
-            link.meet_plane()
+            link.meet_plane(jobs.pairs)
         for job in bound:
-            job.start()
+            if job not in chains[1:]:
+                job.start()
         for ref in (dq, dk, dv):
             ref[...] = jnp.zeros_like(ref)
         kx[...] = key_extra(n, len_ref[0])
@@ -753,9 +883,9 @@
                 step()
 
     steps = chain_steps(chains) if chains else []
-    for number, some in zip((2, 4, 5, 6), steps):
+    for number, some in zip((1, 2, 4, 6, 7), steps):
         at_head(number, some)
-    at_head(heads - 2, [job.forward for job in bound])
+    at_head(heads - 3, [job.forward for job in bound])
 
     win, keep, lane = head_window(h)
     low = keep.astype(bf16)
@@ -788,9 +918,8 @@
             cols = slice(i * value.shape[1], (i + 1) * value.shape[1])
             g_ref[:, cols] = value
             sum_ref[:, cols] = jnp.sum(value.astype(f32), axis=0, keepdims=True)
-        for some in steps[4:]:
-            for step in some:
-                step()
+        for some in steps[5:]:
+            run(some)
         for job in bound:
             job.outward()
         for job in bound:
@@ -831,7 +960,7 @@
     n = x_ref.shape[0]
     width = o_ref.shape[1]
     base = link.slots(n // ROWS)
-    link.meet_plane()
+    link.meet_plane(jobs.pairs)
     for job in bound:
         job.start()
 
@@ -864,6 +993,8 @@
         swap(i)[1].wait_send()
     for job in bound:
         job.forward()
+    for job in bound:
+        job.inward()
     for job in bound:
         job.finish()
 
@@ -902,15 +1033,16 @@
     acc, dh = refs[3:5] if last else (out_ref, dh_ref)
     refs = refs[5:] if last else refs[3:]
     link, bound, refs = jobs.bind(refs, srcs, dsts)
+    gathers, others = split_gathers(bound)
+    steps = gather_steps(gathers)
     t = pl.program_id(0)
     tiles = pl.num_programs(0)
     n = h_ref.shape[0]
 
     @pl.when(t == 0)
     def _():
-        link.meet_plane()
-        for job in bound:
-            job.start()
+        link.meet_plane(jobs.pairs)
+        run([job.start for job in others] + steps[0])
         if chained:
             sem = refs[0]
             copies = [
@@ -927,10 +1059,14 @@
             acc[...] = jnp.zeros_like(acc)
             dh[...] = jnp.zeros_like(dh)
 
-    @pl.when(t == tiles - 1)
-    def _():
-        for job in bound:
-            job.forward()
+    def at_tile(number, some):
+        if some:
+
+            @pl.when(t == number)
+            def _():
+                run(some)
+
+    at_tile(tiles - 1, [job.forward for job in others])
 
     def step(i, carry):
         rows = pl.ds(pl.multiple_of(i * mc, mc), mc)
@@ -944,8 +1080,11 @@
         return carry
 
     lax.fori_loop(0, n // mc, step, 0)
+
+    at_tile(0, steps[1] if gathers else [])
     dub_ref[...] = jnp.sum(grad[...].astype(f32), axis=0, keepdims=True)
     dup_ref[...] = dot(ht[...], grad[...]).astype(bf16)
+    at_tile(tiles - 1, steps[2] if gathers else [])
     ddn_ref[...] = dot_tn(act[...], dz_ref[...]).astype(bf16)
 
     @pl.when(t == tiles - 1)
@@ -953,8 +1092,9 @@
         if last:
             out_ref[...] = acc[...].astype(out_ref.dtype)
             dh_ref[...] = dh[...].astype(dh_ref.dtype)
-        for job in bound:
-            job.finish()
+        for some in steps[3:]:
+            run(some)
+        run([job.finish for job in bound])
 
 
 def ffn_call(h, dz, up, bias, down, old, last, jobs, number, name):
@@ -1009,6 +1149,9 @@
     dmid_ref, do_ref, dw_ref, sums_ref, layer_ref = refs[9 + count : 14 + count]
     acc, dh_other, out_other = refs[14 + 2 * count : 17 + 2 * count]
     link, bound, _ = jobs.bind(refs[17 + 2 * count :], refs[9 : 9 + count], refs[14 + count : 14 + 2 * count])
+    chains = [job for job in bound if isinstance(job, Chain)]
+    others = [job for job in bound if job not in chains]
+    steps = chain_steps(chains) if chains else []
     i = pl.program_id(0)
     blocks = pl.num_programs(0)
     half = layer_ref.shape[0] // ROWS
@@ -1027,20 +1170,27 @@
 
     @pl.when(i == 0)
     def _():
-        link.meet_plane()
+        if chains:
+            link.meet_all()
+        else:
+            link.meet_plane()
         for j in range(2 * half):
             swap_dh(j).start()
         for j in range(half):
             swap_out(j).start()
-        for job in bound:
-            job.start()
+        run([job.start for job in others + chains[:1]])
         acc[...] = jnp.zeros_like(acc)
         sums_ref[...] = jnp.zeros_like(sums_ref)
 
+    for number, some in zip((2, 4), steps):
+
+        @pl.when(i == number)
+        def _():
+            run(some)
+
     @pl.when(i == blocks - 1)
     def _():
-        for job in bound:
-            job.forward()
+        run([job.forward for job in others])
 
     mid = mid_ref[...]
     xhat, inv = standardize(mid)
@@ -1077,8 +1227,9 @@
             swap_dh(j).wait_send()
         for j in range(half):
             swap_out(j).wait_send()
-        for job in bound:
-            job.finish()
+        for some in steps[2:]:
+            run(some)
+        run([job.outward for job in chains] + [job.finish for job in others + chains])
 
 
 def second_back_call(mid, dh, out, dz, vec, w, o, wide, jobs, number):
@@ -1148,7 +1299,7 @@
     loads = [link.here(x_any.at[own], x, keep), link.here(dmid_any.at[own], dmid, keep + 1)]
     for c in loads:
         c.start()
-    link.meet_plane()
+    link.meet_plane(jobs.pairs)
     for job in bound:
         job.start()
 
@@ -1191,6 +1342,8 @@
         swap(j)[1].wait_send()
     for job in bound:
         job.forward()
+    for job in bound:
+        job.inward()
     for job in bound:
         job.finish()
 
@@ -1232,29 +1385,31 @@
         return self.ref.at[pl.ds(start, part.size)]
 
 
-def back_kernel(*refs, jobs, parts):
+def back_kernel(*refs, jobs):
     count = len(jobs.jobs)
-    g_ref, w_ref, vec_ref, h_ref, early_ref, x_any, dmid_any = refs[:7]
-    tokens_any, small_ref, both_any = refs[7 + count : 10 + count]
-    rest = list(refs[10 + 2 * count :])
-    x, dmid, mine, other, dx, dw, own, total, came = rest[:9]
-    rest = rest[9:]
+    g_ref, vec_ref, h_ref, early_ref, *w_refs = refs[:7]
+    x_any, dmid_any = refs[7:9]
+    tokens_any, small_ref, both_any = refs[9 + count : 12 + count]
+    rest = list(refs[12 + 2 * count :])
+    x, dmid, mine, other, dx, dw, own, total, came, stage = rest[:10]
+    rest = rest[10:]
     small_bufs, rest = rest[:3], rest[3:]
-    reduce_bufs, rest = [rest[10 * i : 10 * i + 10] for i in range(parts)], rest[10 * parts :]
-    chain_bufs, rest = [rest[3 * i : 3 * i + 3] for i in range(2 * parts)], rest[6 * parts :]
-    link, chains, _ = jobs.bind(rest, refs[7 : 7 + count], refs[10 + count : 10 + 2 * count])
+    reduce_bufs, rest = [rest[10 * i : 10 * i + 10] for i in range(3)], rest[30:]
+    chain_bufs, rest = [rest[3 * i : 3 * i + 3] for i in range(6)], rest[18:]
+    link, bound, _ = jobs.bind(rest, refs[9 : 9 + count], refs[12 + count : 12 + 2 * count])
+    ready = [job for job in bound if isinstance(job, Chain)]
+    others = [job for job in bound if job not in ready]
     size, d = dx.shape
     half = size // ROWS
-    owned = own.shape[0]
-    piece = owned // parts
-    reduces = [
-        Reduce(link, Blocks(dw, owned, i * piece), own.at[pl.ds(i * piece, piece)], reduce_bufs[i]) for i in range(parts)
-    ]
-    for i in range(2 * parts):
-        rows = pl.ds(i * (piece // 2), piece // 2)
-        chains.append(Chain(link, own.at[rows], both_any.at[:, rows], chain_bufs[i]))
-    ready, last = chains[:count], chains[count:]
-    to_owners = FromClip(link, dx, tokens_any, None)
+    _, owned, width = own.shape
+    order = (2, 1, 0)
+    reduces = [Reduce(link, Blocks(dw.at[c], owned, 0), own.at[c], reduce_bufs[c]) for c in order]
+    last = []
+    for c in order:
+        for i in range(2):
+            rows, cols = pl.ds(i * (owned // 2), owned // 2), pl.ds(c * width, width)
+            last.append(Chain(link, own.at[c, rows], both_any.at[:, rows, cols], chain_bufs[len(last)]))
+    to_owners = FromClip(link, dx, tokens_any, [stage])
     base = link.slots(half)
     keep = link.local_slots(2)
     swap_base = link.slots(3)
@@ -1266,21 +1421,21 @@
     for c in loads:
         c.start()
     link.meet_all()
-    for job in ready:
-        job.start()
-
-    def weight(i, carry):
-        part = pl.ds(pl.multiple_of(i * 256, 256), 256)
-        dw[part, :] = dot_tn(h_ref[:, part], g_ref[...]).astype(bf16)
-        return carry
-
-    lax.fori_loop(0, d // 256, weight, 0)
-    for job in reduces:
+    ready[0].start()
+    for c, job in zip(order, reduces):
+
+        def weight(i, carry):
+            part = pl.ds(pl.multiple_of(i * 256, 256), 256)
+            dw[c, part, :] = dot_tn(h_ref[:, part], g_ref[:, c * width : (c + 1) * width]).astype(bf16)
+            return carry
+
+        lax.fori_loop(0, d // 256, weight, 0)
         job.start()
 
     def product(j):
         rows = pl.ds(pl.multiple_of(j * ROWS, ROWS), ROWS)
-        return dot_nt(g_ref[rows, :], w_ref[...])
+        parts = [dot_nt(g_ref[rows, c * width : (c + 1) * width], w_refs[c][...]) for c in range(3)]
+        return parts[0] + parts[1] + parts[2]
 
     def swap(j):
         rows = pl.ds(pl.multiple_of(j * ROWS, ROWS), ROWS)
@@ -1314,46 +1469,47 @@
             total[first + row : first + row + 1, :] += jnp.sum(value, axis=0, keepdims=True)
         return carry
 
+    steps = chain_steps(ready)
+    run(steps[0])
     total[:first, :] = early_ref[...]
     total[first:, :] = jnp.zeros((total.shape[0] - first, d), f32)
     lax.fori_loop(0, half, send, 0)
     for c in loads:
         c.wait()
-    steps = chain_steps(ready)
-    for step in steps[0]:
-        step()
     reduces[0].forward()
-    lax.fori_loop(0, half, norm, 0)
+    after = {0: steps[1] + [reduces[1].forward], 1: [reduces[2].forward]}
+    for j in range(half):
+        norm(j, 0)
+        run(after.get(j, []))
     swaps[0].start()
-    for some in steps[1:]:
-        for step in some:
-            step()
-    for job in reduces[1:]:
-        job.forward()
-    to_owners.start()
+    run(steps[2])
+    reduces[0].collect()
+    last[0].start()
+    reduces[1].collect()
     swaps[0].wait()
     total[...] += came[0]
     swaps[1].start()
-    reduces[0].collect()
-    for c in last[:2]:
-        c.start()
+    reduces[2].collect()
+    for some in steps[3:]:
+        run(some)
     swaps[1].wait()
     total[...] += came[1]
     swaps[2].start()
-    for i in range(1, parts):
-        reduces[i].collect()
-        for c in last[2 * i : 2 * i + 2]:
-            c.start()
-    swaps[2].wait()
-    total[...] += came[2]
-    small.start()
-    for some in chain_steps(last):
-        for step in some:
-            step()
-    small.inward()
+    for number, some in enumerate(chain_steps(last)):
+        run(some)
+        if number == 0:
+            swaps[2].wait()
+            total[...] += came[2]
+            small.start()
+        if number == 2:
+            run([job.start for job in [to_owners] + others])
+        if number == 3:
+            small.inward()
+            small.sent()
+        if number == 5:
+            small.across()
     for c in ready + last:
         c.outward()
-    small.across()
     small.outward()
     for job in ready + last + [small]:
         job.finish()
@@ -1361,29 +1517,27 @@
         job.close()
     for j in range(half):
         swap(j)[1].wait_send()
-    to_owners.finish()
-
-
-def back_call(grads, w, vec, h, early, x, dmid, jobs, clips, number):
+    run([job.finish for job in [to_owners] + others])
+
+
+def back_call(grads, weights, vec, h, early, x, dmid, jobs, clips, number):
     n, d = x.shape
     size = n // 2
-    cols = grads.shape[1]
+    width = grads.shape[1] // 3
     groups = lax.axis_size("shard")
     owned = d // groups
-    parts = 2
     rows = early.shape[0] + 8
     small = pltpu.VMEM((rows, d), f32)
-    piece = owned // parts // 2
     vmem = pl.BlockSpec(memory_space=pltpu.VMEM)
     hbm = pl.BlockSpec(memory_space=pl.ANY)
     return pl.pallas_call(
-        functools.partial(back_kernel, jobs=jobs, parts=parts),
-        in_specs=[vmem] * 5 + [hbm] * 2 + jobs.in_specs(),
+        functools.partial(back_kernel, jobs=jobs),
+        in_specs=[vmem] * 7 + [hbm] * 2 + jobs.in_specs(),
         out_specs=[hbm, vmem, hbm] + jobs.in_specs(),
         out_shape=[
             jax.ShapeDtypeStruct((clips, size // clips, d), bf16),
             jax.ShapeDtypeStruct((2, rows, d), f32),
-            jax.ShapeDtypeStruct((2, owned, cols), bf16),
+            jax.ShapeDtypeStruct((2, owned, 3 * width), bf16),
         ]
         + jobs.out_shapes(),
         scratch_shapes=[
@@ -1392,27 +1546,26 @@
             pltpu.VMEM((size, d), bf16),
             pltpu.VMEM((size, d), bf16),
             pltpu.VMEM((size, d), bf16),
-            pltpu.VMEM((d, cols), bf16),
-            pltpu.VMEM((owned, cols), bf16),
+            pltpu.VMEM((3, d, width), bf16),
+            pltpu.VMEM((3, owned, width), bf16),
             small,
             pltpu.VMEM((3, rows, d), f32),
+            pltpu.VMEM((size // clips, d), bf16),
         ]
         + [small] * 3
-        + [pltpu.VMEM((piece, cols), bf16)] * (16 * parts)
-        + jobs.scratch(64),
+        + [pltpu.VMEM((owned // 2, width), bf16)] * 48
+        + jobs.scratch(80),
         compiler_params=comm_params(number, 62),
-        cost_estimate=cost(4 * n * w.size, 20 * n * d),
+        cost_estimate=cost(12 * n * weights[0].size, 20 * n * d),
         name="back",
-    )(grads, w, vec, h, early, x, dmid, *jobs.sources())
+    )(grads, vec, h, early, *weights, x, dmid, *jobs.sources())
 
 
 def place_kernel(*refs, groups):
-    up_refs, down_refs = refs[:3], refs[3:6]
-    out_ref, in_ref = refs[6:8]
-    up, down, wo = refs[8:11]
-    qkv = refs[11:14]
-    places = refs[14]
-    t = pl.program_id(0)
+    up_refs, down_refs = refs[:4], refs[4:8]
+    out_ref, in_ref = refs[8:10]
+    up, down, wo = refs[10:13]
+    qkv = refs[13:16]
 
     def put(target, axis, pieces):
         first = 0
@@ -1425,28 +1578,21 @@
                 target[span, :] = value.astype(f32)
             first += size
 
-    halves = [jnp.concatenate([up_refs[1][c], up_refs[2][c]], axis=0) for c in range(2)]
-    put(up, 1, [up_refs[0][0], halves[0], up_refs[0][1], halves[1]])
+    cut = up_refs[0].shape[1]
+    for part in range(2):
+        put(up.at[pl.ds(part * cut, cut)], 1, [r[c] for c in range(2) for r in (up_refs[part], up_refs[2 + part])])
     put(down, 0, [r[c] for c in range(2) for r in down_refs])
     put(wo, 0, [out_ref[c] for c in range(2)])
     rows = in_ref.shape[1]
     width = in_ref.shape[2] // 3
     part = width // groups
 
-    @pl.when(t == 0)
-    def _():
-        row = lax.broadcasted_iota(jnp.int32, (width, 2 * width), 0)
-        ahead = lax.broadcasted_iota(jnp.int32, (width, 2 * width), 1) - row
+    for i, out in enumerate(qkv):
         for c in range(2):
-            place = jnp.zeros((width, 2 * width), f32)
+            value = in_ref[c, :, i * width : (i + 1) * width].astype(f32)
             for s in range(groups):
-                here = (row >= s * part) & (row < (s + 1) * part) & (ahead == (s + c) * part)
-                place = jnp.where(here, 1.0, place)
-            places[c] = place.astype(bf16)
-
-    for i, out in enumerate(qkv):
-        cols = slice(i * width, (i + 1) * width)
-        out[...] = dot(in_ref[0, :, cols], places[0]) + dot(in_ref[1, :, cols], places[1])
+                first = (2 * s + c) * part
+                out[:, first : first + part] = value[:, s * part : (s + 1) * part]
 
 
 def place_call(ups, downs, wo, qkv, groups):
@@ -1457,7 +1603,7 @@
     take = [pl.BlockSpec((2, a.shape[1], a.shape[2] // groups), lambda i: (0, 0, jnp.minimum(i, groups - 1))) for a in ups]
     wide = d // steps
     per = own_d // steps
-    ff = 2 * ups[0].shape[2] + 2 * ups[1].shape[2]
+    ff = 2 * ups[0].shape[2] + 2 * ups[2].shape[2]
     return pl.pallas_call(
         functools.partial(place_kernel, groups=groups),
         grid=(steps,),
@@ -1479,7 +1625,6 @@
             jax.ShapeDtypeStruct((own_d, d), f32),
         ]
         + [jax.ShapeDtypeStruct((own_d, d), f32)] * 3,
-        scratch_shapes=[pltpu.VMEM((2, cols // 3, d), bf16)],
         compiler_params=params(),
         name="place",
     )(*ups, *downs, wo, qkv)
@@ -1543,6 +1688,8 @@
     first_n = ffn_cols * 2 // 5
     pieces = ((0, first_n), (first_n, ffn_cols))
 
+    fast = g == 4 and lax.axis_size("rep") == 8
+    weights = PairGather if fast else Gather
     positions = shard * rows + jnp.arange(rows, dtype=jnp.int32)
     live = positions[None, :] < lengths[:, None]
     masked = jnp.where(live[:, :, None], cotangent, jnp.zeros_like(cotangent))
@@ -1557,21 +1704,19 @@
         return jnp.where(core == 0, of(0), of(1))
 
     vectors = (first_gain, first_shift, query_bias, value_bias, out_bias, second_gain, second_shift, down_bias)
-    lens = jnp.pad(lengths.astype(f32), (0, own_d - cl)).reshape(1, own_d)
-    small = jnp.concatenate(
-        [jnp.stack(vectors).astype(f32), lens, up_bias.astype(f32).reshape(-1, own_d)], axis=0
-    )
-    small = jnp.pad(small, ((0, 16 - small.shape[0]), (0, -own_d % 128)))
-    qkv_own = jnp.concatenate(
-        [core_cols(w, attn_cols, 0, attn_cols) for w in (query_weight, key_weight, value_weight)], axis=1
-    )
+    lens = jnp.pad(lengths, (0, own_d - cl)).astype(f32)
+    flat = jnp.concatenate([*vectors, up_bias]).astype(f32)
+    cut = len(vectors) * own_d
+    flat = jnp.concatenate([flat[:cut], lens, flat[cut:], jnp.zeros((16 * own_d - flat.shape[0] - own_d,), f32)])
+    small = jnp.pad(flat.reshape(16, own_d), ((0, 0), (0, -own_d % 128)))
+    own = [core_cols(w, attn_cols, 0, attn_cols) for w in (query_weight, key_weight, value_weight)]
     jobs = Jobs(
         (ToClip, tokens, (n, d)),
-        (Gather, qkv_own, (g,) + qkv_own.shape),
         (Gather, small, (g,) + small.shape),
+        *[(weights, w, (g,) + w.shape) for w in own],
     )
-    x, w_qkv, smalls, other_small = exchange_call(jobs, small, 0, "first_exchange")
-    w_qkv = w_qkv.reshape(d, 3 * width)
+    x, smalls, *w_qkv, other_small = exchange_call(jobs, small, 0, "first_exchange")
+    w_qkv = [w.reshape(d, width) for w in w_qkv]
     vec = smalls[:, :, :own_d].transpose(1, 0, 2).reshape(16, d)
     near = lax.div(shard, cl) == core
     lens = jnp.where(near, small[LENGTHS], other_small[LENGTHS])[0]
@@ -1600,25 +1745,23 @@
 
     def gathered(a, part=None):
         if part is None:
-            return (Gather, a, (g,) + a.shape)
-        return (Gather, a, (g, part[0]) + a.shape[1:], part[1])
-
-    jobs = Jobs((ToClip, masked, (n, d)))
-    h1, q, k, v, dz = qkv_call(x, vec, w_qkv, bias, wide, jobs, 9)
+            return (weights, a, (g,) + a.shape)
+        return (weights, a, (g, part[0]) + a.shape[1:], part[1])
+
+    h1, q, k, v = qkv_call(x, vec, bias, w_qkv, wide)
     jobs = Jobs(
-        gathered(out_weight, half_rows(out_weight)),
         gathered(ups[0]),
         gathered(down_weight, half_rows(down_weight, *pieces[0])),
+        gathered(out_weight, half_rows(out_weight)),
     )
-    o, lse, w_out, up, down = attn_fwd_call(length, q, k, v, width, heads, jobs, 1)
+    o, lse, up, down, w_out = attn_fwd_call(length, q, k, v, width, heads, jobs, 1)
     w_out = w_out.reshape(width, d)
-    jobs = Jobs(gathered(ups[1]))
-    mid, h2, o_wide, up1 = middle_call(o, w_out, x, vec, wide, jobs, 2)
+    jobs = Jobs((ToClip, masked, (n, d)))
+    mid, h2, o_wide, dz = middle_call(o, w_out, x, vec, wide, jobs, 2)
 
     def hidden_bias(piece):
         return ubias[:, piece[0] : piece[1]].reshape(1, -1)
 
-    fast = g == 4 and lax.axis_size("rep") == 8
 
     def to_owners(a):
         if fast:
@@ -1631,12 +1774,16 @@
     def chained(a):
         return (Chain, a, (2,) + a.shape)
 
-    def upper(a):
+    def chained_halves(a):
         half = a.shape[0] // 2
-        return [a[:half], a[half:]]
-
-    jobs = Jobs(gathered(down_weight, half_rows(down_weight, *pieces[1])))
-    out, dh2, dup0, ddn0, dub0, down1 = ffn_call(
+
+        def part(i):
+            return lambda ref: ref.at[pl.ds(i * half, half)]
+
+        return [(Chain, a, (2, half, a.shape[1]), part(i)) for i in range(2)]
+
+    jobs = Jobs(gathered(ups[1]), gathered(down_weight, half_rows(down_weight, *pieces[1])))
+    out, dh2, dup0, ddn0, dub0, up1, down1 = ffn_call(
         h2, dz, up.reshape(d, -1), hidden_bias(pieces[0]), down.reshape(-1, d), None, False, jobs, 3, "hidden0"
     )
     dup0, ddn0 = dup0.reshape(g, own_d, -1), ddn0.reshape(g, -1, d)
@@ -1647,15 +1794,20 @@
     dup1, ddn1 = dup1.reshape(g, own_d, -1), ddn1.reshape(g, -1, d)
     up0_own, down0_own = owned(dup0, dup0_in), owned(ddn0, ddn0_in)
 
-    jobs = Jobs(to_owners(dup1))
-    dmid, do, dwo, sums2, layer_own, dup1_in = second_back_call(mid, dh2, out, dz, vec, w_out, o, wide, jobs, 5)
+    jobs = [to_owners(dup1)]
+    if fast:
+        jobs += chained_halves(up0_own)
+    dmid, do, dwo, sums2, layer_own, dup1_in, *sums0 = second_back_call(
+        mid, dh2, out, dz, vec, w_out, o, wide, Jobs(*jobs), 5
+    )
     dwo = dwo.reshape(g, -1, d)
     up1_own = owned(dup1, dup1_in)
 
-    jobs = [to_owners(ddn1), to_owners(dwo), (FromClip, layer_own, (cl, rows, d))]
+    to_tokens = (FromClip, layer_own, (cl, rows, d))
+    jobs = [to_owners(ddn1), to_owners(dwo), to_tokens]
     if fast:
-        jobs += [chained(a) for a in [up0_own, down0_own] + upper(up1_own)]
-    grads, bias_sums, ddn1_in, dwo_in, layer_out, *sums0 = attn_bwd_call(
+        jobs += chained_halves(down0_own) + chained_halves(up1_own)
+    grads, bias_sums, ddn1_in, dwo_in, layer_out, *later = attn_bwd_call(
         length, q, k, v, o_wide, do, lse, width, heads, Jobs(*jobs), 6
     )
     down1_own, out_own_grad = owned(ddn1, ddn1_in), owned(dwo, dwo_in)
@@ -1677,16 +1829,16 @@
     early = jnp.pad(early, ((0, -early.shape[0] % 8), (0, 0)))
 
     if fast:
-        jobs = Jobs(*[chained(a) for a in upper(down1_own) + [out_own_grad]])
+        jobs = Jobs(*chained_halves(down1_own), chained(out_own_grad))
         tokens_grad, smalls, qkv_all, *sums = back_call(grads, w_qkv, vec, h1, early, x, dmid, jobs, cl, 7)
         up_grad, down_grad, out_grad, *qkv_grads = place_call(
-            (sums0[0], sums0[2], sums0[3]), (sums0[1], sums[0], sums[1]), sums[2], qkv_all, g
+            (*sums0, *later[2:]), (*later[:2], *sums[:2]), sums[2], qkv_all, g
         )
         smalls = lax.dynamic_index_in_dim(smalls, core, 0, keepdims=False)
     else:
         dwqkv = dw_call(h1, grads).reshape(g, own_d, 3 * width)
         jobs = Jobs(to_owners(dwqkv))
-        dx, sums1, dwqkv_in = first_back_call(grads, w_qkv, vec, x, dmid, jobs, 7)
+        dx, sums1, dwqkv_in = first_back_call(grads, jnp.concatenate(w_qkv, axis=1), vec, x, dmid, jobs, 7)
         jobs = Jobs((FromClip, dx, (cl, rows, d)))
         tokens_grad, _ = exchange_call(jobs, sums1, 8, "last_exchange")
         ups_all = [over_reps(a).reshape(2, own_d, g, -1) for a in (up0_own, up1_own)]

time: 657 us -> 596 us (0.907)
  Pallas kernels: 619 us -> 554 us
    pallas_call x2, Pallas kernels: 166 us -> 119 us  [the longest x1 102 us: back_call(): pl.pallas_call(functools.partial(back_kernel, jobs=jobs), in_specs=[vmem]...]
    pallas_call x2, Pallas kernels: 112 us -> 139 us  [ffn_call(): pl.pallas_call(functools.partial(ffn_kernel, chained=chained, last=last,...]
    pallas_call x1, Pallas kernels: 99 us -> 85.3 us  [attn_bwd_call(): pl.pallas_call(functools.partial(attn_bwd_kernel, bk=256, jobs=jobs), gri...]
    pallas_call x1, Pallas kernels: 73.2 us -> 63.4 us  [exchange_call(): pl.pallas_call(kernel, in_specs=jobs.in_specs() + [pl.BlockSpec(memory_sp...]
    pallas_call x1, Pallas kernels: 64.6 us -> 55.5 us  [attn_fwd_call(): pl.pallas_call(functools.partial(attn_fwd_kernel, bq=256, jobs=jobs), gri...]
    pallas_call x1, Pallas kernels: 45.8 us -> 37.5 us  [middle_call(): pl.pallas_call(functools.partial(middle_kernel, jobs=jobs), in_specs=[vme...]
where the time goes in v5:
time: 596 us; the launch traced here: 592 us
  Pallas kernels  554 us (93%)
  local copies, waits for them, and re-layouts  23.6 us (4%)
  other arithmetic  12.6 us (2%)
    pallas_call x2, Pallas kernels, ffn_call(): pl.pallas_call(functools.partial(ffn_kernel, chained=chained, last=last,...  139 us
    pallas_call x1, Pallas kernels, back_call(): pl.pallas_call(functools.partial(back_kernel, jobs=jobs), in_specs=[vmem]...  102 us
    pallas_call x1, Pallas kernels, attn_bwd_call(): pl.pallas_call(functools.partial(attn_bwd_kernel, bk=256, jobs=jobs), gri...  85.3 us
    pallas_call x1, Pallas kernels, exchange_call(): pl.pallas_call(kernel, in_specs=jobs.in_specs() + [pl.BlockSpec(memory_sp...  63.4 us
    pallas_call x1, Pallas kernels, attn_fwd_call(): pl.pallas_call(functools.partial(attn_fwd_kernel, bq=256, jobs=jobs), gri...  55.5 us
    pallas_call x1, Pallas kernels, second_back_call(): pl.pallas_call(functools.partial(second_back_kernel, jobs=jobs), grid=(n...  43 us
    pallas_call x1, Pallas kernels, middle_call(): pl.pallas_call(functools.partial(middle_kernel, jobs=jobs), in_specs=[vme...  37.5 us
    pallas_call x1, Pallas kernels, qkv_call(): pl.pallas_call(qkv_kernel, grid=(n // ROWS,), in_specs=[row_block(ROWS, d...  16.7 us

profile of v5, /device:TPU:0, one launch (start us, length us, event | category | flops | bytes accessed | tf_op | source)
XLA Modules:
  0.0 591.9 jit_solution(10564918548128819981)
XLA Ops:
  0.7 6.4 %concatenate.45 = bf16[3840]{0:T(1024)(128)(2,1)S(1)} concatenate(bf16[320]{0:T(512)(128)(2,1)} %param.21, bf16[320]{0:T(512)(128)(2,1)} %param.22, bf16[320]{0:T(512)(128)(2,1)} %param.24, bf16[320]{0:T(512)(128)(2,1)} %param.27, bf16[320]{0:T(512)(128)(2,1)} %param.29, bf16[320]{0:T(512)(128)(2,1)} %param.30, bf16[320]{0:T(512)(128)(2,1)} %param.31, bf16[320]{0:T(512)(128)(2,1)} %param.35, ...), dimensions={0} | concatenate | bytes 15360 | tf_op jit(solution)/shard_map/concatenate | solution.py:1708
  7.1 0.7 pad_convert_fusion
  7.9 0.6 pad.13.refs_1_.refs_5_
  8.5 1.9 fusion.6
  10.9 2.1 maximum_select_fusion.2
  13.4 1.3 maximum_select_fusion.4.refs_4_
  14.7 63.4 %first_exchange.1 = (bf16[1536,1280]{1,0:T(8,128)(2,1)}, f32[4,16,384]{2,1,0:T(8,128)}, bf16[4,320,640]{2,1,0:T(8,128)(2,1)}, bf16[4,320,640]{2,1,0:T(8,128)(2,1...) custom-call(bf16[2,384,1280]{2,1,0:T(8,128)(2,1)} %refs_0_.1, f32[16,384]{1,0:T(8,128)} %pad.13.refs_1_.refs_5_, ...), custom_call_target="tpu_custom_call" | custom-call | tf_op jit(solution)/shard_map/first_exchange/pallas_call | solution.py:719
  78.1 0.7 slice.225
  79.4 1.2 fusion.7
  81.3 0.9 slice_bitcast_fusion
  82.2 0.8 reshape.187.vec_ref.refs_3_.refs_4_.refs_1_
  84.0 16.7 %project.1 = (bf16[1536,1280]{1,0:T(8,128)(2,1)}, bf16[1536,768]{1,0:T(8,128)(2,1)}, bf16[1536,768]{1,0:T(8,128)(2,1)}, bf16[1536,768]{1,0:T(8,128)(2,1)}) custom-call(bf16[1536,1280]{1,0:T(8,128)(2,1)} %get-tuple-element.80.x_ref.refs_2_.refs_7_, f32[16,1280]{1,0:T(8,128)} %reshape.187.vec_ref.refs_3_.refs_4_.refs_1_, f32[1,1920]{1,0:T(1,128)} %fusion.bias_ref, ...), custom_call_target="tpu_custom_call" | custom-call | flops 7549747200 | bytes 19857408 | tf_op jit(solution)/shard_map/project/pallas_call | solution.py:744
  100.8 1.0 maximum_select_fusion.1.refs_4_
  101.8 55.5 %attend.1 = (bf16[1536,640]{1,0:T(8,128)(2,1)}, f32[1536,128]{1,0:T(8,128)}, bf16[4,320,1024]{2,1,0:T(8,128)(2,1)}, bf16[4,256,1280]{2,1,0:T(8,128)(2,1)}, bf16[4,160,1280]{2,1,0:T(8,128)(2,1)}) custom-call(s32[1]{0:T(128)} %bitcast.refs_0_, bf16[1536,768]{1,0:T(8,128)(2,1)} %get-tuple-element.85.refs_1_, bf16[1536,768]{1,0:T(8,128)(2,1)} %get-tuple-element.86.refs_2_, ...), custom_call_target="tpu_custom_call" | custom-call | flops 19327352832 | bytes 9437184 | tf_op jit(solution)/shard_map/attend/pallas_call | solution.py:841
  157.4 3.0 broadcast_select_fusion.refs_4_
  160.4 37.5 %middle.1 = (f32[1536,1280]{1,0:T(8,128)}, bf16[1536,1280]{1,0:T(8,128)(2,1)}, bf16[1536,768]{1,0:T(8,128)(2,1)}, bf16[1536,1280]{1,0:T(8,128)(2,1)}) custom-call(bf16[1536,640]{1,0:T(8,128)(2,1)} %get-tuple-element.88.refs_0_.refs_6_, bf16[640,1280]{1,0:T(8,128)(2,1)} %bitcast.32, bf16[1536,1280]{1,0:T(8,128)(2,1)} %get-tuple-element.80.x_ref.refs_2_.refs_7_, ...), custom_call_target="tpu_custom_call" | custom-call | flops 2516582400 | bytes 27525120 | tf_op jit(solution)/shard_map/middle/pallas_call | solution.py:1005
  198.9 1.2 maximum_select_fusion.refs_5_
  200.1 78.4 %hidden0.1 = (f32[1536,1280]{1,0:T(8,128)}, f32[1536,1280]{1,0:T(8,128)}, bf16[1280,1024]{1,0:T(8,128)(2,1)}, bf16[1024,1280]{1,0:T(8,128)(2,1)}, f32[1,1024]{1,...) custom-call(bf16[1536,1280]{1,0:T(8,128)(2,1)} %get-tuple-element.92.refs_0_, ...), custom_call_target="tpu_custom_call" | custom-call | flops 24159191040 | bytes 34078720 | tf_op jit(solution)/shard_map/hidden0/pallas_call | solution.py:1107
  279.2 60.9 %hidden1.1 = (bf16[1536,1280]{1,0:T(8,128)(2,1)}, bf16[1536,1280]{1,0:T(8,128)(2,1)}, bf16[1280,1536]{1,0:T(8,128)(2,1)}, bf16[1536,1280]{1,0:T(8,128)(2,1)}, f3...) custom-call(bf16[1536,1280]{1,0:T(8,128)(2,1)} %get-tuple-element.92.refs_0_, ...), custom_call_target="tpu_custom_call" | custom-call | flops 36238786560 | bytes 39321600 | tf_op jit(solution)/shard_map/hidden1/pallas_call | solution.py:1107
  340.0 43.0 %second_back.1 = (f32[1536,1280]{1,0:T(8,128)}, bf16[1536,768]{1,0:T(8,128)(2,1)}, bf16[640,1280]{1,0:T(8,128)(2,1)}, f32[8,1280]{1,0:T(8,128)}, bf16[768,1280]{...) custom-call(f32[1536,1280]{1,0:T(8,128)} %get-tuple-element.91.refs_0_, ...), custom_call_target="tpu_custom_call" | custom-call | flops 5033164800 | bytes 27525120 | tf_op jit(solution)/shard_map/second_back/pallas_call | solution.py:1240
  383.1 85.3 %attend_back.1 = (bf16[1536,1920]{1,0:T(8,128)(2,1)}, f32[1,1920]{1,0:T(1,128)}, bf16[384,1280]{1,0:T(8,128)(2,1)}, bf16[160,1280]{1,0:T(8,128)(2,1)}, bf16[2,38...) custom-call(s32[1]{0:T(128)} %bitcast.refs_0_, ...), custom_call_target="tpu_custom_call" | custom-call | flops 48318382080 | bytes 23592960 | tf_op jit(solution)/shard_map/attend_back/pallas_call | solution.py:931
  468.9 0.7 reduce.32
  469.7 0.7 slice_reduce_fusion.3
  470.9 0.7 select_maximum_fusion.refs_3_
  471.6 101.9 %back.1 = (bf16[2,384,1280]{2,1,0:T(8,128)(2,1)}, f32[2,24,1280]{2,1,0:T(8,128)}, bf16[2,320,1920]{2,1,0:T(8,128)(2,1)}, bf16[2,192,1280]{2,1,0:T(8,128)(2,1)}, ...) custom-call(bf16[1536,1920]{1,0:T(8,128)(2,1)} %get-tuple-element.114.refs_0_, ...), custom_call_target="tpu_custom_call" | custom-call | flops 15099494400 | bytes 39321600 | tf_op jit(solution)/shard_map/back/pallas_call | solution.py:1533
  573.5 1.7 dynamic-slice_reduce_fusion.2
  575.2 11.4 %place.1 = (f32[320,5120]{1,0:T(8,128)}, f32[1280,1280]{1,0:T(8,128)}, f32[320,1280]{1,0:T(8,128)}, f32[320,1280]{1,0:T(8,128)}, f32[320,1280]{1,0:T(8,128)}, /*index=5*/f32[320,1280]{1,0:T(8,128)}) custom-call(bf16[2,160,1024]{2,1,0:T(8,128)(2,1)} %get-tuple-element.125.refs_0_, bf16[2,160,1024]{2,1,0:T(8,128)(2,1)} %get-tuple-element.126.refs_1_, ...), custom_call_target="tpu_custom_call" | custom-call | tf_op jit(solution)/shard_map/place/pallas_call | solution.py:1607
  586.6 0.9 constant_dynamic-slice_fusion.2
  587.5 0.7 dynamic_slice.30
  588.2 1.3 copy.54
  589.4 1.0 copy-done.4
  590.4 1.3 copy.55
  (68 shorter events, 5.5 us)
Async XLA Ops:
  0.7 9.8 %copy-start.1 = (bf16[320,1280]{1,0:T(8,128)(2,1)S(1)}, bf16[320,1280]{1,0:T(8,128)(2,1)}, u32[]{:S(2)}) copy-start(bf16[320,1280]{1,0:T(8,128)(2,1)} %param.25) | copy-start | bytes 2457604
  10.8 2.1 copy-start.2
  84.0 16.7 %copy-start = (bf16[320,5120]{1,0:T(8,128)(2,1)S(1)}, bf16[320,5120]{1,0:T(8,128)(2,1)}, u32[]{:S(2)}) copy-start(bf16[320,5120]{1,0:T(8,128)(2,1)} %param.32) | copy-start | bytes 9830404
  101.8 55.5 %copy-start.8 = (s32[2]{0:T(128)S(1)}, s32[2]{0:T(128)}, u32[]{:S(2)}) copy-start(s32[2]{0:T(128)} %param.19) | copy-start | bytes 28
  383.0 85.3 %copy-start.6 = (f32[1,1536]{1,0:T(1,128)S(1)}, f32[1,1536]{1,0:T(1,128)}, u32[]{:S(2)}) copy-start(f32[1,1536]{1,0:T(1,128)} %get-tuple-element.119) | copy-start | bytes 18436
  383.1 85.9 %copy-start.7 = (f32[1,1024]{1,0:T(1,128)S(1)}, f32[1,1024]{1,0:T(1,128)}, u32[]{:S(2)}) copy-start(f32[1,1024]{1,0:T(1,128)} %get-tuple-element.118) | copy-start | bytes 12292
  383.1 86.7 %copy-start.5 = (f32[8,1280]{1,0:T(8,128)S(1)}, f32[8,1280]{1,0:T(8,128)}, u32[]{:S(2)}) copy-start(f32[8,1280]{1,0:T(8,128)} %get-tuple-element.117) | copy-start | bytes 122884
  575.2 13.0 %copy-start.3 = (bf16[2,384,1280]{2,1,0:T(8,128)(2,1)S(1)}, bf16[2,384,1280]{2,1,0:T(8,128)(2,1)}, u32[]{:S(2)}) copy-start(bf16[2,384,1280]{2,1,0:T(8,128)(2,1)} %get-tuple-element.212) | copy-start | bytes 5898244
  588.2 2.3 copy-start.4

commit v6 on v5

--- a/solution.py
+++ b/solution.py
@@ -727,30 +727,127 @@
     )(*jobs.sources(), sibling)
 
 
-def qkv_kernel(x_ref, vec_ref, bias_ref, wq_ref, wk_ref, wv_ref, h_ref, q_ref, k_ref, v_ref):
-    xhat, _ = standardize(x_ref[...].astype(f32))
-    h = (xhat * vec_ref[GAIN1] + vec_ref[SHIFT1]).astype(bf16)
-    h_ref[...] = h
-    for i, (w_ref, ref) in enumerate(((wq_ref, q_ref), (wk_ref, k_ref), (wv_ref, v_ref))):
-        width = w_ref.shape[1]
-        z = dot(h, w_ref[...]) + bias_ref[:, i * width : (i + 1) * width]
-        ref[:, :width] = z.astype(bf16)
-        ref[:, width:] = jnp.zeros((ref.shape[0], ref.shape[1] - width), bf16)
-
-
-def qkv_call(x, vec, bias, weights, wide):
-    n, d = x.shape
-    out = jax.ShapeDtypeStruct((n, wide), bf16)
+def pack_kernel(*refs, count):
+    out_ref = refs[-1]
+    lens_ref = refs[count]
+    out_ref[...] = jnp.zeros_like(out_ref)
+    row = 0
+    for ref in refs[:count]:
+        size = refs[0].shape[0]
+        for part in range(ref.shape[0] // size):
+            value = ref[part * size : (part + 1) * size].astype(f32)
+            out_ref[row : row + 1, :size] = value.reshape(1, size)
+            row += 1
+        if row == LENGTHS.start:
+            lane = lax.broadcasted_iota(jnp.int32, (1, out_ref.shape[1]), 1)
+            value = jnp.zeros(lane.shape, f32)
+            for clip in range(lens_ref.shape[0]):
+                value = jnp.where(lane == clip, lens_ref[clip].astype(f32), value)
+            out_ref[row : row + 1, :] = value
+            row += 1
+
+
+def pack_call(vectors, lengths):
+    vmem = pl.BlockSpec(memory_space=pltpu.VMEM)
+    lanes = pl.cdiv(vectors[0].shape[0], 128) * 128
     return pl.pallas_call(
-        qkv_kernel,
-        grid=(n // ROWS,),
-        in_specs=[row_block(ROWS, d), whole(vec.shape), whole(bias.shape)] + [once(w.shape) for w in weights],
-        out_specs=[row_block(ROWS, d)] + [row_block(ROWS, wide)] * 3,
-        out_shape=[jax.ShapeDtypeStruct((n, d), bf16), out, out, out],
-        compiler_params=params(),
-        cost_estimate=cost(6 * n * weights[0].size, 4 * n * d + 6 * weights[0].size + 6 * n * wide),
-        name="project",
-    )(x, vec, bias, *weights)
+        functools.partial(pack_kernel, count=len(vectors)),
+        in_specs=[vmem] * len(vectors) + [pl.BlockSpec(memory_space=pltpu.SMEM)],
+        out_specs=vmem,
+        out_shape=jax.ShapeDtypeStruct((16, lanes), f32),
+        name="pack",
+    )(*vectors, lengths)
+
+
+def first_kernel(*refs, jobs, size):
+    count = len(jobs.jobs)
+    srcs, mine = refs[:count], refs[count]
+    h_ref, *heads, vec_ref = refs[count + 1 : count + 6]
+    dsts, other = refs[count + 6 : 2 * count + 6], refs[2 * count + 6]
+    x, small, weight, bias, sems = refs[2 * count + 7 : 2 * count + 12]
+    link, bound, _ = jobs.bind(refs[2 * count + 12 :], srcs, dsts)
+    tokens, smalls, *gathers = bound
+    slot = link.slots(1)
+    swap = link.remote(mine, other, slot, slot, link.sibling())
+    n = x.shape[0]
+    width = weight.shape[2]
+    part = size // 2
+
+    def load(src, dst, i):
+        return pltpu.make_async_copy(src, dst, sems.at[i])
+
+    link.meet_plane(jobs.pairs)
+    steps = gather_steps(gathers)
+    swap.start()
+    run([smalls.start, tokens.start] + steps[0])
+    run([smalls.forward, smalls.finish])
+    load(dsts[1], small, 0).start()
+    run(steps[1])
+    load(dsts[1], small, 0).wait()
+    bias[...] = jnp.zeros_like(bias)
+    for s in range(small.shape[0]):
+        vec_ref[:, s * size : (s + 1) * size] = small[s][:, :size]
+        for row, first in ((QBIAS, 0), (VBIAS, 2 * width)):
+            value = jnp.where(link.core == 0, small[s, row, :part], small[s, row, part:size])
+            bias[:, first + s * part : first + (s + 1) * part] = value
+    tokens.forward()
+    run(steps[2])
+    tokens.finish()
+    load(dsts[0], x, 0).start()
+    load(dsts[0], x, 0).wait()
+
+    def norm(i, carry):
+        rows = pl.ds(pl.multiple_of(i * ROWS, ROWS), ROWS)
+        xhat, _ = standardize(x[rows, :].astype(f32))
+        h_ref[rows, :] = (xhat * vec_ref[GAIN1] + vec_ref[SHIFT1]).astype(bf16)
+        return carry
+
+    lax.fori_loop(0, n // ROWS, norm, 0)
+    for ref in heads:
+        ref[:, width:] = jnp.zeros((n, ref.shape[1] - width), bf16)
+    for i, (gather, ref) in enumerate(zip(gathers, heads)):
+        run(steps[3 + i] if 3 + i < len(steps) else [])
+        gather.finish()
+        for s in range(small.shape[0]):
+            load(dsts[2 + i].at[s], weight.at[i, pl.ds(s * size, size)], 1 + s).start()
+        for s in range(small.shape[0]):
+            load(dsts[2 + i].at[s], weight.at[i, pl.ds(s * size, size)], 1 + s).wait()
+
+        def project(j, carry):
+            rows = pl.ds(pl.multiple_of(j * ROWS, ROWS), ROWS)
+            z = dot(h_ref[rows, :], weight[i]) + bias[:, i * width : (i + 1) * width]
+            ref[rows, :width] = z.astype(bf16)
+            return carry
+
+        lax.fori_loop(0, n // ROWS, project, 0)
+    swap.wait()
+
+
+def first_call(jobs, small, wide, number):
+    (n, d), groups = jobs.jobs[0][2], lax.axis_size("shard")
+    width = jobs.jobs[2][2][2]
+    vmem = pl.BlockSpec(memory_space=pltpu.VMEM)
+    hbm = pl.BlockSpec(memory_space=pl.ANY)
+    head = jax.ShapeDtypeStruct((n, wide), bf16)
+    return pl.pallas_call(
+        functools.partial(first_kernel, jobs=jobs, size=d // groups),
+        in_specs=jobs.in_specs() + [hbm],
+        out_specs=[vmem] * 5 + jobs.in_specs() + [hbm],
+        out_shape=[jax.ShapeDtypeStruct((n, d), bf16), head, head, head, jax.ShapeDtypeStruct((16, d), f32)]
+        + jobs.out_shapes()
+        + [jax.ShapeDtypeStruct(small.shape, small.dtype)],
+        scratch_shapes=[
+            pltpu.VMEM((n, d), bf16),
+            pltpu.VMEM((groups,) + small.shape, f32),
+            pltpu.VMEM((3, d, width), bf16),
+            pltpu.VMEM((1, 3 * width), f32),
+            pltpu.SemaphoreType.DMA((1 + groups,)),
+        ]
+        + jobs.scratch(1),
+        compiler_params=comm_params(number),
+        cost_estimate=cost(6 * n * d * width, 12 * n * d),
+        name="first",
+    )(*jobs.sources(), small)
 
 
 def head_window(h):
@@ -1704,28 +1801,19 @@
         return jnp.where(core == 0, of(0), of(1))
 
     vectors = (first_gain, first_shift, query_bias, value_bias, out_bias, second_gain, second_shift, down_bias)
-    lens = jnp.pad(lengths, (0, own_d - cl)).astype(f32)
-    flat = jnp.concatenate([*vectors, up_bias]).astype(f32)
-    cut = len(vectors) * own_d
-    flat = jnp.concatenate([flat[:cut], lens, flat[cut:], jnp.zeros((16 * own_d - flat.shape[0] - own_d,), f32)])
-    small = jnp.pad(flat.reshape(16, own_d), ((0, 0), (0, -own_d % 128)))
+    small = pack_call((*vectors, up_bias), lengths)
     own = [core_cols(w, attn_cols, 0, attn_cols) for w in (query_weight, key_weight, value_weight)]
     jobs = Jobs(
         (ToClip, tokens, (n, d)),
         (Gather, small, (g,) + small.shape),
         *[(weights, w, (g,) + w.shape) for w in own],
     )
-    x, smalls, *w_qkv, other_small = exchange_call(jobs, small, 0, "first_exchange")
+    h1, q, k, v, vec, x, _, *w_qkv, other_small = first_call(jobs, small, wide, 0)
     w_qkv = [w.reshape(d, width) for w in w_qkv]
-    vec = smalls[:, :, :own_d].transpose(1, 0, 2).reshape(16, d)
     near = lax.div(shard, cl) == core
     lens = jnp.where(near, small[LENGTHS], other_small[LENGTHS])[0]
     length = lens[lax.rem(shard, cl)].astype(jnp.int32).reshape(1)
 
-    def bias_cols(b):
-        return lax.dynamic_index_in_dim(vec[b].reshape(1, g, 2, attn_cols), core, 2).reshape(1, width)
-
-    bias = jnp.concatenate([bias_cols(QBIAS), jnp.zeros((1, width), f32), bias_cols(VBIAS)], axis=1)
     ubias = lax.dynamic_index_in_dim(
         vec[UBIAS : UBIAS + own_f // own_d].reshape(-1, g, own_d).transpose(1, 0, 2).reshape(g, 2, ffn_cols),
         core,
@@ -1748,7 +1836,6 @@
             return (weights, a, (g,) + a.shape)
         return (weights, a, (g, part[0]) + a.shape[1:], part[1])
 
-    h1, q, k, v = qkv_call(x, vec, bias, w_qkv, wide)
     jobs = Jobs(
         gathered(ups[0]),
         gathered(down_weight, half_rows(down_weight, *pieces[0])),

time: 596 us -> 587 us (0.985)
  local copies, waits for them, and re-layouts: 23.6 us -> 15.1 us
    concatenate x3 -> x0, local copies, waits for them, and re-layouts: 6.46 us -> none  [the longest x1 6.37 us: on_device(): flat = jnp.concatenate([*vectors, up_bias]).astype(f32)]
where the time goes in v6:
time: 587 us; the launch traced here: 583 us
  Pallas kernels  554 us (94%)
  local copies, waits for them, and re-layouts  15.1 us (3%)
  other arithmetic  11.3 us (2%)
    pallas_call x2, Pallas kernels, ffn_call(): pl.pallas_call(functools.partial(ffn_kernel, chained=chained, last=last,...  139 us
    pallas_call x1, Pallas kernels, back_call(): pl.pallas_call(functools.partial(back_kernel, jobs=jobs), in_specs=[vmem]...  101 us
    pallas_call x1, Pallas kernels, attn_bwd_call(): pl.pallas_call(functools.partial(attn_bwd_kernel, bk=256, jobs=jobs), gri...  85.5 us
    pallas_call x1, Pallas kernels, first_call(): pl.pallas_call(functools.partial(first_kernel, jobs=jobs, size=d // group...  77.8 us
    pallas_call x1, Pallas kernels, attn_fwd_call(): pl.pallas_call(functools.partial(attn_fwd_kernel, bq=256, jobs=jobs), gri...  56.8 us
    pallas_call x1, Pallas kernels, second_back_call(): pl.pallas_call(functools.partial(second_back_kernel, jobs=jobs), grid=(n...  43.3 us
    pallas_call x1, Pallas kernels, middle_call(): pl.pallas_call(functools.partial(middle_kernel, jobs=jobs), in_specs=[vme...  38 us

profile of v6, /device:TPU:0, one launch (start us, length us, event | category | flops | bytes accessed | tf_op | source)
XLA Modules:
  0.0 582.7 jit_solution(2493450992430173101)
XLA Ops:
  0.7 1.6 pack.1.refs_1_.refs_5_
  2.3 1.9 fusion.4
  4.6 2.1 maximum_select_fusion.2
  7.2 1.3 maximum_select_fusion.4.refs_4_
  8.5 77.8 %first.1 = (bf16[1536,1280]{1,0:T(8,128)(2,1)}, bf16[1536,768]{1,0:T(8,128)(2,1)}, bf16[1536,768]{1,0:T(8,128)(2,1)}, bf16[1536,768]{1,0:T(8,128)(2,1)}, f32[16,...) custom-call(bf16[2,384,1280]{2,1,0:T(8,128)(2,1)} %refs_0_.3, ...), custom_call_target="tpu_custom_call" | custom-call | flops 7549747200 | bytes 23592960 | tf_op jit(solution)/shard_map/first/pallas_call | solution.py:832
  86.3 0.7 slice.205
  87.0 0.6 constant_dynamic-slice_fusion.3
  87.6 1.2 fusion.5
  89.6 1.0 maximum_select_fusion.1.refs_4_
  90.6 56.8 %attend.1 = (bf16[1536,640]{1,0:T(8,128)(2,1)}, f32[1536,128]{1,0:T(8,128)}, bf16[4,320,1024]{2,1,0:T(8,128)(2,1)}, bf16[4,256,1280]{2,1,0:T(8,128)(2,1)}, bf16[4,160,1280]{2,1,0:T(8,128)(2,1)}) custom-call(s32[1]{0:T(128)} %bitcast.refs_0_, bf16[1536,768]{1,0:T(8,128)(2,1)} %get-tuple-element.80.refs_1_, bf16[1536,768]{1,0:T(8,128)(2,1)} %get-tuple-element.81.refs_2_, ...), custom_call_target="tpu_custom_call" | custom-call | flops 19327352832 | bytes 9437184 | tf_op jit(solution)/shard_map/attend/pallas_call | solution.py:938
  147.5 3.0 broadcast_select_fusion.refs_4_
  150.6 38.0 %middle.1 = (f32[1536,1280]{1,0:T(8,128)}, bf16[1536,1280]{1,0:T(8,128)(2,1)}, bf16[1536,768]{1,0:T(8,128)(2,1)}, bf16[1536,1280]{1,0:T(8,128)(2,1)}) custom-call(bf16[1536,640]{1,0:T(8,128)(2,1)} %get-tuple-element.83.refs_0_.refs_6_, bf16[640,1280]{1,0:T(8,128)(2,1)} %bitcast.31, bf16[1536,1280]{1,0:T(8,128)(2,1)} %get-tuple-element.85.refs_2_.refs_7_, ...), custom_call_target="tpu_custom_call" | custom-call | flops 2516582400 | bytes 27525120 | tf_op jit(solution)/shard_map/middle/pallas_call | solution.py:1102
  188.6 0.8 slice.214
  189.6 0.6 copy.41
  190.4 1.2 maximum_select_fusion.refs_5_
  191.6 77.4 %hidden0.1 = (f32[1536,1280]{1,0:T(8,128)}, f32[1536,1280]{1,0:T(8,128)}, bf16[1280,1024]{1,0:T(8,128)(2,1)}, bf16[1024,1280]{1,0:T(8,128)(2,1)}, f32[1,1024]{1,...) custom-call(bf16[1536,1280]{1,0:T(8,128)(2,1)} %get-tuple-element.89.refs_0_, ...), custom_call_target="tpu_custom_call" | custom-call | flops 24159191040 | bytes 34078720 | tf_op jit(solution)/shard_map/hidden0/pallas_call | solution.py:1204
  269.0 0.6 copy.42
  269.6 61.2 %hidden1.1 = (bf16[1536,1280]{1,0:T(8,128)(2,1)}, bf16[1536,1280]{1,0:T(8,128)(2,1)}, bf16[1280,1536]{1,0:T(8,128)(2,1)}, bf16[1536,1280]{1,0:T(8,128)(2,1)}, f3...) custom-call(bf16[1536,1280]{1,0:T(8,128)(2,1)} %get-tuple-element.89.refs_0_, ...), custom_call_target="tpu_custom_call" | custom-call | flops 36238786560 | bytes 39321600 | tf_op jit(solution)/shard_map/hidden1/pallas_call | solution.py:1204
  330.9 43.3 %second_back.1 = (f32[1536,1280]{1,0:T(8,128)}, bf16[1536,768]{1,0:T(8,128)(2,1)}, bf16[640,1280]{1,0:T(8,128)(2,1)}, f32[8,1280]{1,0:T(8,128)}, bf16[768,1280]{...) custom-call(f32[1536,1280]{1,0:T(8,128)} %get-tuple-element.88.refs_0_, ...), custom_call_target="tpu_custom_call" | custom-call | flops 5033164800 | bytes 27525120 | tf_op jit(solution)/shard_map/second_back/pallas_call | solution.py:1337
  374.2 85.5 %attend_back.1 = (bf16[1536,1920]{1,0:T(8,128)(2,1)}, f32[1,1920]{1,0:T(1,128)}, bf16[384,1280]{1,0:T(8,128)(2,1)}, bf16[160,1280]{1,0:T(8,128)(2,1)}, bf16[2,38...) custom-call(s32[1]{0:T(128)} %bitcast.refs_0_, ...), custom_call_target="tpu_custom_call" | custom-call | flops 48318382080 | bytes 23592960 | tf_op jit(solution)/shard_map/attend_back/pallas_call | solution.py:1028
  459.8 0.5 broadcast.55
  460.3 0.7 reduce.24
  461.1 0.7 slice_reduce_fusion.1
  462.3 0.7 select_maximum_fusion.refs_3_
  462.9 101.3 %back.1 = (bf16[2,384,1280]{2,1,0:T(8,128)(2,1)}, f32[2,24,1280]{2,1,0:T(8,128)}, bf16[2,320,1920]{2,1,0:T(8,128)(2,1)}, bf16[2,192,1280]{2,1,0:T(8,128)(2,1)}, ...) custom-call(bf16[1536,1920]{1,0:T(8,128)(2,1)} %get-tuple-element.111.refs_0_, ...), custom_call_target="tpu_custom_call" | custom-call | flops 15099494400 | bytes 39321600 | tf_op jit(solution)/shard_map/back/pallas_call | solution.py:1630
  564.3 1.7 dynamic-slice_reduce_fusion
  565.9 11.4 %place.1 = (f32[320,5120]{1,0:T(8,128)}, f32[1280,1280]{1,0:T(8,128)}, f32[320,1280]{1,0:T(8,128)}, f32[320,1280]{1,0:T(8,128)}, f32[320,1280]{1,0:T(8,128)}, /*index=5*/f32[320,1280]{1,0:T(8,128)}) custom-call(bf16[2,160,1024]{2,1,0:T(8,128)(2,1)} %get-tuple-element.125.refs_0_, bf16[2,160,1024]{2,1,0:T(8,128)(2,1)} %get-tuple-element.126.refs_1_, ...), custom_call_target="tpu_custom_call" | custom-call | tf_op jit(solution)/shard_map/place/pallas_call | solution.py:1704
  577.3 0.9 constant_dynamic-slice_fusion.1
  578.3 0.7 dynamic_slice.21
  578.9 1.3 copy.53
  580.2 1.0 copy-done.4
  581.2 1.3 copy.54
  (50 shorter events, 2.1 us)
Async XLA Ops:
  0.7 3.5 copy-start.1
  4.6 2.1 copy-start.2
  8.5 79.1 %slice-start = ((f32[16,384]{1,0:T(8,128)}), f32[1,384]{1,0:T(1,128)S(1)}, s32[]{:S(2)}) async-start(f32[16,384]{1,0:T(8,128)} %pack.1.refs_1_.refs_5_), calls=%async_computation | async-start | bytes 3072 | tf_op jit(solution)/shard_map/slice | solution.py:1814
  8.5 81.0 %copy-start = (bf16[320,5120]{1,0:T(8,128)(2,1)S(1)}, bf16[320,5120]{1,0:T(8,128)(2,1)}, u32[]{:S(2)}) copy-start(bf16[320,5120]{1,0:T(8,128)(2,1)} %param.32) | copy-start | bytes 9830404
  90.6 56.9 %copy-start.8 = (s32[2]{0:T(128)S(1)}, s32[2]{0:T(128)}, u32[]{:S(2)}) copy-start(s32[2]{0:T(128)} %refs_9_.1) | copy-start | bytes 28
  374.2 85.5 %copy-start.6 = (f32[1,1536]{1,0:T(1,128)S(1)}, f32[1,1536]{1,0:T(1,128)}, u32[]{:S(2)}) copy-start(f32[1,1536]{1,0:T(1,128)} %get-tuple-element.116) | copy-start | bytes 18436
  374.2 86.1 %copy-start.7 = (f32[1,1024]{1,0:T(1,128)S(1)}, f32[1,1024]{1,0:T(1,128)}, u32[]{:S(2)}) copy-start(f32[1,1024]{1,0:T(1,128)} %get-tuple-element.115) | copy-start | bytes 12292
  374.2 86.9 %copy-start.5 = (f32[8,1280]{1,0:T(8,128)S(1)}, f32[8,1280]{1,0:T(8,128)}, u32[]{:S(2)}) copy-start(f32[8,1280]{1,0:T(8,128)} %get-tuple-element.114) | copy-start | bytes 122884
  565.9 13.0 %copy-start.3 = (bf16[2,384,1280]{2,1,0:T(8,128)(2,1)S(1)}, bf16[2,384,1280]{2,1,0:T(8,128)(2,1)}, u32[]{:S(2)}) copy-start(bf16[2,384,1280]{2,1,0:T(8,128)(2,1)} %get-tuple-element.210) | copy-start | bytes 5898244
  578.9 2.3 copy-start.4

commit v7 on v6

--- a/solution.py
+++ b/solution.py
@@ -762,10 +762,10 @@
 def first_kernel(*refs, jobs, size):
     count = len(jobs.jobs)
     srcs, mine = refs[:count], refs[count]
-    h_ref, *heads, vec_ref = refs[count + 1 : count + 6]
+    *results, vec_ref = refs[count + 1 : count + 6]
     dsts, other = refs[count + 6 : 2 * count + 6], refs[2 * count + 6]
-    x, small, weight, bias, sems = refs[2 * count + 7 : 2 * count + 12]
-    link, bound, _ = jobs.bind(refs[2 * count + 12 :], srcs, dsts)
+    x, small, weight, bias, sems, h_ref, *heads = refs[2 * count + 7 : 2 * count + 16]
+    link, bound, _ = jobs.bind(refs[2 * count + 16 :], srcs, dsts)
     tokens, smalls, *gathers = bound
     slot = link.slots(1)
     swap = link.remote(mine, other, slot, slot, link.sibling())
@@ -776,6 +776,8 @@
     def load(src, dst, i):
         return pltpu.make_async_copy(src, dst, sems.at[i])
 
+    first_store = 1 + small.shape[0]
+    stores = [load(a, b, first_store + i) for i, (a, b) in enumerate(zip([h_ref] + heads, results))]
     link.meet_plane(jobs.pairs)
     steps = gather_steps(gathers)
     swap.start()
@@ -803,6 +805,7 @@
         return carry
 
     lax.fori_loop(0, n // ROWS, norm, 0)
+    stores[0].start()
     for ref in heads:
         ref[:, width:] = jnp.zeros((n, ref.shape[1] - width), bf16)
     for i, (gather, ref) in enumerate(zip(gathers, heads)):
@@ -820,7 +823,10 @@
             return carry
 
         lax.fori_loop(0, n // ROWS, project, 0)
+        stores[1 + i].start()
     swap.wait()
+    for c in stores:
+        c.wait()
 
 
 def first_call(jobs, small, wide, number):
@@ -832,7 +838,7 @@
     return pl.pallas_call(
         functools.partial(first_kernel, jobs=jobs, size=d // groups),
         in_specs=jobs.in_specs() + [hbm],
-        out_specs=[vmem] * 5 + jobs.in_specs() + [hbm],
+        out_specs=[hbm] * 4 + [vmem] + jobs.in_specs() + [hbm],
         out_shape=[jax.ShapeDtypeStruct((n, d), bf16), head, head, head, jax.ShapeDtypeStruct((16, d), f32)]
         + jobs.out_shapes()
         + [jax.ShapeDtypeStruct(small.shape, small.dtype)],
@@ -841,8 +847,10 @@
             pltpu.VMEM((groups,) + small.shape, f32),
             pltpu.VMEM((3, d, width), bf16),
             pltpu.VMEM((1, 3 * width), f32),
-            pltpu.SemaphoreType.DMA((1 + groups,)),
+            pltpu.SemaphoreType.DMA((5 + groups,)),
+            pltpu.VMEM((n, d), bf16),
         ]
+        + [pltpu.VMEM((n, wide), bf16)] * 3
         + jobs.scratch(1),
         compiler_params=comm_params(number),
         cost_estimate=cost(6 * n * d * width, 12 * n * d),
@@ -1051,12 +1059,14 @@
 def middle_kernel(*refs, jobs):
     count = len(jobs.jobs)
     o_ref, w_ref, x_ref, vec_ref = refs[:4]
-    mid_ref, h_ref, owide_ref = refs[4 + count : 7 + count]
-    mine, other = refs[7 + 2 * count : 9 + 2 * count]
-    link, bound, _ = jobs.bind(refs[9 + 2 * count :], refs[4 : 4 + count], refs[7 + count : 7 + 2 * count])
+    results = refs[4 + count : 7 + count]
+    mid_ref, h_ref, owide_ref, mine, other = refs[7 + 2 * count : 12 + 2 * count]
+    link, bound, _ = jobs.bind(refs[12 + 2 * count :], refs[4 : 4 + count], refs[7 + count : 7 + 2 * count])
     n = x_ref.shape[0]
     width = o_ref.shape[1]
     base = link.slots(n // ROWS)
+    keep = link.local_slots(3)
+    stores = [link.here(a, b, keep + i) for i, (a, b) in enumerate(zip((mid_ref, h_ref, owide_ref), results))]
     link.meet_plane(jobs.pairs)
     for job in bound:
         job.start()
@@ -1085,7 +1095,10 @@
     lax.fori_loop(0, n // ROWS, project, 0)
     owide_ref[:, :width] = o_ref[...]
     owide_ref[:, width:] = jnp.zeros((n, owide_ref.shape[1] - width), bf16)
+    stores[2].start()
     lax.fori_loop(0, n // ROWS, norm, 0)
+    stores[0].start()
+    stores[1].start()
     for i in range(n // ROWS):
         swap(i)[1].wait_send()
     for job in bound:
@@ -1094,6 +1107,8 @@
         job.inward()
     for job in bound:
         job.finish()
+    for c in stores:
+        c.wait()
 
 
 def middle_call(o, w, x, vec, wide, jobs, number):
@@ -1102,14 +1117,16 @@
     return pl.pallas_call(
         functools.partial(middle_kernel, jobs=jobs),
         in_specs=[vmem] * 4 + jobs.in_specs(),
-        out_specs=[vmem] * 3 + jobs.in_specs(),
+        out_specs=[pl.BlockSpec(memory_space=pl.ANY)] * 3 + jobs.in_specs(),
         out_shape=[
             jax.ShapeDtypeStruct((n, d), f32),
             jax.ShapeDtypeStruct((n, d), bf16),
             jax.ShapeDtypeStruct((n, wide), bf16),
         ]
         + jobs.out_shapes(),
-        scratch_shapes=[pltpu.VMEM((n, d), bf16)] * 2 + jobs.scratch(n // ROWS),
+        scratch_shapes=[pltpu.VMEM((n, d), f32), pltpu.VMEM((n, d), bf16), pltpu.VMEM((n, wide), bf16)]
+        + [pltpu.VMEM((n, d), bf16)] * 2
+        + jobs.scratch(n // ROWS),
         compiler_params=comm_params(number),
         cost_estimate=cost(2 * n * w.size, 14 * n * d),
         name="middle",
@@ -1127,9 +1144,15 @@
     out_ref, dh_ref, dup_ref, ddn_ref, dub_ref = refs[:5]
     dsts, refs = refs[5 : 5 + count], refs[5 + count :]
     ht, act, grad = refs[:3]
-    acc, dh = refs[3:5] if last else (out_ref, dh_ref)
-    refs = refs[5:] if last else refs[3:]
-    link, bound, refs = jobs.bind(refs, srcs, dsts)
+    acc, dh = refs[3:5]
+    link, bound, (sem,) = jobs.bind(refs[5:], srcs, dsts)
+    loads = stores = []
+    if chained:
+        pairs = ((old_out, acc), (old_dh, dh))
+        loads = [pltpu.make_async_copy(a, b, sem.at[i]) for i, (a, b) in enumerate(pairs)]
+    if not last:
+        pairs = ((acc, out_ref), (dh, dh_ref))
+        stores = [pltpu.make_async_copy(a, b, sem.at[2 + i]) for i, (a, b) in enumerate(pairs)]
     gathers, others = split_gathers(bound)
     steps = gather_steps(gathers)
     t = pl.program_id(0)
@@ -1141,16 +1164,9 @@
         link.meet_plane(jobs.pairs)
         run([job.start for job in others] + steps[0])
         if chained:
-            sem = refs[0]
-            copies = [
-                pltpu.make_async_copy(src, dst, sem.at[i])
-                for i, (src, dst) in enumerate(((old_out, acc), (old_dh, dh)))
-            ]
-            for c in copies:
+            for c in loads:
                 c.start()
             ht[...] = h_ref[...].T
-            for c in copies:
-                c.wait()
         else:
             ht[...] = h_ref[...].T
             acc[...] = jnp.zeros_like(acc)
@@ -1172,6 +1188,13 @@
         da = (dot_nt(dz_ref[rows, :], dn_ref[...]) * slope).astype(bf16)
         act[rows, :] = g
         grad[rows, :] = da
+        if chained:
+
+            @pl.when((t == 0) & (i == 0))
+            def _():
+                for c in loads:
+                    c.wait()
+
         acc[rows, :] += dot(g, dn_ref[...])
         dh[rows, :] += dot_nt(da, up_ref[...])
         return carry
@@ -1189,9 +1212,13 @@
         if last:
             out_ref[...] = acc[...].astype(out_ref.dtype)
             dh_ref[...] = dh[...].astype(dh_ref.dtype)
+        for c in stores:
+            c.start()
         for some in steps[3:]:
             run(some)
         run([job.finish for job in bound])
+        for c in stores:
+            c.wait()
 
 
 def ffn_call(h, dz, up, bias, down, old, last, jobs, number, name):
@@ -1213,9 +1240,8 @@
         ]
         + ([pl.BlockSpec(memory_space=pl.ANY)] * 2 if chained else [])
         + jobs.in_specs(),
-        out_specs=[
-            kept,
-            kept,
+        out_specs=([kept] * 2 if last else [pl.BlockSpec(memory_space=pl.ANY)] * 2)
+        + [
             pl.BlockSpec((d, bt), lambda t: (0, t)),
             pl.BlockSpec((bt, d), lambda t: (t, 0)),
             pl.BlockSpec((1, bt), lambda t: (0, t)),
@@ -1231,9 +1257,9 @@
         + jobs.out_shapes(),
         scratch_shapes=[pltpu.VMEM((d, n), bf16)]
         + [pltpu.VMEM((n, bt), bf16)] * 2
-        + ([pltpu.VMEM((n, d), f32)] * 2 if last else [])
+        + [pltpu.VMEM((n, d), f32)] * 2
         + jobs.scratch()
-        + ([pltpu.SemaphoreType.DMA((2,))] if chained else []),
+        + [pltpu.SemaphoreType.DMA((4,))],
         compiler_params=comm_params(number),
         cost_estimate=cost(12 * n * d * hidden, 8 * d * hidden + 12 * n * d),
         name=name,
@@ -1484,12 +1510,13 @@
 
 def back_kernel(*refs, jobs):
     count = len(jobs.jobs)
-    g_ref, vec_ref, h_ref, early_ref, *w_refs = refs[:7]
+    g_ref, vec_ref, h_ref, early_ref, *w_anys = refs[:7]
     x_any, dmid_any = refs[7:9]
     tokens_any, small_ref, both_any = refs[9 + count : 12 + count]
     rest = list(refs[12 + 2 * count :])
     x, dmid, mine, other, dx, dw, own, total, came, stage = rest[:10]
     rest = rest[10:]
+    w_refs, rest = rest[:3], rest[3:]
     small_bufs, rest = rest[:3], rest[3:]
     reduce_bufs, rest = [rest[10 * i : 10 * i + 10] for i in range(3)], rest[30:]
     chain_bufs, rest = [rest[3 * i : 3 * i + 3] for i in range(6)], rest[18:]
@@ -1508,13 +1535,14 @@
             last.append(Chain(link, own.at[c, rows], both_any.at[:, rows, cols], chain_bufs[len(last)]))
     to_owners = FromClip(link, dx, tokens_any, [stage])
     base = link.slots(half)
-    keep = link.local_slots(2)
+    keep = link.local_slots(5)
     swap_base = link.slots(3)
     peers = [link.sibling()] + [(link.rep, link.shard ^ bit) for bit in (1, 2)]
     swaps = [link.remote(total, came.at[i], swap_base + i, swap_base + i, to) for i, to in enumerate(peers)]
     small = Chain(link, total, small_ref, small_bufs)
     mine_rows = pl.ds(pl.multiple_of(link.core * size, size), size)
     loads = [link.here(x_any.at[mine_rows], x, keep), link.here(dmid_any.at[mine_rows], dmid, keep + 1)]
+    loads += [link.here(a, b, keep + 2 + i) for i, (a, b) in enumerate(zip(w_anys, w_refs))]
     for c in loads:
         c.start()
     link.meet_all()
@@ -1570,9 +1598,9 @@
     run(steps[0])
     total[:first, :] = early_ref[...]
     total[first:, :] = jnp.zeros((total.shape[0] - first, d), f32)
-    lax.fori_loop(0, half, send, 0)
     for c in loads:
         c.wait()
+    lax.fori_loop(0, half, send, 0)
     reduces[0].forward()
     after = {0: steps[1] + [reduces[1].forward], 1: [reduces[2].forward]}
     for j in range(half):
@@ -1629,7 +1657,7 @@
     hbm = pl.BlockSpec(memory_space=pl.ANY)
     return pl.pallas_call(
         functools.partial(back_kernel, jobs=jobs),
-        in_specs=[vmem] * 7 + [hbm] * 2 + jobs.in_specs(),
+        in_specs=[vmem] * 4 + [hbm] * 5 + jobs.in_specs(),
         out_specs=[hbm, vmem, hbm] + jobs.in_specs(),
         out_shape=[
             jax.ShapeDtypeStruct((clips, size // clips, d), bf16),
@@ -1649,6 +1677,7 @@
             pltpu.VMEM((3, rows, d), f32),
             pltpu.VMEM((size // clips, d), bf16),
         ]
+        + [pltpu.VMEM((d, width), bf16)] * 3
         + [small] * 3
         + [pltpu.VMEM((owned // 2, width), bf16)] * 48
         + jobs.scratch(80),

time: 587 us -> 572 us (0.974)
  Pallas kernels: 554 us -> 540 us
    pallas_call x2, Pallas kernels: 139 us -> 132 us  [ffn_call(): pl.pallas_call(functools.partial(ffn_kernel, chained=chained, last=last,...]
where the time goes in v7:
time: 572 us; the launch traced here: 568 us
  Pallas kernels  540 us (94%)
  local copies, waits for them, and re-layouts  15.1 us (3%)
  other arithmetic  11.3 us (2%)
    pallas_call x2, Pallas kernels, ffn_call(): pl.pallas_call(functools.partial(ffn_kernel, chained=chained, last=last,...  132 us
    pallas_call x1, Pallas kernels, back_call(): pl.pallas_call(functools.partial(back_kernel, jobs=jobs), in_specs=[vmem]...  100 us
    pallas_call x1, Pallas kernels, attn_bwd_call(): pl.pallas_call(functools.partial(attn_bwd_kernel, bk=256, jobs=jobs), gri...  85.4 us
    pallas_call x1, Pallas kernels, first_call(): pl.pallas_call(functools.partial(first_kernel, jobs=jobs, size=d // group...  76.7 us
    pallas_call x1, Pallas kernels, attn_fwd_call(): pl.pallas_call(functools.partial(attn_fwd_kernel, bq=256, jobs=jobs), gri...  56.8 us
    pallas_call x1, Pallas kernels, second_back_call(): pl.pallas_call(functools.partial(second_back_kernel, jobs=jobs), grid=(n...  43.2 us
    pallas_call x1, Pallas kernels, middle_call(): pl.pallas_call(functools.partial(middle_kernel, jobs=jobs), in_specs=[vme...  32.8 us

profile of v7, /device:TPU:0, one launch (start us, length us, event | category | flops | bytes accessed | tf_op | source)
XLA Modules:
  0.0 568.3 jit_solution(13511055741690442360)
XLA Ops:
  0.7 1.6 pack.1.refs_1_.refs_5_
  2.3 1.9 fusion.4
  4.6 2.1 maximum_select_fusion.2
  7.2 1.3 maximum_select_fusion.4.refs_4_
  8.5 76.7 %first.1 = (bf16[1536,1280]{1,0:T(8,128)(2,1)}, bf16[1536,768]{1,0:T(8,128)(2,1)}, bf16[1536,768]{1,0:T(8,128)(2,1)}, bf16[1536,768]{1,0:T(8,128)(2,1)}, f32[16,...) custom-call(bf16[2,384,1280]{2,1,0:T(8,128)(2,1)} %refs_0_.3, ...), custom_call_target="tpu_custom_call" | custom-call | flops 7549747200 | bytes 23592960 | tf_op jit(solution)/shard_map/first/pallas_call | solution.py:838
  85.2 0.7 slice.205
  85.9 0.6 constant_dynamic-slice_fusion.3
  86.5 1.2 fusion.5
  88.4 1.0 maximum_select_fusion.1.refs_4_
  89.5 56.8 %attend.1 = (bf16[1536,640]{1,0:T(8,128)(2,1)}, f32[1536,128]{1,0:T(8,128)}, bf16[4,320,1024]{2,1,0:T(8,128)(2,1)}, bf16[4,256,1280]{2,1,0:T(8,128)(2,1)}, bf16[4,160,1280]{2,1,0:T(8,128)(2,1)}) custom-call(s32[1]{0:T(128)} %bitcast.refs_0_, bf16[1536,768]{1,0:T(8,128)(2,1)} %get-tuple-element.80.refs_1_, bf16[1536,768]{1,0:T(8,128)(2,1)} %get-tuple-element.81.refs_2_, ...), custom_call_target="tpu_custom_call" | custom-call | flops 19327352832 | bytes 9437184 | tf_op jit(solution)/shard_map/attend/pallas_call | solution.py:946
  146.4 3.0 broadcast_select_fusion.refs_4_
  149.4 32.8 %middle.1 = (f32[1536,1280]{1,0:T(8,128)}, bf16[1536,1280]{1,0:T(8,128)(2,1)}, bf16[1536,768]{1,0:T(8,128)(2,1)}, bf16[1536,1280]{1,0:T(8,128)(2,1)}) custom-call(bf16[1536,640]{1,0:T(8,128)(2,1)} %get-tuple-element.83.refs_0_.refs_6_, bf16[640,1280]{1,0:T(8,128)(2,1)} %bitcast.31, bf16[1536,1280]{1,0:T(8,128)(2,1)} %get-tuple-element.85.refs_2_.refs_7_, ...), custom_call_target="tpu_custom_call" | custom-call | flops 2516582400 | bytes 27525120 | tf_op jit(solution)/shard_map/middle/pallas_call | solution.py:1117
  182.3 0.8 slice.214
  183.3 0.6 copy.41
  184.1 1.2 maximum_select_fusion.refs_5_
  185.3 72.6 %hidden0.1 = (f32[1536,1280]{1,0:T(8,128)}, f32[1536,1280]{1,0:T(8,128)}, bf16[1280,1024]{1,0:T(8,128)(2,1)}, bf16[1024,1280]{1,0:T(8,128)(2,1)}, f32[1,1024]{1,...) custom-call(bf16[1536,1280]{1,0:T(8,128)(2,1)} %get-tuple-element.89.refs_0_, ...), custom_call_target="tpu_custom_call" | custom-call | flops 24159191040 | bytes 34078720 | tf_op jit(solution)/shard_map/hidden0/pallas_call | solution.py:1231
  257.9 0.6 copy.42
  258.5 59.5 %hidden1.1 = (bf16[1536,1280]{1,0:T(8,128)(2,1)}, bf16[1536,1280]{1,0:T(8,128)(2,1)}, bf16[1280,1536]{1,0:T(8,128)(2,1)}, bf16[1536,1280]{1,0:T(8,128)(2,1)}, f3...) custom-call(bf16[1536,1280]{1,0:T(8,128)(2,1)} %get-tuple-element.89.refs_0_, ...), custom_call_target="tpu_custom_call" | custom-call | flops 36238786560 | bytes 39321600 | tf_op jit(solution)/shard_map/hidden1/pallas_call | solution.py:1231
  318.0 43.2 %second_back.1 = (f32[1536,1280]{1,0:T(8,128)}, bf16[1536,768]{1,0:T(8,128)(2,1)}, bf16[640,1280]{1,0:T(8,128)(2,1)}, f32[8,1280]{1,0:T(8,128)}, bf16[768,1280]{...) custom-call(f32[1536,1280]{1,0:T(8,128)} %get-tuple-element.88.refs_0_, ...), custom_call_target="tpu_custom_call" | custom-call | flops 5033164800 | bytes 27525120 | tf_op jit(solution)/shard_map/second_back/pallas_call | solution.py:1363
  361.3 85.4 %attend_back.1 = (bf16[1536,1920]{1,0:T(8,128)(2,1)}, f32[1,1920]{1,0:T(1,128)}, bf16[384,1280]{1,0:T(8,128)(2,1)}, bf16[160,1280]{1,0:T(8,128)(2,1)}, bf16[2,38...) custom-call(s32[1]{0:T(128)} %bitcast.refs_0_, ...), custom_call_target="tpu_custom_call" | custom-call | flops 48318382080 | bytes 23592960 | tf_op jit(solution)/shard_map/attend_back/pallas_call | solution.py:1036
  446.8 0.5 broadcast.55
  447.3 0.7 reduce.24
  448.1 0.7 slice_reduce_fusion.1
  449.3 0.7 select_maximum_fusion.refs_3_
  449.9 100.0 %back.1 = (bf16[2,384,1280]{2,1,0:T(8,128)(2,1)}, f32[2,24,1280]{2,1,0:T(8,128)}, bf16[2,320,1920]{2,1,0:T(8,128)(2,1)}, bf16[2,192,1280]{2,1,0:T(8,128)(2,1)}, ...) custom-call(bf16[1536,1920]{1,0:T(8,128)(2,1)} %get-tuple-element.111.refs_0_, ...), custom_call_target="tpu_custom_call" | custom-call | flops 15099494400 | bytes 39321600 | tf_op jit(solution)/shard_map/back/pallas_call | solution.py:1658
  549.9 1.7 dynamic-slice_reduce_fusion
  551.6 11.4 %place.1 = (f32[320,5120]{1,0:T(8,128)}, f32[1280,1280]{1,0:T(8,128)}, f32[320,1280]{1,0:T(8,128)}, f32[320,1280]{1,0:T(8,128)}, f32[320,1280]{1,0:T(8,128)}, /*index=5*/f32[320,1280]{1,0:T(8,128)}) custom-call(bf16[2,160,1024]{2,1,0:T(8,128)(2,1)} %get-tuple-element.125.refs_0_, bf16[2,160,1024]{2,1,0:T(8,128)(2,1)} %get-tuple-element.126.refs_1_, ...), custom_call_target="tpu_custom_call" | custom-call | tf_op jit(solution)/shard_map/place/pallas_call | solution.py:1733
  563.0 0.9 constant_dynamic-slice_fusion.1
  563.9 0.7 dynamic_slice.21
  564.6 1.3 copy.53
  565.9 1.0 copy-done.4
  566.9 1.3 copy.54
  (50 shorter events, 2.1 us)
Async XLA Ops:
  0.7 3.5 copy-start.1
  4.6 2.1 copy-start.2
  8.5 78.0 %slice-start = ((f32[16,384]{1,0:T(8,128)}), f32[1,384]{1,0:T(1,128)S(1)}, s32[]{:S(2)}) async-start(f32[16,384]{1,0:T(8,128)} %pack.1.refs_1_.refs_5_), calls=%async_computation | async-start | bytes 3072 | tf_op jit(solution)/shard_map/slice | solution.py:1843
  8.5 79.9 %copy-start = (bf16[320,5120]{1,0:T(8,128)(2,1)S(1)}, bf16[320,5120]{1,0:T(8,128)(2,1)}, u32[]{:S(2)}) copy-start(bf16[320,5120]{1,0:T(8,128)(2,1)} %param.32) | copy-start | bytes 9830404
  89.5 56.9 %copy-start.8 = (s32[2]{0:T(128)S(1)}, s32[2]{0:T(128)}, u32[]{:S(2)}) copy-start(s32[2]{0:T(128)} %refs_9_.1) | copy-start | bytes 28
  361.2 85.5 %copy-start.6 = (f32[1,1536]{1,0:T(1,128)S(1)}, f32[1,1536]{1,0:T(1,128)}, u32[]{:S(2)}) copy-start(f32[1,1536]{1,0:T(1,128)} %get-tuple-element.116) | copy-start | bytes 18436
  361.2 86.0 %copy-start.7 = (f32[1,1024]{1,0:T(1,128)S(1)}, f32[1,1024]{1,0:T(1,128)}, u32[]{:S(2)}) copy-start(f32[1,1024]{1,0:T(1,128)} %get-tuple-element.115) | copy-start | bytes 12292
  361.3 86.8 %copy-start.5 = (f32[8,1280]{1,0:T(8,128)S(1)}, f32[8,1280]{1,0:T(8,128)}, u32[]{:S(2)}) copy-start(f32[8,1280]{1,0:T(8,128)} %get-tuple-element.114) | copy-start | bytes 122884
  551.6 13.0 %copy-start.3 = (bf16[2,384,1280]{2,1,0:T(8,128)(2,1)S(1)}, bf16[2,384,1280]{2,1,0:T(8,128)(2,1)}, u32[]{:S(2)}) copy-start(bf16[2,384,1280]{2,1,0:T(8,128)(2,1)} %get-tuple-element.210) | copy-start | bytes 5898244
  564.6 2.3 copy-start.4

commit v8 on v7

--- a/solution.py
+++ b/solution.py
@@ -889,10 +889,10 @@
 
 def attn_fwd_kernel(*refs, bq, jobs):
     count = len(jobs.jobs)
-    len_ref, q_ref, k_ref, v_ref = refs[:4]
+    len_ref, *sources = refs[:4]
     o_ref, lse_ref = refs[4 + count : 6 + count]
-    acc, kx = refs[6 + 2 * count : 8 + 2 * count]
-    link, bound, _ = jobs.bind(refs[8 + 2 * count :], refs[4 : 4 + count], refs[6 + count : 6 + 2 * count])
+    acc, kx, q_ref, k_ref, v_ref = refs[6 + 2 * count : 11 + 2 * count]
+    link, bound, _ = jobs.bind(refs[11 + 2 * count :], refs[4 : 4 + count], refs[6 + count : 6 + 2 * count])
     h = pl.program_id(0)
     heads = pl.num_programs(0)
     n = q_ref.shape[0]
@@ -901,13 +901,20 @@
     gathers, others = split_gathers(bound)
     steps = gather_steps(gathers)
 
+    keep = link.local_slots(3)
+    loads = [link.here(a, b, keep + i) for i, (a, b) in enumerate(zip(sources, (q_ref, k_ref, v_ref)))]
+
     @pl.when(h == 0)
     def _():
+        for c in loads:
+            c.start()
         link.meet_plane(jobs.pairs)
         run([job.start for job in others] + steps[0])
         acc[...] = jnp.zeros_like(acc)
         lse_ref[...] = jnp.zeros_like(lse_ref)
         kx[...] = key_extra(n, len_ref[0])
+        for c in loads:
+            c.wait()
 
     for number, some in zip((2, 4, 6, 7), steps[1:]):
 
@@ -946,10 +953,12 @@
     return pl.pallas_call(
         functools.partial(attn_fwd_kernel, bq=256, jobs=jobs),
         grid=(heads,),
-        in_specs=[pl.BlockSpec(memory_space=pltpu.SMEM)] + [whole((n, wide))] * 3 + jobs.in_specs(),
+        in_specs=[pl.BlockSpec(memory_space=pltpu.SMEM)] + [pl.BlockSpec(memory_space=pl.ANY)] * 3 + jobs.in_specs(),
         out_specs=[whole((n, width)), whole((n, 128))] + jobs.in_specs(),
         out_shape=[jax.ShapeDtypeStruct((n, width), bf16), jax.ShapeDtypeStruct((n, 128), f32)] + jobs.out_shapes(),
-        scratch_shapes=[pltpu.VMEM((n, wide), f32), pltpu.VMEM((n, WIN), bf16)] + jobs.scratch(),
+        scratch_shapes=[pltpu.VMEM((n, wide), f32), pltpu.VMEM((n, WIN), bf16)]
+        + [pltpu.VMEM((n, wide), bf16)] * 3
+        + jobs.scratch(3),
         compiler_params=comm_params(number),
         cost_estimate=cost(4 * n * n * WIN * heads, 8 * n * wide),
         name="attend",
@@ -1058,14 +1067,17 @@
 
 def middle_kernel(*refs, jobs):
     count = len(jobs.jobs)
-    o_ref, w_ref, x_ref, vec_ref = refs[:4]
+    *sources, vec_ref = refs[:4]
     results = refs[4 + count : 7 + count]
-    mid_ref, h_ref, owide_ref, mine, other = refs[7 + 2 * count : 12 + 2 * count]
-    link, bound, _ = jobs.bind(refs[12 + 2 * count :], refs[4 : 4 + count], refs[7 + count : 7 + 2 * count])
+    mid_ref, h_ref, owide_ref, mine, other, o_ref, w_ref, x_ref = refs[7 + 2 * count : 15 + 2 * count]
+    link, bound, _ = jobs.bind(refs[15 + 2 * count :], refs[4 : 4 + count], refs[7 + count : 7 + 2 * count])
     n = x_ref.shape[0]
     width = o_ref.shape[1]
     base = link.slots(n // ROWS)
-    keep = link.local_slots(3)
+    keep = link.local_slots(6)
+    loads = [link.here(a, b, keep + 3 + i) for i, (a, b) in enumerate(zip(sources, (o_ref, w_ref, x_ref)))]
+    for c in loads:
+        c.start()
     stores = [link.here(a, b, keep + i) for i, (a, b) in enumerate(zip((mid_ref, h_ref, owide_ref), results))]
     link.meet_plane(jobs.pairs)
     for job in bound:
@@ -1092,6 +1104,8 @@
         h_ref[rows, :] = (xhat * vec_ref[GAIN2] + vec_ref[SHIFT2]).astype(bf16)
         return carry
 
+    for c in loads:
+        c.wait()
     lax.fori_loop(0, n // ROWS, project, 0)
     owide_ref[:, :width] = o_ref[...]
     owide_ref[:, width:] = jnp.zeros((n, owide_ref.shape[1] - width), bf16)
@@ -1116,7 +1130,7 @@
     vmem = pl.BlockSpec(memory_space=pltpu.VMEM)
     return pl.pallas_call(
         functools.partial(middle_kernel, jobs=jobs),
-        in_specs=[vmem] * 4 + jobs.in_specs(),
+        in_specs=[pl.BlockSpec(memory_space=pl.ANY)] * 3 + [vmem] + jobs.in_specs(),
         out_specs=[pl.BlockSpec(memory_space=pl.ANY)] * 3 + jobs.in_specs(),
         out_shape=[
             jax.ShapeDtypeStruct((n, d), f32),
@@ -1126,6 +1140,7 @@
         + jobs.out_shapes(),
         scratch_shapes=[pltpu.VMEM((n, d), f32), pltpu.VMEM((n, d), bf16), pltpu.VMEM((n, wide), bf16)]
         + [pltpu.VMEM((n, d), bf16)] * 2
+        + [pltpu.VMEM(o.shape, bf16), pltpu.VMEM(w.shape, bf16), pltpu.VMEM((n, d), bf16)]
         + jobs.scratch(n // ROWS),
         compiler_params=comm_params(number),
         cost_estimate=cost(2 * n * w.size, 14 * n * d),
@@ -1135,7 +1150,7 @@
 
 def ffn_kernel(*refs, chained, last, mc, jobs):
     count = len(jobs.jobs)
-    h_ref, dz_ref, up_ref, ub_ref, dn_ref = refs[:5]
+    h_any, dz_any, up_ref, ub_ref, dn_ref = refs[:5]
     refs = refs[5:]
     if chained:
         old_out, old_dh = refs[:2]
@@ -1144,8 +1159,9 @@
     out_ref, dh_ref, dup_ref, ddn_ref, dub_ref = refs[:5]
     dsts, refs = refs[5 : 5 + count], refs[5 + count :]
     ht, act, grad = refs[:3]
-    acc, dh = refs[3:5]
-    link, bound, (sem,) = jobs.bind(refs[5:], srcs, dsts)
+    acc, dh, h_ref, dz_ref = refs[3:7]
+    link, bound, (sem,) = jobs.bind(refs[7:], srcs, dsts)
+    fetch = [pltpu.make_async_copy(a, b, sem.at[4 + i]) for i, (a, b) in enumerate(((h_any, h_ref), (dz_any, dz_ref)))]
     loads = stores = []
     if chained:
         pairs = ((old_out, acc), (old_dh, dh))
@@ -1157,20 +1173,25 @@
     steps = gather_steps(gathers)
     t = pl.program_id(0)
     tiles = pl.num_programs(0)
-    n = h_ref.shape[0]
+    n = h_any.shape[0]
 
     @pl.when(t == 0)
     def _():
+        for c in fetch:
+            c.start()
         link.meet_plane(jobs.pairs)
         run([job.start for job in others] + steps[0])
         if chained:
             for c in loads:
                 c.start()
+            fetch[0].wait()
             ht[...] = h_ref[...].T
         else:
-            ht[...] = h_ref[...].T
             acc[...] = jnp.zeros_like(acc)
             dh[...] = jnp.zeros_like(dh)
+            fetch[0].wait()
+            ht[...] = h_ref[...].T
+        fetch[1].wait()
 
     def at_tile(number, some):
         if some:
@@ -1232,8 +1253,8 @@
         functools.partial(ffn_kernel, chained=chained, last=last, mc=FFN_ROWS, jobs=jobs),
         grid=(hidden // bt,),
         in_specs=[
-            kept,
-            kept,
+            pl.BlockSpec(memory_space=pl.ANY),
+            pl.BlockSpec(memory_space=pl.ANY),
             pl.BlockSpec((d, bt), lambda t: (0, t)),
             pl.BlockSpec((1, bt), lambda t: (0, t)),
             pl.BlockSpec((bt, d), lambda t: (t, 0)),
@@ -1258,8 +1279,9 @@
         scratch_shapes=[pltpu.VMEM((d, n), bf16)]
         + [pltpu.VMEM((n, bt), bf16)] * 2
         + [pltpu.VMEM((n, d), f32)] * 2
+        + [pltpu.VMEM((n, d), bf16)] * 2
         + jobs.scratch()
-        + [pltpu.SemaphoreType.DMA((4,))],
+        + [pltpu.SemaphoreType.DMA((6,))],
         compiler_params=comm_params(number),
         cost_estimate=cost(12 * n * d * hidden, 8 * d * hidden + 12 * n * d),
         name=name,
@@ -1510,13 +1532,14 @@
 
 def back_kernel(*refs, jobs):
     count = len(jobs.jobs)
-    g_ref, vec_ref, h_ref, early_ref, *w_anys = refs[:7]
+    g_any, vec_ref, h_any, early_ref, *w_anys = refs[:7]
     x_any, dmid_any = refs[7:9]
     tokens_any, small_ref, both_any = refs[9 + count : 12 + count]
     rest = list(refs[12 + 2 * count :])
     x, dmid, mine, other, dx, dw, own, total, came, stage = rest[:10]
     rest = rest[10:]
     w_refs, rest = rest[:3], rest[3:]
+    (g_ref, h_ref), rest = rest[:2], rest[2:]
     small_bufs, rest = rest[:3], rest[3:]
     reduce_bufs, rest = [rest[10 * i : 10 * i + 10] for i in range(3)], rest[30:]
     chain_bufs, rest = [rest[3 * i : 3 * i + 3] for i in range(6)], rest[18:]
@@ -1535,7 +1558,10 @@
             last.append(Chain(link, own.at[c, rows], both_any.at[:, rows, cols], chain_bufs[len(last)]))
     to_owners = FromClip(link, dx, tokens_any, [stage])
     base = link.slots(half)
-    keep = link.local_slots(5)
+    keep = link.local_slots(7)
+    rows_in = [link.here(a, b, keep + 5 + i) for i, (a, b) in enumerate(((g_any, g_ref), (h_any, h_ref)))]
+    for c in rows_in:
+        c.start()
     swap_base = link.slots(3)
     peers = [link.sibling()] + [(link.rep, link.shard ^ bit) for bit in (1, 2)]
     swaps = [link.remote(total, came.at[i], swap_base + i, swap_base + i, to) for i, to in enumerate(peers)]
@@ -1547,6 +1573,8 @@
         c.start()
     link.meet_all()
     ready[0].start()
+    for c in rows_in:
+        c.wait()
     for c, job in zip(order, reduces):
 
         def weight(i, carry):
@@ -1657,7 +1685,7 @@
     hbm = pl.BlockSpec(memory_space=pl.ANY)
     return pl.pallas_call(
         functools.partial(back_kernel, jobs=jobs),
-        in_specs=[vmem] * 4 + [hbm] * 5 + jobs.in_specs(),
+        in_specs=[hbm, vmem, hbm, vmem] + [hbm] * 5 + jobs.in_specs(),
         out_specs=[hbm, vmem, hbm] + jobs.in_specs(),
         out_shape=[
             jax.ShapeDtypeStruct((clips, size // clips, d), bf16),
@@ -1678,6 +1706,7 @@
             pltpu.VMEM((size // clips, d), bf16),
         ]
         + [pltpu.VMEM((d, width), bf16)] * 3
+        + [pltpu.VMEM(grads.shape, bf16), pltpu.VMEM((n, d), bf16)]
         + [small] * 3
         + [pltpu.VMEM((owned // 2, width), bf16)] * 48
         + jobs.scratch(80),

time: 572 us -> 561 us (0.981)
  Pallas kernels: 540 us -> 528 us
where the time goes in v8:
time: 561 us; the launch traced here: 557 us
  Pallas kernels  528 us (94%)
  local copies, waits for them, and re-layouts  15.1 us (3%)
  other arithmetic  11.3 us (2%)
    pallas_call x2, Pallas kernels, ffn_call(): pl.pallas_call(functools.partial(ffn_kernel, chained=chained, last=last,...  128 us
    pallas_call x1, Pallas kernels, back_call(): pl.pallas_call(functools.partial(back_kernel, jobs=jobs), in_specs=[hbm,...  98 us
    pallas_call x1, Pallas kernels, attn_bwd_call(): pl.pallas_call(functools.partial(attn_bwd_kernel, bk=256, jobs=jobs), gri...  85.7 us
    pallas_call x1, Pallas kernels, first_call(): pl.pallas_call(functools.partial(first_kernel, jobs=jobs, size=d // group...  76.7 us
    pallas_call x1, Pallas kernels, attn_fwd_call(): pl.pallas_call(functools.partial(attn_fwd_kernel, bq=256, jobs=jobs), gri...  53.8 us
    pallas_call x1, Pallas kernels, second_back_call(): pl.pallas_call(functools.partial(second_back_kernel, jobs=jobs), grid=(n...  43.1 us
    pallas_call x1, Pallas kernels, middle_call(): pl.pallas_call(functools.partial(middle_kernel, jobs=jobs), in_specs=[pl....  30.5 us
    pallas_call x1, Pallas kernels, place_call(): pl.pallas_call(functools.partial(place_kernel, groups=groups), grid=(step...  11.4 us

profile of v8, /device:TPU:0, one launch (start us, length us, event | category | flops | bytes accessed | tf_op | source)
XLA Modules:
  0.0 556.8 jit_solution(7707991173807698906)
XLA Ops:
  0.7 1.6 pack.1.refs_1_.refs_5_
  2.3 1.9 fusion.4
  4.6 2.1 maximum_select_fusion.2
  7.2 1.3 maximum_select_fusion.4.refs_4_
  8.5 76.7 %first.1 = (bf16[1536,1280]{1,0:T(8,128)(2,1)}, bf16[1536,768]{1,0:T(8,128)(2,1)}, bf16[1536,768]{1,0:T(8,128)(2,1)}, bf16[1536,768]{1,0:T(8,128)(2,1)}, f32[16,...) custom-call(bf16[2,384,1280]{2,1,0:T(8,128)(2,1)} %refs_0_.3, ...), custom_call_target="tpu_custom_call" | custom-call | flops 7549747200 | bytes 23592960 | tf_op jit(solution)/shard_map/first/pallas_call | solution.py:838
  85.2 0.7 slice.205
  85.9 0.6 constant_dynamic-slice_fusion.3
  86.5 1.2 fusion.5
  88.4 1.0 maximum_select_fusion.1.refs_4_
  89.5 53.8 %attend.1 = (bf16[1536,640]{1,0:T(8,128)(2,1)}, f32[1536,128]{1,0:T(8,128)}, bf16[4,320,1024]{2,1,0:T(8,128)(2,1)}, bf16[4,256,1280]{2,1,0:T(8,128)(2,1)}, bf16[4,160,1280]{2,1,0:T(8,128)(2,1)}) custom-call(s32[1]{0:T(128)} %bitcast.refs_0_, bf16[1536,768]{1,0:T(8,128)(2,1)} %get-tuple-element.80.refs_1_, bf16[1536,768]{1,0:T(8,128)(2,1)} %get-tuple-element.81.refs_2_, ...), custom_call_target="tpu_custom_call" | custom-call | flops 19327352832 | bytes 9437184 | tf_op jit(solution)/shard_map/attend/pallas_call | solution.py:953
  143.4 3.0 broadcast_select_fusion.refs_4_
  146.4 30.5 %middle.1 = (f32[1536,1280]{1,0:T(8,128)}, bf16[1536,1280]{1,0:T(8,128)(2,1)}, bf16[1536,768]{1,0:T(8,128)(2,1)}, bf16[1536,1280]{1,0:T(8,128)(2,1)}) custom-call(bf16[1536,640]{1,0:T(8,128)(2,1)} %get-tuple-element.83.refs_0_.refs_6_, bf16[640,1280]{1,0:T(8,128)(2,1)} %bitcast.31, bf16[1536,1280]{1,0:T(8,128)(2,1)} %get-tuple-element.85.refs_2_.refs_7_, ...), custom_call_target="tpu_custom_call" | custom-call | flops 2516582400 | bytes 27525120 | tf_op jit(solution)/shard_map/middle/pallas_call | solution.py:1131
  176.9 0.8 slice.214
  178.0 0.6 copy.41
  178.8 1.2 maximum_select_fusion.refs_5_
  179.9 69.8 %hidden0.1 = (f32[1536,1280]{1,0:T(8,128)}, f32[1536,1280]{1,0:T(8,128)}, bf16[1280,1024]{1,0:T(8,128)(2,1)}, bf16[1024,1280]{1,0:T(8,128)(2,1)}, f32[1,1024]{1,...) custom-call(bf16[1536,1280]{1,0:T(8,128)(2,1)} %get-tuple-element.89.refs_0_, ...), custom_call_target="tpu_custom_call" | custom-call | flops 24159191040 | bytes 34078720 | tf_op jit(solution)/shard_map/hidden0/pallas_call | solution.py:1252
  249.8 0.6 copy.42
  250.4 57.9 %hidden1.1 = (bf16[1536,1280]{1,0:T(8,128)(2,1)}, bf16[1536,1280]{1,0:T(8,128)(2,1)}, bf16[1280,1536]{1,0:T(8,128)(2,1)}, bf16[1536,1280]{1,0:T(8,128)(2,1)}, f3...) custom-call(bf16[1536,1280]{1,0:T(8,128)(2,1)} %get-tuple-element.89.refs_0_, ...), custom_call_target="tpu_custom_call" | custom-call | flops 36238786560 | bytes 39321600 | tf_op jit(solution)/shard_map/hidden1/pallas_call | solution.py:1252
  308.3 43.1 %second_back.1 = (f32[1536,1280]{1,0:T(8,128)}, bf16[1536,768]{1,0:T(8,128)(2,1)}, bf16[640,1280]{1,0:T(8,128)(2,1)}, f32[8,1280]{1,0:T(8,128)}, bf16[768,1280]{...) custom-call(f32[1536,1280]{1,0:T(8,128)} %get-tuple-element.88.refs_0_, ...), custom_call_target="tpu_custom_call" | custom-call | flops 5033164800 | bytes 27525120 | tf_op jit(solution)/shard_map/second_back/pallas_call | solution.py:1385
  351.4 85.7 %attend_back.1 = (bf16[1536,1920]{1,0:T(8,128)(2,1)}, f32[1,1920]{1,0:T(1,128)}, bf16[384,1280]{1,0:T(8,128)(2,1)}, bf16[160,1280]{1,0:T(8,128)(2,1)}, bf16[2,38...) custom-call(s32[1]{0:T(128)} %bitcast.refs_0_, ...), custom_call_target="tpu_custom_call" | custom-call | flops 48318382080 | bytes 23592960 | tf_op jit(solution)/shard_map/attend_back/pallas_call | solution.py:1045
  437.2 0.5 broadcast.55
  437.7 0.7 reduce.24
  438.5 0.7 slice_reduce_fusion.1
  439.7 0.7 select_maximum_fusion.refs_3_
  440.4 98.0 %back.1 = (bf16[2,384,1280]{2,1,0:T(8,128)(2,1)}, f32[2,24,1280]{2,1,0:T(8,128)}, bf16[2,320,1920]{2,1,0:T(8,128)(2,1)}, bf16[2,192,1280]{2,1,0:T(8,128)(2,1)}, ...) custom-call(bf16[1536,1920]{1,0:T(8,128)(2,1)} %get-tuple-element.111.refs_0_, ...), custom_call_target="tpu_custom_call" | custom-call | flops 15099494400 | bytes 39321600 | tf_op jit(solution)/shard_map/back/pallas_call | solution.py:1686
  538.4 1.7 dynamic-slice_reduce_fusion
  540.0 11.4 %place.1 = (f32[320,5120]{1,0:T(8,128)}, f32[1280,1280]{1,0:T(8,128)}, f32[320,1280]{1,0:T(8,128)}, f32[320,1280]{1,0:T(8,128)}, f32[320,1280]{1,0:T(8,128)}, /*index=5*/f32[320,1280]{1,0:T(8,128)}) custom-call(bf16[2,160,1024]{2,1,0:T(8,128)(2,1)} %get-tuple-element.125.refs_0_, bf16[2,160,1024]{2,1,0:T(8,128)(2,1)} %get-tuple-element.126.refs_1_, ...), custom_call_target="tpu_custom_call" | custom-call | tf_op jit(solution)/shard_map/place/pallas_call | solution.py:1762
  551.4 0.9 constant_dynamic-slice_fusion.1
  552.4 0.7 dynamic_slice.21
  553.0 1.3 copy.53
  554.3 1.0 copy-done.4
  555.3 1.3 copy.54
  (50 shorter events, 2.1 us)
Async XLA Ops:
  0.7 3.5 copy-start.1
  4.6 2.1 copy-start.2
  8.5 78.0 %slice-start = ((f32[16,384]{1,0:T(8,128)}), f32[1,384]{1,0:T(1,128)S(1)}, s32[]{:S(2)}) async-start(f32[16,384]{1,0:T(8,128)} %pack.1.refs_1_.refs_5_), calls=%async_computation | async-start | bytes 3072 | tf_op jit(solution)/shard_map/slice | solution.py:1872
  8.5 79.9 %copy-start = (bf16[320,5120]{1,0:T(8,128)(2,1)S(1)}, bf16[320,5120]{1,0:T(8,128)(2,1)}, u32[]{:S(2)}) copy-start(bf16[320,5120]{1,0:T(8,128)(2,1)} %param.32) | copy-start | bytes 9830404
  89.5 53.9 %copy-start.8 = (s32[2]{0:T(128)S(1)}, s32[2]{0:T(128)}, u32[]{:S(2)}) copy-start(s32[2]{0:T(128)} %refs_9_.1) | copy-start | bytes 28
  351.4 85.7 %copy-start.6 = (f32[1,1536]{1,0:T(1,128)S(1)}, f32[1,1536]{1,0:T(1,128)}, u32[]{:S(2)}) copy-start(f32[1,1536]{1,0:T(1,128)} %get-tuple-element.116) | copy-start | bytes 18436
  351.4 86.2 %copy-start.7 = (f32[1,1024]{1,0:T(1,128)S(1)}, f32[1,1024]{1,0:T(1,128)}, u32[]{:S(2)}) copy-start(f32[1,1024]{1,0:T(1,128)} %get-tuple-element.115) | copy-start | bytes 12292
  351.4 87.0 %copy-start.5 = (f32[8,1280]{1,0:T(8,128)S(1)}, f32[8,1280]{1,0:T(8,128)}, u32[]{:S(2)}) copy-start(f32[8,1280]{1,0:T(8,128)} %get-tuple-element.114) | copy-start | bytes 122884
  540.0 13.0 %copy-start.3 = (bf16[2,384,1280]{2,1,0:T(8,128)(2,1)S(1)}, bf16[2,384,1280]{2,1,0:T(8,128)(2,1)}, u32[]{:S(2)}) copy-start(bf16[2,384,1280]{2,1,0:T(8,128)(2,1)} %get-tuple-element.210) | copy-start | bytes 5898244
  553.0 2.3 copy-start.4
